TPU v7x, 32 devices: a whole 2x2x4 slice. The times are simulated.
32 devices in a mesh: expert: 2 (over y), context: 4 (over x, core), dp: 4 (over z).
Axes of the slice: x: 2, y: 2, z: 4, core: 2. Of those that a mesh axis runs over, the one named last changes fastest.
Arguments:
- tokens: bfloat16 [8, 512, 2048], P(('expert', 'dp'), 'context'), may hold values from -6 to 6
- cotangent: float32 [8, 512, 2048], P(('expert', 'dp'), 'context'), may hold values from -6 to 6
- w_attn: float32 [2048, 8192], P(('expert', 'context', 'dp'))
- w_router: float32 [2048, 16], P(('expert', 'context', 'dp')), may hold values from -0.0625 to 0.0625
- norm_gains: float32 [4, 2048], P(None, ('expert', 'context', 'dp')), may hold values from 0.5 to 1.5
- w_experts: float32 [2048, 16, 3072], P('dp', ('expert', 'context'))
- lengths: int32 [8, 4], P(('expert', 'dp')), may hold values from 1 to 480, 512 in all within a row
- block_order: int32 [8, 8], P(('expert', 'dp')), may hold values from 0 to 7, each once within a row
- routes: int32 [8, 512, 8], P(('expert', 'dp'), 'context'), may hold values from 0 to 15, all different within a row; in each aligned block of 128 rows (0 to 127, 128 to 255, ..., all dimensions but the last counted through in order) at most 72 rows name the same one
Outputs:
- output: float32 [8, 512, 2048], P(('expert', 'dp'), 'context')
- grad_tokens: float32 [8, 512, 2048], P(('expert', 'dp'), 'context')
- grad_attn: float32 [2048, 8192], P(('expert', 'context', 'dp'))
- grad_router: float32 [2048, 16], P(('expert', 'context', 'dp'))
- grad_gains: float32 [4, 2048], P(None, ('expert', 'context', 'dp'))
- grad_experts: float32 [2048, 16, 3072], P('dp', ('expert', 'context'))
Inputs may be any that keep to these rules, and one draw needn't show every extreme that they name: `routes`: each row names 8 different experts; among the rows of one device no expert is named more than 72 times, a bound that some block reaches. A pack's lengths sum to 512; its longest document has exactly 480 positions. `block_order`: each pack's row is a permutation.
All inputs are finite; a program needn't handle non-finite values.
Results may differ from a plain program's by a relative error of at most 0.018.
Values may be sent and summed in bfloat16 or wider, within the bound.
No kernel may reach another device: no remote copies, remote signals or barrier semaphores. Data moves between devices by JAX's collectives and lax.ppermute only.
A program may use at most 384 MiB of HBM per device.

v0:
```python
import jax
import jax.numpy as jnp
from jax import lax
from jax.sharding import PartitionSpec as P

HEADS = 16


epsilon = 1e-05
rope_base = 10000.0
masked_score = -1e30


def rms_scale(values, gain_row):
    return (
        values * lax.rsqrt(jnp.mean(values * values, axis=-1, keepdims=True) + epsilon) * gain_row
    )


def rotate(values, offset, head_count):
    row_count, model_width = values.shape
    head_width = model_width // head_count
    half_width = head_width // 2
    freq_table = rope_base ** (-2.0 * jnp.arange(half_width, dtype=jnp.float32) / head_width)
    angle_table = offset.astype(jnp.float32)[:, None] * freq_table[None, :]
    cos_table = jnp.cos(angle_table)[:, None, :]
    sin_table = jnp.sin(angle_table)[:, None, :]
    split_heads = values.reshape(row_count, head_count, head_width)
    first_half = split_heads[..., :half_width]
    second_half = split_heads[..., half_width:]
    turned = jnp.concatenate(
        [
            first_half * cos_table - second_half * sin_table,
            second_half * cos_table + first_half * sin_table,
        ],
        axis=-1,
    )
    return turned.reshape(row_count, model_width)


def locate(stored_rows, doc_lens, blk_order, blk_rows):
    block_ids = stored_rows // blk_rows
    block_hits = block_ids[:, None] == jnp.arange(blk_order.shape[0], dtype=jnp.int32)[None, :]
    placed_at = (
        jnp.sum(jnp.where(block_hits, blk_order[None, :], 0), axis=1) * blk_rows
        + stored_rows % blk_rows
    )
    doc_ends = jnp.cumsum(doc_lens)
    doc_ids = jnp.sum((placed_at[:, None] >= doc_ends[None, :]).astype(jnp.int32), axis=1)
    doc_hits = doc_ids[:, None] == jnp.arange(doc_lens.shape[0], dtype=jnp.int32)[None, :]
    doc_starts = doc_ends - doc_lens
    offset = placed_at - jnp.sum(jnp.where(doc_hits, doc_starts[None, :], 0), axis=1)
    return (placed_at, doc_ids, offset)


def route_rows(slot_values):
    return lax.all_to_all(
        slot_values, ("expert", "context"), split_axis=1, concat_axis=1, tiled=True
    )


def on_device(
    tokens, cotangent, w_attn, w_router, norm_gains, w_experts, lengths, block_order, routes
):
    tok_rows = tokens.shape[1]
    model_width = tokens.shape[2]
    blk_rows = tok_rows // 2
    group_count = lax.axis_size(("expert", "context"))
    ctx_count = lax.axis_size("context")
    pack_rows = tok_rows * ctx_count
    ctx_index = lax.axis_index("context")
    doc_lens = lengths[0]
    blk_order = block_order[0]
    pick_rows = routes[0]
    top_count = pick_rows.shape[1]
    local_experts = w_experts.shape[1]
    expert_count = local_experts * group_count
    slot_cap = tok_rows * top_count * 9 // (8 * expert_count)
    ffn_width = w_experts.shape[2] // 3
    head_count = HEADS
    head_width = model_width // head_count
    score_scale = head_width ** (-0.5)
    attn_w, router_w, gain_rows = (
        lax.all_gather(
            w_attn.astype(jnp.bfloat16), ("expert", "context", "dp"), axis=0, tiled=True
        ),
        lax.all_gather(
            w_router.astype(jnp.bfloat16), ("expert", "context", "dp"), axis=0, tiled=True
        ),
        lax.all_gather(
            norm_gains.astype(jnp.bfloat16), ("expert", "context", "dp"), axis=1, tiled=True
        ),
    )
    gains_f = gain_rows.astype(jnp.float32)
    stored_rows = ctx_index * tok_rows + jnp.arange(tok_rows, dtype=jnp.int32)
    query_place, query_doc, query_offset = locate(stored_rows, doc_lens, blk_order, blk_rows)
    key_place, key_doc, key_offset = locate(
        jnp.arange(pack_rows, dtype=jnp.int32), doc_lens, blk_order, blk_rows
    )
    inputs = tokens[0].astype(jnp.float32)
    normed_one, norm_one_pull = jax.vjp(rms_scale, inputs, gains_f[0])
    normed_one_b = normed_one.astype(jnp.bfloat16)
    qkv_all = jnp.dot(
        normed_one_b, attn_w[:, : 3 * model_width], preferred_element_type=jnp.float32
    )

    def shape_rows(raw_part, gain_row):
        return rotate(rms_scale(raw_part, gain_row), query_offset, head_count)

    query_f, query_pull = jax.vjp(shape_rows, qkv_all[:, :model_width], gains_f[2])
    key_f, key_pull = jax.vjp(shape_rows, qkv_all[:, model_width : 2 * model_width], gains_f[3])
    query_b = query_f.astype(jnp.bfloat16)
    key_b = key_f.astype(jnp.bfloat16)
    value_b = qkv_all[:, 2 * model_width :].astype(jnp.bfloat16)
    all_keys, all_values = (
        lax.all_gather(key_b, "context", axis=0, tiled=True),
        lax.all_gather(value_b, "context", axis=0, tiled=True),
    )
    key_block = 512
    block_count = pack_rows // key_block
    query_heads = query_b.reshape(tok_rows, head_count, head_width)
    key_spots = key_place.reshape(block_count, key_block)
    key_docs = key_doc.reshape(block_count, key_block)

    def block_scores(key_part, spots, docs):
        raw = (
            jnp.einsum("qhd,khd->hqk", query_heads, key_part, preferred_element_type=jnp.float32)
            * score_scale
        )
        allowed = (query_doc[:, None] == docs[None, :]) & (spots[None, :] <= query_place[:, None])
        return (raw, allowed[None])

    def max_step(carry_pair, block_item):
        run_max, run_sum = carry_pair
        key_part, spots, docs = block_item
        raw, allowed = block_scores(key_part, spots, docs)
        new_max = jnp.maximum(run_max, jnp.max(jnp.where(allowed, raw, masked_score), axis=2))
        new_sum = run_sum * jnp.exp(run_max - new_max) + jnp.sum(
            jnp.where(allowed, jnp.exp(raw - new_max[:, :, None]), 0.0), axis=2
        )
        return ((new_max, new_sum), None)

    def split_keys(key_rows, value_rows):
        return (
            key_rows.reshape(block_count, key_block, head_count, head_width),
            value_rows.reshape(block_count, key_block, head_count, head_width),
        )

    key_heads, value_heads = split_keys(all_keys, all_values)
    start_max = jnp.full((head_count, tok_rows), masked_score, jnp.float32)
    start_sum = jnp.zeros((head_count, tok_rows), jnp.float32)
    (final_max, final_sum), _ = lax.scan(
        max_step, (start_max, start_sum), (key_heads, key_spots, key_docs)
    )
    log_total = final_max + jnp.log(final_sum)

    def block_probs(key_part, spots, docs):
        raw, allowed = block_scores(key_part, spots, docs)
        return jnp.where(allowed, jnp.exp(raw - log_total[:, :, None]), 0.0)

    def value_step(accum, block_item):
        key_part, value_part, spots, docs = block_item
        probs_b = block_probs(key_part, spots, docs).astype(jnp.bfloat16)
        return (
            accum
            + jnp.einsum("hqk,khd->qhd", probs_b, value_part, preferred_element_type=jnp.float32),
            None,
        )

    start_mix = jnp.zeros((tok_rows, head_count, head_width), jnp.float32)
    mixed, _ = lax.scan(value_step, start_mix, (key_heads, value_heads, key_spots, key_docs))
    mixed_b = mixed.reshape(tok_rows, model_width).astype(jnp.bfloat16)
    hidden = inputs + jnp.dot(
        mixed_b, attn_w[:, 3 * model_width :], preferred_element_type=jnp.float32
    )
    normed_two, norm_two_pull = jax.vjp(rms_scale, hidden, gains_f[1])
    normed_two_b = normed_two.astype(jnp.bfloat16)
    logits = jnp.dot(normed_two_b, router_w, preferred_element_type=jnp.float32)
    probs = jax.nn.softmax(logits, axis=-1)
    expert_ids = jnp.arange(expert_count, dtype=jnp.int32)
    pick_hits = (pick_rows[:, :, None] == expert_ids[None, None, :]).astype(jnp.float32)
    gates = jnp.sum(probs[:, None, :] * pick_hits, axis=2)
    pick_flat = pick_rows.reshape(tok_rows * top_count)
    expert_hits = (pick_flat[:, None] == expert_ids[None, :]).astype(jnp.int32)
    slot_rank = jnp.sum((jnp.cumsum(expert_hits, axis=0) - 1) * expert_hits, axis=1)
    slot_dest = (
        pick_flat % local_experts * (group_count * slot_cap)
        + pick_flat // local_experts * slot_cap
        + slot_rank
    )
    total_slots = local_experts * group_count * slot_cap
    pair_ids = jnp.arange(tok_rows * top_count, dtype=jnp.int32)
    slot_pair = jnp.zeros((total_slots,), jnp.int32).at[slot_dest].set(pair_ids)
    filled_b = (
        jnp.zeros((total_slots,), jnp.int32).at[slot_dest].set(1).astype(jnp.bfloat16)[:, None]
    )
    slot_shape = (local_experts, group_count, slot_cap, model_width)
    send_rows = (normed_two_b[slot_pair // top_count] * filled_b).reshape(slot_shape)
    received = route_rows(send_rows).reshape(local_experts, group_count * slot_cap, model_width)
    expert_w = lax.all_gather(w_experts.astype(jnp.bfloat16), "dp", axis=0, tiled=True)
    gate_up = jnp.einsum(
        "erd,dej->erj",
        received,
        expert_w[:, :, : 2 * ffn_width],
        preferred_element_type=jnp.float32,
    )
    gate_part = gate_up[..., :ffn_width]
    up_part = gate_up[..., ffn_width:]
    sigmoid_gate = jax.nn.sigmoid(gate_part)
    silu_gate = gate_part * sigmoid_gate
    activ_b = (silu_gate * up_part).astype(jnp.bfloat16)
    expert_out = jnp.einsum(
        "erf,def->erd", activ_b, expert_w[:, :, 2 * ffn_width :], preferred_element_type=jnp.float32
    ).astype(jnp.bfloat16)
    returned = route_rows(expert_out.reshape(slot_shape)).reshape(total_slots, model_width)
    picked = returned[slot_dest].reshape(tok_rows, top_count, model_width).astype(jnp.float32)
    output = hidden + jnp.sum(gates[:, :, None] * picked, axis=1)
    grad_out = cotangent[0]
    grad_gates = jnp.sum(picked * grad_out[:, None, :], axis=2)
    pair_grad = (
        (gates[:, :, None] * grad_out[:, None, :])
        .astype(jnp.bfloat16)
        .reshape(tok_rows * top_count, model_width)
    )
    slot_grad = (pair_grad[slot_pair] * filled_b).reshape(slot_shape)
    grad_rows = route_rows(slot_grad).reshape(local_experts, group_count * slot_cap, model_width)
    expert_again = lax.all_gather(w_experts.astype(jnp.bfloat16), "dp", axis=0, tiled=True)
    grad_activ = jnp.einsum(
        "erd,def->erf",
        grad_rows,
        expert_again[:, :, 2 * ffn_width :],
        preferred_element_type=jnp.float32,
    )
    grad_gate = grad_activ * up_part * sigmoid_gate * (1.0 + gate_part * (1.0 - sigmoid_gate))
    grad_up = grad_activ * silu_gate
    grad_gu_b = jnp.concatenate([grad_gate, grad_up], axis=-1).astype(jnp.bfloat16)
    grad_received = jnp.einsum(
        "erj,dej->erd",
        grad_gu_b,
        expert_again[:, :, : 2 * ffn_width],
        preferred_element_type=jnp.float32,
    ).astype(jnp.bfloat16)
    first_term = jnp.einsum("erd,erj->dej", received, grad_gu_b, preferred_element_type=jnp.float32)
    second_term = jnp.einsum("erd,erf->def", grad_rows, activ_b, preferred_element_type=jnp.float32)
    grad_experts = lax.psum_scatter(
        jnp.concatenate([first_term, second_term], axis=2).astype(jnp.bfloat16),
        "dp",
        scatter_dimension=0,
        tiled=True,
    ).astype(jnp.float32)
    back_rows = route_rows(grad_received.reshape(slot_shape)).reshape(total_slots, model_width)
    grad_normed_two = jnp.sum(
        back_rows[slot_dest].reshape(tok_rows, top_count, model_width).astype(jnp.float32), axis=1
    )
    grad_probs = jnp.sum(grad_gates[:, :, None] * pick_hits, axis=1)
    grad_logits_b = (
        probs * (grad_probs - jnp.sum(probs * grad_probs, axis=-1, keepdims=True))
    ).astype(jnp.bfloat16)
    grad_normed_two = grad_normed_two + jnp.einsum(
        "te,de->td", grad_logits_b, router_w, preferred_element_type=jnp.float32
    )
    router_term = jnp.einsum(
        "td,te->de", normed_two_b, grad_logits_b, preferred_element_type=jnp.float32
    )
    grad_hidden_norm, grad_gain_two = norm_two_pull(grad_normed_two)
    grad_hidden = grad_out + grad_hidden_norm
    grad_hidden_b = grad_hidden.astype(jnp.bfloat16)
    grad_mixed_b = jnp.einsum(
        "te,de->td", grad_hidden_b, attn_w[:, 3 * model_width :], preferred_element_type=jnp.float32
    ).astype(jnp.bfloat16)
    grad_mixed_heads = grad_mixed_b.reshape(tok_rows, head_count, head_width)
    keys_back, values_back = (
        lax.all_gather(key_b, "context", axis=0, tiled=True),
        lax.all_gather(value_b, "context", axis=0, tiled=True),
    )
    key_heads, value_heads = split_keys(keys_back, values_back)

    def delta_step(accum, block_item):
        key_part, value_part, spots, docs = block_item
        probs_f = block_probs(key_part, spots, docs)
        grad_pr = jnp.einsum(
            "qhd,khd->hqk", grad_mixed_heads, value_part, preferred_element_type=jnp.float32
        )
        return (accum + jnp.sum(probs_f * grad_pr, axis=2), None)

    start_delta = jnp.zeros((head_count, tok_rows), jnp.float32)
    row_delta, _ = lax.scan(delta_step, start_delta, (key_heads, value_heads, key_spots, key_docs))

    def grad_step(accum, block_item):
        key_part, value_part, spots, docs = block_item
        probs_f = block_probs(key_part, spots, docs)
        grad_pr = jnp.einsum(
            "qhd,khd->hqk", grad_mixed_heads, value_part, preferred_element_type=jnp.float32
        )
        grad_scores = (probs_f * (grad_pr - row_delta[:, :, None])).astype(jnp.bfloat16)
        new_accum = (
            accum
            + jnp.einsum("hqk,khd->qhd", grad_scores, key_part, preferred_element_type=jnp.float32)
            * score_scale
        )
        key_grad = (
            jnp.einsum("hqk,qhd->khd", grad_scores, query_heads, preferred_element_type=jnp.float32)
            * score_scale
        )
        value_grad = jnp.einsum(
            "hqk,qhd->khd",
            probs_f.astype(jnp.bfloat16),
            grad_mixed_heads,
            preferred_element_type=jnp.float32,
        )
        return (new_accum, (key_grad, value_grad))

    grad_query, (key_grads, value_grads) = lax.scan(
        grad_step, start_mix, (key_heads, value_heads, key_spots, key_docs)
    )
    grad_key_local, grad_value_local = (
        lax.psum_scatter(
            key_grads.reshape(pack_rows, model_width).astype(jnp.bfloat16),
            "context",
            scatter_dimension=0,
            tiled=True,
        ).astype(jnp.float32),
        lax.psum_scatter(
            value_grads.reshape(pack_rows, model_width).astype(jnp.bfloat16),
            "context",
            scatter_dimension=0,
            tiled=True,
        ).astype(jnp.float32),
    )
    grad_query_raw, grad_gain_query = query_pull(grad_query.reshape(tok_rows, model_width))
    grad_key_raw, grad_gain_key = key_pull(grad_key_local)
    grad_qkv_b = jnp.concatenate([grad_query_raw, grad_key_raw, grad_value_local], axis=-1).astype(
        jnp.bfloat16
    )
    first_term = jnp.einsum(
        "td,tj->dj", normed_one_b, grad_qkv_b, preferred_element_type=jnp.float32
    )
    second_term = jnp.einsum(
        "td,tj->dj", mixed_b, grad_hidden_b, preferred_element_type=jnp.float32
    )
    grad_attn = lax.psum_scatter(
        jnp.concatenate([first_term, second_term], axis=1),
        ("expert", "context", "dp"),
        scatter_dimension=0,
        tiled=True,
    )
    grad_normed_one = jnp.einsum(
        "tj,dj->td", grad_qkv_b, attn_w[:, : 3 * model_width], preferred_element_type=jnp.float32
    )
    grad_input_norm, grad_gain_one = norm_one_pull(grad_normed_one)
    grad_tokens = grad_hidden + grad_input_norm
    gains_term = jnp.stack([grad_gain_one, grad_gain_two, grad_gain_query, grad_gain_key], axis=0)
    grad_router, grad_gains = (
        lax.psum_scatter(router_term, ("expert", "context", "dp"), scatter_dimension=0, tiled=True),
        lax.psum_scatter(gains_term, ("expert", "context", "dp"), scatter_dimension=1, tiled=True),
    )
    return (output[None], grad_tokens[None], grad_attn, grad_router, grad_gains, grad_experts)


def solution(mesh):
    in_specs = (
        P(("expert", "dp"), "context", None),
        P(("expert", "dp"), "context", None),
        P(("expert", "context", "dp"), None),
        P(("expert", "context", "dp"), None),
        P(None, ("expert", "context", "dp")),
        P("dp", ("expert", "context"), None),
        P(("expert", "dp"), None),
        P(("expert", "dp"), None),
        P(("expert", "dp"), "context", None),
    )
    out_specs = (
        P(("expert", "dp"), "context", None),
        P(("expert", "dp"), "context", None),
        P(("expert", "context", "dp"), None),
        P(("expert", "context", "dp"), None),
        P(None, ("expert", "context", "dp")),
        P("dp", ("expert", "context"), None),
    )
    return jax.shard_map(
        on_device, mesh=mesh, in_specs=in_specs, out_specs=out_specs, check_vma=False
    )
```

profile of v0, /device:TPU:0, one launch (start us, length us, event | category | flops | bytes accessed | tf_op | source)
XLA Modules:
  0.0 3075.2 jit_solution(17597594091256441848)
XLA Ops:
  7.3 2.7 convert_element_type.146
  10.1 70.9 %all-gather = bf16[32,64,4]{1,2,0:T(4,128)(2,1)S(1)} all-gather(bf16[1,64,4]{1,2,0:T(4,128)(2,1)S(1)} %convert_bitcast_fusion.3), channel_id=1, replica_groups=mesh['expert'=2,'context'=4,'dp'=4] {'expert','context','dp'}, dimensions={0}, use_global_device_ids=true | all-gather | bytes 16896 | tf_op jit(solution)/shard_map/all_gather | solution.py:90
  82.2 127.2 %all-gather.7.cloned.1.call-done = bf16[2048,8192]{1,0:T(8,128)(2,1)} async-done(((bf16[64,8192]{1,0:T(8,128)(2,1)}), bf16[2048,8192]{1,0:T(8,128)(2,1)}) %all-gather.7.cloned.1.call-update) | async-done | bytes 33554448 | tf_op jit(solution)/shard_map/all_gather | solution.py:84
  209.4 10.2 fusion.2
  222.0 2.4 subtract_convert_fusion.1
  225.5 2.0 copy.222
  228.6 11.0 copy.309
  240.7 4.5 reduce-window.11
  245.7 4.6 scatter_custom_fusion.1
  250.4 4.3 scatter_custom_fusion
  254.8 90.8 %all-gather.1 = bf16[32,64,16]{1,2,0:T(8,128)(2,1)S(1)} all-gather(bf16[1,64,16]{1,2,0:T(8,128)(2,1)S(1)} %convert_bitcast_fusion.2), channel_id=1, replica_groups=mesh['expert'=2,'context'=4,'dp'=4] {'expert','context','dp'}, dimensions={0}, use_global_device_ids=true | all-gather | bytes 67584 | tf_op jit(solution)/shard_map/all_gather | solution.py:87
  346.2 2.7 select_reduce_fusion.1
  348.9 2.1 copy-done.2
  352.4 4.3 fusion.40
  356.7 4.9 multiply_reduce_fusion.5
  363.3 6.0 gather_fusion
  369.3 2.4 fusion.10
  371.7 13.4 gather_fusion.2
  385.1 6.8 copy_multiply_fusion
  391.9 76.3 %all_to_all.20 = bf16[2,8,72,2048]{3,2,0,1:T(8,128)(2,1)} all-to-all(bf16[2,8,72,2048]{3,2,0,1:T(8,128)(2,1)S(1)} %get-tuple-element.227), channel_id=1, replica_groups=mesh['expert'=2,'context'=4,'dp'=4] {'expert','context'}, dimensions={1} | all-to-all | bytes 9437184 | tf_op jit(solution)/shard_map/all_to_all | solution.py:57
  468.3 16.2 all-to-all-start
  484.5 5.2 copy.240
  489.7 49.3 %all-to-all-done = bf16[2,8,72,2048]{3,2,0,1:T(8,128)(2,1)} async-done(((bf16[2,8,72,2048]{3,2,0,1:T(8,128)(2,1)}), bf16[2,8,72,2048]{3,2,0,1:T(8,128)(2,1)}, u32[]{:S(2)}, u32[]{:S(2)}) %all-to-all-start) | async-done | bytes 4718624 | tf_op jit(solution)/shard_map/all_to_all | solution.py:57
  539.0 5.3 copy.234
  544.3 156.4 %all-gather.13.cloned.1.call-done = bf16[2048,2,3072]{2,0,1:T(8,128)(2,1)} async-done(((bf16[512,2,3072]{2,0,1:T(8,128)(2,1)}), bf16[2048,2,3072]{2,0,1:T(8,128)(2,1)}) %all-gather.13.cloned.1.call-update) | async-done | bytes 25165840 | tf_op jit(solution)/shard_map/all_gather | solution.py:200
  700.7 17.2 fusion.6
  718.0 13.0 multiply_convert_fusion.1
  731.0 9.5 fusion.20
  740.6 2.5 copy.236
  743.1 4.6 all-to-all-start.1
  747.7 16.4 fusion.23
  764.2 5.3 copy.241
  769.4 33.1 %all-to-all-done.1 = bf16[2,8,72,2048]{3,2,0,1:T(8,128)(2,1)} async-done(((bf16[2,8,72,2048]{3,2,0,1:T(8,128)(2,1)}), bf16[2,8,72,2048]{3,2,0,1:T(8,128)(2,1)}, u32[]{:S(2)}, u32[]{:S(2)}) %all-to-all-start.1) | async-done | bytes 4718624 | tf_op jit(solution)/shard_map/all_to_all | solution.py:57
  802.5 4.6 all-to-all-start.3
  807.2 5.2 copy.237
  812.4 12.2 gather_fusion.1
  824.6 4.9 fusion.9
  829.6 32.3 %all-to-all-done.3 = bf16[2,8,72,2048]{3,2,0,1:T(8,128)(2,1)} async-done(((bf16[2,8,72,2048]{3,2,0,1:T(8,128)(2,1)}), bf16[2,8,72,2048]{3,2,0,1:T(8,128)(2,1)}, u32[]{:S(2)}, u32[]{:S(2)}) %all-to-all-start.3) | async-done | bytes 4718624 | tf_op jit(solution)/shard_map/all_to_all | solution.py:57
  861.9 5.2 copy.242
  867.1 11.8 gather_fusion.3
  878.9 5.1 convert_reduce_fusion
  886.9 6.4 fusion.29
  893.7 3.8 multiply_reduce_fusion
  897.5 1.7 multiply_convert_fusion.4
  899.2 2.3 multiply_convert_fusion.3
  901.5 4.0 copy.261
  905.6 4.8 convolution_convert_fusion
  910.4 4.0 copy.260
  914.5 11.7 convert_bitcast_fusion.1
  926.2 20.0 convert_bitcast_fusion
  947.5 3.3 fusion.39
  958.9 8.6 reduce-scatter.13.cloned.1.call-done
  967.6 14.2 fusion.46
  983.2 27.1 pad_maximum_fusion.1
  1011.7 8.1 fusion.57
  1019.8 20.6 fusion.56
  1040.3 43.2 %pad_maximum_fusion = f32[2048,8192]{1,0:T(8,128)} fusion(f32[2048,2048]{1,0:T(8,128)} %fusion.57, f32[2048,6144]{1,0:T(8,128)} %fusion.56), kind=kLoop, calls=%fused_computation.6 | loop fusion | flops 16777216 | bytes 134217728 | tf_op jit(solution)/shard_map/concatenate | solution.py:342
  1083.6 21.6 reduce-scatter.21.cloned.1.call-done
  1105.2 1.4 copy.264
  1107.9 131.4 %reduce-scatter.23.cloned.1.call-done = f32[64,4]{1,0:T(8,128)} async-done(((f32[2048,4]{1,0:T(8,128)}), f32[64,4]{1,0:T(8,128)}) %reduce-scatter.23.cloned.1.call-update) | async-done | bytes 1040
  1239.4 1.4 copy.266
  1240.8 411.8 %reduce-scatter.17.cloned.1.call-done = bf16[512,2,3072]{0,2,1:T(8,128)(2,1)} async-done(((bf16[2048,2,3072]{0,2,1:T(8,128)(2,1)}), bf16[512,2,3072]{0,2,1:T(8,128)(2,1)}) %reduce-scatter.17.cloned.1.call-update) | async-done | bytes 6291472 | tf_op jit(solution)/shard_map/reduce_scatter | solution.py:245
  1652.6 17.2 copy.255
  1669.7 1398.2 %reduce-scatter.15.cloned.1.call-done = f32[64,8192]{1,0:T(8,128)} async-done(((f32[2048,8192]{1,0:T(8,128)}), f32[64,8192]{1,0:T(8,128)}) %reduce-scatter.15.cloned.1.call-update) | async-done | bytes 2097168 | tf_op jit(solution)/shard_map/reduce_scatter | solution.py:341
  (241 shorter events, 27.4 us)
Async XLA Ops:
  7.2 2.9 copy-start.51
  7.2 73.9 %copy-start.59 = (s32[1,4]{1,0:T(1,128)S(1)}, s32[1,4]{1,0:T(1,128)}, u32[]{:S(2)}) copy-start(s32[1,4]{1,0:T(1,128)} %param.15) | copy-start | bytes 52
  7.2 74.1 %copy-start.58 = (s32[1,8]{1,0:T(1,128)S(1)}, s32[1,8]{1,0:T(1,128)}, u32[]{:S(2)}) copy-start(s32[1,8]{1,0:T(1,128)} %param.16) | copy-start | bytes 100
  7.2 74.4 %copy-start.12 = (bf16[1,128,2048]{2,1,0:T(8,128)(2,1)S(1)}, bf16[1,128,2048]{2,1,0:T(8,128)(2,1)}, u32[]{:S(2)}) copy-start(bf16[1,128,2048]{2,1,0:T(8,128)(2,1)} %param.9) | copy-start | bytes 1572868
  7.2 202.2 %all-gather.7.cloned.1.call-start = ((), (), s32[]{:S(2)}) async-start(), calls=%async_computation.10 | async-start | bytes 34603008 | tf_op jit(solution)/shard_map/all_gather | solution.py:84
  10.0 336.2 %all-gather.11.cloned.1.call-start = ((), (), s32[]{:S(2)}) async-start(), calls=%async_computation.12 | async-start | bytes 2621440 | tf_op jit(solution)/shard_map/all_gather | solution.py:116
  81.8 127.6 %copy-start.56 = (f32[128]{0:T(128)}, f32[128]{0:T(128)S(1)}, u32[]{:S(2)}) copy-start(f32[128]{0:T(128)S(1)} %fusion.52) | copy-start | bytes 1540
  81.8 137.9 %copy-start.42 = (f32[128]{0:T(128)}, f32[128]{0:T(128)S(1)}, u32[]{:S(2)}) copy-start(f32[128]{0:T(128)S(1)} %fusion.89) | copy-start | bytes 1540
  82.1 139.8 %copy-start.25 = (f32[128,64]{1,0:T(8,128)}, f32[128,64]{1,0:T(8,128)S(1)}, u32[]{:S(2)}) copy-start(f32[128,64]{1,0:T(8,128)S(1)} %get-tuple-element.229) | copy-start | bytes 98308
  82.2 139.8 %copy-start.27 = (f32[128,64]{1,0:T(8,128)}, f32[128,64]{1,0:T(8,128)S(1)}, u32[]{:S(2)}) copy-start(f32[128,64]{1,0:T(8,128)S(1)} %get-tuple-element.230) | copy-start | bytes 98308
  82.2 137.5 %copy-start.31 = (f32[1,2048]{1,0:T(1,128)}, f32[1,2048]{1,0:T(1,128)S(1)}, u32[]{:S(2)}) copy-start(f32[1,2048]{1,0:T(1,128)S(1)} %get-tuple-element.224) | copy-start | bytes 24580
  82.2 138.4 %copy-start.37 = (f32[1,2048]{1,0:T(1,128)}, f32[1,2048]{1,0:T(1,128)S(1)}, u32[]{:S(2)}) copy-start(f32[1,2048]{1,0:T(1,128)S(1)} %get-tuple-element.222) | copy-start | bytes 24580
  82.2 138.4 %copy-start.39 = (f32[1,2048]{1,0:T(1,128)}, f32[1,2048]{1,0:T(1,128)S(1)}, u32[]{:S(2)}) copy-start(f32[1,2048]{1,0:T(1,128)S(1)} %get-tuple-element.223) | copy-start | bytes 24580
  82.2 279.4 %copy-start.33 = (f32[1,2048]{1,0:T(1,128)}, f32[1,2048]{1,0:T(1,128)S(1)}, u32[]{:S(2)}) copy-start(f32[1,2048]{1,0:T(1,128)S(1)} %get-tuple-element.221) | copy-start | bytes 24580
  219.7 7.9 copy-start.4
  227.6 124.8 %all-gather.9.cloned.1.call-start = ((), (), s32[]{:S(2)}) async-start(), calls=%async_computation.11 | async-start | bytes 2621440 | tf_op jit(solution)/shard_map/all_gather | solution.py:117
  228.5 472.2 %all-gather.13.cloned.1.call-start = ((), (), s32[]{:S(2)}) async-start(), calls=%async_computation.13 | async-start | bytes 31457280 | tf_op jit(solution)/shard_map/all_gather | solution.py:200
  239.6 15.1 copy-start.44
  239.6 106.6 %copy-start.15 = (bf16[128,16,64]{2,0,1:T(8,128)(2,1)S(1)}, bf16[128,16,64]{2,0,1:T(8,128)(2,1)}, u32[]{:S(2)}) copy-start(bf16[128,16,64]{2,0,1:T(8,128)(2,1)} %get-tuple-element.203) | copy-start | bytes 786436
  239.6 106.6 %copy-start.17 = (bf16[128,16,64]{2,0,1:T(8,128)(2,1)S(1)}, bf16[128,16,64]{2,0,1:T(8,128)(2,1)}, u32[]{:S(2)}) copy-start(bf16[128,16,64]{2,0,1:T(8,128)(2,1)} %get-tuple-element.204) | copy-start | bytes 786436
  345.7 17.0 copy-start.29
  346.1 6.2 copy-start.19
  348.9 2.1 copy-start.2
  352.3 4.3 copy-start.35
  352.3 4.4 copy-start.13
  356.7 5.0 copy-start.23
  362.8 6.5 copy-start
  363.3 6.0 copy-start.8
  468.3 70.7 %all-to-all-start = ((bf16[2,8,72,2048]{3,2,0,1:T(8,128)(2,1)}), bf16[2,8,72,2048]{3,2,0,1:T(8,128)(2,1)}, u32[]{:S(2)}, u32[]{:S(2)}) async-start(bf16[2,8,72,2048]{3,2,0,1:T(8,128)(2,1)} %get-tuple-element.228), calls=%async_computation | async-start | bytes 9437184 | tf_op jit(solution)/shard_map/all_to_all | solution.py:57
  539.0 178.9 %slice-start = ((s8[4718592]{0:T(1024)(128)(4,1)}), s8[524288]{0:T(1024)(128)(4,1)S(1)}, s32[]{:S(2)}) async-start(s8[4718592]{0:T(1024)(128)(4,1)} %bitcast.187), calls=%async_computation.20 | async-start | bytes 1048576
  700.7 17.2 slice-start.1
  731.0 9.6 copy-start.62
  743.1 59.4 %all-to-all-start.1 = ((bf16[2,8,72,2048]{3,2,0,1:T(8,128)(2,1)}), bf16[2,8,72,2048]{3,2,0,1:T(8,128)(2,1)}, u32[]{:S(2)}, u32[]{:S(2)}) async-start(bf16[2,8,72,2048]{3,2,0,1:T(8,128)(2,1)} %copy.236), calls=%async_computation.1 | async-start | bytes 9437184 | tf_op jit(solution)/shard_map/all_to_all | solution.py:57
  802.5 59.4 %all-to-all-start.3 = ((bf16[2,8,72,2048]{3,2,0,1:T(8,128)(2,1)}), bf16[2,8,72,2048]{3,2,0,1:T(8,128)(2,1)}, u32[]{:S(2)}, u32[]{:S(2)}) async-start(bf16[2,8,72,2048]{3,2,0,1:T(8,128)(2,1)} %copy.241), calls=%async_computation.3 | async-start | bytes 9437184 | tf_op jit(solution)/shard_map/all_to_all | solution.py:57
  807.1 144.0 %reduce-scatter.19.cloned.1.call-start = ((), (), s32[]{:S(2)}) async-start(), calls=%async_computation.17 | async-start | bytes 2621440
  878.9 5.2 copy-start.7
  878.9 5.2 copy-start.30
  878.9 5.2 copy-start.34
  878.9 5.2 copy-start.50
  878.9 5.7 copy-start.61
  886.9 6.7 copy-start.20
  886.9 6.7 copy-start.21
  886.9 6.7 copy-start.36
  893.7 3.8 copy-start.3
  905.5 62.1 %reduce-scatter.13.cloned.1.call-start = ((), (), s32[]{:S(2)}) async-start(), calls=%async_computation.14 | async-start | bytes 2621440 | tf_op jit(solution)/shard_map/reduce_scatter | solution.py:323
  914.4 190.8 %reduce-scatter.21.cloned.1.call-start = ((), (), s32[]{:S(2)}) async-start(), calls=%async_computation.18 | async-start | bytes 1081344
  926.2 20.0 copy-start.1
  950.8 4.3 copy-start.11
  950.8 4.3 copy-start.26
  950.8 4.3 copy-start.28
  950.8 288.5 %reduce-scatter.23.cloned.1.call-start = ((), (), s32[]{:S(2)}) async-start(), calls=%async_computation.19 | async-start | bytes 1081344
  955.2 1.9 copy-start.5
  955.2 1.9 copy-start.38
  955.2 1.9 copy-start.40
  955.2 1.9 copy-start.46
  956.0 2.0 copy-start.53
  956.0 2.0 copy-start.55
  958.0 9.6 copy-start.14
  958.0 9.6 copy-start.32
  958.0 9.6 copy-start.43
  983.2 669.4 %reduce-scatter.17.cloned.1.call-start = ((), (), s32[]{:S(2)}) async-start(), calls=%async_computation.16 | async-start | bytes 31457280 | tf_op jit(solution)/shard_map/reduce_scatter | solution.py:245
  1010.4 2057.6 %reduce-scatter.15.cloned.1.call-start = ((), (), s32[]{:S(2)}) async-start(), calls=%async_computation.15 | async-start | bytes 69206016 | tf_op jit(solution)/shard_map/reduce_scatter | solution.py:341
  1083.5 23.1 copy-start.57
  1083.5 23.1 copy-start.22
  (14 other events, 17.3 us)
Sparse Core Ops, SparseCore 0:
  11.5 197.8 all-gather.6
  227.7 21.0 all-gather.10
  250.9 22.7 all-gather.8
  275.7 425.0 all-gather.12
  905.6 27.8 reduce-scatter.18
  936.1 31.4 reduce-scatter.12
  969.8 135.3 reduce-scatter.20
  1107.5 131.7 reduce-scatter.22
  1241.7 410.7 reduce-scatter.16
  1655.5 1412.4 reduce-scatter.14
where the time goes:
time: 3090 us; the launch traced here: 3080 us
  waiting for transfers between devices  2370 us (77%)
  blocking collectives  238 us (8%)
  matrix products  176 us (6%)
  local copies, waits for them, and re-layouts  139 us (4%)
  other arithmetic  111 us (4%)
    reduce_scatter x1, waiting for transfers between devices, on_device(): lax.psum_scatter(jnp.concatenate([first_term, second_term], axis=1), ('ex...  1400 us
    reduce_scatter x1, waiting for transfers between devices, on_device(): lax.psum_scatter(jnp.concatenate([first_term, second_term], axis=2).astyp...  412 us
    all_gather x1, waiting for transfers between devices, on_device(): lax.all_gather(w_experts.astype(jnp.bfloat16), 'dp', axis=0, tiled=True)  156 us
    unnamed x13, waiting for transfers between devices  153 us
    all_gather x1, waiting for transfers between devices, on_device(): lax.all_gather(w_attn.astype(jnp.bfloat16), ('expert', 'context', 'dp'),...  127 us
    all_to_all x3, waiting for transfers between devices, route_rows(): lax.all_to_all(slot_values, ('expert', 'context'), split_axis=1, concat_a...  115 us
    all_gather x1, blocking collectives, on_device(): lax.all_gather(w_router.astype(jnp.bfloat16), ('expert', 'context', 'dp')...  90.8 us
    all_to_all x1, blocking collectives, route_rows(): lax.all_to_all(slot_values, ('expert', 'context'), split_axis=1, concat_a...  76.3 us
  transfers between devices with their start and end apart: 13, of which 10 were waited for; matrix products, arithmetic and copies ran while one was open for 10% of the time, Pallas kernels for 0%

commit v1 on v0

v1 whole, which is shorter than its diff:
```python
import jax
import jax.numpy as jnp
from jax import lax
from jax.sharding import PartitionSpec as P

HEADS = 16
epsilon = 1e-05
rope_base = 10000.0
masked_score = -1e30
bf16 = jnp.bfloat16
f32 = jnp.float32
EVERY = ("expert", "context", "dp")


def mm(a, b):
    return jnp.dot(a, b, preferred_element_type=f32)


def mm_nt(a, b):
    return lax.dot_general(a, b, (((1,), (1,)), ((), ())), preferred_element_type=f32)


def mm_tn(a, b):
    return lax.dot_general(a, b, (((0,), (0,)), ((), ())), preferred_element_type=f32)


def swap(value, axis, bit):
    count = lax.axis_size(axis)
    return lax.ppermute(value, axis, [(i, i ^ bit) for i in range(count)])


def shift(value, axis, step):
    count = lax.axis_size(axis)
    return lax.ppermute(value, axis, [(i, (i + step) % count) for i in range(count)])


def bits_of(axis):
    count = lax.axis_size(axis)
    return [1 << i for i in range(count.bit_length() - 1)]


def spread(value):
    total = lax.axis_size(EVERY)
    return lax.all_to_all(value, EVERY, 0, 0, tiled=True) if value.shape[0] == total else None


def locate(stored_rows, doc_lens, blk_order, blk_rows):
    block_ids = stored_rows // blk_rows
    block_hits = block_ids[:, None] == jnp.arange(blk_order.shape[0], dtype=jnp.int32)[None, :]
    placed_at = (
        jnp.sum(jnp.where(block_hits, blk_order[None, :], 0), axis=1) * blk_rows
        + stored_rows % blk_rows
    )
    doc_count = doc_lens.shape[0]
    upto = jnp.arange(doc_count)[:, None] >= jnp.arange(doc_count)[None, :]
    doc_ends = jnp.sum(jnp.where(upto, doc_lens[None, :], 0), axis=1)
    doc_ids = jnp.sum((placed_at[:, None] >= doc_ends[None, :]).astype(jnp.int32), axis=1)
    doc_hits = doc_ids[:, None] == jnp.arange(doc_count, dtype=jnp.int32)[None, :]
    doc_starts = doc_ends - doc_lens
    offset = placed_at - jnp.sum(jnp.where(doc_hits, doc_starts[None, :], 0), axis=1)
    return placed_at, doc_ids, offset


def context_gather(value):
    me = lax.axis_index("context")
    parts = [value]
    for bit in reversed(bits_of("context")):
        parts = parts + [swap(part, "context", bit) for part in parts]
    count = len(parts)
    order = []
    for r in range(count):
        source = 0
        for i, bit in enumerate(reversed(bits_of("context"))):
            if r >> i & 1:
                source |= bit
        order.append(source)
    stack = [None] * count
    for r in range(count):
        stack[order[r]] = parts[r]
    rows = []
    for target in range(count):
        rows.append(
            sum(
                jnp.where(me == target ^ m, stack[m], jnp.zeros_like(stack[m])) for m in range(count)
            )
        )
    return jnp.concatenate(rows, axis=0)


def half_step(value, axis, bit, dim):
    mine = (lax.axis_index(axis) // bit) % 2
    keep = lax.dynamic_index_in_dim(value, mine, dim, keepdims=False)
    send = lax.dynamic_index_in_dim(value, 1 - mine, dim, keepdims=False).astype(bf16)
    return keep.astype(f32) + swap(send, axis, bit).astype(f32)


def context_scatter(value):
    bits = bits_of("context")
    rows = value.shape[0] >> len(bits)
    value = value.reshape((2,) * len(bits) + (rows, value.shape[1]))
    left = list(reversed(bits))
    for bit in bits:
        dim = left.index(bit)
        value = half_step(value, "context", bit, dim)
        left.remove(bit)
    return value


def token_scatter(value):
    steps_e = [("expert", b) for b in bits_of("expert")]
    steps_c = [("context", b) for b in bits_of("context")]
    z_count = lax.axis_size("dp")
    rows, width = value.shape[1:]
    dims = list(reversed(steps_e)) + list(reversed(steps_c))
    value = value.reshape((2,) * len(dims) + (z_count, rows, width))
    first, rest = steps_c[0], steps_c[1:] + steps_e
    dim = dims.index(first)
    value = half_step(value, first[0], first[1], dim).astype(bf16)
    dims = dims[:dim] + dims[dim + 1 :]
    half = width // 2
    outs = []
    for part, order in ((value[..., :half], rest), (value[..., half:], rest[::-1])):
        left = list(dims)
        for step in order:
            dim = left.index(step)
            part = half_step(part, step[0], step[1], dim).astype(bf16)
            left.remove(step)
        got = lax.all_to_all(part, "dp", 0, 0, tiled=True)
        outs.append(jnp.sum(got.astype(f32), axis=0))
    return jnp.concatenate(outs, axis=1)


def relative_gather(piece):
    around = [piece]
    for _ in range(lax.axis_size("dp") - 1):
        around.append(shift(around[-1], "dp", 1))
    held = [around]
    for bit in bits_of("expert"):
        held = held + [[swap(part, "expert", bit) for part in row] for row in held]
    return held


def relative_scatter(value):
    for bit in reversed(bits_of("expert")):
        half = value.shape[0] // 2
        value = value[:half].astype(f32) + swap(value[half:].astype(bf16), "expert", bit).astype(f32)
    value = value[0]
    total = value[0].astype(f32)
    for k in range(1, lax.axis_size("dp")):
        total = total + shift(value[k].astype(bf16), "dp", -k).astype(f32)
    return total


def on_device(
    tokens, cotangent, w_attn, w_router, norm_gains, w_experts, lengths, block_order, routes
):
    tok_rows, width = tokens.shape[1:]
    blk_rows = tok_rows // 2
    e_count, c_count, z_count = (lax.axis_size(a) for a in EVERY)
    total = e_count * c_count * z_count
    me_e, me_c, me_z = (lax.axis_index(a) for a in EVERY)
    pack_rows = tok_rows * c_count
    pick_rows = routes[0]
    top_count = pick_rows.shape[1]
    local_experts = w_experts.shape[1]
    expert_count = local_experts * e_count * c_count
    slot_cap = tok_rows * top_count * 9 // (8 * expert_count)
    ffn = w_experts.shape[2] // 3
    halves = z_count // local_experts
    ffh = ffn // halves
    head_width = width // HEADS
    local_heads = HEADS // c_count
    cols = local_heads * head_width
    w_rows = w_attn.shape[0]
    score_scale = head_width ** (-0.5)
    block_rows = z_count * w_rows
    aligned = block_rows % head_width == 0
    head_run = block_rows // head_width if aligned else local_heads
    runs = local_heads // head_run
    run_cols = head_run * head_width

    expert_ids = jnp.arange(expert_count, dtype=jnp.int32)
    pick_hits = (pick_rows[:, :, None] == expert_ids[None, None, :]).astype(f32)
    named = jnp.sum(pick_hits, axis=1)
    earlier = jnp.arange(tok_rows)[:, None] > jnp.arange(tok_rows)[None, :]
    ranks = mm(earlier.astype(bf16), named.astype(bf16))
    rank_rows = jnp.repeat(jnp.where(named > 0, ranks, -1.0).T, halves, axis=0)
    own_row = jnp.concatenate(
        [w_router.astype(bf16).reshape(-1), norm_gains.astype(bf16).reshape(-1)]
    )
    small_sent = jnp.concatenate(
        [jnp.broadcast_to(own_row[None], (total, own_row.shape[0])), rank_rows.astype(bf16)], axis=1
    )
    small = lax.all_to_all(small_sent, EVERY, 0, 0, tiled=True)
    n_router = w_router.size
    router_w = small[:, :n_router].reshape(width, expert_count)
    gains = (
        small[:, n_router : n_router + norm_gains.size]
        .reshape(total, 4, norm_gains.shape[1])
        .transpose(1, 0, 2)
        .reshape(4, width)
        .astype(f32)
    )
    slot_of = small[:, n_router + norm_gains.size :].astype(jnp.int32)

    wqkv = (
        w_attn[:, : 3 * width]
        .astype(bf16)
        .reshape(w_rows, 3, runs, c_count, run_cols)
        .transpose(3, 0, 1, 2, 4)
        .reshape(c_count, w_rows, 3 * cols)
    )
    wqkv = lax.all_to_all(wqkv, "context", 0, 0, tiled=True).reshape(c_count * w_rows, 3 * cols)
    held = relative_gather(wqkv)
    wqkv_all = jnp.concatenate([part for row in held for part in row], axis=0)
    wo_own = w_attn[:, 3 * width :].astype(bf16)
    if aligned:
        wo_all = jnp.concatenate([part for row in relative_gather(wo_own) for part in row], axis=0)
    else:
        wo_full = lax.all_gather(wo_own, EVERY, axis=0, tiled=True)
        wo_all = lax.dynamic_slice_in_dim(wo_full, me_c * cols, cols, axis=0)

    def place_of(r_e, r_z, c, row):
        return (((me_e ^ r_e) * c_count + c) * z_count + (me_z - r_z) % z_count) * w_rows + row

    spots = jnp.arange(width, dtype=jnp.int32)
    per_e = z_count * c_count * w_rows
    feature_of = place_of(
        spots // per_e,
        spots // (c_count * w_rows) % z_count,
        spots // w_rows % c_count,
        spots % w_rows,
    )
    order_n = (spots[:, None] == feature_of[None, :]).astype(bf16)
    if aligned:
        near = jnp.arange(cols, dtype=jnp.int32)
        local_of = (
            (me_e ^ (near // block_rows)) * block_rows
            + (me_z - near // w_rows % z_count) % z_count * w_rows
            + near % w_rows
        )
        order_o = (near[:, None] == local_of[None, :]).astype(bf16)

    wx = (
        w_experts.astype(bf16)
        .reshape(w_experts.shape[0], local_experts, 3, halves, ffh)
        .transpose(1, 3, 0, 2, 4)
        .reshape(z_count, w_experts.shape[0], 3 * ffh)
    )
    wx = lax.all_to_all(wx, "dp", 0, 0, tiled=True).reshape(width, 3 * ffh)
    w_gu, w_down = wx[:, : 2 * ffh], wx[:, 2 * ffh :]

    grad_out = cotangent[0]
    inputs = tokens[0].astype(f32)
    pack_x = context_gather(tokens[0]).astype(f32)
    scale_one = lax.rsqrt(jnp.mean(pack_x * pack_x, axis=-1, keepdims=True) + epsilon)
    normed_one = (pack_x * scale_one * gains[0]).astype(bf16)
    normed_one_r = mm(normed_one, order_n).astype(bf16)
    qkv = mm(normed_one_r, wqkv_all)
    place, doc, offset = locate(
        jnp.arange(pack_rows, dtype=jnp.int32), lengths[0], block_order[0], blk_rows
    )
    half_width = head_width // 2
    freq = rope_base ** (-2.0 * jnp.arange(half_width, dtype=f32) / head_width)
    angle = offset.astype(f32)[:, None] * freq[None, :]
    cos_t, sin_t = jnp.cos(angle), jnp.sin(angle)
    cos_all = jnp.concatenate([cos_t, cos_t], axis=1)[:, None, :]
    sin_all = jnp.concatenate([-sin_t, sin_t], axis=1)[:, None, :]

    def turn(v):
        v = v.reshape(pack_rows, local_heads, head_width)
        return v * cos_all + jnp.roll(v, half_width, axis=2) * sin_all

    def turn_back(v):
        return (v * cos_all + jnp.roll(v * sin_all, half_width, axis=2)).reshape(pack_rows, cols)

    my_gains = lax.dynamic_index_in_dim(
        gains[2:].reshape(2, runs, c_count, run_cols), me_c, 2, keepdims=False
    ).reshape(2, cols)
    raw_q, raw_k = qkv[:, :cols], qkv[:, cols : 2 * cols]
    value = qkv[:, 2 * cols :].astype(bf16).reshape(pack_rows, local_heads, head_width)
    squares = jnp.stack([jnp.sum(raw_q * raw_q, axis=1), jnp.sum(raw_k * raw_k, axis=1)])
    scale_qk = lax.rsqrt(lax.psum(squares, "context") / width + epsilon)[:, :, None]
    unit_q, unit_k = raw_q * scale_qk[0], raw_k * scale_qk[1]
    query = turn(unit_q * my_gains[0]).astype(bf16)
    key = turn(unit_k * my_gains[1]).astype(bf16)
    scores = jnp.einsum("qhd,khd->hqk", query, key, preferred_element_type=f32) * score_scale
    allowed = (doc[:, None] == doc[None, :]) & (place[None, :] <= place[:, None])
    scores = jnp.where(allowed[None], scores, masked_score)
    top = jnp.max(scores, axis=2, keepdims=True)
    raised = jnp.exp(scores - top)
    soft = raised / jnp.sum(raised, axis=2, keepdims=True)
    soft_b = soft.astype(bf16)
    mixed = (
        jnp.einsum("hqk,khd->qhd", soft_b, value, preferred_element_type=f32)
        .reshape(pack_rows, cols)
        .astype(bf16)
    )
    mixed_r = mm(mixed, order_o).astype(bf16) if aligned else mixed
    hidden = inputs + context_scatter(mm(mixed_r, wo_all))
    scale_two = lax.rsqrt(jnp.mean(hidden * hidden, axis=-1, keepdims=True) + epsilon)
    normed_two = (hidden * scale_two * gains[1]).astype(bf16)
    logits = mm(normed_two, router_w)
    probs = jax.nn.softmax(logits, axis=-1)

    all_grad = lax.all_gather(grad_out.astype(bf16), EVERY, axis=0, tiled=True)
    all_grad = all_grad.reshape(total, tok_rows, width)
    all_normed = lax.all_gather(normed_two, EVERY, axis=0, tiled=True)
    all_normed = all_normed.reshape(total, tok_rows, width)
    gate_rows = lax.all_to_all(jnp.repeat(probs.T, halves, axis=0), EVERY, 0, 0, tiled=True)
    slots = jnp.arange(slot_cap, dtype=jnp.int32)
    pick = (slot_of[:, None, :] == slots[None, :, None]).astype(bf16)
    put = (slot_of[:, :, None] == slots[None, None, :]).astype(bf16)

    def take_rows(rows):
        got = jnp.einsum("sct,std->scd", pick, rows, preferred_element_type=f32)
        return got.astype(bf16).reshape(total * slot_cap, width)

    def put_rows(rows):
        rows = rows.astype(bf16).reshape(total, slot_cap, width)
        return jnp.einsum("stc,scd->std", put, rows, preferred_element_type=f32).astype(bf16)

    gate = jnp.sum(
        jnp.where(slot_of[:, None, :] == slots[None, :, None], gate_rows[:, None, :], 0.0), axis=2
    ).reshape(total * slot_cap, 1)
    g_rows = take_rows(all_grad)
    back = mm(g_rows, w_down)
    n_rows = take_rows(all_normed)
    gate_up = mm(n_rows, w_gu)
    gate_part, up_part = gate_up[:, :ffh], gate_up[:, ffh:]
    sig = jax.nn.sigmoid(gate_part)
    silu = gate_part * sig
    act = (silu * up_part).astype(bf16)
    act_f = act.astype(f32)
    grad_gate_slot = jnp.sum(act_f * back, axis=1).reshape(total, slot_cap)
    grad_act = back * gate
    grad_gu = jnp.concatenate(
        [grad_act * up_part * sig * (1.0 + gate_part * (1.0 - sig)), grad_act * silu], axis=1
    ).astype(bf16)
    grad_rows = mm_nt(grad_gu, w_gu)
    grad_n2 = token_scatter(put_rows(grad_rows))
    sent_gates = jnp.sum(
        jnp.where(slot_of[:, :, None] == slots[None, None, :], grad_gate_slot[:, None, :], 0.0),
        axis=2,
    )
    got_gates = lax.all_to_all(sent_gates, EVERY, 0, 0, tiled=True)
    grad_probs = jnp.sum(got_gates.reshape(expert_count, halves, tok_rows), axis=1).T

    act_scaled = (act_f * gate).astype(bf16)
    grad_wx = jnp.concatenate([mm_tn(n_rows, grad_gu), mm_tn(g_rows, act_scaled)], axis=1)
    grad_wx = grad_wx.astype(bf16).reshape(z_count, width // z_count, 3 * ffh)
    grad_wx = lax.all_to_all(grad_wx, "dp", 0, 0, tiled=True)
    grad_experts = (
        grad_wx.astype(f32)
        .reshape(local_experts, halves, width // z_count, 3, ffh)
        .transpose(2, 0, 3, 1, 4)
        .reshape(width // z_count, local_experts, 3 * ffn)
    )
    mixture = token_scatter(put_rows(mm_nt(act, w_down) * gate))
    output = hidden + mixture

    grad_logits = (
        probs * (grad_probs - jnp.sum(probs * grad_probs, axis=-1, keepdims=True))
    ).astype(bf16)
    grad_n2 = grad_n2 + mm_nt(grad_logits, router_w)
    router_term = mm_tn(normed_two, grad_logits)

    def norm_back(v, scale, gain, grad):
        pulled = grad * gain
        inner = jnp.mean(v * pulled, axis=-1, keepdims=True)
        return scale * pulled - v * (scale * scale * scale * inner)

    gain_two = jnp.sum(grad_n2 * hidden * scale_two, axis=0)
    grad_hidden = grad_out + norm_back(hidden, scale_two, gains[1], grad_n2)
    grad_hidden_b = grad_hidden.astype(bf16)

    pack_dh = context_gather(grad_hidden_b)
    grad_mixed = mm_nt(pack_dh, wo_all).astype(bf16)
    if aligned:
        grad_mixed = mm_nt(grad_mixed, order_o).astype(bf16)
    grad_mixed_h = grad_mixed.reshape(pack_rows, local_heads, head_width)
    grad_soft = jnp.einsum("qhd,khd->hqk", grad_mixed_h, value, preferred_element_type=f32)
    delta = jnp.sum(soft * grad_soft, axis=2, keepdims=True)
    grad_scores = (soft * (grad_soft - delta)).astype(bf16)
    grad_query = jnp.einsum("hqk,khd->qhd", grad_scores, key, preferred_element_type=f32)
    grad_key = jnp.einsum("hqk,qhd->khd", grad_scores, query, preferred_element_type=f32)
    grad_value = jnp.einsum("hqk,qhd->khd", soft_b, grad_mixed_h, preferred_element_type=f32)
    back_q, back_k = turn_back(grad_query * score_scale), turn_back(grad_key * score_scale)
    gain_q = jnp.sum(back_q * unit_q, axis=0)
    gain_k = jnp.sum(back_k * unit_k, axis=0)
    pull_q, pull_k = back_q * my_gains[0], back_k * my_gains[1]
    inner = jnp.stack([jnp.sum(raw_q * pull_q, axis=1), jnp.sum(raw_k * pull_k, axis=1)])
    inner = (lax.psum(inner, "context") / width)[:, :, None]
    grad_qkv = jnp.concatenate(
        [
            scale_qk[0] * pull_q - raw_q * (scale_qk[0] ** 3 * inner[0]),
            scale_qk[1] * pull_k - raw_k * (scale_qk[1] ** 3 * inner[1]),
            grad_value.reshape(pack_rows, cols),
        ],
        axis=1,
    ).astype(bf16)
    grad_n1 = mm(context_pull(grad_qkv, wqkv_all), order_n_t(order_n))
    grad_n1 = context_scatter(grad_n1)
    own_scale = lax.rsqrt(jnp.mean(inputs * inputs, axis=-1, keepdims=True) + epsilon)
    gain_one = jnp.sum(grad_n1 * inputs * own_scale, axis=0)
    grad_tokens = grad_hidden + norm_back(inputs, own_scale, gains[0], grad_n1)

    grad_wqkv = mm_tn(normed_one_r, grad_qkv).reshape(e_count, z_count, c_count, w_rows, 3 * cols)
    grad_wqkv = relative_scatter(grad_wqkv).astype(bf16)
    grad_wqkv = (
        lax.all_to_all(grad_wqkv, "context", 0, 0, tiled=True)
        .reshape(c_count, w_rows, 3, runs, run_cols)
        .transpose(1, 2, 3, 0, 4)
        .reshape(w_rows, 3 * width)
        .astype(f32)
    )
    grad_wo = mm_tn(mixed_r, pack_dh)
    if aligned:
        grad_wo = relative_scatter(grad_wo.reshape(e_count, z_count, w_rows, width))
    else:
        whole_wo = lax.dynamic_update_slice_in_dim(
            jnp.zeros((width, width), f32), grad_wo, me_c * cols, axis=0
        )
        grad_wo = lax.psum_scatter(
            whole_wo.astype(bf16), EVERY, scatter_dimension=0, tiled=True
        ).astype(f32)
    grad_attn = jnp.concatenate([grad_wqkv, grad_wo], axis=1)

    mine = jnp.arange(c_count)[None, None, :, None] == me_c
    gain_qk = jnp.where(mine, jnp.stack([gain_q, gain_k]).reshape(2, runs, 1, run_cols), 0.0)
    gain_rows = jnp.concatenate([jnp.stack([gain_one, gain_two]), gain_qk.reshape(2, width)])
    gain_rows = gain_rows.reshape(4, total, -1).transpose(1, 0, 2).reshape(total, -1)
    small_grads = jnp.concatenate([router_term.reshape(total, -1), gain_rows], axis=1)
    small_grads = jnp.sum(lax.all_to_all(small_grads, EVERY, 0, 0, tiled=True), axis=0)
    grad_router = small_grads[:n_router].reshape(w_router.shape)
    grad_gains = small_grads[n_router:].reshape(norm_gains.shape)
    return (output[None], grad_tokens[None], grad_attn, grad_router, grad_gains, grad_experts)


def context_pull(grad_qkv, wqkv_all):
    return mm_nt(grad_qkv, wqkv_all).astype(bf16)


def order_n_t(order_n):
    return order_n.T


def solution(mesh):
    in_specs = (
        P(("expert", "dp"), "context", None),
        P(("expert", "dp"), "context", None),
        P(EVERY, None),
        P(EVERY, None),
        P(None, EVERY),
        P("dp", ("expert", "context"), None),
        P(("expert", "dp"), None),
        P(("expert", "dp"), None),
        P(("expert", "dp"), "context", None),
    )
    out_specs = (
        P(("expert", "dp"), "context", None),
        P(("expert", "dp"), "context", None),
        P(EVERY, None),
        P(EVERY, None),
        P(None, EVERY),
        P("dp", ("expert", "context"), None),
    )
    return jax.shard_map(
        on_device, mesh=mesh, in_specs=in_specs, out_specs=out_specs, check_vma=False
    )
```

time: 3090 us -> 1270 us (0.41)
  waiting for transfers between devices: 2370 us -> 642 us
  blocking collectives: 238 us -> 13.2 us
  starting transfers between devices: 26.4 us -> 135 us
  local copies, waits for them, and re-layouts: 139 us -> 186 us
    reduce_scatter x3 -> x0, waiting for transfers between devices: 1820 us -> none  [the longest x1 1400 us: on_device(): lax.psum_scatter(jnp.concatenate([first_term, second_term], axis=1), ('ex...]
    ppermute x0 -> x42, waiting for transfers between devices: none -> 321 us  [the longest x30 192 us: swap(): return lax.ppermute(value, axis, [(i, i ^ bit) for i in range(count)])]
    all_gather x4 -> x2, waiting for transfers between devices: 284 us -> 0.01 us  [the longest x1 0.01 us: on_device(): all_grad = lax.all_gather(grad_out.astype(bf16), EVERY, axis=0, tiled=True)]
    all_to_all x3 -> x12, waiting for transfers between devices: 115 us -> 321 us  [the longest x1 198 us: on_device(): wx = lax.all_to_all(wx, 'dp', 0, 0, tiled=True).reshape(width, 3 * ffh)]
    all_gather x2 -> x0, blocking collectives: 162 us -> none  [the longest x1 90.8 us: on_device(): lax.all_gather(w_router.astype(jnp.bfloat16), ('expert', 'context', 'dp')...]
    unnamed x13 -> x2, waiting for transfers between devices: 153 us -> 0.03 us
    all_to_all x1 -> x0, blocking collectives: 76.3 us -> none  [route_rows(): lax.all_to_all(slot_values, ('expert', 'context'), split_axis=1, concat_a...]
    concatenate x3, other arithmetic: 71.4 us -> 5.78 us  [the longest x1 3.26 us: on_device(): jnp.concatenate([mm_tn(n_rows, grad_gu), mm_tn(g_rows, act_scaled)], axis=1)]
  transfers between devices with their start and end apart: 13 -> 56, of which waited for: 10 -> 26; matrix products, arithmetic and copies ran while one was open for 10% -> 29% of each run, Pallas kernels for 0% -> 0%
where the time goes in v1:
time: 1270 us; the launch traced here: 1260 us
  waiting for transfers between devices  642 us (51%)
  local copies, waits for them, and re-layouts  186 us (15%)
  matrix products  168 us (13%)
  starting transfers between devices  135 us (11%)
  other arithmetic  97.3 us (8%)
  between operations  15.9 us (1%)
  blocking collectives  13.2 us (1%)
    all_to_all x1, waiting for transfers between devices, on_device(): wx = lax.all_to_all(wx, 'dp', 0, 0, tiled=True).reshape(width, 3 * ffh)  198 us
    ppermute x30, waiting for transfers between devices, swap(): return lax.ppermute(value, axis, [(i, i ^ bit) for i in range(count)])  192 us
    ppermute x12, waiting for transfers between devices, shift(): lax.ppermute(value, axis, [(i, (i + step) % count) for i in range(count)])  128 us
    all_to_all x1, waiting for transfers between devices, on_device(): grad_wx = lax.all_to_all(grad_wx, 'dp', 0, 0, tiled=True)  72.1 us
    unnamed x201, local copies, waits for them, and re-layouts  59 us
    dot_general x9, matrix products, mm(): return jnp.dot(a, b, preferred_element_type=f32)  57.3 us
    all_to_all x1, waiting for transfers between devices, on_device(): got_gates = lax.all_to_all(sent_gates, EVERY, 0, 0, tiled=True)  39.6 us
    all_to_all x1, starting transfers between devices, on_device(): lax.all_to_all(small_grads, EVERY, 0, 0, tiled=True)  38 us
  transfers between devices with their start and end apart: 56, of which 26 were waited for; matrix products, arithmetic and copies ran while one was open for 29% of the time, Pallas kernels for 0%

profile of v1, /device:TPU:0, one launch (start us, length us, event | category | flops | bytes accessed | tf_op | source)
XLA Modules:
  0.0 1257.5 jit_solution(4494542527608984671)
XLA Ops:
  29.1 3.5 all-to-all-done
  38.7 8.3 collective-permute-done.11
  48.7 14.5 %collective-permute-done.12 = bf16[64,2048]{1,0:T(8,128)(2,1)} collective-permute-done((bf16[64,2048]{1,0:T(8,128)(2,1)S(1)}, bf16[64,2048]{1,0:T(8,128)(2,1)}, u32[]{:S(2)}, u32[]{:S(2)}) %collective-permute-start.12) | collective-permute-done | bytes 262176 | tf_op jit(solution)/shard_map/ppermute | solution.py:34
  69.5 5.0 collective-permute-done.15
  76.0 17.9 %collective-permute-done.3 = bf16[256,1536]{1,0:T(8,128)(2,1)S(1)} collective-permute-done((bf16[256,1536]{1,0:T(8,128)(2,1)S(1)}, bf16[256,1536]{1,0:T(8,128)(2,1)S(1)}, u32[]{:S(2)}, u32[]{:S(2)}) %collective-permute-start.3) | collective-permute-done | bytes 786464 | tf_op jit(solution)/shard_map/ppermute | solution.py:34
  96.1 36.3 %collective-permute-done.4 = bf16[256,1536]{1,0:T(8,128)(2,1)S(1)} collective-permute-done((bf16[256,1536]{1,0:T(8,128)(2,1)S(1)}, bf16[256,1536]{1,0:T(8,128)(2,1)S(1)}, u32[]{:S(2)}, u32[]{:S(2)}) %collective-permute-start.4) | collective-permute-done | bytes 786464 | tf_op jit(solution)/shard_map/ppermute | solution.py:34
  132.4 11.8 collective-permute-start.5
  144.2 8.8 fusion.23
  156.0 18.8 %collective-permute-done.5 = bf16[256,1536]{1,0:T(8,128)(2,1)S(1)} collective-permute-done((bf16[256,1536]{1,0:T(8,128)(2,1)S(1)}, bf16[256,1536]{1,0:T(8,128)(2,1)S(1)}, u32[]{:S(2)}, u32[]{:S(2)}) %collective-permute-start.5) | collective-permute-done | bytes 786464 | tf_op jit(solution)/shard_map/ppermute | solution.py:34
  176.5 14.6 %collective-permute-done.8 = bf16[256,1536]{1,0:T(8,128)(2,1)S(1)} collective-permute-done((bf16[256,1536]{1,0:T(8,128)(2,1)S(1)}, bf16[256,1536]{1,0:T(8,128)(2,1)S(1)}, u32[]{:S(2)}, u32[]{:S(2)}) %collective-permute-start.8) | collective-permute-done | bytes 786464 | tf_op jit(solution)/shard_map/ppermute | solution.py:29
  191.2 15.6 %collective-permute-done.9 = bf16[256,1536]{1,0:T(8,128)(2,1)S(1)} collective-permute-done((bf16[256,1536]{1,0:T(8,128)(2,1)S(1)}, bf16[256,1536]{1,0:T(8,128)(2,1)S(1)}, u32[]{:S(2)}, u32[]{:S(2)}) %collective-permute-start.9) | collective-permute-done | bytes 786464 | tf_op jit(solution)/shard_map/ppermute | solution.py:29
  210.5 6.5 psum.14
  227.5 4.9 fusion.162
  246.8 12.6 collective-permute-done.18
  264.9 4.5 all-to-all-start.3
  269.5 17.2 %copy.206 = bf16[512,2,3072]{0,2,1:T(8,128)(2,1)} copy(f32[512,2,3072]{2,1,0:T(2,128)} %param.14) | data formatting | bytes 18874368 | tf_op args[5]
  286.7 5.9 copy.207
  292.6 5.4 all-to-all-start.2
  298.8 198.4 %all-to-all-done.2 = bf16[4,512,1536]{1,2,0:T(8,128)(2,1)} async-done(((bf16[4,512,1536]{1,2,0:T(8,128)(2,1)}), bf16[4,512,1536]{1,2,0:T(8,128)(2,1)}, u32[]{:S(2)}, u32[]{:S(2)}) %all-to-all-start.2) | async-done | bytes 6291488 | tf_op jit(solution)/shard_map/all_to_all | solution.py:250
  497.1 8.6 copy.208
  505.8 12.0 convolution_convert_fusion.3
  517.8 12.3 convolution_convert_fusion.4
  530.0 15.5 %fusion.20 = f32[2304,1024]{0,1:T(8,128)} fusion(bf16[2304,2048]{1,0:T(8,128)(2,1)} %bitcast.301, bf16[2048,1536]{1,0:T(8,128)(2,1)} %bitcast.325), kind=kOutput, calls=%fused_computation.51 | convolution fusion | flops 9663676416 | bytes 23068672 | tf_op jit(solution)/shard_map/dot_general | solution.py:16
  545.5 13.4 %multiply_convert_fusion.2 = (bf16[2304,512]{0,1:T(8,128)(2,1)}, bf16[2304,512]{0,1:T(8,128)(2,1)}, f32[2304]{0:T(1024)S(1)}, bf16[2304,512]{0,1:T(8,128)(2,1)}) fusion(f32[2304,1024]{0,1:T(8,128)} %fusion.20, f32[2304]{0:T(1024)S(1)} %mul.517, bf16[2304,2048]{1,0:T(8,128)(2,1)S(1)} %bitcast.300, bf16[2048,1536]{1,0:T(8,128)(2,1)} %bitcast.326), kind=kOutput, calls=%fused_computation.31 | convolution fusion | flops 4854249472 | bytes 28067840 | tf_op jit(solution)/shard_map/dot_general | solution.py:16
  559.0 8.4 multiply_convert_fusion
  567.4 8.2 convolution_convert_fusion.1
  575.6 8.3 dynamic-slice_bitcast_fusion.1
  583.9 13.7 %convolution_convert_fusion.2 = bf16[2304,2048]{1,0:T(8,128)(2,1)S(1)} fusion(bf16[2048,1536]{1,0:T(8,128)(2,1)} %bitcast.328, bf16[2304,512]{0,1:T(8,128)(2,1)} %get-tuple-element.59, bf16[2304,512]{0,1:T(8,128)(2,1)} %get-tuple-element.58), kind=kOutput, calls=%fused_computation.11 | convolution fusion | flops 9677832192 | bytes 18350080 | tf_op jit(solution)/shard_map/dot_general | solution.py:20
  597.7 8.3 convolution_convert_fusion
  605.9 8.3 dynamic-slice_bitcast_fusion
  614.8 8.3 fusion.2
  627.9 5.8 fusion.1
  641.5 33.2 %collective-permute-done.20 = bf16[2,4,128,1024]{3,2,1,0:T(8,128)(2,1)} collective-permute-done((bf16[2,4,128,1024]{3,2,1,0:T(8,128)(2,1)S(1)}, bf16[2,4,128,1024]{3,2,1,0:T(8,128)(2,1)}, u32[]{:S(2)}, u32[]{:S(2)}) %collective-permute-start.20) | collective-permute-done | bytes 2097184 | tf_op jit(solution)/shard_map/ppermute | solution.py:29
  684.3 3.6 all-to-all-start.8
  687.9 16.6 %collective-permute-done.21 = bf16[4,128,1024]{2,1,0:T(8,128)(2,1)} collective-permute-done((bf16[4,128,1024]{2,1,0:T(8,128)(2,1)S(1)}, bf16[4,128,1024]{2,1,0:T(8,128)(2,1)}, u32[]{:S(2)}, u32[]{:S(2)}) %collective-permute-start.21) | collective-permute-done | bytes 1048608 | tf_op jit(solution)/shard_map/ppermute | solution.py:29
  707.1 39.6 %all-to-all-done.8 = f32[32,1,128]{2,1,0:T(1,128)S(1)} async-done(((f32[32,1,128]{2,1,0:T(1,128)}), f32[32,1,128]{2,1,0:T(1,128)S(1)}, u32[]{:S(2)}, u32[]{:S(2)}) %all-to-all-start.8) | async-done | bytes 16416 | tf_op jit(solution)/shard_map/all_to_all | solution.py:346
  757.5 22.3 %collective-permute-done.26 = bf16[4,128,1024]{2,1,0:T(8,128)(2,1)S(1)} collective-permute-done((bf16[4,128,1024]{2,1,0:T(8,128)(2,1)S(1)}, bf16[4,128,1024]{2,1,0:T(8,128)(2,1)S(1)}, u32[]{:S(2)}, u32[]{:S(2)}) %collective-permute-start.26) | collective-permute-done | bytes 1048608 | tf_op jit(solution)/shard_map/ppermute | solution.py:29
  781.1 5.1 all-to-all-start.6
  791.1 21.1 %collective-permute-done.28 = bf16[4,128,1024]{2,1,0:T(8,128)(2,1)S(1)} collective-permute-done((bf16[4,128,1024]{2,1,0:T(8,128)(2,1)S(1)}, bf16[4,128,1024]{2,1,0:T(8,128)(2,1)S(1)}, u32[]{:S(2)}, u32[]{:S(2)}) %collective-permute-start.28) | collective-permute-done | bytes 1048608 | tf_op jit(solution)/shard_map/ppermute | solution.py:29
  813.5 4.8 all-to-all-start.7
  818.3 5.6 collective-permute-done.22
  828.8 22.9 %collective-permute-done.23 = bf16[4,128,1024]{2,1,0:T(8,128)(2,1)S(1)} collective-permute-done((bf16[4,128,1024]{2,1,0:T(8,128)(2,1)S(1)}, bf16[4,128,1024]{2,1,0:T(8,128)(2,1)S(1)}, u32[]{:S(2)}, u32[]{:S(2)}) %collective-permute-start.23) | collective-permute-done | bytes 1048608 | tf_op jit(solution)/shard_map/ppermute | solution.py:29
  853.1 4.7 all-to-all-start.5
  858.0 12.7 %copy.224 = bf16[2048,2304]{1,0:T(8,128)(2,1)} copy(bf16[2048,2304]{0,1:T(8,128)(2,1)} %bitcast.297) | data formatting | bytes 18874368 | tf_op jit(solution)/shard_map/dot_general | solution.py:24
  870.6 12.2 copy.222
  892.9 14.1 %fusion.24 = bf16[4,512,1024]{2,1,0:T(8,128)(2,1)S(1)} fusion(bf16[4,512,2304]{2,1,0:T(8,128)(2,1)} %bitcast.317, bf16[2304,512]{0,1:T(8,128)(2,1)} %get-tuple-element.59, bf16[2304,512]{0,1:T(8,128)(2,1)} %get-tuple-element.58), kind=kOutput, calls=%fused_computation.56 | convolution fusion | flops 9675210752 | bytes 18350080 | tf_op jit(solution)/shard_map/dot_general | solution.py:24
  907.6 7.0 fusion.41
  917.9 5.5 all-to-all-start.11
  926.1 4.8 convolution_convert_fusion.6
  944.5 4.0 convolution_convert_fusion.9
  952.7 6.8 psum.15
  962.6 3.6 fusion.68
  966.1 4.6 copy-done
  974.2 12.7 %fusion.3 = f32[512,2048]{1,0:T(8,128)} fusion(s32[2048]{0:T(1024)S(1)} %copy-done.63, bf16[2048,1536]{1,0:T(8,128)(2,1)} %copy-done.44, bf16[512,512]{1,0:T(8,128)(2,1)S(1)} %copy-done.32, bf16[512,512]{1,0:T(8,128)(2,1)S(1)} %copy-done.30, bf16[512,512]{1,0:T(8,128)(2,1)S(1)} %copy-done.28), kind=kOutput, calls=%fused_computation.7 | convolution fusion | flops 7526154240 | bytes 12066816 | tf_op jit(solution)/shard_map/dot_general | solution.py:16
  990.3 72.1 %all-to-all-done.11 = bf16[4,512,1536]{2,1,0:T(8,128)(2,1)} async-done(((bf16[4,512,1536]{2,1,0:T(8,128)(2,1)}), bf16[4,512,1536]{2,1,0:T(8,128)(2,1)}, u32[]{:S(2)}, u32[]{:S(2)}) %all-to-all-start.11) | async-done | bytes 6291488 | tf_op jit(solution)/shard_map/all_to_all | solution.py:352
  1062.4 9.6 copy.226
  1072.0 10.7 copy.227
  1082.7 19.3 %copy.229 = f32[512,2,3072]{2,1,0:T(2,128)} copy(f32[512,2,3072]{0,2,1:T(8,128)} %bitcast.304) | data formatting | bytes 25165824
  1113.3 19.8 %collective-permute-done.38 = bf16[1,4,64,2048]{3,2,1,0:T(8,128)(2,1)} collective-permute-done((bf16[1,4,64,2048]{3,2,1,0:T(8,128)(2,1)}, bf16[1,4,64,2048]{3,2,1,0:T(8,128)(2,1)}, u32[]{:S(2)}, u32[]{:S(2)}) %collective-permute-start.38) | collective-permute-done | bytes 1048608 | tf_op jit(solution)/shard_map/ppermute | solution.py:29
  1137.0 5.7 fusion.149
  1148.5 9.8 collective-permute-done.40
  1166.2 38.0 %all-to-all-start.10 = ((f32[32,1,1280]{2,1,0:T(1,128)}), f32[32,1,1280]{2,1,0:T(1,128)}, u32[]{:S(2)}, u32[]{:S(2)}) async-start(f32[32,1,1280]{2,1,0:T(1,128)} %copy.221), calls=%async_computation.10 | async-start | bytes 327680 | tf_op jit(solution)/shard_map/all_to_all | solution.py:434
  1204.3 22.7 %collective-permute-done.36 = bf16[4,64,1536]{2,1,0:T(8,128)(2,1)} collective-permute-done((bf16[4,64,1536]{2,1,0:T(8,128)(2,1)}, bf16[4,64,1536]{2,1,0:T(8,128)(2,1)}, u32[]{:S(2)}, u32[]{:S(2)}) %collective-permute-start.36) | collective-permute-done | bytes 786464 | tf_op jit(solution)/shard_map/ppermute | solution.py:34
  1238.7 6.5 all-to-all-done.9
  (452 shorter events, 218.4 us)
Async XLA Ops:
  7.2 498.5 %all-gather.5.cloned.1.call-start = ((), (), s32[]{:S(2)}) async-start(), calls=%async_computation.13 | async-start | bytes 17301504 | tf_op jit(solution)/shard_map/all_gather | solution.py:306
  9.4 56.9 %collective-permute-start.1 = (bf16[128,2048]{1,0:T(8,128)(2,1)}, bf16[128,2048]{1,0:T(8,128)(2,1)}, u32[]{:S(2)}, u32[]{:S(2)}) collective-permute-start(bf16[128,2048]{1,0:T(8,128)(2,1)} %bitcast.323), channel_id=1, source_target_pairs={{0,8},{4,12},{8,0},{12,4},{1,9},{5,13},{9,1},{13,5},{2,10},{6,14},... | collective-permute-start | bytes 1572872 | tf_op jit(solution)/shard_map/ppermute | solution.py:29
  12.4 81.5 %collective-permute-start = (bf16[128,2048]{1,0:T(8,128)(2,1)}, bf16[128,2048]{1,0:T(8,128)(2,1)}, u32[]{:S(2)}, u32[]{:S(2)}) collective-permute-start(bf16[128,2048]{1,0:T(8,128)(2,1)} %bitcast.324), channel_id=1, source_target_pairs={{0,4},{4,0},{8,12},{12,8},{1,5},{5,1},{9,13},{13,9},{2,6},{6,2},{1... | collective-permute-start | bytes 1572872 | tf_op jit(solution)/shard_map/ppermute | solution.py:29
  14.9 21.7 %collective-permute-start.10 = (bf16[64,2048]{1,0:T(8,128)(2,1)S(1)}, bf16[64,2048]{1,0:T(8,128)(2,1)S(1)}, u32[]{:S(2)}, u32[]{:S(2)}) collective-permute-start(bf16[64,2048]{1,0:T(8,128)(2,1)S(1)} %get-tuple-element.89), channel_id=1, source_target_pairs={{0,1},{1,2},{2,3},{3,0},{4,5},{5,6},{6,7},{7,4},{8,9},{9,10},{10,1... | collective-permute-start | bytes 786440 | tf_op jit(solution)/shard_map/ppermute | solution.py:34
  16.5 48.7 %collective-permute-start.13 = (bf16[64,2048]{1,0:T(8,128)(2,1)S(1)}, bf16[64,2048]{1,0:T(8,128)(2,1)S(1)}, u32[]{:S(2)}, u32[]{:S(2)}) collective-permute-start(bf16[64,2048]{1,0:T(8,128)(2,1)S(1)} %get-tuple-element.89), channel_id=1, source_target_pairs={{0,16},{16,0},{1,17},{17,1},{2,18},{18,2},{3,19},{19,3},{4,20},{20... | collective-permute-start | bytes 786440 | tf_op jit(solution)/shard_map/ppermute | solution.py:29
  20.5 12.1 all-to-all-start
  23.6 120.6 %copy-start.62 = (s32[2048]{0:T(1024)}, s32[2048]{0:T(1024)S(1)}, u32[]{:S(2)}) copy-start(s32[2048]{0:T(1024)S(1)} %fusion.100) | copy-start | bytes 24580
  25.5 209.9 %copy-start.70 = (s32[512]{0:T(512)}, s32[512]{0:T(512)S(1)}, u32[]{:S(2)}) copy-start(s32[512]{0:T(512)S(1)} %fusion.124) | copy-start | bytes 6148
  32.6 16.1 %all-to-all-start.1 = ((bf16[4,64,1536]{2,1,0:T(8,128)(2,1)}), bf16[4,64,1536]{2,1,0:T(8,128)(2,1)S(1)}, u32[]{:S(2)}, u32[]{:S(2)}) async-start(bf16[4,64,1536]{2,1,0:T(8,128)(2,1)} %reshape.639), calls=%async_computation.1 | async-start | bytes 1572864 | tf_op jit(solution)/shard_map/all_to_all | solution.py:213
  36.1 481.7 %all-gather.3.cloned.1.call-start = ((), (), s32[]{:S(2)}) async-start(), calls=%async_computation.12 | async-start | bytes 17301504 | tf_op jit(solution)/shard_map/all_gather | solution.py:308
  36.5 10.5 collective-permute-start.11
  37.4 179.6 %copy-start.51 = (f32[1,2,1,256]{3,2,1,0:T(1,128)}, f32[1,2,1,256]{3,2,1,0:T(1,128)S(1)}, u32[]{:S(2)}) copy-start(f32[1,2,1,256]{3,2,1,0:T(1,128)S(1)} %get-tuple-element.108) | copy-start | bytes 6148
  37.4 179.6 %copy-start.53 = (f32[1,2,1,256]{3,2,1,0:T(1,128)}, f32[1,2,1,256]{3,2,1,0:T(1,128)S(1)}, u32[]{:S(2)}) copy-start(f32[1,2,1,256]{3,2,1,0:T(1,128)S(1)} %get-tuple-element.109) | copy-start | bytes 6148
  37.5 106.7 %copy-start.45 = (f32[2048]{0:T(1024)}, f32[2048]{0:T(1024)S(1)}, u32[]{:S(2)}) copy-start(f32[2048]{0:T(1024)S(1)} %mul.475) | copy-start | bytes 24580
  37.5 29.5 %collective-permute-start.14 = (bf16[64,2048]{1,0:T(8,128)(2,1)S(1)}, bf16[64,2048]{1,0:T(8,128)(2,1)}, u32[]{:S(2)}, u32[]{:S(2)}) collective-permute-start(bf16[64,2048]{1,0:T(8,128)(2,1)S(1)} %collective-permute-done.10), channel_id=1, source_target_pairs={{0,16},{16,0},{1,17},{17,1},{2,18},{18,2},{3,19},{19,3},{4,20},{20... | collective-permute-start | bytes 786440 | tf_op jit(solution)/shard_map/ppermute | solution.py:29
  47.0 16.2 %collective-permute-start.12 = (bf16[64,2048]{1,0:T(8,128)(2,1)S(1)}, bf16[64,2048]{1,0:T(8,128)(2,1)}, u32[]{:S(2)}, u32[]{:S(2)}) collective-permute-start(bf16[64,2048]{1,0:T(8,128)(2,1)S(1)} %collective-permute-done.11), channel_id=1, source_target_pairs={{0,1},{1,2},{2,3},{3,0},{4,5},{5,6},{6,7},{7,4},{8,9},{9,10},{10,1... | collective-permute-start | bytes 786440 | tf_op jit(solution)/shard_map/ppermute | solution.py:34
  63.3 30.7 %collective-permute-start.3 = (bf16[256,1536]{1,0:T(8,128)(2,1)S(1)}, bf16[256,1536]{1,0:T(8,128)(2,1)S(1)}, u32[]{:S(2)}, u32[]{:S(2)}) collective-permute-start(bf16[256,1536]{1,0:T(8,128)(2,1)S(1)} %bitcast.333), channel_id=1, source_target_pairs={{0,1},{1,2},{2,3},{3,0},{4,5},{5,6},{6,7},{7,4},{8,9},{9,10},{10,1... | collective-permute-start | bytes 2359304 | tf_op jit(solution)/shard_map/ppermute | solution.py:34
  65.1 9.5 collective-permute-start.15
  66.3 27.7 %collective-permute-start.2 = (bf16[128,2048]{1,0:T(8,128)(2,1)}, bf16[128,2048]{1,0:T(8,128)(2,1)S(1)}, u32[]{:S(2)}, u32[]{:S(2)}) collective-permute-start(bf16[128,2048]{1,0:T(8,128)(2,1)} %collective-permute-done.1), channel_id=1, source_target_pairs={{0,4},{4,0},{8,12},{12,8},{1,5},{5,1},{9,13},{13,9},{2,6},{6,2},{1... | collective-permute-start | bytes 1572872 | tf_op jit(solution)/shard_map/ppermute | solution.py:29
  67.0 109.4 %collective-permute-start.6 = (bf16[256,1536]{1,0:T(8,128)(2,1)S(1)}, bf16[256,1536]{1,0:T(8,128)(2,1)S(1)}, u32[]{:S(2)}, u32[]{:S(2)}) collective-permute-start(bf16[256,1536]{1,0:T(8,128)(2,1)S(1)} %bitcast.334), channel_id=1, source_target_pairs={{0,16},{16,0},{1,17},{17,1},{2,18},{18,2},{3,19},{19,3},{4,20},{20... | collective-permute-start | bytes 2359304 | tf_op jit(solution)/shard_map/ppermute | solution.py:29
  74.6 78.5 %collective-permute-start.16 = (bf16[64,2048]{1,0:T(8,128)(2,1)}, bf16[64,2048]{1,0:T(8,128)(2,1)S(1)}, u32[]{:S(2)}, u32[]{:S(2)}) collective-permute-start(bf16[64,2048]{1,0:T(8,128)(2,1)} %collective-permute-done.12), channel_id=1, source_target_pairs={{0,16},{16,0},{1,17},{17,1},{2,18},{18,2},{3,19},{19,3},{4,20},{20... | collective-permute-start | bytes 786440 | tf_op jit(solution)/shard_map/ppermute | solution.py:29
  93.9 38.5 %collective-permute-start.4 = (bf16[256,1536]{1,0:T(8,128)(2,1)S(1)}, bf16[256,1536]{1,0:T(8,128)(2,1)S(1)}, u32[]{:S(2)}, u32[]{:S(2)}) collective-permute-start(bf16[256,1536]{1,0:T(8,128)(2,1)S(1)} %collective-permute-done.3), channel_id=1, source_target_pairs={{0,1},{1,2},{2,3},{3,0},{4,5},{5,6},{6,7},{7,4},{8,9},{9,10},{10,1... | collective-permute-start | bytes 2359304 | tf_op jit(solution)/shard_map/ppermute | solution.py:34
  132.4 42.4 %collective-permute-start.5 = (bf16[256,1536]{1,0:T(8,128)(2,1)S(1)}, bf16[256,1536]{1,0:T(8,128)(2,1)S(1)}, u32[]{:S(2)}, u32[]{:S(2)}) collective-permute-start(bf16[256,1536]{1,0:T(8,128)(2,1)S(1)} %collective-permute-done.4), channel_id=1, source_target_pairs={{0,1},{1,2},{2,3},{3,0},{4,5},{5,6},{6,7},{7,4},{8,9},{9,10},{10,1... | collective-permute-start | bytes 2359304 | tf_op jit(solution)/shard_map/ppermute | solution.py:34
  153.8 22.6 %collective-permute-start.7 = (bf16[256,1536]{1,0:T(8,128)(2,1)S(1)}, bf16[256,1536]{1,0:T(8,128)(2,1)S(1)}, u32[]{:S(2)}, u32[]{:S(2)}) collective-permute-start(bf16[256,1536]{1,0:T(8,128)(2,1)S(1)} %collective-permute-done.3), channel_id=1, source_target_pairs={{0,16},{16,0},{1,17},{17,1},{2,18},{18,2},{3,19},{19,3},{4,20},{20... | collective-permute-start | bytes 2359304 | tf_op jit(solution)/shard_map/ppermute | solution.py:29
  155.6 35.5 %collective-permute-start.8 = (bf16[256,1536]{1,0:T(8,128)(2,1)S(1)}, bf16[256,1536]{1,0:T(8,128)(2,1)S(1)}, u32[]{:S(2)}, u32[]{:S(2)}) collective-permute-start(bf16[256,1536]{1,0:T(8,128)(2,1)S(1)} %collective-permute-done.4), channel_id=1, source_target_pairs={{0,16},{16,0},{1,17},{17,1},{2,18},{18,2},{3,19},{19,3},{4,20},{20... | collective-permute-start | bytes 2359304 | tf_op jit(solution)/shard_map/ppermute | solution.py:29
  174.8 32.0 %collective-permute-start.9 = (bf16[256,1536]{1,0:T(8,128)(2,1)S(1)}, bf16[256,1536]{1,0:T(8,128)(2,1)S(1)}, u32[]{:S(2)}, u32[]{:S(2)}) collective-permute-start(bf16[256,1536]{1,0:T(8,128)(2,1)S(1)} %collective-permute-done.5), channel_id=1, source_target_pairs={{0,16},{16,0},{1,17},{17,1},{2,18},{18,2},{3,19},{19,3},{4,20},{20... | collective-permute-start | bytes 2359304 | tf_op jit(solution)/shard_map/ppermute | solution.py:29
  239.3 2.9 collective-permute-start.17
  245.2 14.2 %collective-permute-start.18 = (bf16[128,2048]{1,0:T(8,128)(2,1)}, bf16[128,2048]{1,0:T(8,128)(2,1)S(1)}, u32[]{:S(2)}, u32[]{:S(2)}) collective-permute-start(bf16[128,2048]{1,0:T(8,128)(2,1)} %fusion.73), channel_id=1, source_target_pairs={{0,8},{4,12},{8,0},{12,4},{1,9},{5,13},{9,1},{13,5},{2,10},{6,14},... | collective-permute-start | bytes 1572872 | tf_op jit(solution)/shard_map/ppermute | solution.py:29
  264.9 27.7 %all-to-all-start.3 = ((f32[32,1,128]{2,1,0:T(1,128)}), f32[32,1,128]{2,1,0:T(1,128)S(1)}, u32[]{:S(2)}, u32[]{:S(2)}) async-start(f32[32,1,128]{2,1,0:T(1,128)} %bitcast.32), calls=%async_computation.3 | async-start | bytes 32768 | tf_op jit(solution)/shard_map/all_to_all | solution.py:310
  292.6 204.5 %all-to-all-start.2 = ((bf16[4,512,1536]{1,2,0:T(8,128)(2,1)}), bf16[4,512,1536]{1,2,0:T(8,128)(2,1)}, u32[]{:S(2)}, u32[]{:S(2)}) async-start(bf16[4,512,1536]{1,2,0:T(8,128)(2,1)} %bitcast.307), calls=%async_computation.2 | async-start | bytes 12582912 | tf_op jit(solution)/shard_map/all_to_all | solution.py:250
  583.9 30.9 %collective-permute-start.19 = (bf16[2,2,4,128,2048]{4,3,2,1,0:T(8,128)(2,1)}, bf16[2,2,4,128,2048]{4,3,2,1,0:T(8,128)(2,1)}, u32[]{:S(2)}, u32[]{:S(2)}) collective-permute-start(bf16[2,2,4,128,2048]{4,3,2,1,0:T(8,128)(2,1)} %dynamic-slice_bitcast_fusion.1), channel_id=1, source_target_pairs={{0,4},{4,0},{8,12},{12,8},{1,5},{5,1},{9,13},{13,9},{2,6},{6,2},{1... | collective-permute-start | bytes 25165832 | tf_op jit(solution)/shard_map/ppermute | solution.py:29
  614.3 13.6 %collective-permute-start.24 = (bf16[2,2,4,128,2048]{4,3,2,1,0:T(8,128)(2,1)}, bf16[2,2,4,128,2048]{4,3,2,1,0:T(8,128)(2,1)}, u32[]{:S(2)}, u32[]{:S(2)}) collective-permute-start(bf16[2,2,4,128,2048]{4,3,2,1,0:T(8,128)(2,1)} %dynamic-slice_bitcast_fusion), channel_id=1, source_target_pairs={{0,4},{4,0},{8,12},{12,8},{1,5},{5,1},{9,13},{13,9},{2,6},{6,2},{1... | collective-permute-start | bytes 25165832 | tf_op jit(solution)/shard_map/ppermute | solution.py:29
  626.1 48.7 %collective-permute-start.20 = (bf16[2,4,128,1024]{3,2,1,0:T(8,128)(2,1)S(1)}, bf16[2,4,128,1024]{3,2,1,0:T(8,128)(2,1)}, u32[]{:S(2)}, u32[]{:S(2)}) collective-permute-start(bf16[2,4,128,1024]{3,2,1,0:T(8,128)(2,1)S(1)} %dynamic-slice_bitcast_fusion.5), channel_id=1, source_target_pairs={{0,8},{4,12},{8,0},{12,4},{1,9},{5,13},{9,1},{13,5},{2,10},{6,14},... | collective-permute-start | bytes 6291464 | tf_op jit(solution)/shard_map/ppermute | solution.py:29
  640.0 110.1 %collective-permute-start.25 = (bf16[2,4,128,1024]{3,2,1,0:T(8,128)(2,1)}, bf16[2,4,128,1024]{3,2,1,0:T(8,128)(2,1)}, u32[]{:S(2)}, u32[]{:S(2)}) collective-permute-start(bf16[2,4,128,1024]{3,2,1,0:T(8,128)(2,1)} %dynamic-slice_bitcast_fusion.3), channel_id=1, source_target_pairs={{0,8},{4,12},{8,0},{12,4},{1,9},{5,13},{9,1},{13,5},{2,10},{6,14},... | collective-permute-start | bytes 6291464 | tf_op jit(solution)/shard_map/ppermute | solution.py:29
  678.1 26.4 %collective-permute-start.21 = (bf16[4,128,1024]{2,1,0:T(8,128)(2,1)S(1)}, bf16[4,128,1024]{2,1,0:T(8,128)(2,1)}, u32[]{:S(2)}, u32[]{:S(2)}) collective-permute-start(bf16[4,128,1024]{2,1,0:T(8,128)(2,1)S(1)} %dynamic-slice_bitcast_fusion.9), channel_id=1, source_target_pairs={{0,16},{16,0},{1,17},{17,1},{2,18},{18,2},{3,19},{19,3},{4,20},{20... | collective-permute-start | bytes 3145736 | tf_op jit(solution)/shard_map/ppermute | solution.py:29
  682.7 103.5 %collective-permute-start.27 = (bf16[2,4,128,1024]{3,2,1,0:T(8,128)(2,1)}, bf16[2,4,128,1024]{3,2,1,0:T(8,128)(2,1)}, u32[]{:S(2)}, u32[]{:S(2)}) collective-permute-start(bf16[2,4,128,1024]{3,2,1,0:T(8,128)(2,1)} %dynamic-slice_bitcast_fusion.2), channel_id=1, source_target_pairs={{0,16},{16,0},{1,17},{17,1},{2,18},{18,2},{3,19},{19,3},{4,20},{20... | collective-permute-start | bytes 6291464 | tf_op jit(solution)/shard_map/ppermute | solution.py:29
  684.3 62.3 %all-to-all-start.8 = ((f32[32,1,128]{2,1,0:T(1,128)}), f32[32,1,128]{2,1,0:T(1,128)S(1)}, u32[]{:S(2)}, u32[]{:S(2)}) async-start(f32[32,1,128]{2,1,0:T(1,128)} %bitcast.62), calls=%async_computation.8 | async-start | bytes 32768 | tf_op jit(solution)/shard_map/all_to_all | solution.py:346
  746.6 34.5 %all-to-all-start.4 = ((bf16[4,128,1024]{2,1,0:T(8,128)(2,1)}), bf16[4,128,1024]{2,1,0:T(8,128)(2,1)S(1)}, u32[]{:S(2)}, u32[]{:S(2)}) async-start(bf16[4,128,1024]{2,1,0:T(8,128)(2,1)} %fusion.35), calls=%async_computation.4 | async-start | bytes 2097152 | tf_op jit(solution)/shard_map/all_to_all | solution.py:128
  753.7 26.1 %collective-permute-start.26 = (bf16[4,128,1024]{2,1,0:T(8,128)(2,1)S(1)}, bf16[4,128,1024]{2,1,0:T(8,128)(2,1)S(1)}, u32[]{:S(2)}, u32[]{:S(2)}) collective-permute-start(bf16[4,128,1024]{2,1,0:T(8,128)(2,1)S(1)} %dynamic-slice_bitcast_fusion.7), channel_id=1, source_target_pairs={{0,16},{16,0},{1,17},{17,1},{2,18},{18,2},{3,19},{19,3},{4,20},{20... | collective-permute-start | bytes 3145736 | tf_op jit(solution)/shard_map/ppermute | solution.py:29
  756.9 67.1 %collective-permute-start.22 = (bf16[2,4,128,1024]{3,2,1,0:T(8,128)(2,1)}, bf16[2,4,128,1024]{3,2,1,0:T(8,128)(2,1)}, u32[]{:S(2)}, u32[]{:S(2)}) collective-permute-start(bf16[2,4,128,1024]{3,2,1,0:T(8,128)(2,1)} %dynamic-slice_bitcast_fusion.4), channel_id=1, source_target_pairs={{0,16},{16,0},{1,17},{17,1},{2,18},{18,2},{3,19},{19,3},{4,20},{20... | collective-permute-start | bytes 6291464 | tf_op jit(solution)/shard_map/ppermute | solution.py:29
  781.1 32.4 %all-to-all-start.6 = ((bf16[4,128,1024]{2,1,0:T(8,128)(2,1)}), bf16[4,128,1024]{2,1,0:T(8,128)(2,1)S(1)}, u32[]{:S(2)}, u32[]{:S(2)}) async-start(bf16[4,128,1024]{2,1,0:T(8,128)(2,1)} %fusion.33), calls=%async_computation.6 | async-start | bytes 2097152 | tf_op jit(solution)/shard_map/all_to_all | solution.py:128
  789.6 22.6 %collective-permute-start.28 = (bf16[4,128,1024]{2,1,0:T(8,128)(2,1)S(1)}, bf16[4,128,1024]{2,1,0:T(8,128)(2,1)S(1)}, u32[]{:S(2)}, u32[]{:S(2)}) collective-permute-start(bf16[4,128,1024]{2,1,0:T(8,128)(2,1)S(1)} %dynamic-slice_bitcast_fusion.6), channel_id=1, source_target_pairs={{0,8},{4,12},{8,0},{12,4},{1,9},{5,13},{9,1},{13,5},{2,10},{6,14},... | collective-permute-start | bytes 3145736 | tf_op jit(solution)/shard_map/ppermute | solution.py:29
  813.5 39.6 %all-to-all-start.7 = ((bf16[4,128,1024]{2,1,0:T(8,128)(2,1)}), bf16[4,128,1024]{2,1,0:T(8,128)(2,1)}, u32[]{:S(2)}, u32[]{:S(2)}) async-start(bf16[4,128,1024]{2,1,0:T(8,128)(2,1)} %fusion.32), calls=%async_computation.7 | async-start | bytes 2097152 | tf_op jit(solution)/shard_map/all_to_all | solution.py:128
  827.3 24.4 %collective-permute-start.23 = (bf16[4,128,1024]{2,1,0:T(8,128)(2,1)S(1)}, bf16[4,128,1024]{2,1,0:T(8,128)(2,1)S(1)}, u32[]{:S(2)}, u32[]{:S(2)}) collective-permute-start(bf16[4,128,1024]{2,1,0:T(8,128)(2,1)S(1)} %dynamic-slice_bitcast_fusion.8), channel_id=1, source_target_pairs={{0,8},{4,12},{8,0},{12,4},{1,9},{5,13},{9,1},{13,5},{2,10},{6,14},... | collective-permute-start | bytes 3145736 | tf_op jit(solution)/shard_map/ppermute | solution.py:29
  853.1 33.7 %all-to-all-start.5 = ((bf16[4,128,1024]{2,1,0:T(8,128)(2,1)}), bf16[4,128,1024]{2,1,0:T(8,128)(2,1)}, u32[]{:S(2)}, u32[]{:S(2)}) async-start(bf16[4,128,1024]{2,1,0:T(8,128)(2,1)} %fusion.34), calls=%async_computation.5 | async-start | bytes 2097152 | tf_op jit(solution)/shard_map/all_to_all | solution.py:128
  891.5 15.6 %collective-permute-start.30 = (bf16[128,2048]{1,0:T(8,128)(2,1)}, bf16[128,2048]{1,0:T(8,128)(2,1)S(1)}, u32[]{:S(2)}, u32[]{:S(2)}) collective-permute-start(bf16[128,2048]{1,0:T(8,128)(2,1)} %get-tuple-element.52), channel_id=1, source_target_pairs={{0,8},{4,12},{8,0},{12,4},{1,9},{5,13},{9,1},{13,5},{2,10},{6,14},... | collective-permute-start | bytes 1572872 | tf_op jit(solution)/shard_map/ppermute | solution.py:29
  907.0 16.4 %collective-permute-start.29 = (bf16[128,2048]{1,0:T(8,128)(2,1)}, bf16[128,2048]{1,0:T(8,128)(2,1)S(1)}, u32[]{:S(2)}, u32[]{:S(2)}) collective-permute-start(bf16[128,2048]{1,0:T(8,128)(2,1)} %get-tuple-element.52), channel_id=1, source_target_pairs={{0,4},{4,0},{8,12},{12,8},{1,5},{5,1},{9,13},{13,9},{2,6},{6,2},{1... | collective-permute-start | bytes 1572872 | tf_op jit(solution)/shard_map/ppermute | solution.py:29
  907.1 16.3 %collective-permute-start.31 = (bf16[128,2048]{1,0:T(8,128)(2,1)S(1)}, bf16[128,2048]{1,0:T(8,128)(2,1)S(1)}, u32[]{:S(2)}, u32[]{:S(2)}) collective-permute-start(bf16[128,2048]{1,0:T(8,128)(2,1)S(1)} %collective-permute-done.30), channel_id=1, source_target_pairs={{0,4},{4,0},{8,12},{12,8},{1,5},{5,1},{9,13},{13,9},{2,6},{6,2},{1... | collective-permute-start | bytes 1572872 | tf_op jit(solution)/shard_map/ppermute | solution.py:29
  917.9 144.5 %all-to-all-start.11 = ((bf16[4,512,1536]{2,1,0:T(8,128)(2,1)}), bf16[4,512,1536]{2,1,0:T(8,128)(2,1)}, u32[]{:S(2)}, u32[]{:S(2)}) async-start(bf16[4,512,1536]{2,1,0:T(8,128)(2,1)} %pad_maximum_fusion), calls=%async_computation.11 | async-start | bytes 12582912 | tf_op jit(solution)/shard_map/all_to_all | solution.py:352
  972.8 164.3 %collective-permute-start.34 = (bf16[1,4,4,64,1536]{4,3,2,1,0:T(8,128)(2,1)}, bf16[1,4,4,64,1536]{4,3,2,1,0:T(8,128)(2,1)}, u32[]{:S(2)}, u32[]{:S(2)}) collective-permute-start(bf16[1,4,4,64,1536]{4,3,2,1,0:T(8,128)(2,1)} %bitcast.83), channel_id=1, source_target_pairs={{0,16},{16,0},{1,17},{17,1},{2,18},{18,2},{3,19},{19,3},{4,20},{20... | collective-permute-start | bytes 9437192 | tf_op jit(solution)/shard_map/ppermute | solution.py:29
  988.7 121.7 %collective-permute-start.32 = (bf16[2,128,2048]{2,1,0:T(8,128)(2,1)S(1)}, bf16[2,128,2048]{2,1,0:T(8,128)(2,1)}, u32[]{:S(2)}, u32[]{:S(2)}) collective-permute-start(bf16[2,128,2048]{2,1,0:T(8,128)(2,1)S(1)} %fusion.60), channel_id=1, source_target_pairs={{0,4},{4,0},{8,12},{12,8},{1,5},{5,1},{9,13},{13,9},{2,6},{6,2},{1... | collective-permute-start | bytes 3145736 | tf_op jit(solution)/shard_map/ppermute | solution.py:29
  1108.2 25.0 %collective-permute-start.38 = (bf16[1,4,64,2048]{3,2,1,0:T(8,128)(2,1)}, bf16[1,4,64,2048]{3,2,1,0:T(8,128)(2,1)}, u32[]{:S(2)}, u32[]{:S(2)}) collective-permute-start(bf16[1,4,64,2048]{3,2,1,0:T(8,128)(2,1)} %bitcast.90), channel_id=1, source_target_pairs={{0,16},{16,0},{1,17},{17,1},{2,18},{18,2},{3,19},{19,3},{4,20},{20... | collective-permute-start | bytes 3145736 | tf_op jit(solution)/shard_map/ppermute | solution.py:29
  1112.7 46.5 %collective-permute-start.33 = (bf16[128,2048]{1,0:T(8,128)(2,1)S(1)}, bf16[128,2048]{1,0:T(8,128)(2,1)S(1)}, u32[]{:S(2)}, u32[]{:S(2)}) collective-permute-start(bf16[128,2048]{1,0:T(8,128)(2,1)S(1)} %fusion.74), channel_id=1, source_target_pairs={{0,8},{4,12},{8,0},{12,4},{1,9},{5,13},{9,1},{13,5},{2,10},{6,14},... | collective-permute-start | bytes 1572872 | tf_op jit(solution)/shard_map/ppermute | solution.py:29
  1134.9 12.4 collective-permute-start.39
  1136.4 21.9 %collective-permute-start.40 = (bf16[64,2048]{1,0:T(8,128)(2,1)S(1)}, bf16[64,2048]{1,0:T(8,128)(2,1)S(1)}, u32[]{:S(2)}, u32[]{:S(2)}) collective-permute-start(bf16[64,2048]{1,0:T(8,128)(2,1)S(1)} %get-tuple-element.83), channel_id=1, source_target_pairs={{0,2},{1,3},{2,0},{3,1},{4,6},{5,7},{6,4},{7,5},{8,10},{9,11},{10,... | collective-permute-start | bytes 786440 | tf_op jit(solution)/shard_map/ppermute | solution.py:34
  1136.4 21.9 %collective-permute-start.41 = (bf16[64,2048]{1,0:T(8,128)(2,1)S(1)}, bf16[64,2048]{1,0:T(8,128)(2,1)S(1)}, u32[]{:S(2)}, u32[]{:S(2)}) collective-permute-start(bf16[64,2048]{1,0:T(8,128)(2,1)S(1)} %get-tuple-element.82), channel_id=1, source_target_pairs={{0,1},{1,2},{2,3},{3,0},{4,5},{5,6},{6,7},{7,4},{8,9},{9,10},{10,1... | collective-permute-start | bytes 786440 | tf_op jit(solution)/shard_map/ppermute | solution.py:34
  1144.2 60.1 %collective-permute-start.35 = (bf16[4,64,1536]{2,1,0:T(8,128)(2,1)}, bf16[4,64,1536]{2,1,0:T(8,128)(2,1)S(1)}, u32[]{:S(2)}, u32[]{:S(2)}) collective-permute-start(bf16[4,64,1536]{2,1,0:T(8,128)(2,1)} %get-tuple-element.66), channel_id=1, source_target_pairs={{0,3},{1,0},{2,1},{3,2},{4,7},{5,4},{6,5},{7,6},{8,11},{9,8},{10,9... | collective-permute-start | bytes 2359304 | tf_op jit(solution)/shard_map/ppermute | solution.py:34
  1147.4 79.6 %collective-permute-start.36 = (bf16[4,64,1536]{2,1,0:T(8,128)(2,1)}, bf16[4,64,1536]{2,1,0:T(8,128)(2,1)}, u32[]{:S(2)}, u32[]{:S(2)}) collective-permute-start(bf16[4,64,1536]{2,1,0:T(8,128)(2,1)} %get-tuple-element.68), channel_id=1, source_target_pairs={{0,2},{1,3},{2,0},{3,1},{4,6},{5,7},{6,4},{7,5},{8,10},{9,11},{10,... | collective-permute-start | bytes 2359304 | tf_op jit(solution)/shard_map/ppermute | solution.py:34
  1158.3 68.6 %collective-permute-start.37 = (bf16[4,64,1536]{2,1,0:T(8,128)(2,1)}, bf16[4,64,1536]{2,1,0:T(8,128)(2,1)}, u32[]{:S(2)}, u32[]{:S(2)}) collective-permute-start(bf16[4,64,1536]{2,1,0:T(8,128)(2,1)} %get-tuple-element.67), channel_id=1, source_target_pairs={{0,1},{1,2},{2,3},{3,0},{4,5},{5,6},{6,7},{7,4},{8,9},{9,10},{10,1... | collective-permute-start | bytes 2359304 | tf_op jit(solution)/shard_map/ppermute | solution.py:34
  1161.6 72.0 %copy-start.73 = (f32[128]{0:T(128)S(1)}, f32[128]{0:T(128)}, u32[]{:S(2)}) copy-start(f32[128]{0:T(128)} %get-tuple-element.95) | copy-start | bytes 1540
  1161.6 72.0 %copy-start.68 = (f32[128]{0:T(128)S(1)}, f32[128]{0:T(128)}, u32[]{:S(2)}) copy-start(f32[128]{0:T(128)} %add_rsqrt_fusion.2) | copy-start | bytes 1540
  1165.4 68.2 %copy-start.76 = (f32[128]{0:T(128)S(1)}, f32[128]{0:T(128)}, u32[]{:S(2)}) copy-start(f32[128]{0:T(128)} %get-tuple-element.41) | copy-start | bytes 1540
  1166.2 63.8 %all-to-all-start.10 = ((f32[32,1,1280]{2,1,0:T(1,128)}), f32[32,1,1280]{2,1,0:T(1,128)}, u32[]{:S(2)}, u32[]{:S(2)}) async-start(f32[32,1,1280]{2,1,0:T(1,128)} %copy.221), calls=%async_computation.10 | async-start | bytes 327680 | tf_op jit(solution)/shard_map/all_to_all | solution.py:434
  1230.0 15.1 %all-to-all-start.9 = ((bf16[4,64,1536]{2,1,0:T(8,128)(2,1)}), bf16[4,64,1536]{2,1,0:T(8,128)(2,1)S(1)}, u32[]{:S(2)}, u32[]{:S(2)}) async-start(bf16[4,64,1536]{2,1,0:T(8,128)(2,1)} %fusion.50), calls=%async_computation.9 | async-start | bytes 1572864 | tf_op jit(solution)/shard_map/all_to_all | solution.py:411
  (84 other events, 818.1 us)
Sparse Core Ops, SparseCore 0:
  11.0 157.0 all-gather.4
  262.4 203.1 all-gather.2

commit v2 on v1

--- a/solution.py
+++ b/solution.py
@@ -1,6 +1,8 @@
 import jax
 import jax.numpy as jnp
 from jax import lax
+from jax.experimental import pallas as pl
+from jax.experimental.pallas import tpu as pltpu
 from jax.sharding import PartitionSpec as P
 
 HEADS = 16
@@ -37,11 +39,6 @@
 def bits_of(axis):
     count = lax.axis_size(axis)
     return [1 << i for i in range(count.bit_length() - 1)]
-
-
-def spread(value):
-    total = lax.axis_size(EVERY)
-    return lax.all_to_all(value, EVERY, 0, 0, tiled=True) if value.shape[0] == total else None
 
 
 def locate(stored_rows, doc_lens, blk_order, blk_rows):
@@ -106,28 +103,118 @@
     return value
 
 
-def token_scatter(value):
-    steps_e = [("expert", b) for b in bits_of("expert")]
-    steps_c = [("context", b) for b in bits_of("context")]
-    z_count = lax.axis_size("dp")
-    rows, width = value.shape[1:]
-    dims = list(reversed(steps_e)) + list(reversed(steps_c))
-    value = value.reshape((2,) * len(dims) + (z_count, rows, width))
-    first, rest = steps_c[0], steps_c[1:] + steps_e
-    dim = dims.index(first)
-    value = half_step(value, first[0], first[1], dim).astype(bf16)
-    dims = dims[:dim] + dims[dim + 1 :]
-    half = width // 2
-    outs = []
-    for part, order in ((value[..., :half], rest), (value[..., half:], rest[::-1])):
-        left = list(dims)
-        for step in order:
-            dim = left.index(step)
-            part = half_step(part, step[0], step[1], dim).astype(bf16)
-            left.remove(step)
-        got = lax.all_to_all(part, "dp", 0, 0, tiled=True)
-        outs.append(jnp.sum(got.astype(f32), axis=0))
-    return jnp.concatenate(outs, axis=1)
+def far_steps(k):
+    steps = [("context", b) for b in bits_of("context")[1:]]
+    steps = steps + [("expert", b) for b in bits_of("expert")]
+    return steps[::-1] if k % 2 else steps
+
+
+def near_step():
+    return ("context", bits_of("context")[0])
+
+
+def group_keys(k):
+    steps = [near_step()] + far_steps(k)
+    keys = []
+    for i in range(1 << len(steps)):
+        masks = {"expert": 0, "context": 0}
+        for j, (axis, bit) in enumerate(steps):
+            if i >> (len(steps) - 1 - j) & 1:
+                masks[axis] |= bit
+        keys.append((masks["expert"], masks["context"]))
+    return keys
+
+
+def token_gather(value):
+    around = [value]
+    for _ in range(lax.axis_size("dp") - 1):
+        around.append(shift(around[-1], "dp", 1))
+    groups = []
+    for k, start in enumerate(around):
+        held = {(0, 0): start}
+        for axis, bit in far_steps(k) + [near_step()]:
+            for key in list(held):
+                new = (key[0] | bit, key[1]) if axis == "expert" else (key[0], key[1] | bit)
+                held[new] = swap(held[key], axis, bit)
+        groups.append([held[key] for key in group_keys(k)])
+    return groups
+
+
+def group_scatter(value, k):
+    for axis, bit in [near_step()] + far_steps(k):
+        half = value.shape[0] // 2
+        got = swap(value[half:], axis, bit)
+        value = (value[:half].astype(f32) + got.astype(f32)).astype(bf16)
+    value = value[0]
+    return shift(value, "dp", -k) if k else value
+
+
+def around_dp(blocks):
+    count = lax.axis_size("dp")
+    me = lax.axis_index("dp")
+    got = []
+    for k in range(count):
+        block = lax.dynamic_index_in_dim(blocks, (me + k) % count, 0, keepdims=False)
+        got.append(shift(block, "dp", k) if k else block)
+    return got
+
+
+def split_kernel(experts, halves, w_ref, out_ref):
+    ffh = out_ref.shape[2] // 3
+    for e in range(experts):
+        rows = w_ref[:, e, :].astype(bf16)
+        for h in range(halves):
+            for j in range(3):
+                at = (j * halves + h) * ffh
+                out_ref[e * halves + h, :, j * ffh : (j + 1) * ffh] = rows[:, at : at + ffh]
+
+
+def split_experts(w, halves):
+    rows, experts, width = w.shape
+    block = 64
+    return pl.pallas_call(
+        lambda w_ref, out_ref: split_kernel(experts, halves, w_ref, out_ref),
+        grid=(rows // block,),
+        in_specs=[pl.BlockSpec((block, experts, width), lambda i: (i, 0, 0))],
+        out_specs=pl.BlockSpec(
+            (experts * halves, block, width // halves), lambda i: (0, i, 0)
+        ),
+        out_shape=jax.ShapeDtypeStruct((experts * halves, rows, width // halves), bf16),
+        compiler_params=pltpu.CompilerParams(vmem_limit_bytes=32 * 2**20),
+    )(w)
+
+
+def join_kernel(experts, halves, me_ref, *refs):
+    *parts, out_ref = refs
+    count = len(parts)
+    ffh = parts[0].shape[1] // 3
+    me = me_ref[0]
+    for t in range(count):
+        e, h = divmod(t, halves)
+        for j in range(3):
+            piece = parts[0][:, j * ffh : (j + 1) * ffh].astype(f32)
+            for k in range(1, count):
+                other = parts[k][:, j * ffh : (j + 1) * ffh].astype(f32)
+                piece = jnp.where((me - t - k) % count == 0, other, piece)
+            at = (j * halves + h) * ffh
+            out_ref[:, e, at : at + ffh] = piece
+
+
+def join_experts(parts, experts, halves):
+    rows, width = parts[0].shape
+    block = 64
+    me = lax.axis_index("dp").astype(jnp.int32).reshape(1) + len(parts)
+    return pl.pallas_call(
+        lambda me_ref, *refs: join_kernel(experts, halves, me_ref, *refs),
+        grid_spec=pltpu.PrefetchScalarGridSpec(
+            num_scalar_prefetch=1,
+            grid=(rows // block,),
+            in_specs=[pl.BlockSpec((block, width), lambda i, m: (i, 0)) for _ in parts],
+            out_specs=pl.BlockSpec((block, experts, width * halves), lambda i, m: (i, 0, 0)),
+        ),
+        out_shape=jax.ShapeDtypeStruct((rows, experts, width * halves), f32),
+        compiler_params=pltpu.CompilerParams(vmem_limit_bytes=32 * 2**20),
+    )(me, *parts)
 
 
 def relative_gather(piece):
@@ -140,14 +227,33 @@
     return held
 
 
+def absolute(held, rows, shape):
+    me_e, me_z = lax.axis_index("expert"), lax.axis_index("dp")
+    z_count = len(held[0])
+    first = shape(held[0][0])
+    whole = jnp.zeros((len(held), first.shape[1], z_count) + first.shape[3:], first.dtype)
+    for r, row in enumerate(held):
+        for k, part in enumerate(row):
+            at = (me_e ^ r, 0, (me_z - k) % z_count, 0, 0)
+            whole = lax.dynamic_update_slice(whole, shape(part), at)
+    return whole
+
+
 def relative_scatter(value):
+    me_e, me_z = lax.axis_index("expert"), lax.axis_index("dp")
     for bit in reversed(bits_of("expert")):
-        half = value.shape[0] // 2
-        value = value[:half].astype(f32) + swap(value[half:].astype(bf16), "expert", bit).astype(f32)
+        value = value.reshape((value.shape[0] // 2, 2) + value.shape[1:]) if bit == 1 else value
+        if bit == 1:
+            value = half_step(value, "expert", 1, 1)
+        else:
+            value = value.reshape((2, value.shape[0] // 2) + value.shape[1:])
+            value = half_step(value, "expert", bit, 0)
     value = value[0]
-    total = value[0].astype(f32)
-    for k in range(1, lax.axis_size("dp")):
-        total = total + shift(value[k].astype(bf16), "dp", -k).astype(f32)
+    z_count = lax.axis_size("dp")
+    total = lax.dynamic_index_in_dim(value, me_z, 0, keepdims=False).astype(f32)
+    for k in range(1, z_count):
+        part = lax.dynamic_index_in_dim(value, (me_z - k) % z_count, 0, keepdims=False)
+        total = total + shift(part.astype(bf16), "dp", -k).astype(f32)
     return total
 
 
@@ -212,42 +318,23 @@
     )
     wqkv = lax.all_to_all(wqkv, "context", 0, 0, tiled=True).reshape(c_count * w_rows, 3 * cols)
     held = relative_gather(wqkv)
-    wqkv_all = jnp.concatenate([part for row in held for part in row], axis=0)
+    z_done = held[0][-1]
+    wqkv_all = absolute(held, c_count * w_rows, lambda v: v.reshape(1, c_count, 1, w_rows, -1))
+    wqkv_all = wqkv_all.reshape(width, 3 * cols)
     wo_own = w_attn[:, 3 * width :].astype(bf16)
     if aligned:
-        wo_all = jnp.concatenate([part for row in relative_gather(wo_own) for part in row], axis=0)
+        wo_all = absolute(relative_gather(wo_own), w_rows, lambda v: v.reshape(1, 1, 1, w_rows, -1))
+        wo_all = wo_all.reshape(cols, width)
     else:
         wo_full = lax.all_gather(wo_own, EVERY, axis=0, tiled=True)
         wo_all = lax.dynamic_slice_in_dim(wo_full, me_c * cols, cols, axis=0)
 
-    def place_of(r_e, r_z, c, row):
-        return (((me_e ^ r_e) * c_count + c) * z_count + (me_z - r_z) % z_count) * w_rows + row
-
-    spots = jnp.arange(width, dtype=jnp.int32)
-    per_e = z_count * c_count * w_rows
-    feature_of = place_of(
-        spots // per_e,
-        spots // (c_count * w_rows) % z_count,
-        spots // w_rows % c_count,
-        spots % w_rows,
-    )
-    order_n = (spots[:, None] == feature_of[None, :]).astype(bf16)
-    if aligned:
-        near = jnp.arange(cols, dtype=jnp.int32)
-        local_of = (
-            (me_e ^ (near // block_rows)) * block_rows
-            + (me_z - near // w_rows % z_count) % z_count * w_rows
-            + near % w_rows
-        )
-        order_o = (near[:, None] == local_of[None, :]).astype(bf16)
-
-    wx = (
-        w_experts.astype(bf16)
-        .reshape(w_experts.shape[0], local_experts, 3, halves, ffh)
-        .transpose(1, 3, 0, 2, 4)
-        .reshape(z_count, w_experts.shape[0], 3 * ffh)
-    )
-    wx = lax.all_to_all(wx, "dp", 0, 0, tiled=True).reshape(width, 3 * ffh)
+    wx, _ = lax.optimization_barrier((split_experts(w_experts, halves), z_done))
+    d_rows = w_experts.shape[0]
+    wx_all = jnp.zeros((z_count, d_rows, 3 * ffh), bf16)
+    for k, part in enumerate(around_dp(wx)):
+        wx_all = lax.dynamic_update_slice(wx_all, part[None], ((me_z - k) % z_count, 0, 0))
+    wx = wx_all.reshape(width, 3 * ffh)
     w_gu, w_down = wx[:, : 2 * ffh], wx[:, 2 * ffh :]
 
     grad_out = cotangent[0]
@@ -255,8 +342,7 @@
     pack_x = context_gather(tokens[0]).astype(f32)
     scale_one = lax.rsqrt(jnp.mean(pack_x * pack_x, axis=-1, keepdims=True) + epsilon)
     normed_one = (pack_x * scale_one * gains[0]).astype(bf16)
-    normed_one_r = mm(normed_one, order_n).astype(bf16)
-    qkv = mm(normed_one_r, wqkv_all)
+    qkv = mm(normed_one, wqkv_all)
     place, doc, offset = locate(
         jnp.arange(pack_rows, dtype=jnp.int32), lengths[0], block_order[0], blk_rows
     )
@@ -296,68 +382,95 @@
         .reshape(pack_rows, cols)
         .astype(bf16)
     )
-    mixed_r = mm(mixed, order_o).astype(bf16) if aligned else mixed
-    hidden = inputs + context_scatter(mm(mixed_r, wo_all))
+    hidden = inputs + context_scatter(mm(mixed, wo_all))
     scale_two = lax.rsqrt(jnp.mean(hidden * hidden, axis=-1, keepdims=True) + epsilon)
     normed_two = (hidden * scale_two * gains[1]).astype(bf16)
     logits = mm(normed_two, router_w)
     probs = jax.nn.softmax(logits, axis=-1)
 
-    all_grad = lax.all_gather(grad_out.astype(bf16), EVERY, axis=0, tiled=True)
-    all_grad = all_grad.reshape(total, tok_rows, width)
-    all_normed = lax.all_gather(normed_two, EVERY, axis=0, tiled=True)
-    all_normed = all_normed.reshape(total, tok_rows, width)
+    own_grad, _ = lax.optimization_barrier((grad_out.astype(bf16), z_done))
+    all_grad = token_gather(own_grad)
+    all_normed = token_gather(normed_two)
     gate_rows = lax.all_to_all(jnp.repeat(probs.T, halves, axis=0), EVERY, 0, 0, tiled=True)
     slots = jnp.arange(slot_cap, dtype=jnp.int32)
-    pick = (slot_of[:, None, :] == slots[None, :, None]).astype(bf16)
-    put = (slot_of[:, :, None] == slots[None, None, :]).astype(bf16)
-
-    def take_rows(rows):
-        got = jnp.einsum("sct,std->scd", pick, rows, preferred_element_type=f32)
-        return got.astype(bf16).reshape(total * slot_cap, width)
-
-    def put_rows(rows):
-        rows = rows.astype(bf16).reshape(total, slot_cap, width)
-        return jnp.einsum("stc,scd->std", put, rows, preferred_element_type=f32).astype(bf16)
-
-    gate = jnp.sum(
-        jnp.where(slot_of[:, None, :] == slots[None, :, None], gate_rows[:, None, :], 0.0), axis=2
-    ).reshape(total * slot_cap, 1)
-    g_rows = take_rows(all_grad)
-    back = mm(g_rows, w_down)
-    n_rows = take_rows(all_normed)
-    gate_up = mm(n_rows, w_gu)
-    gate_part, up_part = gate_up[:, :ffh], gate_up[:, ffh:]
-    sig = jax.nn.sigmoid(gate_part)
-    silu = gate_part * sig
-    act = (silu * up_part).astype(bf16)
-    act_f = act.astype(f32)
-    grad_gate_slot = jnp.sum(act_f * back, axis=1).reshape(total, slot_cap)
-    grad_act = back * gate
-    grad_gu = jnp.concatenate(
-        [grad_act * up_part * sig * (1.0 + gate_part * (1.0 - sig)), grad_act * silu], axis=1
-    ).astype(bf16)
-    grad_rows = mm_nt(grad_gu, w_gu)
-    grad_n2 = token_scatter(put_rows(grad_rows))
+    sources = [
+        jnp.stack(
+            [
+                ((me_e ^ m_e) * c_count + (me_c ^ m_c)) * z_count + (me_z - k) % z_count
+                for m_e, m_c in group_keys(k)
+            ]
+        )
+        for k in range(z_count)
+    ]
+    n_src = len(group_keys(0))
+    n_rows, g_rows, acts, scaled, gus, puts, gate_parts, scattered = ([] for _ in range(8))
+    dgate_rows = []
+    for k in range(z_count):
+        slot_k = slot_of[sources[k]]
+        hit = slot_k[:, None, :] == slots[None, :, None]
+        pick = hit.astype(bf16)
+        put = (slot_k[:, :, None] == slots[None, None, :]).astype(bf16)
+        gate_in = gate_rows[sources[k]]
+        gate = jnp.sum(jnp.where(hit, gate_in[:, None, :], 0.0), axis=2)
+        gate = gate.reshape(n_src * slot_cap, 1)
+
+        def take_rows(rows):
+            got = jnp.einsum("sct,std->scd", pick, jnp.stack(rows), preferred_element_type=f32)
+            return got.astype(bf16).reshape(n_src * slot_cap, width)
+
+        g_k = take_rows(all_grad[k])
+        back = mm(g_k, w_down)
+        n_k = take_rows(all_normed[k])
+        gate_up = mm(n_k, w_gu)
+        gate_part, up_part = gate_up[:, :ffh], gate_up[:, ffh:]
+        sig = jax.nn.sigmoid(gate_part)
+        silu = gate_part * sig
+        act = (silu * up_part).astype(bf16)
+        act_f = act.astype(f32)
+        dgate = jnp.sum(act_f * back, axis=1).reshape(n_src, 1, slot_cap)
+        put_hit = slot_k[:, :, None] == slots[None, None, :]
+        dgate_rows.append(jnp.sum(jnp.where(put_hit, dgate, 0.0), axis=2))
+        grad_act = back * gate
+        grad_gu = jnp.concatenate(
+            [grad_act * up_part * sig * (1.0 + gate_part * (1.0 - sig)), grad_act * silu], axis=1
+        ).astype(bf16)
+        grad_rows = mm_nt(grad_gu, w_gu).astype(bf16).reshape(n_src, slot_cap, width)
+        grad_rows = jnp.einsum("stc,scd->std", put, grad_rows, preferred_element_type=f32)
+        scattered.append(group_scatter(grad_rows.astype(bf16), k))
+        n_rows.append(n_k)
+        g_rows.append(g_k)
+        acts.append(act)
+        scaled.append((act_f * gate).astype(bf16))
+        gus.append(grad_gu)
+        puts.append(put)
+        gate_parts.append(gate)
+    grad_n2 = sum(part.astype(f32) for part in scattered)
+    hits = jnp.arange(total)[:, None] == jnp.concatenate(sources)[None, :]
     sent_gates = jnp.sum(
-        jnp.where(slot_of[:, :, None] == slots[None, None, :], grad_gate_slot[:, None, :], 0.0),
-        axis=2,
+        jnp.where(hits[:, :, None], jnp.concatenate(dgate_rows)[None], 0.0), axis=1
     )
     got_gates = lax.all_to_all(sent_gates, EVERY, 0, 0, tiled=True)
     grad_probs = jnp.sum(got_gates.reshape(expert_count, halves, tok_rows), axis=1).T
 
-    act_scaled = (act_f * gate).astype(bf16)
-    grad_wx = jnp.concatenate([mm_tn(n_rows, grad_gu), mm_tn(g_rows, act_scaled)], axis=1)
-    grad_wx = grad_wx.astype(bf16).reshape(z_count, width // z_count, 3 * ffh)
-    grad_wx = lax.all_to_all(grad_wx, "dp", 0, 0, tiled=True)
-    grad_experts = (
-        grad_wx.astype(f32)
-        .reshape(local_experts, halves, width // z_count, 3, ffh)
-        .transpose(2, 0, 3, 1, 4)
-        .reshape(width // z_count, local_experts, 3 * ffn)
-    )
-    mixture = token_scatter(put_rows(mm_nt(act, w_down) * gate))
-    output = hidden + mixture
+    n_all, g_all = jnp.concatenate(n_rows), jnp.concatenate(g_rows)
+    grad_wx = jnp.concatenate(
+        [
+            mm_tn(n_all, jnp.concatenate(gus)).astype(bf16),
+            mm_tn(g_all, jnp.concatenate(scaled)).astype(bf16),
+        ],
+        axis=1,
+    )
+    grad_experts = join_experts(
+        around_dp(grad_wx.reshape(z_count, d_rows, 3 * ffh)), local_experts, halves
+    )
+    mixture = []
+    for k in range(z_count):
+        y = (mm_nt(acts[k], w_down) * gate_parts[k]).astype(bf16)
+        y = y.reshape(n_src, slot_cap, width)
+        y = jnp.einsum("stc,scd->std", puts[k], y, preferred_element_type=f32).astype(bf16)
+        y, _ = lax.optimization_barrier((y, scattered[-1]))
+        mixture.append(group_scatter(y, k))
+    output = hidden + sum(part.astype(f32) for part in mixture)
 
     grad_logits = (
         probs * (grad_probs - jnp.sum(probs * grad_probs, axis=-1, keepdims=True))
@@ -376,8 +489,6 @@
 
     pack_dh = context_gather(grad_hidden_b)
     grad_mixed = mm_nt(pack_dh, wo_all).astype(bf16)
-    if aligned:
-        grad_mixed = mm_nt(grad_mixed, order_o).astype(bf16)
     grad_mixed_h = grad_mixed.reshape(pack_rows, local_heads, head_width)
     grad_soft = jnp.einsum("qhd,khd->hqk", grad_mixed_h, value, preferred_element_type=f32)
     delta = jnp.sum(soft * grad_soft, axis=2, keepdims=True)
@@ -399,14 +510,13 @@
         ],
         axis=1,
     ).astype(bf16)
-    grad_n1 = mm(context_pull(grad_qkv, wqkv_all), order_n_t(order_n))
-    grad_n1 = context_scatter(grad_n1)
+    grad_n1 = context_scatter(mm_nt(grad_qkv, wqkv_all))
     own_scale = lax.rsqrt(jnp.mean(inputs * inputs, axis=-1, keepdims=True) + epsilon)
     gain_one = jnp.sum(grad_n1 * inputs * own_scale, axis=0)
     grad_tokens = grad_hidden + norm_back(inputs, own_scale, gains[0], grad_n1)
 
-    grad_wqkv = mm_tn(normed_one_r, grad_qkv).reshape(e_count, z_count, c_count, w_rows, 3 * cols)
-    grad_wqkv = relative_scatter(grad_wqkv).astype(bf16)
+    grad_wqkv = mm_tn(normed_one, grad_qkv).reshape(e_count, c_count, z_count, w_rows, 3 * cols)
+    grad_wqkv = relative_scatter(grad_wqkv.transpose(0, 2, 1, 3, 4)).astype(bf16)
     grad_wqkv = (
         lax.all_to_all(grad_wqkv, "context", 0, 0, tiled=True)
         .reshape(c_count, w_rows, 3, runs, run_cols)
@@ -414,7 +524,7 @@
         .reshape(w_rows, 3 * width)
         .astype(f32)
     )
-    grad_wo = mm_tn(mixed_r, pack_dh)
+    grad_wo = mm_tn(mixed, pack_dh)
     if aligned:
         grad_wo = relative_scatter(grad_wo.reshape(e_count, z_count, w_rows, width))
     else:
@@ -435,14 +545,6 @@
     grad_router = small_grads[:n_router].reshape(w_router.shape)
     grad_gains = small_grads[n_router:].reshape(norm_gains.shape)
     return (output[None], grad_tokens[None], grad_attn, grad_router, grad_gains, grad_experts)
-
-
-def context_pull(grad_qkv, wqkv_all):
-    return mm_nt(grad_qkv, wqkv_all).astype(bf16)
-
-
-def order_n_t(order_n):
-    return order_n.T
 
 
 def solution(mesh):

time: 1270 us -> 1360 us (1.071)
  starting transfers between devices: 135 us -> 244 us
  Pallas kernels: 0 us -> 22.9 us
  other arithmetic: 97.3 us -> 82 us
    all_to_all x6 -> x0, waiting for transfers between devices: 270 us -> none  [the longest x1 198 us: on_device(): wx = lax.all_to_all(wx, 'dp', 0, 0, tiled=True).reshape(width, 3 * ffh)]
    ppermute x30 -> x100, waiting for transfers between devices: 192 us -> 358 us  [swap(): return lax.ppermute(value, axis, [(i, i ^ bit) for i in range(count)])]
    ppermute x12 -> x30, waiting for transfers between devices: 128 us -> 267 us  [shift(): lax.ppermute(value, axis, [(i, (i + step) % count) for i in range(count)])]
    ppermute x12 -> x30, starting transfers between devices: 20.8 us -> 139 us  [shift(): lax.ppermute(value, axis, [(i, (i + step) % count) for i in range(count)])]
    ppermute x30 -> x100, starting transfers between devices: 29.3 us -> 73.5 us  [swap(): return lax.ppermute(value, axis, [(i, i ^ bit) for i in range(count)])]
    all_to_all x1, waiting for transfers between devices: 39.6 us -> 0.01 us  [on_device(): got_gates = lax.all_to_all(sent_gates, EVERY, 0, 0, tiled=True)]
    all_to_all x6 -> x0, starting transfers between devices: 28.9 us -> none  [the longest x4 18.1 us: token_scatter(): got = lax.all_to_all(part, 'dp', 0, 0, tiled=True)]
    dot_general x9 -> x12, matrix products: 57.3 us -> 28.7 us  [mm(): return jnp.dot(a, b, preferred_element_type=f32)]
  transfers between devices with their start and end apart: 56 -> 136, of which waited for: 26 -> 47; matrix products, arithmetic and copies ran while one was open for 29% -> 27% of each run, Pallas kernels for 0% -> 2%
where the time goes in v2:
time: 1360 us; the launch traced here: 1350 us
  waiting for transfers between devices  637 us (47%)
  starting transfers between devices  244 us (18%)
  local copies, waits for them, and re-layouts  183 us (13%)
  matrix products  163 us (12%)
  other arithmetic  82 us (6%)
  Pallas kernels  22.9 us (2%)
    ppermute x100, waiting for transfers between devices, swap(): return lax.ppermute(value, axis, [(i, i ^ bit) for i in range(count)])  358 us
    ppermute x30, waiting for transfers between devices, shift(): lax.ppermute(value, axis, [(i, (i + step) % count) for i in range(count)])  267 us
    ppermute x30, starting transfers between devices, shift(): lax.ppermute(value, axis, [(i, (i + step) % count) for i in range(count)])  139 us
    unnamed x369, local copies, waits for them, and re-layouts  82.1 us
    ppermute x100, starting transfers between devices, swap(): return lax.ppermute(value, axis, [(i, i ^ bit) for i in range(count)])  73.5 us
    dot_general x5, matrix products, mm_tn(): lax.dot_general(a, b, (((0,), (0,)), ((), ())), preferred_element_type=f32)  42.7 us
    dot_general x11, matrix products, mm_nt(): lax.dot_general(a, b, (((1,), (1,)), ((), ())), preferred_element_type=f32)  32.8 us
    dot_general x12, matrix products, mm(): return jnp.dot(a, b, preferred_element_type=f32)  28.7 us
  transfers between devices with their start and end apart: 136, of which 47 were waited for; matrix products, arithmetic and copies ran while one was open for 27% of the time, Pallas kernels for 2%

profile of v2, /device:TPU:0, one launch (start us, length us, event | category | flops | bytes accessed | tf_op | source)
XLA Modules:
  0.0 1349.5 jit_solution(4601082088827410928)
XLA Ops:
  30.5 4.6 copy-done.1
  35.1 12.8 shard_map.136
  64.3 8.0 collective-permute-done.11
  74.7 7.3 collective-permute-done.12
  87.2 19.0 %collective-permute-done.3 = bf16[256,1536]{1,0:T(8,128)(2,1)} collective-permute-done((bf16[256,1536]{1,0:T(8,128)(2,1)S(1)}, bf16[256,1536]{1,0:T(8,128)(2,1)}, u32[]{:S(2)}, u32[]{:S(2)}) %collective-permute-start.3) | collective-permute-done | bytes 786464 | tf_op jit(solution)/shard_map/ppermute | solution.py:36
  111.2 16.0 %collective-permute-done.4 = bf16[256,1536]{1,0:T(8,128)(2,1)} collective-permute-done((bf16[256,1536]{1,0:T(8,128)(2,1)}, bf16[256,1536]{1,0:T(8,128)(2,1)}, u32[]{:S(2)}, u32[]{:S(2)}) %collective-permute-start.4) | collective-permute-done | bytes 786464 | tf_op jit(solution)/shard_map/ppermute | solution.py:36
  132.6 14.7 %collective-permute-done.5 = bf16[256,1536]{1,0:T(8,128)(2,1)S(1)} collective-permute-done((bf16[256,1536]{1,0:T(8,128)(2,1)}, bf16[256,1536]{1,0:T(8,128)(2,1)S(1)}, u32[]{:S(2)}, u32[]{:S(2)}) %collective-permute-start.5) | collective-permute-done | bytes 786464 | tf_op jit(solution)/shard_map/ppermute | solution.py:36
  158.1 7.4 collective-permute-done.8
  177.1 14.1 %collective-permute-done.9 = bf16[256,1536]{1,0:T(8,128)(2,1)S(1)} collective-permute-done((bf16[256,1536]{1,0:T(8,128)(2,1)S(1)}, bf16[256,1536]{1,0:T(8,128)(2,1)S(1)}, u32[]{:S(2)}, u32[]{:S(2)}) %collective-permute-start.9) | collective-permute-done | bytes 786464 | tf_op jit(solution)/shard_map/ppermute | solution.py:31
  195.2 6.1 psum.14
  211.8 5.0 fusion.236
  224.8 22.9 %collective-permute-done.30 = bf16[128,2048]{1,0:T(8,128)(2,1)} collective-permute-done((bf16[128,2048]{1,0:T(8,128)(2,1)}, bf16[128,2048]{1,0:T(8,128)(2,1)}, u32[]{:S(2)}, u32[]{:S(2)}) %collective-permute-start.30) | collective-permute-done | bytes 524320 | tf_op jit(solution)/shard_map/ppermute | solution.py:36
  252.0 10.8 collective-permute-done.93
  262.8 31.0 %collective-permute-start.26 = (bf16[512,1536]{1,0:T(8,128)(2,1)S(1)}, bf16[512,1536]{1,0:T(8,128)(2,1)S(1)}, u32[]{:S(2)}, u32[]{:S(2)}) collective-permute-start(bf16[512,1536]{1,0:T(8,128)(2,1)S(1)} %copy-done.67), channel_id=1, source_target_pairs={{0,1},{1,2},{2,3},{3,0},{4,5},{5,6},{6,7},{7,4},{8,9},{9,10},{10,1... | collective-permute-start | bytes 4718600 | tf_op jit(solution)/shard_map/ppermute | solution.py:36
  295.8 10.5 collective-permute-start.31
  308.0 29.1 %collective-permute-done.31 = bf16[128,2048]{1,0:T(8,128)(2,1)S(1)} collective-permute-done((bf16[128,2048]{1,0:T(8,128)(2,1)}, bf16[128,2048]{1,0:T(8,128)(2,1)S(1)}, u32[]{:S(2)}, u32[]{:S(2)}) %collective-permute-start.31) | collective-permute-done | bytes 524320 | tf_op jit(solution)/shard_map/ppermute | solution.py:36
  340.0 12.1 collective-permute-done.104
  352.2 7.5 collective-permute-done.94
  373.8 12.6 collective-permute-done.32
  393.6 10.3 collective-permute-done.33
  409.4 5.4 all-to-all-start.2
  416.7 5.2 all-to-all-done.2
  436.7 4.5 convolution_convert_fusion.8
  453.0 10.4 collective-permute-done.40
  470.9 8.8 collective-permute-done.21
  497.5 8.0 collective-permute-done.68
  514.8 8.2 collective-permute-done.41
  548.1 4.3 convolution_convert_fusion.17
  567.7 5.7 collective-permute-done.43
  593.1 4.1 convolution_convert_fusion.16
  621.8 3.9 convolution_convert_fusion.19
  625.8 24.9 %fusion.35 = bf16[2048,1024]{0,1:T(8,128)(2,1)} fusion(bf16[576,512]{1,0:T(8,128)(2,1)} %copy-done.142, bf16[576,512]{1,0:T(8,128)(2,1)} %copy-done.141, bf16[576,512]{1,0:T(8,128)(2,1)} %copy-done.140, bf16[576,512]{1,0:T(8,128)(2,1)} %copy-done.139, bf16[576,512]{1,0:T(8,128)(2,1)} %copy-done.138, bf16[576,512]{1,0:T(8,128)(2,1)} %copy-done.137, ...), kind=kOutput, calls=%fused_computation.64 | convolution fusion | flops 9741271040 | bytes 18350080 | tf_op jit(solution)/shard_map/dot_general | solution.py:26
  659.6 6.8 fusion.42
  666.4 4.5 multiply_convert_fusion
  675.3 8.7 copy.262
  686.5 5.2 dynamic-slice_bitcast_fusion
  707.3 21.1 %collective-permute-done.50 = bf16[2,128,2048]{2,1,0:T(8,128)(2,1)S(1)} collective-permute-done((bf16[2,128,2048]{2,1,0:T(8,128)(2,1)S(1)}, bf16[2,128,2048]{2,1,0:T(8,128)(2,1)S(1)}, u32[]{:S(2)}, u32[]{:S(2)}) %collective-permute-start.50) | collective-permute-done | bytes 1048608 | tf_op jit(solution)/shard_map/ppermute | solution.py:31
  733.8 10.0 collective-permute-done.51
  748.2 6.8 collective-permute-done.52
  757.1 9.1 collective-permute-done.111
  768.5 20.2 %collective-permute-done.90 = bf16[2,128,2048]{2,1,0:T(8,128)(2,1)S(1)} collective-permute-done((bf16[2,128,2048]{2,1,0:T(8,128)(2,1)S(1)}, bf16[2,128,2048]{2,1,0:T(8,128)(2,1)S(1)}, u32[]{:S(2)}, u32[]{:S(2)}) %collective-permute-start.90) | collective-permute-done | bytes 1048608 | tf_op jit(solution)/shard_map/ppermute | solution.py:31
  790.2 6.6 collective-permute-done.101
  808.8 29.2 %collective-permute-done.79 = bf16[2,128,2048]{2,1,0:T(8,128)(2,1)S(1)} collective-permute-done((bf16[2,128,2048]{2,1,0:T(8,128)(2,1)S(1)}, bf16[2,128,2048]{2,1,0:T(8,128)(2,1)S(1)}, u32[]{:S(2)}, u32[]{:S(2)}) %collective-permute-start.79) | collective-permute-done | bytes 1048608 | tf_op jit(solution)/shard_map/ppermute | solution.py:31
  839.9 19.6 %collective-permute-done.64 = bf16[2,128,2048]{2,1,0:T(8,128)(2,1)S(1)} collective-permute-done((bf16[2,128,2048]{2,1,0:T(8,128)(2,1)S(1)}, bf16[2,128,2048]{2,1,0:T(8,128)(2,1)S(1)}, u32[]{:S(2)}, u32[]{:S(2)}) %collective-permute-start.64) | collective-permute-done | bytes 1048608 | tf_op jit(solution)/shard_map/ppermute | solution.py:31
  863.2 22.4 %collective-permute-done.54 = bf16[2,128,2048]{2,1,0:T(8,128)(2,1)S(1)} collective-permute-done((bf16[2,128,2048]{2,1,0:T(8,128)(2,1)S(1)}, bf16[2,128,2048]{2,1,0:T(8,128)(2,1)S(1)}, u32[]{:S(2)}, u32[]{:S(2)}) %collective-permute-start.54) | collective-permute-done | bytes 1048608 | tf_op jit(solution)/shard_map/ppermute | solution.py:31
  887.6 9.3 collective-permute-done.80
  898.5 7.7 collective-permute-done.65
  912.6 29.8 %collective-permute-done.113 = bf16[128,2048]{1,0:T(8,128)(2,1)S(1)} collective-permute-done((bf16[128,2048]{1,0:T(8,128)(2,1)S(1)}, bf16[128,2048]{1,0:T(8,128)(2,1)S(1)}, u32[]{:S(2)}, u32[]{:S(2)}) %collective-permute-start.113) | collective-permute-done | bytes 524320 | tf_op jit(solution)/shard_map/ppermute | solution.py:36
  947.1 49.7 %collective-permute-start.127 = (bf16[512,1536]{1,0:T(8,128)(2,1)}, bf16[512,1536]{1,0:T(8,128)(2,1)}, u32[]{:S(2)}, u32[]{:S(2)}) collective-permute-start(bf16[512,1536]{1,0:T(8,128)(2,1)} %get-tuple-element.71), channel_id=1, source_target_pairs={{0,1},{1,2},{2,3},{3,0},{4,5},{5,6},{6,7},{7,4},{8,9},{9,10},{10,1... | collective-permute-start | bytes 4718600 | tf_op jit(solution)/shard_map/ppermute | solution.py:36
  996.8 44.0 %collective-permute-done.77 = bf16[128,2048]{1,0:T(8,128)(2,1)S(1)} collective-permute-done((bf16[128,2048]{1,0:T(8,128)(2,1)S(1)}, bf16[128,2048]{1,0:T(8,128)(2,1)S(1)}, u32[]{:S(2)}, u32[]{:S(2)}) %collective-permute-start.77) | collective-permute-done | bytes 524320 | tf_op jit(solution)/shard_map/ppermute | solution.py:36
  1044.2 12.4 collective-permute-done.115
  1061.6 12.9 collective-permute-done.128.refs_2_
  1074.5 10.1 shard_map.137
  1101.0 5.1 fusion.52
  1118.3 7.1 psum.15
  1131.3 4.5 copy-done.24
  1141.8 5.6 fusion.57
  1150.3 79.0 %collective-permute-done.123 = bf16[1,4,64,2048]{3,2,1,0:T(8,128)(2,1)} collective-permute-done((bf16[1,4,64,2048]{3,2,1,0:T(8,128)(2,1)S(1)}, bf16[1,4,64,2048]{3,2,1,0:T(8,128)(2,1)}, u32[]{:S(2)}, u32[]{:S(2)}) %collective-permute-start.123) | collective-permute-done | bytes 1048608 | tf_op jit(solution)/shard_map/ppermute | solution.py:31
  1237.4 5.1 bitcast_add_fusion
  1246.7 4.2 collective-permute-start.122
  1250.9 15.4 %collective-permute-start.121 = (bf16[4,64,1536]{2,1,0:T(8,128)(2,1)}, bf16[4,64,1536]{2,1,0:T(8,128)(2,1)}, u32[]{:S(2)}, u32[]{:S(2)}) collective-permute-start(bf16[4,64,1536]{2,1,0:T(8,128)(2,1)} %get-tuple-element.75), channel_id=1, source_target_pairs={{0,2},{1,3},{2,0},{3,1},{4,6},{5,7},{6,4},{7,5},{8,10},{9,11},{10,... | collective-permute-start | bytes 2359304 | tf_op jit(solution)/shard_map/ppermute | solution.py:36
  1274.2 12.9 all-to-all-start.5
  1287.3 38.2 %collective-permute-done.121 = bf16[4,64,1536]{2,1,0:T(8,128)(2,1)} collective-permute-done((bf16[4,64,1536]{2,1,0:T(8,128)(2,1)}, bf16[4,64,1536]{2,1,0:T(8,128)(2,1)}, u32[]{:S(2)}, u32[]{:S(2)}) %collective-permute-start.121) | collective-permute-done | bytes 786464 | tf_op jit(solution)/shard_map/ppermute | solution.py:36
  1337.5 6.5 all-to-all-done.4
  (887 shorter events, 460.1 us)
Async XLA Ops:
  0.7 73.4 %collective-permute-start.1 = (bf16[128,2048]{1,0:T(8,128)(2,1)}, bf16[128,2048]{1,0:T(8,128)(2,1)}, u32[]{:S(2)}, u32[]{:S(2)}) collective-permute-start(bf16[128,2048]{1,0:T(8,128)(2,1)} %bitcast.571), channel_id=1, source_target_pairs={{0,8},{4,12},{8,0},{12,4},{1,9},{5,13},{9,1},{13,5},{2,10},{6,14},... | collective-permute-start | bytes 1572872 | tf_op jit(solution)/shard_map/ppermute | solution.py:31
  3.7 105.0 %collective-permute-start = (bf16[128,2048]{1,0:T(8,128)(2,1)}, bf16[128,2048]{1,0:T(8,128)(2,1)}, u32[]{:S(2)}, u32[]{:S(2)}) collective-permute-start(bf16[128,2048]{1,0:T(8,128)(2,1)} %bitcast.572), channel_id=1, source_target_pairs={{0,4},{4,0},{8,12},{12,8},{1,5},{5,1},{9,13},{13,9},{2,6},{6,2},{1... | collective-permute-start | bytes 1572872 | tf_op jit(solution)/shard_map/ppermute | solution.py:31
  6.1 54.0 %collective-permute-start.10 = (bf16[64,2048]{1,0:T(8,128)(2,1)}, bf16[64,2048]{1,0:T(8,128)(2,1)}, u32[]{:S(2)}, u32[]{:S(2)}) collective-permute-start(bf16[64,2048]{1,0:T(8,128)(2,1)} %slice.407), channel_id=1, source_target_pairs={{0,1},{1,2},{2,3},{3,0},{4,5},{5,6},{6,7},{7,4},{8,9},{9,10},{10,1... | collective-permute-start | bytes 786440 | tf_op jit(solution)/shard_map/ppermute | solution.py:36
  7.7 75.3 %collective-permute-start.13 = (bf16[64,2048]{1,0:T(8,128)(2,1)}, bf16[64,2048]{1,0:T(8,128)(2,1)}, u32[]{:S(2)}, u32[]{:S(2)}) collective-permute-start(bf16[64,2048]{1,0:T(8,128)(2,1)} %slice.407), channel_id=1, source_target_pairs={{0,16},{16,0},{1,17},{17,1},{2,18},{18,2},{3,19},{19,3},{4,20},{20... | collective-permute-start | bytes 786440 | tf_op jit(solution)/shard_map/ppermute | solution.py:31
  13.7 38.0 %all-to-all-start = ((bf16[32,2,704]{2,1,0:T(2,128)(2,1)}), bf16[32,2,704]{2,1,0:T(2,128)(2,1)}, u32[]{:S(2)}, u32[]{:S(2)}) async-start(bf16[32,2,704]{2,1,0:T(2,128)(2,1)} %reshape.1970), calls=%async_computation | async-start | bytes 196608 | tf_op jit(solution)/shard_map/all_to_all | solution.py:300
  83.0 70.5 %collective-permute-start.6 = (bf16[256,1536]{1,0:T(8,128)(2,1)S(1)}, bf16[256,1536]{1,0:T(8,128)(2,1)}, u32[]{:S(2)}, u32[]{:S(2)}) collective-permute-start(bf16[256,1536]{1,0:T(8,128)(2,1)S(1)} %bitcast.607), channel_id=1, source_target_pairs={{0,16},{16,0},{1,17},{17,1},{2,18},{18,2},{3,19},{19,3},{4,20},{20... | collective-permute-start | bytes 2359304 | tf_op jit(solution)/shard_map/ppermute | solution.py:31
  127.9 27.5 %collective-permute-start.7 = (bf16[256,1536]{1,0:T(8,128)(2,1)}, bf16[256,1536]{1,0:T(8,128)(2,1)}, u32[]{:S(2)}, u32[]{:S(2)}) collective-permute-start(bf16[256,1536]{1,0:T(8,128)(2,1)} %collective-permute-done.3), channel_id=1, source_target_pairs={{0,16},{16,0},{1,17},{17,1},{2,18},{18,2},{3,19},{19,3},{4,20},{20... | collective-permute-start | bytes 2359304 | tf_op jit(solution)/shard_map/ppermute | solution.py:31
  130.6 34.9 %collective-permute-start.8 = (bf16[256,1536]{1,0:T(8,128)(2,1)}, bf16[256,1536]{1,0:T(8,128)(2,1)}, u32[]{:S(2)}, u32[]{:S(2)}) collective-permute-start(bf16[256,1536]{1,0:T(8,128)(2,1)} %collective-permute-done.4), channel_id=1, source_target_pairs={{0,16},{16,0},{1,17},{17,1},{2,18},{18,2},{3,19},{19,3},{4,20},{20... | collective-permute-start | bytes 2359304 | tf_op jit(solution)/shard_map/ppermute | solution.py:31
  147.3 146.6 %collective-permute-start.85 = (bf16[128,2048]{1,0:T(8,128)(2,1)}, bf16[128,2048]{1,0:T(8,128)(2,1)}, u32[]{:S(2)}, u32[]{:S(2)}) collective-permute-start(bf16[128,2048]{1,0:T(8,128)(2,1)} %bitcast_convert_fusion.3), channel_id=1, source_target_pairs={{0,4},{4,0},{8,12},{12,8},{1,5},{5,1},{9,13},{13,9},{2,6},{6,2},{1... | collective-permute-start | bytes 1572872 | tf_op jit(solution)/shard_map/ppermute | solution.py:31
  148.2 27.5 %collective-permute-start.83 = (bf16[128,2048]{1,0:T(8,128)(2,1)}, bf16[128,2048]{1,0:T(8,128)(2,1)S(1)}, u32[]{:S(2)}, u32[]{:S(2)}) collective-permute-start(bf16[128,2048]{1,0:T(8,128)(2,1)} %bitcast_convert_fusion.3), channel_id=1, source_target_pairs={{0,8},{4,12},{8,0},{12,4},{1,9},{5,13},{9,1},{13,5},{2,10},{6,14},... | collective-permute-start | bytes 1572872 | tf_op jit(solution)/shard_map/ppermute | solution.py:31
  165.6 201.3 %collective-permute-start.28 = (bf16[512,1536]{1,0:T(8,128)(2,1)}, bf16[512,1536]{1,0:T(8,128)(2,1)}, u32[]{:S(2)}, u32[]{:S(2)}) collective-permute-start(bf16[512,1536]{1,0:T(8,128)(2,1)} %get-tuple-element.76), channel_id=1, source_target_pairs={{0,3},{1,0},{2,1},{3,2},{4,7},{5,4},{6,5},{7,6},{8,11},{9,8},{10,9... | collective-permute-start | bytes 4718600 | tf_op jit(solution)/shard_map/ppermute | solution.py:36
  170.6 194.2 %collective-permute-start.27 = (bf16[512,1536]{1,0:T(8,128)(2,1)}, bf16[512,1536]{1,0:T(8,128)(2,1)}, u32[]{:S(2)}, u32[]{:S(2)}) collective-permute-start(bf16[512,1536]{1,0:T(8,128)(2,1)} %get-tuple-element.77), channel_id=1, source_target_pairs={{0,2},{1,3},{2,0},{3,1},{4,6},{5,7},{6,4},{7,5},{8,10},{9,11},{10,... | collective-permute-start | bytes 4718600 | tf_op jit(solution)/shard_map/ppermute | solution.py:36
  175.7 74.6 %collective-permute-start.92 = (bf16[128,2048]{1,0:T(8,128)(2,1)}, bf16[128,2048]{1,0:T(8,128)(2,1)}, u32[]{:S(2)}, u32[]{:S(2)}) collective-permute-start(bf16[128,2048]{1,0:T(8,128)(2,1)} %collective-permute-done.29), channel_id=1, source_target_pairs={{0,8},{4,12},{8,0},{12,4},{1,9},{5,13},{9,1},{13,5},{2,10},{6,14},... | collective-permute-start | bytes 1572872 | tf_op jit(solution)/shard_map/ppermute | solution.py:31
  191.3 56.4 %collective-permute-start.30 = (bf16[128,2048]{1,0:T(8,128)(2,1)}, bf16[128,2048]{1,0:T(8,128)(2,1)}, u32[]{:S(2)}, u32[]{:S(2)}) collective-permute-start(bf16[128,2048]{1,0:T(8,128)(2,1)} %collective-permute-done.29), channel_id=1, source_target_pairs={{0,1},{1,2},{2,3},{3,0},{4,5},{5,6},{6,7},{7,4},{8,9},{9,10},{10,1... | collective-permute-start | bytes 1572872 | tf_op jit(solution)/shard_map/ppermute | solution.py:36
  250.3 43.5 %collective-permute-start.84 = (bf16[128,2048]{1,0:T(8,128)(2,1)S(1)}, bf16[128,2048]{1,0:T(8,128)(2,1)S(1)}, u32[]{:S(2)}, u32[]{:S(2)}) collective-permute-start(bf16[128,2048]{1,0:T(8,128)(2,1)S(1)} %copy-done.80), channel_id=1, source_target_pairs={{0,16},{16,0},{1,17},{17,1},{2,18},{18,2},{3,19},{19,3},{4,20},{20... | collective-permute-start | bytes 1572872 | tf_op jit(solution)/shard_map/ppermute | solution.py:31
  262.8 101.7 %collective-permute-start.26 = (bf16[512,1536]{1,0:T(8,128)(2,1)S(1)}, bf16[512,1536]{1,0:T(8,128)(2,1)S(1)}, u32[]{:S(2)}, u32[]{:S(2)}) collective-permute-start(bf16[512,1536]{1,0:T(8,128)(2,1)S(1)} %copy-done.67), channel_id=1, source_target_pairs={{0,1},{1,2},{2,3},{3,0},{4,5},{5,6},{6,7},{7,4},{8,9},{9,10},{10,1... | collective-permute-start | bytes 4718600 | tf_op jit(solution)/shard_map/ppermute | solution.py:36
  295.8 41.3 %collective-permute-start.31 = (bf16[128,2048]{1,0:T(8,128)(2,1)}, bf16[128,2048]{1,0:T(8,128)(2,1)S(1)}, u32[]{:S(2)}, u32[]{:S(2)}) collective-permute-start(bf16[128,2048]{1,0:T(8,128)(2,1)} %collective-permute-done.30), channel_id=1, source_target_pairs={{0,1},{1,2},{2,3},{3,0},{4,5},{5,6},{6,7},{7,4},{8,9},{9,10},{10,1... | collective-permute-start | bytes 1572872 | tf_op jit(solution)/shard_map/ppermute | solution.py:36
  306.4 32.3 %collective-permute-start.103 = (bf16[128,2048]{1,0:T(8,128)(2,1)}, bf16[128,2048]{1,0:T(8,128)(2,1)S(1)}, u32[]{:S(2)}, u32[]{:S(2)}) collective-permute-start(bf16[128,2048]{1,0:T(8,128)(2,1)} %collective-permute-done.30), channel_id=1, source_target_pairs={{0,16},{16,0},{1,17},{17,1},{2,18},{18,2},{3,19},{19,3},{4,20},{20... | collective-permute-start | bytes 1572872 | tf_op jit(solution)/shard_map/ppermute | solution.py:31
  364.8 39.2 %collective-permute-start.108 = (bf16[128,2048]{1,0:T(8,128)(2,1)S(1)}, bf16[128,2048]{1,0:T(8,128)(2,1)S(1)}, u32[]{:S(2)}, u32[]{:S(2)}) collective-permute-start(bf16[128,2048]{1,0:T(8,128)(2,1)S(1)} %collective-permute-done.104), channel_id=1, source_target_pairs={{0,4},{4,0},{8,12},{12,8},{1,5},{5,1},{9,13},{13,9},{2,6},{6,2},{1... | collective-permute-start | bytes 1572872 | tf_op jit(solution)/shard_map/ppermute | solution.py:31
  388.4 39.4 %collective-permute-start.35 = (bf16[128,2048]{1,0:T(8,128)(2,1)S(1)}, bf16[128,2048]{1,0:T(8,128)(2,1)}, u32[]{:S(2)}, u32[]{:S(2)}) collective-permute-start(bf16[128,2048]{1,0:T(8,128)(2,1)S(1)} %collective-permute-done.31), channel_id=1, source_target_pairs={{0,4},{4,0},{8,12},{12,8},{1,5},{5,1},{9,13},{13,9},{2,6},{6,2},{1... | collective-permute-start | bytes 1572872 | tf_op jit(solution)/shard_map/ppermute | solution.py:31
  393.6 41.0 %collective-permute-start.109 = (bf16[128,2048]{1,0:T(8,128)(2,1)}, bf16[128,2048]{1,0:T(8,128)(2,1)}, u32[]{:S(2)}, u32[]{:S(2)}) collective-permute-start(bf16[128,2048]{1,0:T(8,128)(2,1)} %collective-permute-done.105), channel_id=1, source_target_pairs={{0,4},{4,0},{8,12},{12,8},{1,5},{5,1},{9,13},{13,9},{2,6},{6,2},{1... | collective-permute-start | bytes 1572872 | tf_op jit(solution)/shard_map/ppermute | solution.py:31
  404.0 28.2 %collective-permute-start.37 = (bf16[128,2048]{1,0:T(8,128)(2,1)}, bf16[128,2048]{1,0:T(8,128)(2,1)}, u32[]{:S(2)}, u32[]{:S(2)}) collective-permute-start(bf16[128,2048]{1,0:T(8,128)(2,1)} %collective-permute-done.33), channel_id=1, source_target_pairs={{0,4},{4,0},{8,12},{12,8},{1,5},{5,1},{9,13},{13,9},{2,6},{6,2},{1... | collective-permute-start | bytes 1572872 | tf_op jit(solution)/shard_map/ppermute | solution.py:31
  427.8 51.9 %collective-permute-start.22 = (bf16[128,2048]{1,0:T(8,128)(2,1)S(1)}, bf16[128,2048]{1,0:T(8,128)(2,1)S(1)}, u32[]{:S(2)}, u32[]{:S(2)}) collective-permute-start(bf16[128,2048]{1,0:T(8,128)(2,1)S(1)} %get-tuple-element.66), channel_id=1, source_target_pairs={{0,4},{4,0},{8,12},{12,8},{1,5},{5,1},{9,13},{13,9},{2,6},{6,2},{1... | collective-permute-start | bytes 1572872 | tf_op jit(solution)/shard_map/ppermute | solution.py:31
  441.3 82.5 %collective-permute-start.59 = (bf16[128,2048]{1,0:T(8,128)(2,1)}, bf16[128,2048]{1,0:T(8,128)(2,1)}, u32[]{:S(2)}, u32[]{:S(2)}) collective-permute-start(bf16[128,2048]{1,0:T(8,128)(2,1)} %collective-permute-done.39), channel_id=1, source_target_pairs={{0,4},{4,0},{8,12},{12,8},{1,5},{5,1},{9,13},{13,9},{2,6},{6,2},{1... | collective-permute-start | bytes 1572872 | tf_op jit(solution)/shard_map/ppermute | solution.py:31
  479.6 55.2 %collective-permute-start.61 = (bf16[128,2048]{1,0:T(8,128)(2,1)}, bf16[128,2048]{1,0:T(8,128)(2,1)}, u32[]{:S(2)}, u32[]{:S(2)}) collective-permute-start(bf16[128,2048]{1,0:T(8,128)(2,1)} %collective-permute-done.57), channel_id=1, source_target_pairs={{0,4},{4,0},{8,12},{12,8},{1,5},{5,1},{9,13},{13,9},{2,6},{6,2},{1... | collective-permute-start | bytes 1572872 | tf_op jit(solution)/shard_map/ppermute | solution.py:31
  496.7 29.6 %collective-permute-start.60 = (bf16[128,2048]{1,0:T(8,128)(2,1)}, bf16[128,2048]{1,0:T(8,128)(2,1)}, u32[]{:S(2)}, u32[]{:S(2)}) collective-permute-start(bf16[128,2048]{1,0:T(8,128)(2,1)} %collective-permute-done.56), channel_id=1, source_target_pairs={{0,4},{4,0},{8,12},{12,8},{1,5},{5,1},{9,13},{13,9},{2,6},{6,2},{1... | collective-permute-start | bytes 1572872 | tf_op jit(solution)/shard_map/ppermute | solution.py:31
  505.6 53.8 %collective-permute-start.70 = (bf16[128,2048]{1,0:T(8,128)(2,1)}, bf16[128,2048]{1,0:T(8,128)(2,1)}, u32[]{:S(2)}, u32[]{:S(2)}) collective-permute-start(bf16[128,2048]{1,0:T(8,128)(2,1)} %collective-permute-done.40), channel_id=1, source_target_pairs={{0,4},{4,0},{8,12},{12,8},{1,5},{5,1},{9,13},{13,9},{2,6},{6,2},{1... | collective-permute-start | bytes 1572872 | tf_op jit(solution)/shard_map/ppermute | solution.py:31
  523.0 221.0 %collective-permute-start.89 = (bf16[4,128,2048]{2,1,0:T(8,128)(2,1)}, bf16[4,128,2048]{2,1,0:T(8,128)(2,1)}, u32[]{:S(2)}, u32[]{:S(2)}) collective-permute-start(bf16[4,128,2048]{2,1,0:T(8,128)(2,1)} %slice.444), channel_id=1, source_target_pairs={{0,4},{4,0},{8,12},{12,8},{1,5},{5,1},{9,13},{13,9},{2,6},{6,2},{1... | collective-permute-start | bytes 6291464 | tf_op jit(solution)/shard_map/ppermute | solution.py:31
  534.7 40.6 %collective-permute-start.72 = (bf16[128,2048]{1,0:T(8,128)(2,1)S(1)}, bf16[128,2048]{1,0:T(8,128)(2,1)}, u32[]{:S(2)}, u32[]{:S(2)}) collective-permute-start(bf16[128,2048]{1,0:T(8,128)(2,1)S(1)} %copy-done.82), channel_id=1, source_target_pairs={{0,4},{4,0},{8,12},{12,8},{1,5},{5,1},{9,13},{13,9},{2,6},{6,2},{1... | collective-permute-start | bytes 1572872 | tf_op jit(solution)/shard_map/ppermute | solution.py:31
  553.3 50.5 %collective-permute-start.45 = (bf16[128,2048]{1,0:T(8,128)(2,1)S(1)}, bf16[128,2048]{1,0:T(8,128)(2,1)}, u32[]{:S(2)}, u32[]{:S(2)}) collective-permute-start(bf16[128,2048]{1,0:T(8,128)(2,1)S(1)} %collective-permute-done.41), channel_id=1, source_target_pairs={{0,4},{4,0},{8,12},{12,8},{1,5},{5,1},{9,13},{13,9},{2,6},{6,2},{1... | collective-permute-start | bytes 1572872 | tf_op jit(solution)/shard_map/ppermute | solution.py:31
  567.7 136.4 %collective-permute-start.99 = (bf16[4,128,2048]{2,1,0:T(8,128)(2,1)}, bf16[4,128,2048]{2,1,0:T(8,128)(2,1)}, u32[]{:S(2)}, u32[]{:S(2)}) collective-permute-start(bf16[4,128,2048]{2,1,0:T(8,128)(2,1)} %slice.450), channel_id=1, source_target_pairs={{0,4},{4,0},{8,12},{12,8},{1,5},{5,1},{9,13},{13,9},{2,6},{6,2},{1... | collective-permute-start | bytes 6291464 | tf_op jit(solution)/shard_map/ppermute | solution.py:31
  575.3 34.1 %collective-permute-start.47 = (bf16[128,2048]{1,0:T(8,128)(2,1)}, bf16[128,2048]{1,0:T(8,128)(2,1)}, u32[]{:S(2)}, u32[]{:S(2)}) collective-permute-start(bf16[128,2048]{1,0:T(8,128)(2,1)} %collective-permute-done.43), channel_id=1, source_target_pairs={{0,4},{4,0},{8,12},{12,8},{1,5},{5,1},{9,13},{13,9},{2,6},{6,2},{1... | collective-permute-start | bytes 1572872 | tf_op jit(solution)/shard_map/ppermute | solution.py:31
  603.9 126.5 %collective-permute-start.110 = (bf16[4,128,2048]{2,1,0:T(8,128)(2,1)}, bf16[4,128,2048]{2,1,0:T(8,128)(2,1)}, u32[]{:S(2)}, u32[]{:S(2)}) collective-permute-start(bf16[4,128,2048]{2,1,0:T(8,128)(2,1)} %slice.456), channel_id=1, source_target_pairs={{0,4},{4,0},{8,12},{12,8},{1,5},{5,1},{9,13},{13,9},{2,6},{6,2},{1... | collective-permute-start | bytes 6291464 | tf_op jit(solution)/shard_map/ppermute | solution.py:31
  659.1 39.9 %collective-permute-start.49 = (bf16[4,128,2048]{2,1,0:T(8,128)(2,1)}, bf16[4,128,2048]{2,1,0:T(8,128)(2,1)}, u32[]{:S(2)}, u32[]{:S(2)}) collective-permute-start(bf16[4,128,2048]{2,1,0:T(8,128)(2,1)} %slice.418), channel_id=1, source_target_pairs={{0,4},{4,0},{8,12},{12,8},{1,5},{5,1},{9,13},{13,9},{2,6},{6,2},{1... | collective-permute-start | bytes 6291464 | tf_op jit(solution)/shard_map/ppermute | solution.py:31
  695.1 366.5 %collective-permute-start.129 = (bf16[512,1536]{1,0:T(8,128)(2,1)}, bf16[512,1536]{1,0:T(8,128)(2,1)S(1)}, u32[]{:S(2)}, u32[]{:S(2)}) collective-permute-start(bf16[512,1536]{1,0:T(8,128)(2,1)} %get-tuple-element.69), channel_id=1, source_target_pairs={{0,3},{1,0},{2,1},{3,2},{4,7},{5,4},{6,5},{7,6},{8,11},{9,8},{10,9... | collective-permute-start | bytes 4718600 | tf_op jit(solution)/shard_map/ppermute | solution.py:36
  706.7 48.5 %collective-permute-start.100 = (bf16[2,128,2048]{2,1,0:T(8,128)(2,1)S(1)}, bf16[2,128,2048]{2,1,0:T(8,128)(2,1)S(1)}, u32[]{:S(2)}, u32[]{:S(2)}) collective-permute-start(bf16[2,128,2048]{2,1,0:T(8,128)(2,1)S(1)} %slice.452), channel_id=1, source_target_pairs={{0,16},{16,0},{1,17},{17,1},{2,18},{18,2},{3,19},{19,3},{4,20},{20... | collective-permute-start | bytes 3145736 | tf_op jit(solution)/shard_map/ppermute | solution.py:31
  732.9 33.4 %collective-permute-start.111 = (bf16[2,128,2048]{2,1,0:T(8,128)(2,1)S(1)}, bf16[2,128,2048]{2,1,0:T(8,128)(2,1)S(1)}, u32[]{:S(2)}, u32[]{:S(2)}) collective-permute-start(bf16[2,128,2048]{2,1,0:T(8,128)(2,1)S(1)} %slice.458), channel_id=1, source_target_pairs={{0,8},{4,12},{8,0},{12,4},{1,9},{5,13},{9,1},{13,5},{2,10},{6,14},... | collective-permute-start | bytes 3145736 | tf_op jit(solution)/shard_map/ppermute | solution.py:31
  746.6 42.1 %collective-permute-start.90 = (bf16[2,128,2048]{2,1,0:T(8,128)(2,1)S(1)}, bf16[2,128,2048]{2,1,0:T(8,128)(2,1)S(1)}, u32[]{:S(2)}, u32[]{:S(2)}) collective-permute-start(bf16[2,128,2048]{2,1,0:T(8,128)(2,1)S(1)} %slice.446), channel_id=1, source_target_pairs={{0,8},{4,12},{8,0},{12,4},{1,9},{5,13},{9,1},{13,5},{2,10},{6,14},... | collective-permute-start | bytes 3145736 | tf_op jit(solution)/shard_map/ppermute | solution.py:31
  755.1 45.4 %collective-permute-start.78 = (bf16[4,128,2048]{2,1,0:T(8,128)(2,1)S(1)}, bf16[4,128,2048]{2,1,0:T(8,128)(2,1)S(1)}, u32[]{:S(2)}, u32[]{:S(2)}) collective-permute-start(bf16[4,128,2048]{2,1,0:T(8,128)(2,1)S(1)} %slice.347), channel_id=1, source_target_pairs={{0,4},{4,0},{8,12},{12,8},{1,5},{5,1},{9,13},{13,9},{2,6},{6,2},{1... | collective-permute-start | bytes 6291464 | tf_op jit(solution)/shard_map/ppermute | solution.py:31
  755.6 41.2 %collective-permute-start.101 = (bf16[1,128,2048]{2,1,0:T(8,128)(2,1)S(1)}, bf16[1,128,2048]{2,1,0:T(8,128)(2,1)S(1)}, u32[]{:S(2)}, u32[]{:S(2)}) collective-permute-start(bf16[1,128,2048]{2,1,0:T(8,128)(2,1)S(1)} %slice.454), channel_id=1, source_target_pairs={{0,8},{4,12},{8,0},{12,4},{1,9},{5,13},{9,1},{13,5},{2,10},{6,14},... | collective-permute-start | bytes 1572872 | tf_op jit(solution)/shard_map/ppermute | solution.py:31
  766.7 31.3 %collective-permute-start.112 = (bf16[1,128,2048]{2,1,0:T(8,128)(2,1)S(1)}, bf16[1,128,2048]{2,1,0:T(8,128)(2,1)}, u32[]{:S(2)}, u32[]{:S(2)}) collective-permute-start(bf16[1,128,2048]{2,1,0:T(8,128)(2,1)S(1)} %slice.460), channel_id=1, source_target_pairs={{0,16},{16,0},{1,17},{17,1},{2,18},{18,2},{3,19},{19,3},{4,20},{20... | collective-permute-start | bytes 1572872 | tf_op jit(solution)/shard_map/ppermute | solution.py:31
  800.5 108.2 %collective-permute-start.91 = (bf16[1,128,2048]{2,1,0:T(8,128)(2,1)}, bf16[1,128,2048]{2,1,0:T(8,128)(2,1)}, u32[]{:S(2)}, u32[]{:S(2)}) collective-permute-start(bf16[1,128,2048]{2,1,0:T(8,128)(2,1)} %slice.448), channel_id=1, source_target_pairs={{0,16},{16,0},{1,17},{17,1},{2,18},{18,2},{3,19},{19,3},{4,20},{20... | collective-permute-start | bytes 1572872 | tf_op jit(solution)/shard_map/ppermute | solution.py:31
  803.0 106.1 %collective-permute-start.102 = (bf16[128,2048]{1,0:T(8,128)(2,1)}, bf16[128,2048]{1,0:T(8,128)(2,1)S(1)}, u32[]{:S(2)}, u32[]{:S(2)}) collective-permute-start(bf16[128,2048]{1,0:T(8,128)(2,1)} %fusion.144), channel_id=1, source_target_pairs={{0,3},{1,0},{2,1},{3,2},{4,7},{5,4},{6,5},{7,6},{8,11},{9,8},{10,9... | collective-permute-start | bytes 1572872 | tf_op jit(solution)/shard_map/ppermute | solution.py:36
  804.6 33.4 %collective-permute-start.79 = (bf16[2,128,2048]{2,1,0:T(8,128)(2,1)S(1)}, bf16[2,128,2048]{2,1,0:T(8,128)(2,1)S(1)}, u32[]{:S(2)}, u32[]{:S(2)}) collective-permute-start(bf16[2,128,2048]{2,1,0:T(8,128)(2,1)S(1)} %slice.440), channel_id=1, source_target_pairs={{0,16},{16,0},{1,17},{17,1},{2,18},{18,2},{3,19},{19,3},{4,20},{20... | collective-permute-start | bytes 3145736 | tf_op jit(solution)/shard_map/ppermute | solution.py:31
  806.2 53.3 %collective-permute-start.64 = (bf16[2,128,2048]{2,1,0:T(8,128)(2,1)S(1)}, bf16[2,128,2048]{2,1,0:T(8,128)(2,1)S(1)}, u32[]{:S(2)}, u32[]{:S(2)}) collective-permute-start(bf16[2,128,2048]{2,1,0:T(8,128)(2,1)S(1)} %slice.430), channel_id=1, source_target_pairs={{0,16},{16,0},{1,17},{17,1},{2,18},{18,2},{3,19},{19,3},{4,20},{20... | collective-permute-start | bytes 3145736 | tf_op jit(solution)/shard_map/ppermute | solution.py:31
  861.4 35.4 %collective-permute-start.80 = (bf16[1,128,2048]{2,1,0:T(8,128)(2,1)S(1)}, bf16[1,128,2048]{2,1,0:T(8,128)(2,1)S(1)}, u32[]{:S(2)}, u32[]{:S(2)}) collective-permute-start(bf16[1,128,2048]{2,1,0:T(8,128)(2,1)S(1)} %slice.442), channel_id=1, source_target_pairs={{0,8},{4,12},{8,0},{12,4},{1,9},{5,13},{9,1},{13,5},{2,10},{6,14},... | collective-permute-start | bytes 1572872 | tf_op jit(solution)/shard_map/ppermute | solution.py:31
  906.2 36.2 %collective-permute-start.113 = (bf16[128,2048]{1,0:T(8,128)(2,1)S(1)}, bf16[128,2048]{1,0:T(8,128)(2,1)S(1)}, u32[]{:S(2)}, u32[]{:S(2)}) collective-permute-start(bf16[128,2048]{1,0:T(8,128)(2,1)S(1)} %copy-done.74), channel_id=1, source_target_pairs={{0,2},{1,3},{2,0},{3,1},{4,6},{5,7},{6,4},{7,5},{8,10},{9,11},{10,... | collective-permute-start | bytes 1572872 | tf_op jit(solution)/shard_map/ppermute | solution.py:36
  907.0 37.1 %collective-permute-start.55 = (bf16[1,128,2048]{2,1,0:T(8,128)(2,1)S(1)}, bf16[1,128,2048]{2,1,0:T(8,128)(2,1)S(1)}, u32[]{:S(2)}, u32[]{:S(2)}) collective-permute-start(bf16[1,128,2048]{2,1,0:T(8,128)(2,1)S(1)} %slice.426), channel_id=1, source_target_pairs={{0,16},{16,0},{1,17},{17,1},{2,18},{18,2},{3,19},{19,3},{4,20},{20... | collective-permute-start | bytes 1572872 | tf_op jit(solution)/shard_map/ppermute | solution.py:31
  908.7 38.4 %collective-permute-start.81 = (bf16[128,2048]{1,0:T(8,128)(2,1)S(1)}, bf16[128,2048]{1,0:T(8,128)(2,1)S(1)}, u32[]{:S(2)}, u32[]{:S(2)}) collective-permute-start(bf16[128,2048]{1,0:T(8,128)(2,1)S(1)} %fusion.142), channel_id=1, source_target_pairs={{0,1},{1,2},{2,3},{3,0},{4,5},{5,6},{6,7},{7,4},{8,9},{9,10},{10,1... | collective-permute-start | bytes 1572872 | tf_op jit(solution)/shard_map/ppermute | solution.py:36
  909.2 87.6 %collective-permute-start.66 = (bf16[128,2048]{1,0:T(8,128)(2,1)S(1)}, bf16[128,2048]{1,0:T(8,128)(2,1)S(1)}, u32[]{:S(2)}, u32[]{:S(2)}) collective-permute-start(bf16[128,2048]{1,0:T(8,128)(2,1)S(1)} %fusion.140), channel_id=1, source_target_pairs={{0,3},{1,0},{2,1},{3,2},{4,7},{5,4},{6,5},{7,6},{8,11},{9,8},{10,9... | collective-permute-start | bytes 1572872 | tf_op jit(solution)/shard_map/ppermute | solution.py:36
  942.4 98.4 %collective-permute-start.77 = (bf16[128,2048]{1,0:T(8,128)(2,1)S(1)}, bf16[128,2048]{1,0:T(8,128)(2,1)S(1)}, u32[]{:S(2)}, u32[]{:S(2)}) collective-permute-start(bf16[128,2048]{1,0:T(8,128)(2,1)S(1)} %fusion.141), channel_id=1, source_target_pairs={{0,2},{1,3},{2,0},{3,1},{4,6},{5,7},{6,4},{7,5},{8,10},{9,11},{10,... | collective-permute-start | bytes 1572872 | tf_op jit(solution)/shard_map/ppermute | solution.py:36
  944.1 130.4 %collective-permute-start.128 = (bf16[512,1536]{1,0:T(8,128)(2,1)}, bf16[512,1536]{1,0:T(8,128)(2,1)}, u32[]{:S(2)}, u32[]{:S(2)}) collective-permute-start(bf16[512,1536]{1,0:T(8,128)(2,1)} %get-tuple-element.70), channel_id=1, source_target_pairs={{0,2},{1,3},{2,0},{3,1},{4,6},{5,7},{6,4},{7,5},{8,10},{9,11},{10,... | collective-permute-start | bytes 4718600 | tf_op jit(solution)/shard_map/ppermute | solution.py:36
  947.1 127.4 %collective-permute-start.127 = (bf16[512,1536]{1,0:T(8,128)(2,1)}, bf16[512,1536]{1,0:T(8,128)(2,1)}, u32[]{:S(2)}, u32[]{:S(2)}) collective-permute-start(bf16[512,1536]{1,0:T(8,128)(2,1)} %get-tuple-element.71), channel_id=1, source_target_pairs={{0,1},{1,2},{2,3},{3,0},{4,5},{5,6},{6,7},{7,4},{8,9},{9,10},{10,1... | collective-permute-start | bytes 4718600 | tf_op jit(solution)/shard_map/ppermute | solution.py:36
  1044.2 41.0 %collective-permute-start.114 = (bf16[128,2048]{1,0:T(8,128)(2,1)}, bf16[128,2048]{1,0:T(8,128)(2,1)}, u32[]{:S(2)}, u32[]{:S(2)}) collective-permute-start(bf16[128,2048]{1,0:T(8,128)(2,1)} %get-tuple-element.62), channel_id=1, source_target_pairs={{0,4},{4,0},{8,12},{12,8},{1,5},{5,1},{9,13},{13,9},{2,6},{6,2},{1... | collective-permute-start | bytes 1572872 | tf_op jit(solution)/shard_map/ppermute | solution.py:31
  1056.7 28.6 %collective-permute-start.116 = (bf16[128,2048]{1,0:T(8,128)(2,1)}, bf16[128,2048]{1,0:T(8,128)(2,1)}, u32[]{:S(2)}, u32[]{:S(2)}) collective-permute-start(bf16[128,2048]{1,0:T(8,128)(2,1)} %collective-permute-done.115), channel_id=1, source_target_pairs={{0,4},{4,0},{8,12},{12,8},{1,5},{5,1},{9,13},{13,9},{2,6},{6,2},{1... | collective-permute-start | bytes 1572872 | tf_op jit(solution)/shard_map/ppermute | solution.py:31
  1137.9 99.5 %collective-permute-start.119 = (bf16[1,4,4,64,1536]{4,3,1,2,0:T(8,128)(2,1)}, bf16[1,4,4,64,1536]{4,3,1,2,0:T(8,128)(2,1)}, u32[]{:S(2)}, u32[]{:S(2)}) collective-permute-start(bf16[1,4,4,64,1536]{4,3,1,2,0:T(8,128)(2,1)} %fusion.41), channel_id=1, source_target_pairs={{0,16},{16,0},{1,17},{17,1},{2,18},{18,2},{3,19},{19,3},{4,20},{20... | collective-permute-start | bytes 9437192 | tf_op jit(solution)/shard_map/ppermute | solution.py:31
  1141.2 88.1 %collective-permute-start.123 = (bf16[1,4,64,2048]{3,2,1,0:T(8,128)(2,1)S(1)}, bf16[1,4,64,2048]{3,2,1,0:T(8,128)(2,1)}, u32[]{:S(2)}, u32[]{:S(2)}) collective-permute-start(bf16[1,4,64,2048]{3,2,1,0:T(8,128)(2,1)S(1)} %dynamic-slice_convert_fusion.1), channel_id=1, source_target_pairs={{0,16},{16,0},{1,17},{17,1},{2,18},{18,2},{3,19},{19,3},{4,20},{20... | collective-permute-start | bytes 3145736 | tf_op jit(solution)/shard_map/ppermute | solution.py:31
  1149.5 86.0 %collective-permute-start.117 = (bf16[2,128,2048]{2,1,0:T(8,128)(2,1)S(1)}, bf16[2,128,2048]{2,1,0:T(8,128)(2,1)S(1)}, u32[]{:S(2)}, u32[]{:S(2)}) collective-permute-start(bf16[2,128,2048]{2,1,0:T(8,128)(2,1)S(1)} %fusion.105), channel_id=1, source_target_pairs={{0,4},{4,0},{8,12},{12,8},{1,5},{5,1},{9,13},{13,9},{2,6},{6,2},{1... | collective-permute-start | bytes 3145736 | tf_op jit(solution)/shard_map/ppermute | solution.py:31
  1234.3 32.0 %collective-permute-start.125 = (bf16[64,2048]{1,0:T(8,128)(2,1)S(1)}, bf16[64,2048]{1,0:T(8,128)(2,1)S(1)}, u32[]{:S(2)}, u32[]{:S(2)}) collective-permute-start(bf16[64,2048]{1,0:T(8,128)(2,1)S(1)} %get-tuple-element.102), channel_id=1, source_target_pairs={{0,2},{1,3},{2,0},{3,1},{4,6},{5,7},{6,4},{7,5},{8,10},{9,11},{10,... | collective-permute-start | bytes 786440 | tf_op jit(solution)/shard_map/ppermute | solution.py:36
  1235.9 31.4 %collective-permute-start.118 = (bf16[128,2048]{1,0:T(8,128)(2,1)S(1)}, bf16[128,2048]{1,0:T(8,128)(2,1)S(1)}, u32[]{:S(2)}, u32[]{:S(2)}) collective-permute-start(bf16[128,2048]{1,0:T(8,128)(2,1)S(1)} %fusion.146), channel_id=1, source_target_pairs={{0,8},{4,12},{8,0},{12,4},{1,9},{5,13},{9,1},{13,5},{2,10},{6,14},... | collective-permute-start | bytes 1572872 | tf_op jit(solution)/shard_map/ppermute | solution.py:31
  1244.0 43.2 %collective-permute-start.120 = (bf16[4,64,1536]{2,1,0:T(8,128)(2,1)}, bf16[4,64,1536]{2,1,0:T(8,128)(2,1)S(1)}, u32[]{:S(2)}, u32[]{:S(2)}) collective-permute-start(bf16[4,64,1536]{2,1,0:T(8,128)(2,1)} %get-tuple-element.73), channel_id=1, source_target_pairs={{0,3},{1,0},{2,1},{3,2},{4,7},{5,4},{6,5},{7,6},{8,11},{9,8},{10,9... | collective-permute-start | bytes 2359304 | tf_op jit(solution)/shard_map/ppermute | solution.py:36
  1246.7 40.6 %collective-permute-start.122 = (bf16[4,64,1536]{2,1,0:T(8,128)(2,1)}, bf16[4,64,1536]{2,1,0:T(8,128)(2,1)}, u32[]{:S(2)}, u32[]{:S(2)}) collective-permute-start(bf16[4,64,1536]{2,1,0:T(8,128)(2,1)} %get-tuple-element.74), channel_id=1, source_target_pairs={{0,1},{1,2},{2,3},{3,0},{4,5},{5,6},{6,7},{7,4},{8,9},{9,10},{10,1... | collective-permute-start | bytes 2359304 | tf_op jit(solution)/shard_map/ppermute | solution.py:36
  1250.9 74.6 %collective-permute-start.121 = (bf16[4,64,1536]{2,1,0:T(8,128)(2,1)}, bf16[4,64,1536]{2,1,0:T(8,128)(2,1)}, u32[]{:S(2)}, u32[]{:S(2)}) collective-permute-start(bf16[4,64,1536]{2,1,0:T(8,128)(2,1)} %get-tuple-element.75), channel_id=1, source_target_pairs={{0,2},{1,3},{2,0},{3,1},{4,6},{5,7},{6,4},{7,5},{8,10},{9,11},{10,... | collective-permute-start | bytes 2359304 | tf_op jit(solution)/shard_map/ppermute | solution.py:36
  1274.2 54.4 %all-to-all-start.5 = ((f32[32,1,1280]{2,1,0:T(1,128)}), f32[32,1,1280]{2,1,0:T(1,128)}, u32[]{:S(2)}, u32[]{:S(2)}) async-start(f32[32,1,1280]{2,1,0:T(1,128)} %copy.240), calls=%async_computation.5 | async-start | bytes 327680 | tf_op jit(solution)/shard_map/all_to_all | solution.py:544
  (227 other events, 4316.3 us)

commit v3 on v1

--- a/solution.py
+++ b/solution.py
@@ -1,6 +1,8 @@
 import jax
 import jax.numpy as jnp
 from jax import lax
+from jax.experimental import pallas as pl
+from jax.experimental.pallas import tpu as pltpu
 from jax.sharding import PartitionSpec as P
 
 HEADS = 16
@@ -37,11 +39,6 @@
 def bits_of(axis):
     count = lax.axis_size(axis)
     return [1 << i for i in range(count.bit_length() - 1)]
-
-
-def spread(value):
-    total = lax.axis_size(EVERY)
-    return lax.all_to_all(value, EVERY, 0, 0, tiled=True) if value.shape[0] == total else None
 
 
 def locate(stored_rows, doc_lens, blk_order, blk_rows):
@@ -106,49 +103,239 @@
     return value
 
 
-def token_scatter(value):
-    steps_e = [("expert", b) for b in bits_of("expert")]
-    steps_c = [("context", b) for b in bits_of("context")]
-    z_count = lax.axis_size("dp")
-    rows, width = value.shape[1:]
-    dims = list(reversed(steps_e)) + list(reversed(steps_c))
-    value = value.reshape((2,) * len(dims) + (z_count, rows, width))
-    first, rest = steps_c[0], steps_c[1:] + steps_e
-    dim = dims.index(first)
-    value = half_step(value, first[0], first[1], dim).astype(bf16)
-    dims = dims[:dim] + dims[dim + 1 :]
-    half = width // 2
-    outs = []
-    for part, order in ((value[..., :half], rest), (value[..., half:], rest[::-1])):
-        left = list(dims)
-        for step in order:
+def after(value, *done):
+    return lax.optimization_barrier((value,) + done)[0] if done else value
+
+
+def tie(*values):
+    return lax.optimization_barrier(values)
+
+
+def near_step():
+    return ("context", bits_of("context")[0])
+
+
+def far_steps():
+    steps = [("context", b) for b in bits_of("context")[1:]]
+    return steps + [("expert", b) for b in bits_of("expert")]
+
+
+def source_order():
+    steps = [near_step()] + far_steps()
+    me = {axis: lax.axis_index(axis) for axis in EVERY}
+    c_count, z_count = lax.axis_size("context"), lax.axis_size("dp")
+    order = []
+    for i in range(1 << len(steps)):
+        masks = {"expert": 0, "context": 0}
+        for j, (axis, bit) in enumerate(steps):
+            if i >> (len(steps) - 1 - j) & 1:
+                masks[axis] |= bit
+        column = (me["expert"] ^ masks["expert"]) * c_count + (me["context"] ^ masks["context"])
+        order += [column * z_count + z for z in range(z_count)]
+    return jnp.stack(order).astype(jnp.int32)
+
+
+class Gather:
+    def __init__(self, value):
+        around = [value]
+        for _ in range(lax.axis_size("dp") - 1):
+            around.append(shift(around[-1], "dp", 1))
+        far = far_steps()
+        half = value.shape[1] // 2
+        shape = (-1, value.shape[0], half)
+        self.near, self.other, self.first = [], [], []
+        for i in range(2):
+            held = jnp.stack([part[:, i * half : (i + 1) * half] for part in around])
+            held = held.reshape((1,) * len(far) + held.shape)
+            for level, step in enumerate(far[::-1] if i else far):
+                got = swap(held, *step)
+                self.first += [got] if level == 0 else []
+                held = jnp.concatenate([held, got], axis=far.index(step))
+            self.near.append(held.reshape(shape))
+            self.other.append(swap(held, *near_step()).reshape(shape))
+
+    def order(self):
+        z_count = lax.axis_size("dp")
+        spots = jnp.arange(self.near[0].shape[0], dtype=jnp.int32)
+        return spots // z_count * z_count + (lax.axis_index("dp") - spots) % z_count
+
+
+class Scatter:
+    def __init__(self, send, rows):
+        self.far = far_steps()
+        self.shape = (2,) * len(self.far) + (lax.axis_size("dp"), rows)
+        self.got = swap(send, *near_step())
+
+    def begin(self, keep, *done):
+        far, width = self.far, keep.shape[-1]
+        half = width // 2
+        keep = keep.reshape(self.shape + (width,))
+        got = after(self.got, *done).reshape(self.shape + (width,))
+        self.states = []
+        for i in range(2):
+            cut = slice(i * half, (i + 1) * half)
+            self.states.append((keep[..., cut], got[..., cut], far[::-1] if i else far, list(far)))
+
+    def step(self, *done):
+        sums = []
+        arrived = [state[1] for state in self.states]
+        arrived = after(arrived, *done) if done else arrived
+        for (own, _, order, left), other in zip(self.states, arrived):
+            step = order[len(order) - len(left)]
             dim = left.index(step)
-            part = half_step(part, step[0], step[1], dim).astype(bf16)
-            left.remove(step)
-        got = lax.all_to_all(part, "dp", 0, 0, tiled=True)
-        outs.append(jnp.sum(got.astype(f32), axis=0))
-    return jnp.concatenate(outs, axis=1)
-
-
-def relative_gather(piece):
-    around = [piece]
-    for _ in range(lax.axis_size("dp") - 1):
-        around.append(shift(around[-1], "dp", 1))
-    held = [around]
-    for bit in bits_of("expert"):
-        held = held + [[swap(part, "expert", bit) for part in row] for row in held]
-    return held
-
-
-def relative_scatter(value):
+            first = [slice(None)] * dim + [0]
+            second = [slice(None)] * dim + [1]
+            sent = own[tuple(second)].astype(f32) + other[tuple(second)].astype(f32)
+            kept = own[tuple(first)].astype(f32) + other[tuple(first)].astype(f32)
+            got = swap(sent.astype(bf16), *step)
+            sums.append((kept.astype(bf16), got, order, left[:dim] + left[dim + 1 :]))
+        self.states = sums
+        return [state[1] for state in sums]
+
+    def steps_left(self):
+        return len(self.states[0][3])
+
+    def cross(self, *done):
+        blocks = jnp.concatenate(
+            [
+                (own.astype(f32) + got.astype(f32)).astype(bf16)
+                for own, got, _, _ in self.states
+            ],
+            axis=-1,
+        )
+        return exchange(blocks, *done)
+
+
+def sources_per_block(slot_cap):
+    count = 1
+    while count * slot_cap % 16:
+        count *= 2
+    return count
+
+
+def take_kernel(per, slot_cap, order_ref, slot_ref, *refs):
+    *rows, out_ref = refs
+    places = lax.broadcasted_iota(jnp.int32, (slot_cap, slot_ref.shape[2]), 0)
+    picks = [(slot_ref[j] == places).astype(f32).astype(bf16) for j in range(per)]
+    at = 0
+    for p in range(0, len(rows), per):
+        part = [jnp.dot(picks[j], rows[p + j][0], preferred_element_type=f32) for j in range(per)]
+        width = part[0].shape[1]
+        out_ref[:, at : at + width] = jnp.concatenate(part).astype(bf16)
+        at += width
+
+
+def take_rows(parts, order, slots, slot_cap):
+    count = order.shape[0]
+    tokens = slots.shape[1]
+    per = sources_per_block(slot_cap)
+    width = sum(part.shape[2] for part in parts)
+
+    def block_of(part, j):
+        return pl.BlockSpec(
+            (1, tokens, part.shape[2]), lambda i, order_ref: (order_ref[i * per + j], 0, 0)
+        )
+
+    return pl.pallas_call(
+        lambda *refs: take_kernel(per, slot_cap, *refs),
+        grid_spec=pltpu.PrefetchScalarGridSpec(
+            num_scalar_prefetch=1,
+            grid=(count // per,),
+            in_specs=[pl.BlockSpec((per, 1, tokens), lambda i, order_ref: (i, 0, 0))]
+            + [block_of(part, j) for part in parts for j in range(per)],
+            out_specs=pl.BlockSpec((per * slot_cap, width), lambda i, order_ref: (i, 0)),
+        ),
+        out_shape=jax.ShapeDtypeStruct((count * slot_cap, width), bf16),
+        compiler_params=pltpu.CompilerParams(vmem_limit_bytes=40 * 2**20),
+    )(order, slots.reshape(count, 1, tokens), *[part for part in parts for _ in range(per)])
+
+
+def put_kernel(per, slot_cap, slot_ref, rows_ref, out_ref):
+    places = lax.broadcasted_iota(jnp.int32, (slot_cap, slot_ref.shape[2]), 0)
+    rows = rows_ref[...].astype(f32)
+    for j in range(per):
+        pick = (slot_ref[j] == places).astype(f32).astype(bf16)
+        part = rows[j * slot_cap : (j + 1) * slot_cap].astype(bf16)
+        out_ref[j] = mm_tn(pick, part).astype(bf16)
+
+
+def put_rows(rows, slots, slot_cap, first, count):
+    width = rows.shape[1]
+    total, tokens = slots.shape
+    per = sources_per_block(slot_cap)
+    skip = first // per
+    return pl.pallas_call(
+        lambda *refs: put_kernel(per, slot_cap, *refs),
+        grid=(count // per,),
+        in_specs=[
+            pl.BlockSpec((per, 1, tokens), lambda i: (i + skip, 0, 0)),
+            pl.BlockSpec((per * slot_cap, width), lambda i: (i + skip, 0)),
+        ],
+        out_specs=pl.BlockSpec((per, tokens, width), lambda i: (i, 0, 0)),
+        out_shape=jax.ShapeDtypeStruct((count, tokens, width), bf16),
+        compiler_params=pltpu.CompilerParams(vmem_limit_bytes=40 * 2**20),
+    )(slots.reshape(total, 1, tokens), rows)
+
+
+def exchange(blocks, *done):
+    return lax.all_to_all(after(blocks, *done), "dp", 0, 0, tiled=True)
+
+
+def split_kernel(experts, halves, w_ref, *out_refs):
+    ffh = out_refs[0].shape[2]
+    for e in range(experts):
+        rows = w_ref[:, e, :].astype(bf16)
+        for h in range(halves):
+            for j in range(3):
+                at = (j * halves + h) * ffh
+                out_refs[j][e * halves + h] = rows[:, at : at + ffh]
+
+
+def split_experts(w, halves):
+    rows, experts, width = w.shape
+    block, shares, ffh = 64, experts * halves, width // (3 * halves)
+    return pl.pallas_call(
+        lambda *refs: split_kernel(experts, halves, *refs),
+        grid=(rows // block,),
+        in_specs=[pl.BlockSpec((block, experts, width), lambda i: (i, 0, 0))],
+        out_specs=[pl.BlockSpec((shares, block, ffh), lambda i: (0, i, 0))] * 3,
+        out_shape=[jax.ShapeDtypeStruct((shares, rows, ffh), bf16)] * 3,
+        compiler_params=pltpu.CompilerParams(vmem_limit_bytes=32 * 2**20),
+    )(w)
+
+
+def join_kernel(halves, gate_ref, up_ref, down_ref, out_ref):
+    shares, _, ffh = gate_ref.shape
+    for t in range(shares):
+        e, h = divmod(t, halves)
+        for j, ref in enumerate((gate_ref, up_ref, down_ref)):
+            at = (j * halves + h) * ffh
+            out_ref[:, e, at : at + ffh] = ref[t].astype(f32)
+
+
+def join_experts(gate, up, down, halves):
+    shares, rows, ffh = gate.shape
+    block, experts, width = 64, shares // halves, 3 * ffh * halves
+    return pl.pallas_call(
+        lambda *refs: join_kernel(halves, *refs),
+        grid=(rows // block,),
+        in_specs=[pl.BlockSpec((shares, block, ffh), lambda i: (0, i, 0))] * 3,
+        out_specs=pl.BlockSpec((block, experts, width), lambda i: (i, 0, 0)),
+        out_shape=jax.ShapeDtypeStruct((rows, experts, width), f32),
+        compiler_params=pltpu.CompilerParams(vmem_limit_bytes=32 * 2**20),
+    )(gate, up, down)
+
+
+def relative_scatter(value, *done, late=()):
     for bit in reversed(bits_of("expert")):
-        half = value.shape[0] // 2
-        value = value[:half].astype(f32) + swap(value[half:].astype(bf16), "expert", bit).astype(f32)
-    value = value[0]
-    total = value[0].astype(f32)
-    for k in range(1, lax.axis_size("dp")):
-        total = total + shift(value[k].astype(bf16), "dp", -k).astype(f32)
-    return total
+        value = value.reshape((value.shape[0] // 2, 2) + value.shape[1:]) if bit == 1 else value
+        if bit == 1:
+            value = half_step(value, "expert", 1, 1)
+        else:
+            value = value.reshape((2, value.shape[0] // 2) + value.shape[1:])
+            value = half_step(value, "expert", bit, 0)
+    arrived = exchange(value[0].astype(bf16), *done)
+    return jnp.sum(arrived.astype(f32), axis=0), arrived
 
 
 def on_device(
@@ -191,6 +378,15 @@
     small_sent = jnp.concatenate(
         [jnp.broadcast_to(own_row[None], (total, own_row.shape[0])), rank_rows.astype(bf16)], axis=1
     )
+    wqkv = (
+        w_attn[:, : 3 * width]
+        .astype(bf16)
+        .reshape(w_rows, 3, runs, c_count, run_cols)
+        .transpose(3, 0, 1, 2, 4)
+        .reshape(c_count, w_rows, 3 * cols)
+    )
+    wqkv = lax.all_to_all(wqkv, "context", 0, 0, tiled=True).reshape(c_count * w_rows, 3 * cols)
+    small_sent = after(small_sent, wqkv)
     small = lax.all_to_all(small_sent, EVERY, 0, 0, tiled=True)
     n_router = w_router.size
     router_w = small[:, :n_router].reshape(width, expert_count)
@@ -203,60 +399,33 @@
     )
     slot_of = small[:, n_router + norm_gains.size :].astype(jnp.int32)
 
-    wqkv = (
-        w_attn[:, : 3 * width]
-        .astype(bf16)
-        .reshape(w_rows, 3, runs, c_count, run_cols)
-        .transpose(3, 0, 1, 2, 4)
-        .reshape(c_count, w_rows, 3 * cols)
-    )
-    wqkv = lax.all_to_all(wqkv, "context", 0, 0, tiled=True).reshape(c_count * w_rows, 3 * cols)
-    held = relative_gather(wqkv)
-    wqkv_all = jnp.concatenate([part for row in held for part in row], axis=0)
+    grad_out = cotangent[0]
+    gate_blocks, up_blocks, down_blocks = split_experts(w_experts, halves)
+    around = ("expert", "dp")
+    wqkv_all = lax.all_gather(wqkv, around, axis=0, tiled=True)
+    g_gather = Gather(grad_out.astype(bf16))
+    wqkv_all = (
+        wqkv_all.reshape(e_count, z_count, c_count, w_rows, 3 * cols)
+        .transpose(0, 2, 1, 3, 4)
+        .reshape(width, 3 * cols)
+    )
     wo_own = w_attn[:, 3 * width :].astype(bf16)
     if aligned:
-        wo_all = jnp.concatenate([part for row in relative_gather(wo_own) for part in row], axis=0)
+        wo_all = lax.all_gather(after(wo_own, wqkv_all), around, axis=0, tiled=True)
     else:
         wo_full = lax.all_gather(wo_own, EVERY, axis=0, tiled=True)
         wo_all = lax.dynamic_slice_in_dim(wo_full, me_c * cols, cols, axis=0)
 
-    def place_of(r_e, r_z, c, row):
-        return (((me_e ^ r_e) * c_count + c) * z_count + (me_z - r_z) % z_count) * w_rows + row
-
-    spots = jnp.arange(width, dtype=jnp.int32)
-    per_e = z_count * c_count * w_rows
-    feature_of = place_of(
-        spots // per_e,
-        spots // (c_count * w_rows) % z_count,
-        spots // w_rows % c_count,
-        spots % w_rows,
-    )
-    order_n = (spots[:, None] == feature_of[None, :]).astype(bf16)
-    if aligned:
-        near = jnp.arange(cols, dtype=jnp.int32)
-        local_of = (
-            (me_e ^ (near // block_rows)) * block_rows
-            + (me_z - near // w_rows % z_count) % z_count * w_rows
-            + near % w_rows
-        )
-        order_o = (near[:, None] == local_of[None, :]).astype(bf16)
-
-    wx = (
-        w_experts.astype(bf16)
-        .reshape(w_experts.shape[0], local_experts, 3, halves, ffh)
-        .transpose(1, 3, 0, 2, 4)
-        .reshape(z_count, w_experts.shape[0], 3 * ffh)
-    )
-    wx = lax.all_to_all(wx, "dp", 0, 0, tiled=True).reshape(width, 3 * ffh)
-    w_gu, w_down = wx[:, : 2 * ffh], wx[:, 2 * ffh :]
-
-    grad_out = cotangent[0]
+    w_down = exchange(down_blocks, wqkv_all)
+    w_gate = exchange(gate_blocks, w_down)
+    w_up = exchange(up_blocks, w_gate)
+    w_gu = jnp.concatenate([w_gate.reshape(width, ffh), w_up.reshape(width, ffh)], axis=1)
+
     inputs = tokens[0].astype(f32)
     pack_x = context_gather(tokens[0]).astype(f32)
     scale_one = lax.rsqrt(jnp.mean(pack_x * pack_x, axis=-1, keepdims=True) + epsilon)
     normed_one = (pack_x * scale_one * gains[0]).astype(bf16)
-    normed_one_r = mm(normed_one, order_n).astype(bf16)
-    qkv = mm(normed_one_r, wqkv_all)
+    qkv = mm(after(normed_one, gate_blocks, *g_gather.first), wqkv_all)
     place, doc, offset = locate(
         jnp.arange(pack_rows, dtype=jnp.int32), lengths[0], block_order[0], blk_rows
     )
@@ -290,42 +459,38 @@
     top = jnp.max(scores, axis=2, keepdims=True)
     raised = jnp.exp(scores - top)
     soft = raised / jnp.sum(raised, axis=2, keepdims=True)
-    soft_b = soft.astype(bf16)
+    soft_b = after(soft.astype(bf16), w_down)
     mixed = (
         jnp.einsum("hqk,khd->qhd", soft_b, value, preferred_element_type=f32)
         .reshape(pack_rows, cols)
         .astype(bf16)
     )
-    mixed_r = mm(mixed, order_o).astype(bf16) if aligned else mixed
-    hidden = inputs + context_scatter(mm(mixed_r, wo_all))
+    hidden = after(inputs + context_scatter(mm(mixed, wo_all)), w_gate)
     scale_two = lax.rsqrt(jnp.mean(hidden * hidden, axis=-1, keepdims=True) + epsilon)
     normed_two = (hidden * scale_two * gains[1]).astype(bf16)
     logits = mm(normed_two, router_w)
     probs = jax.nn.softmax(logits, axis=-1)
 
-    all_grad = lax.all_gather(grad_out.astype(bf16), EVERY, axis=0, tiled=True)
-    all_grad = all_grad.reshape(total, tok_rows, width)
+    order = source_order()
     all_normed = lax.all_gather(normed_two, EVERY, axis=0, tiled=True)
     all_normed = all_normed.reshape(total, tok_rows, width)
     gate_rows = lax.all_to_all(jnp.repeat(probs.T, halves, axis=0), EVERY, 0, 0, tiled=True)
     slots = jnp.arange(slot_cap, dtype=jnp.int32)
-    pick = (slot_of[:, None, :] == slots[None, :, None]).astype(bf16)
-    put = (slot_of[:, :, None] == slots[None, None, :]).astype(bf16)
-
-    def take_rows(rows):
-        got = jnp.einsum("sct,std->scd", pick, rows, preferred_element_type=f32)
-        return got.astype(bf16).reshape(total * slot_cap, width)
-
-    def put_rows(rows):
-        rows = rows.astype(bf16).reshape(total, slot_cap, width)
-        return jnp.einsum("stc,scd->std", put, rows, preferred_element_type=f32).astype(bf16)
-
+    slot_of = slot_of[order]
+    gate_rows = gate_rows[order]
     gate = jnp.sum(
         jnp.where(slot_of[:, None, :] == slots[None, :, None], gate_rows[:, None, :], 0.0), axis=2
     ).reshape(total * slot_cap, 1)
-    g_rows = take_rows(all_grad)
+    side = total // 2
+    g_rows = jnp.concatenate(
+        [
+            take_rows(g_gather.near, g_gather.order(), slot_of[:side], slot_cap),
+            take_rows(g_gather.other, g_gather.order(), slot_of[side:], slot_cap),
+        ]
+    )
+    w_down = w_down.reshape(width, ffh)
     back = mm(g_rows, w_down)
-    n_rows = take_rows(all_normed)
+    n_rows = take_rows([after(all_normed, back)], order, slot_of, slot_cap)
     gate_up = mm(n_rows, w_gu)
     gate_part, up_part = gate_up[:, :ffh], gate_up[:, ffh:]
     sig = jax.nn.sigmoid(gate_part)
@@ -337,27 +502,39 @@
     grad_gu = jnp.concatenate(
         [grad_act * up_part * sig * (1.0 + gate_part * (1.0 - sig)), grad_act * silu], axis=1
     ).astype(bf16)
-    grad_rows = mm_nt(grad_gu, w_gu)
-    grad_n2 = token_scatter(put_rows(grad_rows))
+    act_scaled = (act_f * gate).astype(bf16)
+    grad_wd = mm_tn(g_rows, act_scaled).astype(bf16)
+    down_got = exchange(grad_wd.reshape(z_count, -1, ffh))
+    hits = jnp.arange(total)[:, None] == order[None, :]
     sent_gates = jnp.sum(
         jnp.where(slot_of[:, :, None] == slots[None, None, :], grad_gate_slot[:, None, :], 0.0),
         axis=2,
     )
+    sent_gates = jnp.sum(jnp.where(hits[:, :, None], sent_gates[None], 0.0), axis=1)
     got_gates = lax.all_to_all(sent_gates, EVERY, 0, 0, tiled=True)
+    grad_rows = mm_nt(after(grad_gu, grad_wd), w_gu).astype(bf16)
+    grad_rows, got_gates = tie(grad_rows, got_gates)
     grad_probs = jnp.sum(got_gates.reshape(expert_count, halves, tok_rows), axis=1).T
-
-    act_scaled = (act_f * gate).astype(bf16)
-    grad_wx = jnp.concatenate([mm_tn(n_rows, grad_gu), mm_tn(g_rows, act_scaled)], axis=1)
-    grad_wx = grad_wx.astype(bf16).reshape(z_count, width // z_count, 3 * ffh)
-    grad_wx = lax.all_to_all(grad_wx, "dp", 0, 0, tiled=True)
-    grad_experts = (
-        grad_wx.astype(f32)
-        .reshape(local_experts, halves, width // z_count, 3, ffh)
-        .transpose(2, 0, 3, 1, 4)
-        .reshape(width // z_count, local_experts, 3 * ffn)
-    )
-    mixture = token_scatter(put_rows(mm_nt(act, w_down) * gate))
-    output = hidden + mixture
+    n2_sum = Scatter(put_rows(grad_rows, slot_of, slot_cap, side, side), tok_rows)
+    n2_keep = put_rows(grad_rows, slot_of, slot_cap, 0, side)
+    n_late, gu_late, _ = tie(n_rows, grad_gu, n2_keep)
+    grad_wg = mm_tn(n_late, gu_late[:, :ffh]).astype(bf16)
+    grad_wu = mm_tn(n_late, gu_late[:, ffh:]).astype(bf16)
+    n2_sum.begin(n2_keep)
+    n2_spread = n2_sum.step()
+    gate_got = exchange(grad_wg.reshape(z_count, -1, ffh), down_got)
+    y_rows = (mm_nt(after(act, n2_sum.got), w_down) * gate).astype(bf16)
+    y_sum = Scatter(put_rows(y_rows, slot_of, slot_cap, side, side), tok_rows)
+    y_keep = put_rows(y_rows, slot_of, slot_cap, 0, side)
+    n2_spread = n2_sum.step(down_got)
+    while n2_sum.steps_left():
+        n2_spread = n2_sum.step()
+    n2_last = n2_sum.cross(gate_got)
+    y_sum.begin(y_keep, *n2_spread)
+    y_far = y_sum.step()
+    n2_last = tie(n2_last, *y_far)[0]
+    grad_n2 = jnp.sum(n2_last.astype(f32), axis=0)
+    up_got = exchange(grad_wu.reshape(z_count, -1, ffh), n2_last)
 
     grad_logits = (
         probs * (grad_probs - jnp.sum(probs * grad_probs, axis=-1, keepdims=True))
@@ -375,9 +552,12 @@
     grad_hidden_b = grad_hidden.astype(bf16)
 
     pack_dh = context_gather(grad_hidden_b)
+    while y_sum.steps_left():
+        y_far = y_sum.step()
+    pack_dh, *_ = tie(pack_dh, *y_far)
+    y_last = y_sum.cross(up_got, pack_dh)
+    output = hidden + jnp.sum(y_last.astype(f32), axis=0)
     grad_mixed = mm_nt(pack_dh, wo_all).astype(bf16)
-    if aligned:
-        grad_mixed = mm_nt(grad_mixed, order_o).astype(bf16)
     grad_mixed_h = grad_mixed.reshape(pack_rows, local_heads, head_width)
     grad_soft = jnp.einsum("qhd,khd->hqk", grad_mixed_h, value, preferred_element_type=f32)
     delta = jnp.sum(soft * grad_soft, axis=2, keepdims=True)
@@ -385,6 +565,7 @@
     grad_query = jnp.einsum("hqk,khd->qhd", grad_scores, key, preferred_element_type=f32)
     grad_key = jnp.einsum("hqk,qhd->khd", grad_scores, query, preferred_element_type=f32)
     grad_value = jnp.einsum("hqk,qhd->khd", soft_b, grad_mixed_h, preferred_element_type=f32)
+    grad_v = grad_value.reshape(pack_rows, cols).astype(bf16)
     back_q, back_k = turn_back(grad_query * score_scale), turn_back(grad_key * score_scale)
     gain_q = jnp.sum(back_q * unit_q, axis=0)
     gain_k = jnp.sum(back_k * unit_k, axis=0)
@@ -395,28 +576,25 @@
         [
             scale_qk[0] * pull_q - raw_q * (scale_qk[0] ** 3 * inner[0]),
             scale_qk[1] * pull_k - raw_k * (scale_qk[1] ** 3 * inner[1]),
-            grad_value.reshape(pack_rows, cols),
+            grad_v,
         ],
         axis=1,
     ).astype(bf16)
-    grad_n1 = mm(context_pull(grad_qkv, wqkv_all), order_n_t(order_n))
-    grad_n1 = context_scatter(grad_n1)
+    grad_experts = join_experts(gate_got, up_got, down_got, halves)
+    grad_n1 = context_scatter(mm_nt(grad_qkv, wqkv_all))
     own_scale = lax.rsqrt(jnp.mean(inputs * inputs, axis=-1, keepdims=True) + epsilon)
     gain_one = jnp.sum(grad_n1 * inputs * own_scale, axis=0)
     grad_tokens = grad_hidden + norm_back(inputs, own_scale, gains[0], grad_n1)
 
-    grad_wqkv = mm_tn(normed_one_r, grad_qkv).reshape(e_count, z_count, c_count, w_rows, 3 * cols)
-    grad_wqkv = relative_scatter(grad_wqkv).astype(bf16)
-    grad_wqkv = (
-        lax.all_to_all(grad_wqkv, "context", 0, 0, tiled=True)
-        .reshape(c_count, w_rows, 3, runs, run_cols)
-        .transpose(1, 2, 3, 0, 4)
-        .reshape(w_rows, 3 * width)
-        .astype(f32)
-    )
-    grad_wo = mm_tn(mixed_r, pack_dh)
+
+    def weight_blocks(left, right):
+        blocks = mm_tn(left, right).reshape(e_count, c_count, z_count, w_rows, right.shape[1])
+        return blocks.transpose(0, 2, 1, 3, 4)
+
+    grad_v_sum, v_last = relative_scatter(weight_blocks(normed_one, grad_v), y_last)
+    grad_wo = mm_tn(mixed, pack_dh)
     if aligned:
-        grad_wo = relative_scatter(grad_wo.reshape(e_count, z_count, w_rows, width))
+        grad_wo, last = relative_scatter(grad_wo.reshape(e_count, z_count, w_rows, width), v_last)
     else:
         whole_wo = lax.dynamic_update_slice_in_dim(
             jnp.zeros((width, width), f32), grad_wo, me_c * cols, axis=0
@@ -424,6 +602,16 @@
         grad_wo = lax.psum_scatter(
             whole_wo.astype(bf16), EVERY, scatter_dimension=0, tiled=True
         ).astype(f32)
+        last = v_last
+    grad_qk_sum, _ = relative_scatter(weight_blocks(normed_one, grad_qkv[:, : 2 * cols]), last)
+    grad_wqkv = jnp.concatenate([grad_qk_sum, grad_v_sum], axis=2).astype(bf16)
+    grad_wqkv = (
+        lax.all_to_all(grad_wqkv, "context", 0, 0, tiled=True)
+        .reshape(c_count, w_rows, 3, runs, run_cols)
+        .transpose(1, 2, 3, 0, 4)
+        .reshape(w_rows, 3 * width)
+        .astype(f32)
+    )
     grad_attn = jnp.concatenate([grad_wqkv, grad_wo], axis=1)
 
     mine = jnp.arange(c_count)[None, None, :, None] == me_c
@@ -435,14 +623,6 @@
     grad_router = small_grads[:n_router].reshape(w_router.shape)
     grad_gains = small_grads[n_router:].reshape(norm_gains.shape)
     return (output[None], grad_tokens[None], grad_attn, grad_router, grad_gains, grad_experts)
-
-
-def context_pull(grad_qkv, wqkv_all):
-    return mm_nt(grad_qkv, wqkv_all).astype(bf16)
-
-
-def order_n_t(order_n):
-    return order_n.T
 
 
 def solution(mesh):

time: 1270 us -> 1050 us (0.83)
  waiting for transfers between devices: 642 us -> 485 us
  local copies, waits for them, and re-layouts: 186 us -> 81.7 us
  Pallas kernels: 0 us -> 81.8 us
  matrix products: 168 us -> 119 us
  starting transfers between devices: 135 us -> 103 us
  other arithmetic: 97.3 us -> 124 us
  blocking collectives: 13.2 us -> 29.5 us
    all_to_all x7 -> x11, waiting for transfers between devices: 271 us -> 170 us  [exchange(): return lax.all_to_all(after(blocks, *done), 'dp', 0, 0, tiled=True)]
    ppermute x12 -> x3, waiting for transfers between devices: 128 us -> 42.6 us  [shift(): lax.ppermute(value, axis, [(i, (i + step) % count) for i in range(count)])]
    pallas_call x0 -> x9, Pallas kernels: none -> 81.8 us  [the longest x4 29.8 us: put_rows(): pl.pallas_call(lambda *refs: put_kernel(per, slot_cap, *refs), grid=(coun...]
    all_gather x1, waiting for transfers between devices: 0.01 us -> 51 us  [on_device(): all_normed = lax.all_gather(normed_two, EVERY, axis=0, tiled=True)]
    dot_general x4 -> x0, matrix products: 40.7 us -> none  [the longest x2 24.2 us: take_rows(): got = jnp.einsum('sct,std->scd', pick, rows, preferred_element_type=f32)]
    all_to_all x1, waiting for transfers between devices: 39.6 us -> 0.01 us  [on_device(): got_gates = lax.all_to_all(sent_gates, EVERY, 0, 0, tiled=True)]
    all_to_all x1, starting transfers between devices: 38 us -> 2.75 us  [on_device(): lax.all_to_all(small_grads, EVERY, 0, 0, tiled=True)]
    unnamed x201 -> x202, local copies, waits for them, and re-layouts: 59 us -> 29.3 us
  transfers between devices with their start and end apart: 56 -> 51, of which waited for: 26 -> 34; matrix products, arithmetic and copies ran while one was open for 29% -> 22% of each run, Pallas kernels for 0% -> 6%
where the time goes in v3:
time: 1050 us; the launch traced here: 1040 us
  waiting for transfers between devices  485 us (46%)
  other arithmetic  124 us (12%)
  matrix products  119 us (11%)
  starting transfers between devices  103 us (10%)
  Pallas kernels  81.8 us (8%)
  local copies, waits for them, and re-layouts  81.7 us (8%)
  blocking collectives  29.5 us (3%)
  between operations  16 us (2%)
    ppermute x29, waiting for transfers between devices, swap(): return lax.ppermute(value, axis, [(i, i ^ bit) for i in range(count)])  182 us
    all_to_all x11, waiting for transfers between devices, exchange(): return lax.all_to_all(after(blocks, *done), 'dp', 0, 0, tiled=True)  170 us
    all_to_all x11, starting transfers between devices, exchange(): return lax.all_to_all(after(blocks, *done), 'dp', 0, 0, tiled=True)  52.7 us
    all_gather x1, waiting for transfers between devices, on_device(): all_normed = lax.all_gather(normed_two, EVERY, axis=0, tiled=True)  51 us
    ppermute x3, waiting for transfers between devices, shift(): lax.ppermute(value, axis, [(i, (i + step) % count) for i in range(count)])  42.6 us
    dot_general x5, matrix products, mm_nt(): lax.dot_general(a, b, (((1,), (1,)), ((), ())), preferred_element_type=f32)  35.1 us
    dot_general x6, matrix products, mm(): return jnp.dot(a, b, preferred_element_type=f32)  34.1 us
    dot_general x7, matrix products, mm_tn(): lax.dot_general(a, b, (((0,), (0,)), ((), ())), preferred_element_type=f32)  34.1 us
  transfers between devices with their start and end apart: 51, of which 34 were waited for; matrix products, arithmetic and copies ran while one was open for 22% of the time, Pallas kernels for 6%

profile of v3, /device:TPU:0, one launch (start us, length us, event | category | flops | bytes accessed | tf_op | source)
XLA Modules:
  0.0 1039.3 jit_solution(2820777878952550854)
XLA Ops:
  11.6 16.7 %all_to_all.110 = bf16[4,64,1536]{2,1,0:T(8,128)(2,1)} all-to-all(bf16[4,64,1536]{2,1,0:T(8,128)(2,1)} %reshape.1841), channel_id=1, replica_groups=mesh['expert'=2,'context'=4,'dp'=4] {'context'}, dimensions={0} | all-to-all | bytes 1572864 | tf_op jit(solution)/shard_map/all_to_all | solution.py:388
  33.7 15.4 %collective-permute-done.3 = bf16[128,2048]{1,0:T(8,128)(2,1)S(1)} collective-permute-done((bf16[128,2048]{1,0:T(8,128)(2,1)S(1)}, bf16[128,2048]{1,0:T(8,128)(2,1)S(1)}, u32[]{:S(2)}, u32[]{:S(2)}) %collective-permute-start.3) | collective-permute-done | bytes 524320 | tf_op jit(solution)/shard_map/ppermute | solution.py:36
  59.6 13.5 %shard_map.136 = (bf16[4,512,512]{2,1,0:T(8,128)(2,1)}, bf16[4,512,512]{2,1,0:T(8,128)(2,1)}, bf16[4,512,512]{2,1,0:T(8,128)(2,1)}) custom-call(f32[512,2,3072]{2,1,0:T(2,128)S(1)} %copy-done), custom_call_target="tpu_custom_call" | custom-call | tf_op jit(solution)/shard_map/pallas_call | solution.py:297
  75.1 6.8 all-to-all-start.1
  82.0 7.9 all-to-all-done.1
  90.4 27.3 %collective-permute-done.5 = bf16[128,2048]{1,0:T(8,128)(2,1)} collective-permute-done((bf16[128,2048]{1,0:T(8,128)(2,1)S(1)}, bf16[128,2048]{1,0:T(8,128)(2,1)}, u32[]{:S(2)}, u32[]{:S(2)}) %collective-permute-start.5) | collective-permute-done | bytes 524320 | tf_op jit(solution)/shard_map/ppermute | solution.py:36
  127.2 15.4 %collective-permute-done.6 = bf16[1,1,4,128,1024]{4,3,2,1,0:T(8,128)(2,1)S(1)} collective-permute-done((bf16[1,1,4,128,1024]{4,3,2,1,0:T(8,128)(2,1)S(1)}, bf16[1,1,4,128,1024]{4,3,2,1,0:T(8,128)(2,1)S(1)}, u32[]{:S(2)}, u32[]{:S(2)}) %collective-permute-start.6) | collective-permute-done | bytes 1048608 | tf_op jit(solution)/shard_map/ppermute | solution.py:31
  146.1 6.2 all-gather.4.cloned.1.call-done
  152.4 6.1 copy.174
  158.5 6.0 all-to-all-start.2
  164.5 6.2 fusion.135
  171.0 6.1 psum.14
  187.7 4.9 fusion.133
  196.7 34.0 %all-to-all-done.2 = bf16[4,512,512]{2,1,0:T(8,128)(2,1)} async-done(((bf16[4,512,512]{2,1,0:T(8,128)(2,1)}), bf16[4,512,512]{2,1,0:T(8,128)(2,1)}, u32[]{:S(2)}, u32[]{:S(2)}) %all-to-all-start.2) | async-done | bytes 2097184 | tf_op jit(solution)/shard_map/all_to_all | solution.py:281
  239.3 8.7 all-gather.6.cloned.1.call-done
  261.5 12.2 %collective-permute-done.9 = bf16[128,2048]{1,0:T(8,128)(2,1)S(1)} collective-permute-done((bf16[128,2048]{1,0:T(8,128)(2,1)S(1)}, bf16[128,2048]{1,0:T(8,128)(2,1)S(1)}, u32[]{:S(2)}, u32[]{:S(2)}) %collective-permute-start.9) | collective-permute-done | bytes 524320 | tf_op jit(solution)/shard_map/ppermute | solution.py:31
  275.8 6.5 all-to-all-done.3
  288.0 62.9 %collective-permute-done.11 = bf16[1,2,4,128,1024]{4,3,2,1,0:T(8,128)(2,1)S(1)} collective-permute-done((bf16[1,2,4,128,1024]{4,3,2,1,0:T(8,128)(2,1)S(1)}, bf16[1,2,4,128,1024]{4,3,2,1,0:T(8,128)(2,1)S(1)}, u32[]{:S(2)}, u32[]{:S(2)}) %collective-permute-start.11) | collective-permute-done | bytes 2097184 | tf_op jit(solution)/shard_map/ppermute | solution.py:31
  359.7 7.2 all-to-all-done.5
  366.9 4.9 all-to-all-start.4
  372.8 7.4 shard_map.137
  380.2 8.4 shard_map.138
  388.6 10.5 %fusion.2 = f32[2304,512]{0,1:T(8,128)} fusion(bf16[2048,512]{1,0:T(8,128)(2,1)} %bitcast.112, bf16[1152,2048]{1,0:T(8,128)(2,1)S(1)} %shard_map.138, bf16[1152,2048]{1,0:T(8,128)(2,1)S(1)} %shard_map.137), kind=kOutput, calls=%fused_computation.7 | convolution fusion | flops 4850712576 | bytes 16252928 | tf_op jit(solution)/shard_map/dot_general | solution.py:18
  400.4 51.0 %all-gather.8.cloned.1.call-done = bf16[4096,2048]{1,0:T(8,128)(2,1)} async-done(((bf16[128,2048]{1,0:T(8,128)(2,1)}), bf16[4096,2048]{1,0:T(8,128)(2,1)}) %all-gather.8.cloned.1.call-update) | async-done | bytes 16777232 | tf_op jit(solution)/shard_map/all_gather | solution.py:475
  451.4 13.8 %shard_map.139 = bf16[2304,2048]{1,0:T(8,128)(2,1)S(1)} custom-call(s32[32]{0:T(128)S(1)} %stack.302.refs_0_, s32[32,1,128]{2,1,0:T(1,128)S(1)} %bitcast.411, bf16[32,128,2048]{2,1,0:T(8,128)(2,1)} %bitcast.418, bf16[32,128,2048]{2,1,0:T(8,128)(2,1)} %bitcast.419), custom_call_target="tpu_custom_call" | custom-call | tf_op jit(solution)/shard_map/pallas_call | solution.py:239
  469.0 14.1 %fusion.13 = f32[2304,1024]{0,1:T(8,128)S(1)} fusion(bf16[2304,2048]{1,0:T(8,128)(2,1)} %copy-done.1, bf16[2048,512]{1,0:T(8,128)(2,1)} %bitcast.114, bf16[2048,512]{1,0:T(8,128)(2,1)} %bitcast.113), kind=kOutput, calls=%fused_computation.48 | convolution fusion | flops 9672065024 | bytes 23068672 | tf_op jit(solution)/shard_map/dot_general | solution.py:18
  483.0 6.7 multiply_convert_fusion.2
  489.7 8.2 fusion.12
  505.7 15.4 %convolution_convert_fusion.refs_1_ = bf16[2304,2048]{1,0:T(8,128)(2,1)} fusion(bf16[2304,1024]{0,1:T(8,128)(2,1)} %pad_maximum_fusion.3, bf16[2048,512]{1,0:T(8,128)(2,1)} %bitcast.114, bf16[2048,512]{1,0:T(8,128)(2,1)} %bitcast.113), kind=kOutput, calls=%fused_computation.4 | convolution fusion | flops 9676783616 | bytes 18350080 | tf_op jit(solution)/shard_map/dot_general | solution.py:22
  521.1 6.9 shard_map.140
  528.3 12.9 %collective-permute-done.14 = bf16[16,128,2048]{2,1,0:T(8,128)(2,1)S(1)} collective-permute-done((bf16[16,128,2048]{2,1,0:T(8,128)(2,1)S(1)}, bf16[16,128,2048]{2,1,0:T(8,128)(2,1)S(1)}, u32[]{:S(2)}, u32[]{:S(2)}) %collective-permute-start.14) | collective-permute-done | bytes 8388640 | tf_op jit(solution)/shard_map/ppermute | solution.py:31
  541.3 11.7 %multiply_convert_fusion.refs_1_ = bf16[2304,2048]{1,0:T(8,128)(2,1)} fusion(bf16[2304,512]{0,1:T(8,128)(2,1)S(1)} %copy-done.52, bf16[2048,512]{1,0:T(8,128)(2,1)} %bitcast.112, f32[2304]{0:T(1024)S(1)} %mul.551), kind=kOutput, calls=%fused_computation.3 | convolution fusion | flops 4841275392 | bytes 13902848 | tf_op jit(solution)/shard_map/dot_general | solution.py:22
  553.0 9.0 shard_map.142
  562.2 5.0 all-to-all-start.7
  567.2 7.2 shard_map.143
  584.6 7.0 convolution_convert_fusion.1
  591.6 24.3 %all-to-all-done.7.refs_2_ = bf16[4,512,512]{2,1,0:T(8,128)(2,1)S(1)} async-done(((bf16[4,512,512]{2,1,0:T(8,128)(2,1)}), bf16[4,512,512]{2,1,0:T(8,128)(2,1)S(1)}, u32[]{:S(2)}, u32[]{:S(2)}) %all-to-all-start.7) | async-done | bytes 2097184 | tf_op jit(solution)/shard_map/all_to_all | solution.py:281
  620.4 5.6 collective-permute-done.16
  626.0 4.7 collective-permute-done.17
  636.5 20.2 %collective-permute-done.19 = bf16[4,128,1024]{2,1,0:T(8,128)(2,1)S(1)} collective-permute-done((bf16[4,128,1024]{2,1,0:T(8,128)(2,1)S(1)}, bf16[4,128,1024]{2,1,0:T(8,128)(2,1)S(1)}, u32[]{:S(2)}, u32[]{:S(2)}) %collective-permute-start.19) | collective-permute-done | bytes 1048608 | tf_op jit(solution)/shard_map/ppermute | solution.py:31
  662.2 6.1 all-to-all-done.8.refs_0_
  668.3 4.8 all-to-all-start.9
  673.1 6.8 shard_map.141
  679.9 4.9 add_convert_fusion.1
  686.3 4.9 add_convert_fusion.3
  696.9 23.9 %all-to-all-done.9 = bf16[4,128,2048]{2,1,0:T(8,128)(2,1)} async-done(((bf16[4,128,2048]{2,1,0:T(8,128)(2,1)}), bf16[4,128,2048]{2,1,0:T(8,128)(2,1)}, u32[]{:S(2)}, u32[]{:S(2)}) %all-to-all-start.9) | async-done | bytes 2097184 | tf_op jit(solution)/shard_map/all_to_all | solution.py:281
  720.9 10.8 %collective-permute-done.22 = bf16[2,4,128,1024]{3,2,1,0:T(8,128)(2,1)} collective-permute-done((bf16[2,4,128,1024]{3,2,1,0:T(8,128)(2,1)}, bf16[2,4,128,1024]{3,2,1,0:T(8,128)(2,1)}, u32[]{:S(2)}, u32[]{:S(2)}) %collective-permute-start.22) | collective-permute-done | bytes 2097184 | tf_op jit(solution)/shard_map/ppermute | solution.py:31
  731.7 6.2 collective-permute-done.20
  750.6 7.2 collective-permute-done.25
  757.9 10.7 %convolution_convert_fusion.2 = bf16[2048,512]{1,0:T(8,128)(2,1)} fusion(bf16[2304,2048]{1,0:T(8,128)(2,1)} %copy-done.1, bf16[2304,1024]{0,1:T(8,128)(2,1)} %pad_maximum_fusion.3), kind=kOutput, calls=%fused_computation.47 | convolution fusion | flops 4832886784 | bytes 13893632 | tf_op jit(solution)/shard_map/dot_general | solution.py:26
  768.6 5.0 all-to-all-start.10
  809.3 13.2 %all-to-all-done.10.refs_1_ = bf16[4,512,512]{2,1,0:T(8,128)(2,1)} async-done(((bf16[4,512,512]{2,1,0:T(8,128)(2,1)}), bf16[4,512,512]{2,1,0:T(8,128)(2,1)}, u32[]{:S(2)}, u32[]{:S(2)}) %all-to-all-start.10) | async-done | bytes 2097184 | tf_op jit(solution)/shard_map/all_to_all | solution.py:281
  840.6 6.8 psum.15
  853.7 21.4 %all-to-all-done.11 = bf16[4,128,2048]{2,1,0:T(8,128)(2,1)} async-done(((bf16[4,128,2048]{2,1,0:T(8,128)(2,1)}), bf16[4,128,2048]{2,1,0:T(8,128)(2,1)}, u32[]{:S(2)}, u32[]{:S(2)}) %all-to-all-start.11) | async-done | bytes 2097184 | tf_op jit(solution)/shard_map/all_to_all | solution.py:281
  881.7 6.2 fusion.44
  901.6 5.3 all-to-all-done.12
  920.5 8.3 collective-permute-done.28
  931.8 4.6 all-to-all-done.13
  939.2 9.4 collective-permute-done.29
  948.6 4.9 fusion.22
  953.5 5.0 all-to-all-start.14
  963.2 9.0 shard_map.144
  975.6 30.9 %all-to-all-done.14 = bf16[4,4,64,1024]{3,2,1,0:T(8,128)(2,1)} async-done(((bf16[4,4,64,1024]{3,2,1,0:T(8,128)(2,1)}), bf16[4,4,64,1024]{3,2,1,0:T(8,128)(2,1)}, u32[]{:S(2)}, u32[]{:S(2)}) %all-to-all-start.14) | async-done | bytes 2097184 | tf_op jit(solution)/shard_map/all_to_all | solution.py:281
  1017.3 8.4 all-to-all-done.15
  (460 shorter events, 274.0 us)
Async XLA Ops:
  7.2 145.2 %all-gather.4.cloned.1.call-start = ((), (), s32[]{:S(2)}) async-start(), calls=%async_computation.17 | async-start | bytes 7077888 | tf_op jit(solution)/shard_map/all_gather | solution.py:405
  28.3 44.8 %collective-permute-start.1 = (bf16[128,2048]{1,0:T(8,128)(2,1)S(1)}, bf16[128,2048]{1,0:T(8,128)(2,1)}, u32[]{:S(2)}, u32[]{:S(2)}) collective-permute-start(bf16[128,2048]{1,0:T(8,128)(2,1)S(1)} %bitcast.428), channel_id=1, source_target_pairs={{0,8},{4,12},{8,0},{12,4},{1,9},{5,13},{9,1},{13,5},{2,10},{6,14},... | collective-permute-start | bytes 1572872 | tf_op jit(solution)/shard_map/ppermute | solution.py:31
  28.4 92.2 %collective-permute-start = (bf16[128,2048]{1,0:T(8,128)(2,1)S(1)}, bf16[128,2048]{1,0:T(8,128)(2,1)}, u32[]{:S(2)}, u32[]{:S(2)}) collective-permute-start(bf16[128,2048]{1,0:T(8,128)(2,1)S(1)} %bitcast.429), channel_id=1, source_target_pairs={{0,4},{4,0},{8,12},{12,8},{1,5},{5,1},{9,13},{13,9},{2,6},{6,2},{1... | collective-permute-start | bytes 1572872 | tf_op jit(solution)/shard_map/ppermute | solution.py:31
  28.5 20.6 %collective-permute-start.3 = (bf16[128,2048]{1,0:T(8,128)(2,1)S(1)}, bf16[128,2048]{1,0:T(8,128)(2,1)S(1)}, u32[]{:S(2)}, u32[]{:S(2)}) collective-permute-start(bf16[128,2048]{1,0:T(8,128)(2,1)S(1)} %bitcast_convert_fusion.1), channel_id=1, source_target_pairs={{0,1},{1,2},{2,3},{3,0},{4,5},{5,6},{6,7},{7,4},{8,9},{9,10},{10,1... | collective-permute-start | bytes 1572872 | tf_op jit(solution)/shard_map/ppermute | solution.py:36
  49.1 41.1 %collective-permute-start.4 = (bf16[128,2048]{1,0:T(8,128)(2,1)S(1)}, bf16[128,2048]{1,0:T(8,128)(2,1)S(1)}, u32[]{:S(2)}, u32[]{:S(2)}) collective-permute-start(bf16[128,2048]{1,0:T(8,128)(2,1)S(1)} %collective-permute-done.3), channel_id=1, source_target_pairs={{0,1},{1,2},{2,3},{3,0},{4,5},{5,6},{6,7},{7,4},{8,9},{9,10},{10,1... | collective-permute-start | bytes 1572872 | tf_op jit(solution)/shard_map/ppermute | solution.py:36
  73.1 47.4 %collective-permute-start.2 = (bf16[128,2048]{1,0:T(8,128)(2,1)}, bf16[128,2048]{1,0:T(8,128)(2,1)}, u32[]{:S(2)}, u32[]{:S(2)}) collective-permute-start(bf16[128,2048]{1,0:T(8,128)(2,1)} %collective-permute-done.1), channel_id=1, source_target_pairs={{0,4},{4,0},{8,12},{12,8},{1,5},{5,1},{9,13},{13,9},{2,6},{6,2},{1... | collective-permute-start | bytes 1572872 | tf_op jit(solution)/shard_map/ppermute | solution.py:31
  75.1 14.7 %all-to-all-start.1 = ((bf16[32,2,704]{2,1,0:T(2,128)(2,1)}), bf16[32,2,704]{2,1,0:T(2,128)(2,1)S(1)}, u32[]{:S(2)}, u32[]{:S(2)}) async-start(bf16[32,2,704]{2,1,0:T(2,128)(2,1)} %reshape.1916), calls=%async_computation.1 | async-start | bytes 196608 | tf_op jit(solution)/shard_map/all_to_all | solution.py:390
  81.9 166.1 %all-gather.6.cloned.1.call-start = ((), (), s32[]{:S(2)}) async-start(), calls=%async_computation.18 | async-start | bytes 2359296 | tf_op jit(solution)/shard_map/all_gather | solution.py:414
  90.2 27.5 %collective-permute-start.5 = (bf16[128,2048]{1,0:T(8,128)(2,1)S(1)}, bf16[128,2048]{1,0:T(8,128)(2,1)}, u32[]{:S(2)}, u32[]{:S(2)}) collective-permute-start(bf16[128,2048]{1,0:T(8,128)(2,1)S(1)} %collective-permute-done.4), channel_id=1, source_target_pairs={{0,1},{1,2},{2,3},{3,0},{4,5},{5,6},{6,7},{7,4},{8,9},{9,10},{10,1... | collective-permute-start | bytes 1572872 | tf_op jit(solution)/shard_map/ppermute | solution.py:36
  90.4 32.5 %copy-start.64 = (f32[2048]{0:T(1024)}, f32[2048]{0:T(1024)S(1)}, u32[]{:S(2)}) copy-start(f32[2048]{0:T(1024)S(1)} %mul.503) | copy-start | bytes 24580
  90.4 86.7 %copy-start.74 = (f32[1,2,1,256]{3,2,1,0:T(1,128)}, f32[1,2,1,256]{3,2,1,0:T(1,128)S(1)}, u32[]{:S(2)}) copy-start(f32[1,2,1,256]{3,2,1,0:T(1,128)S(1)} %get-tuple-element.168) | copy-start | bytes 6148
  90.4 86.7 %copy-start.76 = (f32[1,2,1,256]{3,2,1,0:T(1,128)}, f32[1,2,1,256]{3,2,1,0:T(1,128)S(1)}, u32[]{:S(2)}) copy-start(f32[1,2,1,256]{3,2,1,0:T(1,128)S(1)} %get-tuple-element.169) | copy-start | bytes 6148
  118.9 23.7 %collective-permute-start.6 = (bf16[1,1,4,128,1024]{4,3,2,1,0:T(8,128)(2,1)S(1)}, bf16[1,1,4,128,1024]{4,3,2,1,0:T(8,128)(2,1)S(1)}, u32[]{:S(2)}, u32[]{:S(2)}) collective-permute-start(bf16[1,1,4,128,1024]{4,3,2,1,0:T(8,128)(2,1)S(1)} %maximum_bitcast_fusion), channel_id=1, source_target_pairs={{0,8},{4,12},{8,0},{12,4},{1,9},{5,13},{9,1},{13,5},{2,10},{6,14},... | collective-permute-start | bytes 3145736 | tf_op jit(solution)/shard_map/ppermute | solution.py:31
  119.9 25.2 %collective-permute-start.7 = (bf16[1,1,4,128,1024]{4,3,2,1,0:T(8,128)(2,1)S(1)}, bf16[1,1,4,128,1024]{4,3,2,1,0:T(8,128)(2,1)S(1)}, u32[]{:S(2)}, u32[]{:S(2)}) collective-permute-start(bf16[1,1,4,128,1024]{4,3,2,1,0:T(8,128)(2,1)S(1)} %maximum_bitcast_fusion.1), channel_id=1, source_target_pairs={{0,16},{16,0},{1,17},{17,1},{2,18},{18,2},{3,19},{19,3},{4,20},{20... | collective-permute-start | bytes 3145736 | tf_op jit(solution)/shard_map/ppermute | solution.py:31
  158.5 72.2 %all-to-all-start.2 = ((bf16[4,512,512]{2,1,0:T(8,128)(2,1)}), bf16[4,512,512]{2,1,0:T(8,128)(2,1)}, u32[]{:S(2)}, u32[]{:S(2)}) async-start(bf16[4,512,512]{2,1,0:T(8,128)(2,1)} %get-tuple-element.40), calls=%async_computation.2 | async-start | bytes 4194304 | tf_op jit(solution)/shard_map/all_to_all | solution.py:281
  170.7 64.5 %copy-start.7 = (f32[512,1536]{1,0:T(8,128)}, f32[512,1536]{1,0:T(8,128)S(1)}, u32[]{:S(2)}) copy-start(f32[512,1536]{1,0:T(8,128)S(1)} %fusion.135) | copy-start | bytes 9437188
  230.7 51.6 %all-to-all-start.3 = ((bf16[4,512,512]{2,1,0:T(8,128)(2,1)}), bf16[4,512,512]{2,1,0:T(8,128)(2,1)}, u32[]{:S(2)}, u32[]{:S(2)}) async-start(bf16[4,512,512]{2,1,0:T(8,128)(2,1)} %get-tuple-element.43), calls=%async_computation.3 | async-start | bytes 4194304 | tf_op jit(solution)/shard_map/all_to_all | solution.py:281
  235.2 216.3 %all-gather.8.cloned.1.call-start = ((), (), s32[]{:S(2)}) async-start(), calls=%async_computation.19 | async-start | bytes 17301504 | tf_op jit(solution)/shard_map/all_gather | solution.py:475
  253.0 2.7 collective-permute-start.8
  253.1 20.5 %copy-start.39 = (bf16[1,128,2048]{2,1,0:T(8,128)(2,1)S(1)}, bf16[1,128,2048]{2,1,0:T(8,128)(2,1)}, u32[]{:S(2)}) copy-start(bf16[1,128,2048]{2,1,0:T(8,128)(2,1)} %param.9) | copy-start | bytes 1572868
  259.0 14.6 %collective-permute-start.9 = (bf16[128,2048]{1,0:T(8,128)(2,1)S(1)}, bf16[128,2048]{1,0:T(8,128)(2,1)S(1)}, u32[]{:S(2)}, u32[]{:S(2)}) collective-permute-start(bf16[128,2048]{1,0:T(8,128)(2,1)S(1)} %fusion.79), channel_id=1, source_target_pairs={{0,8},{4,12},{8,0},{12,4},{1,9},{5,13},{9,1},{13,5},{2,10},{6,14},... | collective-permute-start | bytes 1572872 | tf_op jit(solution)/shard_map/ppermute | solution.py:31
  261.5 21.9 %copy-start.66 = (f32[2048]{0:T(1024)}, f32[2048]{0:T(1024)S(1)}, u32[]{:S(2)}) copy-start(f32[2048]{0:T(1024)S(1)} %mul.545) | copy-start | bytes 24580
  285.0 65.8 %copy-start.50 = (bf16[1,1,4,128,1024]{4,3,2,1,0:T(8,128)(2,1)S(1)}, bf16[1,1,4,128,1024]{4,3,2,1,0:T(8,128)(2,1)}, u32[]{:S(2)}) copy-start(bf16[1,1,4,128,1024]{4,3,2,1,0:T(8,128)(2,1)} %copy-done.49) | copy-start | bytes 3145732
  285.0 65.8 %collective-permute-start.11 = (bf16[1,2,4,128,1024]{4,3,2,1,0:T(8,128)(2,1)S(1)}, bf16[1,2,4,128,1024]{4,3,2,1,0:T(8,128)(2,1)S(1)}, u32[]{:S(2)}, u32[]{:S(2)}) collective-permute-start(bf16[1,2,4,128,1024]{4,3,2,1,0:T(8,128)(2,1)S(1)} %pad_maximum_fusion.13), channel_id=1, source_target_pairs={{0,8},{4,12},{8,0},{12,4},{1,9},{5,13},{9,1},{13,5},{2,10},{6,14},... | collective-permute-start | bytes 6291464 | tf_op jit(solution)/shard_map/ppermute | solution.py:31
  286.5 66.6 %collective-permute-start.10 = (bf16[2,1,4,128,1024]{4,3,2,1,0:T(8,128)(2,1)S(1)}, bf16[2,1,4,128,1024]{4,3,2,1,0:T(8,128)(2,1)S(1)}, u32[]{:S(2)}, u32[]{:S(2)}) collective-permute-start(bf16[2,1,4,128,1024]{4,3,2,1,0:T(8,128)(2,1)S(1)} %pad_maximum_fusion.12), channel_id=1, source_target_pairs={{0,16},{16,0},{1,17},{17,1},{2,18},{18,2},{3,19},{19,3},{4,20},{20... | collective-permute-start | bytes 6291464 | tf_op jit(solution)/shard_map/ppermute | solution.py:31
  353.1 27.1 %collective-permute-start.13 = (bf16[2,2,4,128,1024]{4,3,2,1,0:T(8,128)(2,1)}, bf16[2,2,4,128,1024]{4,3,2,1,0:T(8,128)(2,1)}, u32[]{:S(2)}, u32[]{:S(2)}) collective-permute-start(bf16[2,2,4,128,1024]{4,3,2,1,0:T(8,128)(2,1)} %pad_maximum_fusion.5), channel_id=1, source_target_pairs={{0,4},{4,0},{8,12},{12,8},{1,5},{5,1},{9,13},{13,9},{2,6},{6,2},{1... | collective-permute-start | bytes 12582920 | tf_op jit(solution)/shard_map/ppermute | solution.py:31
  355.3 24.8 %collective-permute-start.12 = (bf16[2,2,4,128,1024]{4,3,2,1,0:T(8,128)(2,1)}, bf16[2,2,4,128,1024]{4,3,2,1,0:T(8,128)(2,1)}, u32[]{:S(2)}, u32[]{:S(2)}) collective-permute-start(bf16[2,2,4,128,1024]{4,3,2,1,0:T(8,128)(2,1)} %pad_maximum_fusion.4), channel_id=1, source_target_pairs={{0,4},{4,0},{8,12},{12,8},{1,5},{5,1},{9,13},{13,9},{2,6},{6,2},{1... | collective-permute-start | bytes 12582920 | tf_op jit(solution)/shard_map/ppermute | solution.py:31
  357.2 9.7 all-to-all-start.5
  366.9 102.1 %all-to-all-start.4 = ((bf16[4,512,512]{2,1,0:T(8,128)(2,1)}), bf16[4,512,512]{2,1,0:T(8,128)(2,1)}, u32[]{:S(2)}, u32[]{:S(2)}) async-start(bf16[4,512,512]{2,1,0:T(8,128)(2,1)} %get-tuple-element.47), calls=%async_computation.4 | async-start | bytes 4194304 | tf_op jit(solution)/shard_map/all_to_all | solution.py:281
  451.4 38.3 %slice-start.3 = ((s8[4718592]{0:T(1024)(128)(4,1)}), s8[524288]{0:T(1024)(128)(4,1)S(1)}, s32[]{:S(2)}) async-start(s8[4718592]{0:T(1024)(128)(4,1)} %bitcast.409), calls=%async_computation.23 | async-start | bytes 1048576
  469.0 20.7 %slice-start.4 = ((s8[4718592]{0:T(1024)(128)(4,1)}), s8[4194304]{0:T(1024)(128)(4,1)S(1)}, s32[]{:S(2)}) async-start(s8[4718592]{0:T(1024)(128)(4,1)} %bitcast.409), calls=%async_computation.24 | async-start | bytes 8388608
  501.7 19.4 %all-to-all-start.6 = ((f32[32,1,128]{2,1,0:T(1,128)}), f32[32,1,128]{2,1,0:T(1,128)S(1)}, u32[]{:S(2)}, u32[]{:S(2)}) async-start(f32[32,1,128]{2,1,0:T(1,128)} %bitcast.119), calls=%async_computation.6 | async-start | bytes 32768 | tf_op jit(solution)/shard_map/all_to_all | solution.py:514
  528.0 13.2 %collective-permute-start.14 = (bf16[16,128,2048]{2,1,0:T(8,128)(2,1)S(1)}, bf16[16,128,2048]{2,1,0:T(8,128)(2,1)S(1)}, u32[]{:S(2)}, u32[]{:S(2)}) collective-permute-start(bf16[16,128,2048]{2,1,0:T(8,128)(2,1)S(1)} %shard_map.140), channel_id=1, source_target_pairs={{0,4},{4,0},{8,12},{12,8},{1,5},{5,1},{9,13},{13,9},{2,6},{6,2},{1... | collective-permute-start | bytes 25165832 | tf_op jit(solution)/shard_map/ppermute | solution.py:31
  561.9 118.0 %collective-permute-start.15 = (bf16[16,128,2048]{2,1,0:T(8,128)(2,1)}, bf16[16,128,2048]{2,1,0:T(8,128)(2,1)}, u32[]{:S(2)}, u32[]{:S(2)}) collective-permute-start(bf16[16,128,2048]{2,1,0:T(8,128)(2,1)} %shard_map.142), channel_id=1, source_target_pairs={{0,4},{4,0},{8,12},{12,8},{1,5},{5,1},{9,13},{13,9},{2,6},{6,2},{1... | collective-permute-start | bytes 25165832 | tf_op jit(solution)/shard_map/ppermute | solution.py:31
  562.2 53.7 %all-to-all-start.7 = ((bf16[4,512,512]{2,1,0:T(8,128)(2,1)}), bf16[4,512,512]{2,1,0:T(8,128)(2,1)S(1)}, u32[]{:S(2)}, u32[]{:S(2)}) async-start(bf16[4,512,512]{2,1,0:T(8,128)(2,1)} %bitcast.447), calls=%async_computation.7 | async-start | bytes 4194304 | tf_op jit(solution)/shard_map/all_to_all | solution.py:281
  578.0 48.0 %collective-permute-start.16 = (bf16[2,4,128,1024]{3,2,1,0:T(8,128)(2,1)}, bf16[2,4,128,1024]{3,2,1,0:T(8,128)(2,1)}, u32[]{:S(2)}, u32[]{:S(2)}) collective-permute-start(bf16[2,4,128,1024]{3,2,1,0:T(8,128)(2,1)} %get-tuple-element.118), channel_id=1, source_target_pairs={{0,8},{4,12},{8,0},{12,4},{1,9},{5,13},{9,1},{13,5},{2,10},{6,14},... | collective-permute-start | bytes 6291464 | tf_op jit(solution)/shard_map/ppermute | solution.py:31
  583.0 47.7 %collective-permute-start.17 = (bf16[2,4,128,1024]{3,2,1,0:T(8,128)(2,1)}, bf16[2,4,128,1024]{3,2,1,0:T(8,128)(2,1)}, u32[]{:S(2)}, u32[]{:S(2)}) collective-permute-start(bf16[2,4,128,1024]{3,2,1,0:T(8,128)(2,1)} %get-tuple-element.117), channel_id=1, source_target_pairs={{0,16},{16,0},{1,17},{17,1},{2,18},{18,2},{3,19},{19,3},{4,20},{20... | collective-permute-start | bytes 6291464 | tf_op jit(solution)/shard_map/ppermute | solution.py:31
  615.9 52.4 %all-to-all-start.8 = ((bf16[4,512,512]{2,1,0:T(8,128)(2,1)}), bf16[4,512,512]{2,1,0:T(8,128)(2,1)}, u32[]{:S(2)}, u32[]{:S(2)}) async-start(bf16[4,512,512]{2,1,0:T(8,128)(2,1)} %bitcast.448), calls=%async_computation.8 | async-start | bytes 4194304 | tf_op jit(solution)/shard_map/all_to_all | solution.py:281
  632.6 24.1 %copy-start.35 = (bf16[2,1,4,128,1024]{4,3,2,1,0:T(8,128)(2,1)S(1)}, bf16[2,1,4,128,1024]{4,3,2,1,0:T(8,128)(2,1)}, u32[]{:S(2)}) copy-start(bf16[2,1,4,128,1024]{4,3,2,1,0:T(8,128)(2,1)} %get-tuple-element.116) | copy-start | bytes 6291460
  632.6 24.1 %collective-permute-start.19 = (bf16[4,128,1024]{2,1,0:T(8,128)(2,1)S(1)}, bf16[4,128,1024]{2,1,0:T(8,128)(2,1)S(1)}, u32[]{:S(2)}, u32[]{:S(2)}) collective-permute-start(bf16[4,128,1024]{2,1,0:T(8,128)(2,1)S(1)} %fusion.63), channel_id=1, source_target_pairs={{0,8},{4,12},{8,0},{12,4},{1,9},{5,13},{9,1},{13,5},{2,10},{6,14},... | collective-permute-start | bytes 3145736 | tf_op jit(solution)/shard_map/ppermute | solution.py:31
  634.9 23.9 %collective-permute-start.18 = (bf16[4,128,1024]{2,1,0:T(8,128)(2,1)S(1)}, bf16[4,128,1024]{2,1,0:T(8,128)(2,1)S(1)}, u32[]{:S(2)}, u32[]{:S(2)}) collective-permute-start(bf16[4,128,1024]{2,1,0:T(8,128)(2,1)S(1)} %fusion.62), channel_id=1, source_target_pairs={{0,16},{16,0},{1,17},{17,1},{2,18},{18,2},{3,19},{19,3},{4,20},{20... | collective-permute-start | bytes 3145736 | tf_op jit(solution)/shard_map/ppermute | solution.py:31
  668.3 52.6 %all-to-all-start.9 = ((bf16[4,128,2048]{2,1,0:T(8,128)(2,1)}), bf16[4,128,2048]{2,1,0:T(8,128)(2,1)}, u32[]{:S(2)}, u32[]{:S(2)}) async-start(bf16[4,128,2048]{2,1,0:T(8,128)(2,1)} %pad_maximum_fusion.15), calls=%async_computation.9 | async-start | bytes 4194304 | tf_op jit(solution)/shard_map/all_to_all | solution.py:281
  684.8 46.9 %collective-permute-start.22 = (bf16[2,4,128,1024]{3,2,1,0:T(8,128)(2,1)}, bf16[2,4,128,1024]{3,2,1,0:T(8,128)(2,1)}, u32[]{:S(2)}, u32[]{:S(2)}) collective-permute-start(bf16[2,4,128,1024]{3,2,1,0:T(8,128)(2,1)} %get-tuple-element.115), channel_id=1, source_target_pairs={{0,16},{16,0},{1,17},{17,1},{2,18},{18,2},{3,19},{19,3},{4,20},{20... | collective-permute-start | bytes 6291464 | tf_op jit(solution)/shard_map/ppermute | solution.py:31
  691.2 46.7 %collective-permute-start.20 = (bf16[2,4,128,1024]{3,2,1,0:T(8,128)(2,1)}, bf16[2,4,128,1024]{3,2,1,0:T(8,128)(2,1)}, u32[]{:S(2)}, u32[]{:S(2)}) collective-permute-start(bf16[2,4,128,1024]{3,2,1,0:T(8,128)(2,1)} %get-tuple-element.113), channel_id=1, source_target_pairs={{0,8},{4,12},{8,0},{12,4},{1,9},{5,13},{9,1},{13,5},{2,10},{6,14},... | collective-permute-start | bytes 6291464 | tf_op jit(solution)/shard_map/ppermute | solution.py:31
  696.8 43.1 %copy-start.6 = (f32[128,2048]{1,0:T(8,128)S(1)}, f32[128,2048]{1,0:T(8,128)}, u32[]{:S(2)}) copy-start(f32[128,2048]{1,0:T(8,128)} %copy-done.5) | copy-start | bytes 3145732
  696.8 43.1 %copy-start.67 = (f32[2048]{0:T(1024)S(1)}, f32[2048]{0:T(1024)}, u32[]{:S(2)}) copy-start(f32[2048]{0:T(1024)} %copy-done.66) | copy-start | bytes 24580
  696.8 43.2 %copy-start.84 = (f32[128]{0:T(128)S(1)}, f32[128]{0:T(128)}, u32[]{:S(2)}) copy-start(f32[128]{0:T(128)} %copy-done.83) | copy-start | bytes 1540
  742.7 15.2 %collective-permute-start.25 = (bf16[128,2048]{1,0:T(8,128)(2,1)}, bf16[128,2048]{1,0:T(8,128)(2,1)}, u32[]{:S(2)}, u32[]{:S(2)}) collective-permute-start(bf16[128,2048]{1,0:T(8,128)(2,1)} %get-tuple-element.108), channel_id=1, source_target_pairs={{0,8},{4,12},{8,0},{12,4},{1,9},{5,13},{9,1},{13,5},{2,10},{6,14},... | collective-permute-start | bytes 1572872 | tf_op jit(solution)/shard_map/ppermute | solution.py:31
  744.2 29.4 %collective-permute-start.24 = (bf16[128,2048]{1,0:T(8,128)(2,1)}, bf16[128,2048]{1,0:T(8,128)(2,1)}, u32[]{:S(2)}, u32[]{:S(2)}) collective-permute-start(bf16[128,2048]{1,0:T(8,128)(2,1)} %get-tuple-element.108), channel_id=1, source_target_pairs={{0,4},{4,0},{8,12},{12,8},{1,5},{5,1},{9,13},{13,9},{2,6},{6,2},{1... | collective-permute-start | bytes 1572872 | tf_op jit(solution)/shard_map/ppermute | solution.py:31
  746.8 30.4 %collective-permute-start.23 = (bf16[4,128,1024]{2,1,0:T(8,128)(2,1)}, bf16[4,128,1024]{2,1,0:T(8,128)(2,1)}, u32[]{:S(2)}, u32[]{:S(2)}) collective-permute-start(bf16[4,128,1024]{2,1,0:T(8,128)(2,1)} %fusion.67), channel_id=1, source_target_pairs={{0,8},{4,12},{8,0},{12,4},{1,9},{5,13},{9,1},{13,5},{2,10},{6,14},... | collective-permute-start | bytes 3145736 | tf_op jit(solution)/shard_map/ppermute | solution.py:31
  750.1 27.1 %collective-permute-start.21 = (bf16[4,128,1024]{2,1,0:T(8,128)(2,1)}, bf16[4,128,1024]{2,1,0:T(8,128)(2,1)}, u32[]{:S(2)}, u32[]{:S(2)}) collective-permute-start(bf16[4,128,1024]{2,1,0:T(8,128)(2,1)} %fusion.65), channel_id=1, source_target_pairs={{0,16},{16,0},{1,17},{17,1},{2,18},{18,2},{3,19},{19,3},{4,20},{20... | collective-permute-start | bytes 3145736 | tf_op jit(solution)/shard_map/ppermute | solution.py:31
  757.9 15.7 %collective-permute-start.26 = (bf16[128,2048]{1,0:T(8,128)(2,1)}, bf16[128,2048]{1,0:T(8,128)(2,1)}, u32[]{:S(2)}, u32[]{:S(2)}) collective-permute-start(bf16[128,2048]{1,0:T(8,128)(2,1)} %collective-permute-done.25), channel_id=1, source_target_pairs={{0,4},{4,0},{8,12},{12,8},{1,5},{5,1},{9,13},{13,9},{2,6},{6,2},{1... | collective-permute-start | bytes 1572872 | tf_op jit(solution)/shard_map/ppermute | solution.py:31
  768.6 53.9 %all-to-all-start.10 = ((bf16[4,512,512]{2,1,0:T(8,128)(2,1)}), bf16[4,512,512]{2,1,0:T(8,128)(2,1)}, u32[]{:S(2)}, u32[]{:S(2)}) async-start(bf16[4,512,512]{2,1,0:T(8,128)(2,1)} %bitcast.446), calls=%async_computation.10 | async-start | bytes 4194304 | tf_op jit(solution)/shard_map/all_to_all | solution.py:281
  789.2 61.9 %collective-permute-start.31 = (bf16[1,4,4,64,512]{4,3,1,2,0:T(8,128)(2,1)}, bf16[1,4,4,64,512]{4,3,1,2,0:T(8,128)(2,1)}, u32[]{:S(2)}, u32[]{:S(2)}) collective-permute-start(bf16[1,4,4,64,512]{4,3,1,2,0:T(8,128)(2,1)} %fusion.60), channel_id=1, source_target_pairs={{0,16},{16,0},{1,17},{17,1},{2,18},{18,2},{3,19},{19,3},{4,20},{20... | collective-permute-start | bytes 3145736 | tf_op jit(solution)/shard_map/ppermute | solution.py:31
  794.7 104.4 %collective-permute-start.30 = (bf16[1,4,64,2048]{3,2,1,0:T(8,128)(2,1)}, bf16[1,4,64,2048]{3,2,1,0:T(8,128)(2,1)}, u32[]{:S(2)}, u32[]{:S(2)}) collective-permute-start(bf16[1,4,64,2048]{3,2,1,0:T(8,128)(2,1)} %dynamic-slice_convert_fusion.1), channel_id=1, source_target_pairs={{0,16},{16,0},{1,17},{17,1},{2,18},{18,2},{3,19},{19,3},{4,20},{20... | collective-permute-start | bytes 3145736 | tf_op jit(solution)/shard_map/ppermute | solution.py:31
  822.5 52.6 %all-to-all-start.11 = ((bf16[4,128,2048]{2,1,0:T(8,128)(2,1)}), bf16[4,128,2048]{2,1,0:T(8,128)(2,1)}, u32[]{:S(2)}, u32[]{:S(2)}) async-start(bf16[4,128,2048]{2,1,0:T(8,128)(2,1)} %pad_maximum_fusion.14), calls=%async_computation.11 | async-start | bytes 4194304 | tf_op jit(solution)/shard_map/all_to_all | solution.py:281
  877.4 29.5 %all-to-all-start.12 = ((bf16[4,4,64,512]{3,2,1,0:T(8,128)(2,1)}), bf16[4,4,64,512]{3,2,1,0:T(8,128)(2,1)}, u32[]{:S(2)}, u32[]{:S(2)}) async-start(bf16[4,4,64,512]{3,2,1,0:T(8,128)(2,1)} %copy.200), calls=%async_computation.12 | async-start | bytes 2097152 | tf_op jit(solution)/shard_map/all_to_all | solution.py:281
  890.2 21.0 %collective-permute-start.27 = (bf16[2,128,2048]{2,1,0:T(8,128)(2,1)}, bf16[2,128,2048]{2,1,0:T(8,128)(2,1)}, u32[]{:S(2)}, u32[]{:S(2)}) collective-permute-start(bf16[2,128,2048]{2,1,0:T(8,128)(2,1)} %fusion.70), channel_id=1, source_target_pairs={{0,4},{4,0},{8,12},{12,8},{1,5},{5,1},{9,13},{13,9},{2,6},{6,2},{1... | collective-permute-start | bytes 3145736 | tf_op jit(solution)/shard_map/ppermute | solution.py:31
  898.6 50.0 %collective-permute-start.29 = (bf16[1,4,4,64,1024]{4,3,2,1,0:T(8,128)(2,1)}, bf16[1,4,4,64,1024]{4,3,2,1,0:T(8,128)(2,1)}, u32[]{:S(2)}, u32[]{:S(2)}) collective-permute-start(bf16[1,4,4,64,1024]{4,3,2,1,0:T(8,128)(2,1)} %fusion.23), channel_id=1, source_target_pairs={{0,16},{16,0},{1,17},{17,1},{2,18},{18,2},{3,19},{19,3},{4,20},{20... | collective-permute-start | bytes 6291464 | tf_op jit(solution)/shard_map/ppermute | solution.py:31
  906.9 29.5 %all-to-all-start.13 = ((bf16[4,64,2048]{2,1,0:T(8,128)(2,1)}), bf16[4,64,2048]{2,1,0:T(8,128)(2,1)}, u32[]{:S(2)}, u32[]{:S(2)}) async-start(bf16[4,64,2048]{2,1,0:T(8,128)(2,1)} %fusion.59), calls=%async_computation.13 | async-start | bytes 2097152 | tf_op jit(solution)/shard_map/all_to_all | solution.py:281
  915.6 13.2 %collective-permute-start.28 = (bf16[128,2048]{1,0:T(8,128)(2,1)}, bf16[128,2048]{1,0:T(8,128)(2,1)}, u32[]{:S(2)}, u32[]{:S(2)}) collective-permute-start(bf16[128,2048]{1,0:T(8,128)(2,1)} %fusion.80), channel_id=1, source_target_pairs={{0,8},{4,12},{8,0},{12,4},{1,9},{5,13},{9,1},{13,5},{2,10},{6,14},... | collective-permute-start | bytes 1572872 | tf_op jit(solution)/shard_map/ppermute | solution.py:31
  936.4 17.1 %all-to-all-start.16 = ((f32[32,1,1280]{2,1,0:T(1,128)}), f32[32,1,1280]{2,1,0:T(1,128)S(1)}, u32[]{:S(2)}, u32[]{:S(2)}) async-start(f32[32,1,1280]{2,1,0:T(1,128)} %copy.204), calls=%async_computation.16 | async-start | bytes 327680 | tf_op jit(solution)/shard_map/all_to_all | solution.py:622
  953.5 53.1 %all-to-all-start.14 = ((bf16[4,4,64,1024]{3,2,1,0:T(8,128)(2,1)}), bf16[4,4,64,1024]{3,2,1,0:T(8,128)(2,1)}, u32[]{:S(2)}, u32[]{:S(2)}) async-start(bf16[4,4,64,1024]{3,2,1,0:T(8,128)(2,1)} %fusion.22), calls=%async_computation.14 | async-start | bytes 4194304 | tf_op jit(solution)/shard_map/all_to_all | solution.py:281
  1009.5 16.2 %all-to-all-start.15 = ((bf16[4,64,1536]{2,1,0:T(8,128)(2,1)}), bf16[4,64,1536]{2,1,0:T(8,128)(2,1)}, u32[]{:S(2)}, u32[]{:S(2)}) async-start(bf16[4,64,1536]{2,1,0:T(8,128)(2,1)} %pad_maximum_fusion.18), calls=%async_computation.15 | async-start | bytes 1572864 | tf_op jit(solution)/shard_map/all_to_all | solution.py:609
  (86 other events, 595.9 us)
Sparse Core Ops, SparseCore 0:
  28.4 123.9 all-gather.3
  158.6 89.3 all-gather.5
  283.5 167.8 all-gather.7

commit v4 on v3

--- a/solution.py
+++ b/solution.py
@@ -12,6 +12,7 @@
 bf16 = jnp.bfloat16
 f32 = jnp.float32
 EVERY = ("expert", "context", "dp")
+QUICK = pl.CostEstimate(flops=1, bytes_accessed=1, transcendentals=0)
 
 
 def mm(a, b):
@@ -140,6 +141,7 @@
         around = [value]
         for _ in range(lax.axis_size("dp") - 1):
             around.append(shift(around[-1], "dp", 1))
+        self.ring, self.around = around[-1], around
         far = far_steps()
         half = value.shape[1] // 2
         shape = (-1, value.shape[0], half)
@@ -176,21 +178,37 @@
             cut = slice(i * half, (i + 1) * half)
             self.states.append((keep[..., cut], got[..., cut], far[::-1] if i else far, list(far)))
 
-    def step(self, *done):
+    def step(self, other=None):
         sums = []
-        arrived = [state[1] for state in self.states]
-        arrived = after(arrived, *done) if done else arrived
-        for (own, _, order, left), other in zip(self.states, arrived):
+        for own, got, order, left in self.states:
             step = order[len(order) - len(left)]
             dim = left.index(step)
             first = [slice(None)] * dim + [0]
             second = [slice(None)] * dim + [1]
-            sent = own[tuple(second)].astype(f32) + other[tuple(second)].astype(f32)
-            kept = own[tuple(first)].astype(f32) + other[tuple(first)].astype(f32)
-            got = swap(sent.astype(bf16), *step)
-            sums.append((kept.astype(bf16), got, order, left[:dim] + left[dim + 1 :]))
-        self.states = sums
-        return [state[1] for state in sums]
+            sent = own[tuple(second)].astype(f32) + got[tuple(second)].astype(f32)
+            kept = own[tuple(first)].astype(f32) + got[tuple(first)].astype(f32)
+            sums.append([kept.astype(bf16), sent.astype(bf16), step, order, left[:dim] + left[dim + 1 :]])
+        if other:
+            sent = other.require(*[entry[1] for entry in sums])
+            for entry, new in zip(sums, sent):
+                entry[1] = new
+        self.states = [
+            (kept, swap(sent, *step), order, left) for kept, sent, step, order, left in sums
+        ]
+
+    def require(self, *values):
+        count = len(self.states)
+        *got, = tie(*[state[1] for state in self.states], *values)
+        self.states = [
+            state[:1] + (new,) + state[2:] for state, new in zip(self.states, got[:count])
+        ]
+        return got[count:]
+
+    def kept(self):
+        return [state[0] for state in self.states]
+
+    def keep(self, kept):
+        self.states = [(own,) + state[1:] for own, state in zip(kept, self.states)]
 
     def steps_left(self):
         return len(self.states[0][3])
@@ -246,35 +264,224 @@
             out_specs=pl.BlockSpec((per * slot_cap, width), lambda i, order_ref: (i, 0)),
         ),
         out_shape=jax.ShapeDtypeStruct((count * slot_cap, width), bf16),
+        cost_estimate=QUICK,
         compiler_params=pltpu.CompilerParams(vmem_limit_bytes=40 * 2**20),
     )(order, slots.reshape(count, 1, tokens), *[part for part in parts for _ in range(per)])
 
 
-def put_kernel(per, slot_cap, slot_ref, rows_ref, out_ref):
+def output_kernel(per, slot_cap, slot_ref, act_ref, gate_ref, w_ref, out_ref):
     places = lax.broadcasted_iota(jnp.int32, (slot_cap, slot_ref.shape[2]), 0)
-    rows = rows_ref[...].astype(f32)
+    rows = mm_nt(act_ref[...], w_ref[...]) * gate_ref[...]
     for j in range(per):
         pick = (slot_ref[j] == places).astype(f32).astype(bf16)
         part = rows[j * slot_cap : (j + 1) * slot_cap].astype(bf16)
         out_ref[j] = mm_tn(pick, part).astype(bf16)
 
 
-def put_rows(rows, slots, slot_cap, first, count):
-    width = rows.shape[1]
+def expert_output(act, gate, w_down, slots, slot_cap, side):
     total, tokens = slots.shape
-    per = sources_per_block(slot_cap)
-    skip = first // per
+    width, ffh = w_down.shape
+    per = max(sources_per_block(slot_cap), 8)
+    steps = total // 2 // per
+    first = side * steps
+
+    def rows_of(columns):
+        return pl.BlockSpec((per * slot_cap, columns), lambda i: (i + first, 0))
+
     return pl.pallas_call(
-        lambda *refs: put_kernel(per, slot_cap, *refs),
-        grid=(count // per,),
+        lambda *refs: output_kernel(per, slot_cap, *refs),
+        grid=(steps,),
         in_specs=[
-            pl.BlockSpec((per, 1, tokens), lambda i: (i + skip, 0, 0)),
-            pl.BlockSpec((per * slot_cap, width), lambda i: (i + skip, 0)),
+            pl.BlockSpec((per, 1, tokens), lambda i: (i + first, 0, 0)),
+            rows_of(ffh),
+            rows_of(1),
+            pl.BlockSpec((width, ffh), lambda i: (0, 0)),
         ],
         out_specs=pl.BlockSpec((per, tokens, width), lambda i: (i, 0, 0)),
-        out_shape=jax.ShapeDtypeStruct((count, tokens, width), bf16),
+        out_shape=jax.ShapeDtypeStruct((total // 2, tokens, width), bf16),
+        cost_estimate=pl.CostEstimate(
+            flops=total * slot_cap * width * (ffh + tokens),
+            bytes_accessed=total * tokens * width,
+            transcendentals=0,
+        ),
+        compiler_params=pltpu.CompilerParams(vmem_limit_bytes=48 * 2**20),
+    )(slots.reshape(total, 1, tokens), act, gate, w_down)
+
+
+def turn(v, cos, sin):
+    return v * cos + pltpu.roll(v, v.shape[1] // 2, 1) * sin
+
+
+def turn_back(v, cos, sin):
+    return v * cos + pltpu.roll(v * sin, v.shape[1] // 2, 1)
+
+
+def soften(query, key, score_scale, spot_ref, spot_t_ref):
+    scores = mm_nt(query, key) * score_scale
+    same = spot_ref[:, 0:1] == spot_t_ref[0:1, :]
+    allowed = same & (spot_t_ref[1:2, :] <= spot_ref[:, 1:2])
+    scores = jnp.where(allowed, scores, masked_score)
+    raised = jnp.exp(scores - jnp.max(scores, axis=1, keepdims=True))
+    return raised / jnp.sum(raised, axis=1, keepdims=True)
+
+
+def mix_kernel(score_scale, q_ref, k_ref, v_ref, scale_ref, gain_ref, cos_ref, sin_ref, *refs):
+    spot_ref, spot_t_ref, query_ref, key_ref, value_ref, mixed_ref = refs
+    cos, sin = cos_ref[...], sin_ref[...]
+    query = turn(q_ref[...] * scale_ref[:, 0:1] * gain_ref[0:1, :], cos, sin).astype(bf16)
+    key = turn(k_ref[...] * scale_ref[:, 1:2] * gain_ref[1:2, :], cos, sin).astype(bf16)
+    value = v_ref[...].astype(bf16)
+    soft = soften(query, key, score_scale, spot_ref, spot_t_ref)
+    query_ref[...], key_ref[...], value_ref[...] = query, key, value
+    mixed_ref[...] = mm(soft.astype(bf16), value).astype(bf16)
+
+
+def mix_back_kernel(score_scale, q_ref, k_ref, scale_ref, gain_ref, cos_ref, sin_ref, *refs):
+    spot_ref, spot_t_ref, query_ref, key_ref, value_ref, dh_ref, wo_ref = refs[:7]
+    pull_q_ref, pull_k_ref, grad_v_ref, gain_out_ref, inner_ref = refs[7:]
+    cos, sin = cos_ref[...], sin_ref[...]
+    query, key, value = query_ref[...], key_ref[...], value_ref[...]
+    grad_mixed = mm_nt(dh_ref[...], wo_ref[...]).astype(bf16)
+    soft = soften(query, key, score_scale, spot_ref, spot_t_ref)
+    grad_soft = mm_nt(grad_mixed, value)
+    delta = jnp.sum(soft * grad_soft, axis=1, keepdims=True)
+    grad_scores = (soft * (grad_soft - delta)).astype(bf16)
+    grad_v_ref[...] = mm_tn(soft.astype(bf16), grad_mixed).astype(bf16)
+    inner = []
+    for i, (grad, raw_ref, out_ref) in enumerate(
+        (
+            (mm(grad_scores, key), q_ref, pull_q_ref),
+            (mm_tn(grad_scores, query), k_ref, pull_k_ref),
+        )
+    ):
+        back = turn_back(grad * score_scale, cos, sin)
+        raw, scale = raw_ref[...], scale_ref[:, i : i + 1]
+        pull = back * gain_ref[i : i + 1, :]
+        gain_out_ref[i : i + 1, :] = jnp.sum(back * raw * scale, axis=0, keepdims=True)
+        inner.append(jnp.sum(raw * pull, axis=1, keepdims=True))
+        out_ref[...] = pull
+    both = jnp.concatenate(inner, axis=1)
+
+    @pl.when(pl.program_id(0) == 0)
+    def _():
+        inner_ref[...] = both
+
+    @pl.when(pl.program_id(0) > 0)
+    def _():
+        inner_ref[...] += both
+
+
+def head_specs(rows, head_width, heads):
+    def part(p):
+        return pl.BlockSpec((rows, head_width), lambda h: (0, h + p * heads))
+
+    def fixed(*shape):
+        return pl.BlockSpec(shape, lambda h: (0,) * len(shape))
+
+    gain = pl.BlockSpec((2, head_width), lambda h: (0, h))
+    return part, fixed, gain
+
+
+def mix(qkv, scale, gains, cos, sin, spots, heads):
+    rows, head_width = cos.shape
+    part, fixed, gain = head_specs(rows, head_width, heads)
+    return pl.pallas_call(
+        lambda *refs: mix_kernel(head_width**-0.5, *refs),
+        grid=(heads,),
+        in_specs=[part(0), part(1), part(2), fixed(rows, 2), gain, fixed(rows, head_width)]
+        + [fixed(rows, head_width), fixed(rows, 2), fixed(2, rows)],
+        out_specs=[part(0)] * 4,
+        out_shape=[jax.ShapeDtypeStruct((rows, heads * head_width), bf16)] * 4,
+        cost_estimate=QUICK,
         compiler_params=pltpu.CompilerParams(vmem_limit_bytes=40 * 2**20),
-    )(slots.reshape(total, 1, tokens), rows)
+    )(qkv, qkv, qkv, scale, gains, cos, sin, spots, spots.T)
+
+
+def mix_back(qkv, scale, gains, cos, sin, spots, heads, query, key, value, dh, wo):
+    rows, head_width = cos.shape
+    part, fixed, gain = head_specs(rows, head_width, heads)
+    cols = heads * head_width
+    return pl.pallas_call(
+        lambda *refs: mix_back_kernel(head_width**-0.5, *refs),
+        grid=(heads,),
+        in_specs=[part(0), part(1), fixed(rows, 2), gain, fixed(rows, head_width)]
+        + [fixed(rows, head_width), fixed(rows, 2), fixed(2, rows), part(0), part(0), part(0)]
+        + [fixed(*dh.shape), pl.BlockSpec((head_width, wo.shape[1]), lambda h: (h, 0))],
+        out_specs=[part(0), part(0), part(0), gain, fixed(rows, 2)],
+        out_shape=[jax.ShapeDtypeStruct((rows, cols), f32)] * 2
+        + [jax.ShapeDtypeStruct((rows, cols), bf16), jax.ShapeDtypeStruct((2, cols), f32)]
+        + [jax.ShapeDtypeStruct((rows, 2), f32)],
+        cost_estimate=QUICK,
+        compiler_params=pltpu.CompilerParams(vmem_limit_bytes=48 * 2**20),
+    )(qkv, qkv, scale, gains, cos, sin, spots, spots.T, query, key, value, dh, wo)
+
+
+def expert_kernel(per, slot_cap, order_ref, slot_ref, *refs):
+    xs, (w_ref, back_ref, gate_ref) = refs[:per], refs[per : per + 3]
+    n_ref, act_ref, scaled_ref, gu_ref, dgate_ref, out_ref = refs[-6:]
+    ffh = act_ref.shape[1]
+    places = lax.broadcasted_iota(jnp.int32, (slot_cap, slot_ref.shape[2]), 0)
+    picks = [(slot_ref[j] == places).astype(f32).astype(bf16) for j in range(per)]
+    rows = jnp.concatenate([mm(picks[j], xs[j][0]) for j in range(per)]).astype(bf16)
+    n_ref[...] = rows
+    gate_up = mm(rows, w_ref[...])
+    gate_part, up_part = gate_up[:, :ffh], gate_up[:, ffh:]
+    sig = jax.nn.sigmoid(gate_part)
+    silu = gate_part * sig
+    act = (silu * up_part).astype(bf16)
+    act_f = act.astype(f32)
+    back, gate = back_ref[...], gate_ref[...]
+    act_ref[...] = act
+    scaled_ref[...] = (act_f * gate).astype(bf16)
+    dgate_ref[...] = jnp.sum(act_f * back, axis=1, keepdims=True)
+    grad_act = back * gate
+    gu_ref[:, :ffh] = (grad_act * up_part * sig * (1.0 + gate_part * (1.0 - sig))).astype(bf16)
+    gu_ref[:, ffh:] = (grad_act * silu).astype(bf16)
+    grad_rows = mm_nt(gu_ref[...], w_ref[...])
+    for j in range(per):
+        part = grad_rows[j * slot_cap : (j + 1) * slot_cap].astype(bf16)
+        out_ref[j] = mm_tn(picks[j], part).astype(bf16)
+
+
+def run_expert(rows, order, slots, slot_cap, w_gu, back, gate, side, held=()):
+    total, tokens, width = rows.shape
+    ffh = back.shape[1]
+    per = max(sources_per_block(slot_cap), 8)
+    steps = total // 2 // per
+    first = side * steps
+    block = per * slot_cap
+
+    def block_of(j):
+        return pl.BlockSpec(
+            (1, tokens, width), lambda i, order_ref: (order_ref[(i + first) * per + j], 0, 0)
+        )
+
+    def rows_of(columns):
+        return pl.BlockSpec((block, columns), lambda i, order_ref: (i + first, 0))
+
+    def whole(columns, dtype):
+        return jax.ShapeDtypeStruct((total * slot_cap, columns), dtype)
+
+    in_specs = [pl.BlockSpec((per, 1, tokens), lambda i, order_ref: (i + first, 0, 0))]
+    in_specs += [block_of(j) for j in range(per)]
+    in_specs += [pl.BlockSpec(w_gu.shape, lambda i, order_ref: (0, 0)), rows_of(ffh), rows_of(1)]
+    aliases = {len(in_specs) + 1 + i: i for i in range(len(held))}
+    in_specs += [pl.BlockSpec(memory_space=pl.ANY) for _ in held]
+    return pl.pallas_call(
+        lambda *refs: expert_kernel(per, slot_cap, *refs),
+        grid_spec=pltpu.PrefetchScalarGridSpec(
+            num_scalar_prefetch=1,
+            grid=(steps,),
+            in_specs=in_specs,
+            out_specs=[rows_of(width), rows_of(ffh), rows_of(ffh), rows_of(2 * ffh), rows_of(1)]
+            + [pl.BlockSpec((per, tokens, width), lambda i, order_ref: (i, 0, 0))],
+        ),
+        out_shape=[whole(width, bf16), whole(ffh, bf16), whole(ffh, bf16), whole(2 * ffh, bf16)]
+        + [whole(1, f32), jax.ShapeDtypeStruct((total // 2, tokens, width), bf16)],
+        input_output_aliases=aliases,
+        cost_estimate=QUICK,
+        compiler_params=pltpu.CompilerParams(vmem_limit_bytes=58 * 2**20),
+    )(order, slots.reshape(total, 1, tokens), *([rows] * per), w_gu, back, gate, *held)
 
 
 def exchange(blocks, *done):
@@ -300,6 +507,7 @@
         in_specs=[pl.BlockSpec((block, experts, width), lambda i: (i, 0, 0))],
         out_specs=[pl.BlockSpec((shares, block, ffh), lambda i: (0, i, 0))] * 3,
         out_shape=[jax.ShapeDtypeStruct((shares, rows, ffh), bf16)] * 3,
+        cost_estimate=QUICK,
         compiler_params=pltpu.CompilerParams(vmem_limit_bytes=32 * 2**20),
     )(w)
 
@@ -322,19 +530,41 @@
         in_specs=[pl.BlockSpec((shares, block, ffh), lambda i: (0, i, 0))] * 3,
         out_specs=pl.BlockSpec((block, experts, width), lambda i: (i, 0, 0)),
         out_shape=jax.ShapeDtypeStruct((rows, experts, width), f32),
+        cost_estimate=QUICK,
         compiler_params=pltpu.CompilerParams(vmem_limit_bytes=32 * 2**20),
     )(gate, up, down)
 
 
-def relative_scatter(value, *done, late=()):
+def near_gather(piece):
+    around = [piece]
+    for _ in range(lax.axis_size("dp") - 1):
+        around.append(shift(around[-1], "dp", 1))
+    held = [jnp.stack(around)]
+    for bit in bits_of("expert"):
+        held = held + [swap(part, "expert", bit) for part in held]
+    me_e, me_z = lax.axis_index("expert"), lax.axis_index("dp")
+    z_count = len(around)
+    whole = jnp.zeros((len(held), z_count) + piece.shape, piece.dtype)
+    for r, part in enumerate(held):
+        for k in range(z_count):
+            at = (me_e ^ r, (me_z - k) % z_count, 0, 0)
+            whole = lax.dynamic_update_slice(whole, part[None, k : k + 1], at)
+    return whole.reshape(-1, piece.shape[1])
+
+
+def halved(value):
     for bit in reversed(bits_of("expert")):
-        value = value.reshape((value.shape[0] // 2, 2) + value.shape[1:]) if bit == 1 else value
         if bit == 1:
+            value = value.reshape((value.shape[0] // 2, 2) + value.shape[1:])
             value = half_step(value, "expert", 1, 1)
         else:
             value = value.reshape((2, value.shape[0] // 2) + value.shape[1:])
             value = half_step(value, "expert", bit, 0)
-    arrived = exchange(value[0].astype(bf16), *done)
+    return value[0].astype(bf16)
+
+
+def sum_over_dp(blocks, *done):
+    arrived = exchange(blocks, *done)
     return jnp.sum(arrived.astype(f32), axis=0), arrived
 
 
@@ -402,21 +632,22 @@
     grad_out = cotangent[0]
     gate_blocks, up_blocks, down_blocks = split_experts(w_experts, halves)
     around = ("expert", "dp")
-    wqkv_all = lax.all_gather(wqkv, around, axis=0, tiled=True)
+    wo_own = w_attn[:, 3 * width :].astype(bf16)
     g_gather = Gather(grad_out.astype(bf16))
+    wqkv = after(wqkv, g_gather.around[1])
+    wqkv_all = packed = lax.all_gather(wqkv, around, axis=0, tiled=True)
+    if aligned:
+        wo_all = near_gather(wo_own)
+    else:
+        wo_full = lax.all_gather(wo_own, EVERY, axis=0, tiled=True)
+        wo_all = lax.dynamic_slice_in_dim(wo_full, me_c * cols, cols, axis=0)
     wqkv_all = (
         wqkv_all.reshape(e_count, z_count, c_count, w_rows, 3 * cols)
         .transpose(0, 2, 1, 3, 4)
         .reshape(width, 3 * cols)
     )
-    wo_own = w_attn[:, 3 * width :].astype(bf16)
-    if aligned:
-        wo_all = lax.all_gather(after(wo_own, wqkv_all), around, axis=0, tiled=True)
-    else:
-        wo_full = lax.all_gather(wo_own, EVERY, axis=0, tiled=True)
-        wo_all = lax.dynamic_slice_in_dim(wo_full, me_c * cols, cols, axis=0)
-
-    w_down = exchange(down_blocks, wqkv_all)
+
+    w_down = exchange(down_blocks, packed)
     w_gate = exchange(gate_blocks, w_down)
     w_up = exchange(up_blocks, w_gate)
     w_gu = jnp.concatenate([w_gate.reshape(width, ffh), w_up.reshape(width, ffh)], axis=1)
@@ -425,7 +656,7 @@
     pack_x = context_gather(tokens[0]).astype(f32)
     scale_one = lax.rsqrt(jnp.mean(pack_x * pack_x, axis=-1, keepdims=True) + epsilon)
     normed_one = (pack_x * scale_one * gains[0]).astype(bf16)
-    qkv = mm(after(normed_one, gate_blocks, *g_gather.first), wqkv_all)
+    qkv = mm(after(normed_one, gate_blocks, wo_all, g_gather.ring), wqkv_all)
     place, doc, offset = locate(
         jnp.arange(pack_rows, dtype=jnp.int32), lengths[0], block_order[0], blk_rows
     )
@@ -433,39 +664,17 @@
     freq = rope_base ** (-2.0 * jnp.arange(half_width, dtype=f32) / head_width)
     angle = offset.astype(f32)[:, None] * freq[None, :]
     cos_t, sin_t = jnp.cos(angle), jnp.sin(angle)
-    cos_all = jnp.concatenate([cos_t, cos_t], axis=1)[:, None, :]
-    sin_all = jnp.concatenate([-sin_t, sin_t], axis=1)[:, None, :]
-
-    def turn(v):
-        v = v.reshape(pack_rows, local_heads, head_width)
-        return v * cos_all + jnp.roll(v, half_width, axis=2) * sin_all
-
-    def turn_back(v):
-        return (v * cos_all + jnp.roll(v * sin_all, half_width, axis=2)).reshape(pack_rows, cols)
-
+    cos_all = jnp.concatenate([cos_t, cos_t], axis=1)
+    sin_all = jnp.concatenate([-sin_t, sin_t], axis=1)
+    spots = jnp.stack([doc, place], axis=1)
     my_gains = lax.dynamic_index_in_dim(
         gains[2:].reshape(2, runs, c_count, run_cols), me_c, 2, keepdims=False
     ).reshape(2, cols)
     raw_q, raw_k = qkv[:, :cols], qkv[:, cols : 2 * cols]
-    value = qkv[:, 2 * cols :].astype(bf16).reshape(pack_rows, local_heads, head_width)
     squares = jnp.stack([jnp.sum(raw_q * raw_q, axis=1), jnp.sum(raw_k * raw_k, axis=1)])
-    scale_qk = lax.rsqrt(lax.psum(squares, "context") / width + epsilon)[:, :, None]
-    unit_q, unit_k = raw_q * scale_qk[0], raw_k * scale_qk[1]
-    query = turn(unit_q * my_gains[0]).astype(bf16)
-    key = turn(unit_k * my_gains[1]).astype(bf16)
-    scores = jnp.einsum("qhd,khd->hqk", query, key, preferred_element_type=f32) * score_scale
-    allowed = (doc[:, None] == doc[None, :]) & (place[None, :] <= place[:, None])
-    scores = jnp.where(allowed[None], scores, masked_score)
-    top = jnp.max(scores, axis=2, keepdims=True)
-    raised = jnp.exp(scores - top)
-    soft = raised / jnp.sum(raised, axis=2, keepdims=True)
-    soft_b = after(soft.astype(bf16), w_down)
-    mixed = (
-        jnp.einsum("hqk,khd->qhd", soft_b, value, preferred_element_type=f32)
-        .reshape(pack_rows, cols)
-        .astype(bf16)
-    )
-    hidden = after(inputs + context_scatter(mm(mixed, wo_all)), w_gate)
+    scale_qk = lax.rsqrt(lax.psum(squares, "context") / width + epsilon).T
+    query, key, value, mixed = mix(qkv, scale_qk, my_gains, cos_all, sin_all, spots, local_heads)
+    hidden = inputs + context_scatter(mm(after(mixed, w_down), wo_all))
     scale_two = lax.rsqrt(jnp.mean(hidden * hidden, axis=-1, keepdims=True) + epsilon)
     normed_two = (hidden * scale_two * gains[1]).astype(bf16)
     logits = mm(normed_two, router_w)
@@ -490,49 +699,40 @@
     )
     w_down = w_down.reshape(width, ffh)
     back = mm(g_rows, w_down)
-    n_rows = take_rows([after(all_normed, back)], order, slot_of, slot_cap)
-    gate_up = mm(n_rows, w_gu)
-    gate_part, up_part = gate_up[:, :ffh], gate_up[:, ffh:]
-    sig = jax.nn.sigmoid(gate_part)
-    silu = gate_part * sig
-    act = (silu * up_part).astype(bf16)
-    act_f = act.astype(f32)
-    grad_gate_slot = jnp.sum(act_f * back, axis=1).reshape(total, slot_cap)
-    grad_act = back * gate
-    grad_gu = jnp.concatenate(
-        [grad_act * up_part * sig * (1.0 + gate_part * (1.0 - sig)), grad_act * silu], axis=1
-    ).astype(bf16)
-    act_scaled = (act_f * gate).astype(bf16)
+    all_normed = after(all_normed, back)
+    *held, n2_send = run_expert(all_normed, order, slot_of, slot_cap, w_gu, back, gate, 1)
+    n2_sum = Scatter(n2_send, tok_rows)
+    *held, n2_keep = run_expert(all_normed, order, slot_of, slot_cap, w_gu, back, gate, 0, held)
+    n_rows, act, act_scaled, grad_gu, grad_gate_slot = held
     grad_wd = mm_tn(g_rows, act_scaled).astype(bf16)
-    down_got = exchange(grad_wd.reshape(z_count, -1, ffh))
+    grad_wd, n2_sum.got, n2_keep = tie(grad_wd, n2_sum.got, n2_keep)
     hits = jnp.arange(total)[:, None] == order[None, :]
+    grad_gate_slot = grad_gate_slot.reshape(total, 1, slot_cap)
     sent_gates = jnp.sum(
-        jnp.where(slot_of[:, :, None] == slots[None, None, :], grad_gate_slot[:, None, :], 0.0),
-        axis=2,
+        jnp.where(slot_of[:, :, None] == slots[None, None, :], grad_gate_slot, 0.0), axis=2
     )
     sent_gates = jnp.sum(jnp.where(hits[:, :, None], sent_gates[None], 0.0), axis=1)
     got_gates = lax.all_to_all(sent_gates, EVERY, 0, 0, tiled=True)
-    grad_rows = mm_nt(after(grad_gu, grad_wd), w_gu).astype(bf16)
-    grad_rows, got_gates = tie(grad_rows, got_gates)
+    grad_wd, got_gates = tie(grad_wd, got_gates)
     grad_probs = jnp.sum(got_gates.reshape(expert_count, halves, tok_rows), axis=1).T
-    n2_sum = Scatter(put_rows(grad_rows, slot_of, slot_cap, side, side), tok_rows)
-    n2_keep = put_rows(grad_rows, slot_of, slot_cap, 0, side)
-    n_late, gu_late, _ = tie(n_rows, grad_gu, n2_keep)
-    grad_wg = mm_tn(n_late, gu_late[:, :ffh]).astype(bf16)
-    grad_wu = mm_tn(n_late, gu_late[:, ffh:]).astype(bf16)
+    down_got = exchange(grad_wd.reshape(z_count, -1, ffh))
     n2_sum.begin(n2_keep)
-    n2_spread = n2_sum.step()
-    gate_got = exchange(grad_wg.reshape(z_count, -1, ffh), down_got)
-    y_rows = (mm_nt(after(act, n2_sum.got), w_down) * gate).astype(bf16)
-    y_sum = Scatter(put_rows(y_rows, slot_of, slot_cap, side, side), tok_rows)
-    y_keep = put_rows(y_rows, slot_of, slot_cap, 0, side)
-    n2_spread = n2_sum.step(down_got)
+    n2_sum.step()
+    n_late, down_got = tie(n_rows, down_got)
+    grad_wg = mm_tn(n_late, grad_gu[:, :ffh]).astype(bf16)
+    gate_got = exchange(grad_wg.reshape(z_count, -1, ffh))
+    act, n_late = n2_sum.require(act, n_late)
+    act, grad_wg = tie(act, grad_wg)
+    y_sum = Scatter(expert_output(act, gate, w_down, slot_of, slot_cap, 1), tok_rows)
+    y_keep = expert_output(act, gate, w_down, slot_of, slot_cap, 0)
+    n_late, y_keep = tie(n_late, y_keep)
+    grad_wu = mm_tn(n_late, grad_gu[:, ffh:]).astype(bf16)
     while n2_sum.steps_left():
-        n2_spread = n2_sum.step()
+        n2_sum.step()
+    y_sum.begin(y_keep)
+    y_sum.step(n2_sum)
     n2_last = n2_sum.cross(gate_got)
-    y_sum.begin(y_keep, *n2_spread)
-    y_far = y_sum.step()
-    n2_last = tie(n2_last, *y_far)[0]
+    n2_last, grad_wu = y_sum.require(n2_last, grad_wu)
     grad_n2 = jnp.sum(n2_last.astype(f32), axis=0)
     up_got = exchange(grad_wu.reshape(z_count, -1, ffh), n2_last)
 
@@ -553,48 +753,43 @@
 
     pack_dh = context_gather(grad_hidden_b)
     while y_sum.steps_left():
-        y_far = y_sum.step()
-    pack_dh, *_ = tie(pack_dh, *y_far)
-    y_last = y_sum.cross(up_got, pack_dh)
-    output = hidden + jnp.sum(y_last.astype(f32), axis=0)
-    grad_mixed = mm_nt(pack_dh, wo_all).astype(bf16)
-    grad_mixed_h = grad_mixed.reshape(pack_rows, local_heads, head_width)
-    grad_soft = jnp.einsum("qhd,khd->hqk", grad_mixed_h, value, preferred_element_type=f32)
-    delta = jnp.sum(soft * grad_soft, axis=2, keepdims=True)
-    grad_scores = (soft * (grad_soft - delta)).astype(bf16)
-    grad_query = jnp.einsum("hqk,khd->qhd", grad_scores, key, preferred_element_type=f32)
-    grad_key = jnp.einsum("hqk,qhd->khd", grad_scores, query, preferred_element_type=f32)
-    grad_value = jnp.einsum("hqk,qhd->khd", soft_b, grad_mixed_h, preferred_element_type=f32)
-    grad_v = grad_value.reshape(pack_rows, cols).astype(bf16)
-    back_q, back_k = turn_back(grad_query * score_scale), turn_back(grad_key * score_scale)
-    gain_q = jnp.sum(back_q * unit_q, axis=0)
-    gain_k = jnp.sum(back_k * unit_k, axis=0)
-    pull_q, pull_k = back_q * my_gains[0], back_k * my_gains[1]
-    inner = jnp.stack([jnp.sum(raw_q * pull_q, axis=1), jnp.sum(raw_k * pull_k, axis=1)])
-    inner = (lax.psum(inner, "context") / width)[:, :, None]
+        y_sum.step()
+    pull_q, pull_k, grad_v, gain_qk, inner = mix_back(
+        qkv, scale_qk, my_gains, cos_all, sin_all, spots, local_heads, query, key, value, pack_dh, wo_all
+    )
+    def weight_blocks(left, right):
+        return mm_tn(left, right).reshape(e_count, c_count, z_count, w_rows, right.shape[1])
+
+    grad_wo = mm_tn(mixed, pack_dh)
+    if aligned:
+        wo_send = halved(grad_wo.reshape(e_count, z_count, w_rows, width))
+    v_send = halved(weight_blocks(normed_one, grad_v)).transpose(1, 0, 2, 3)
+    (inner,) = y_sum.require(inner)
+    inner = lax.psum(inner.T, "context").T / width
     grad_qkv = jnp.concatenate(
         [
-            scale_qk[0] * pull_q - raw_q * (scale_qk[0] ** 3 * inner[0]),
-            scale_qk[1] * pull_k - raw_k * (scale_qk[1] ** 3 * inner[1]),
-            grad_v,
+            scale_qk[:, 0:1] * pull_q - raw_q * (scale_qk[:, 0:1] ** 3 * inner[:, 0:1]),
+            scale_qk[:, 1:2] * pull_k - raw_k * (scale_qk[:, 1:2] ** 3 * inner[:, 1:2]),
         ],
         axis=1,
     ).astype(bf16)
+    grad_qkv = jnp.concatenate([grad_qkv, grad_v], axis=1)
     grad_experts = join_experts(gate_got, up_got, down_got, halves)
+    qk_blocks = weight_blocks(normed_one, grad_qkv[:, : 2 * cols])
+    grad_qkv, qk_blocks = tie(grad_qkv, qk_blocks)
+    if aligned:
+        grad_qkv, wo_send = tie(grad_qkv, wo_send)
+    grad_qkv, v_send = tie(grad_qkv, v_send)
+    y_last = y_sum.cross(up_got)
+    output = hidden + jnp.sum(y_last.astype(f32), axis=0)
     grad_n1 = context_scatter(mm_nt(grad_qkv, wqkv_all))
     own_scale = lax.rsqrt(jnp.mean(inputs * inputs, axis=-1, keepdims=True) + epsilon)
     gain_one = jnp.sum(grad_n1 * inputs * own_scale, axis=0)
     grad_tokens = grad_hidden + norm_back(inputs, own_scale, gains[0], grad_n1)
 
 
-    def weight_blocks(left, right):
-        blocks = mm_tn(left, right).reshape(e_count, c_count, z_count, w_rows, right.shape[1])
-        return blocks.transpose(0, 2, 1, 3, 4)
-
-    grad_v_sum, v_last = relative_scatter(weight_blocks(normed_one, grad_v), y_last)
-    grad_wo = mm_tn(mixed, pack_dh)
     if aligned:
-        grad_wo, last = relative_scatter(grad_wo.reshape(e_count, z_count, w_rows, width), v_last)
+        grad_wo, last = sum_over_dp(wo_send, y_last)
     else:
         whole_wo = lax.dynamic_update_slice_in_dim(
             jnp.zeros((width, width), f32), grad_wo, me_c * cols, axis=0
@@ -602,8 +797,9 @@
         grad_wo = lax.psum_scatter(
             whole_wo.astype(bf16), EVERY, scatter_dimension=0, tiled=True
         ).astype(f32)
-        last = v_last
-    grad_qk_sum, _ = relative_scatter(weight_blocks(normed_one, grad_qkv[:, : 2 * cols]), last)
+        last = y_last
+    grad_v_sum, last = sum_over_dp(v_send, last)
+    grad_qk_sum, _ = sum_over_dp(halved(qk_blocks).transpose(1, 0, 2, 3), last)
     grad_wqkv = jnp.concatenate([grad_qk_sum, grad_v_sum], axis=2).astype(bf16)
     grad_wqkv = (
         lax.all_to_all(grad_wqkv, "context", 0, 0, tiled=True)
@@ -615,7 +811,7 @@
     grad_attn = jnp.concatenate([grad_wqkv, grad_wo], axis=1)
 
     mine = jnp.arange(c_count)[None, None, :, None] == me_c
-    gain_qk = jnp.where(mine, jnp.stack([gain_q, gain_k]).reshape(2, runs, 1, run_cols), 0.0)
+    gain_qk = jnp.where(mine, gain_qk.reshape(2, runs, 1, run_cols), 0.0)
     gain_rows = jnp.concatenate([jnp.stack([gain_one, gain_two]), gain_qk.reshape(2, width)])
     gain_rows = gain_rows.reshape(4, total, -1).transpose(1, 0, 2).reshape(total, -1)
     small_grads = jnp.concatenate([router_term.reshape(total, -1), gain_rows], axis=1)

time: 1050 us -> 972 us (0.926)
  waiting for transfers between devices: 485 us -> 410 us
  matrix products: 119 us -> 69.2 us
  Pallas kernels: 81.8 us -> 121 us
    pallas_call x4 -> x6, Pallas kernels: 29.8 us -> 83.2 us  [the longest x2 43 us: run_expert(): pl.pallas_call(lambda *refs: expert_kernel(per, slot_cap, *refs), grid_sp...]
    all_gather x1, waiting for transfers between devices: 51 us -> 0.01 us  [on_device(): all_normed = lax.all_gather(normed_two, EVERY, axis=0, tiled=True)]
    dot_general x5 -> x2, matrix products: 35.1 us -> 7.56 us  [mm_nt(): lax.dot_general(a, b, (((1,), (1,)), ((), ())), preferred_element_type=f32)]
    all_to_all x11, waiting for transfers between devices: 170 us -> 149 us  [exchange(): return lax.all_to_all(after(blocks, *done), 'dp', 0, 0, tiled=True)]
    psum x2, blocking collectives: 12.8 us -> 30.5 us  [the longest x1 15.3 us: on_device(): scale_qk = lax.rsqrt(lax.psum(squares, 'context') / width + epsilon).T]
    all_to_all x1 -> x0, blocking collectives: 16.7 us -> none  [on_device(): lax.all_to_all(wqkv, 'context', 0, 0, tiled=True)]
    ppermute x29 -> x30, waiting for transfers between devices: 182 us -> 166 us  [swap(): return lax.ppermute(value, axis, [(i, i ^ bit) for i in range(count)])]
    ppermute x3 -> x6, waiting for transfers between devices: 42.6 us -> 27.3 us  [shift(): lax.ppermute(value, axis, [(i, (i + step) % count) for i in range(count)])]
  transfers between devices with their start and end apart: 51 -> 55, of which waited for: 34 -> 28; matrix products, arithmetic and copies ran while one was open for 22% -> 22% of each run, Pallas kernels for 6% -> 9%
where the time goes in v4:
time: 972 us; the launch traced here: 961 us
  waiting for transfers between devices  410 us (42%)
  Pallas kernels  121 us (12%)
  other arithmetic  120 us (12%)
  starting transfers between devices  113 us (12%)
  local copies, waits for them, and re-layouts  80.4 us (8%)
  matrix products  69.2 us (7%)
  blocking collectives  30.5 us (3%)
  between operations  16.3 us (2%)
    ppermute x30, waiting for transfers between devices, swap(): return lax.ppermute(value, axis, [(i, i ^ bit) for i in range(count)])  166 us
    all_to_all x11, waiting for transfers between devices, exchange(): return lax.all_to_all(after(blocks, *done), 'dp', 0, 0, tiled=True)  149 us
    all_to_all x11, starting transfers between devices, exchange(): return lax.all_to_all(after(blocks, *done), 'dp', 0, 0, tiled=True)  49.9 us
    pallas_call x2, Pallas kernels, run_expert(): pl.pallas_call(lambda *refs: expert_kernel(per, slot_cap, *refs), grid_sp...  43 us
    dot_general x7, matrix products, mm_tn(): lax.dot_general(a, b, (((0,), (0,)), ((), ())), preferred_element_type=f32)  42.1 us
    unnamed x231, local copies, waits for them, and re-layouts  31.6 us
    ppermute x6, waiting for transfers between devices, shift(): lax.ppermute(value, axis, [(i, (i + step) % count) for i in range(count)])  27.3 us
    all_gather x1, waiting for transfers between devices, on_device(): wqkv_all = packed = lax.all_gather(wqkv, around, axis=0, tiled=True)  26.9 us
  transfers between devices with their start and end apart: 55, of which 28 were waited for; matrix products, arithmetic and copies ran while one was open for 22% of the time, Pallas kernels for 9%

profile of v4, /device:TPU:0, one launch (start us, length us, event | category | flops | bytes accessed | tf_op | source)
XLA Modules:
  0.0 960.6 jit_solution(4605611554988360156)
XLA Ops:
  14.2 4.4 all-to-all-start
  21.0 14.5 %collective-permute-done.7 = bf16[128,2048]{1,0:T(8,128)(2,1)S(1)} collective-permute-done((bf16[128,2048]{1,0:T(8,128)(2,1)S(1)}, bf16[128,2048]{1,0:T(8,128)(2,1)S(1)}, u32[]{:S(2)}, u32[]{:S(2)}) %collective-permute-start.7) | collective-permute-done | bytes 524320 | tf_op jit(solution)/shard_map/ppermute | solution.py:37
  43.1 5.2 copy-done.4
  48.3 13.5 %shard_map.136 = (bf16[4,512,512]{2,1,0:T(8,128)(2,1)}, bf16[4,512,512]{2,1,0:T(8,128)(2,1)}, bf16[4,512,512]{2,1,0:T(8,128)(2,1)}) custom-call(f32[512,2,3072]{2,1,0:T(2,128)S(1)} %copy-done.4), custom_call_target="tpu_custom_call" | custom-call | flops 1 | bytes 1 | tf_op jit(solution)/shard_map/pallas_call | solution.py:504
  68.6 12.8 %collective-permute-done.4 = bf16[64,2048]{1,0:T(8,128)(2,1)S(1)} collective-permute-done((bf16[64,2048]{1,0:T(8,128)(2,1)}, bf16[64,2048]{1,0:T(8,128)(2,1)S(1)}, u32[]{:S(2)}, u32[]{:S(2)}) %collective-permute-start.4) | collective-permute-done | bytes 262176 | tf_op jit(solution)/shard_map/ppermute | solution.py:37
  84.9 5.3 all-to-all-start.1
  90.2 21.5 %all-to-all-done.1 = bf16[32,2,704]{2,1,0:T(2,128)(2,1)S(1)} async-done(((bf16[32,2,704]{2,1,0:T(2,128)(2,1)}), bf16[32,2,704]{2,1,0:T(2,128)(2,1)S(1)}, u32[]{:S(2)}, u32[]{:S(2)}) %all-to-all-start.1) | async-done | bytes 90144 | tf_op jit(solution)/shard_map/all_to_all | solution.py:620
  121.5 7.7 collective-permute-start.9
  131.5 4.3 fusion.4
  135.8 26.9 %all-gather.3.cloned.1.call-done = bf16[2048,1536]{1,0:T(8,128)(2,1)} async-done(((bf16[256,1536]{1,0:T(8,128)(2,1)}), bf16[2048,1536]{1,0:T(8,128)(2,1)}) %all-gather.3.cloned.1.call-update) | async-done | bytes 6291472 | tf_op jit(solution)/shard_map/all_gather | solution.py:638
  162.7 4.5 all-to-all-start.2
  171.4 4.2 copy.113
  180.5 15.3 %psum.14 = f32[2,512]{0,1:T(8,128)} all-reduce(f32[2,512]{0,1:T(8,128)} %copy.114), channel_id=1, replica_groups=mesh['expert'=2,'context'=4,'dp'=4] {'context'}, use_global_device_ids=true, to_apply=%region_4.5 | all-reduce | flops 1024 | bytes 8192 | tf_op jit(solution)/shard_map/psum | solution.py:675
  198.7 7.1 shard_map.137
  209.7 6.2 all-to-all-done.2
  227.6 13.7 %collective-permute-done.11 = bf16[128,2048]{1,0:T(8,128)(2,1)} collective-permute-done((bf16[128,2048]{1,0:T(8,128)(2,1)}, bf16[128,2048]{1,0:T(8,128)(2,1)}, u32[]{:S(2)}, u32[]{:S(2)}) %collective-permute-start.11) | collective-permute-done | bytes 524320 | tf_op jit(solution)/shard_map/ppermute | solution.py:32
  249.8 25.9 %collective-permute-done.12 = bf16[1,1,4,128,1024]{4,3,2,1,0:T(8,128)(2,1)S(1)} collective-permute-done((bf16[1,1,4,128,1024]{4,3,2,1,0:T(8,128)(2,1)S(1)}, bf16[1,1,4,128,1024]{4,3,2,1,0:T(8,128)(2,1)S(1)}, u32[]{:S(2)}, u32[]{:S(2)}) %collective-permute-start.12) | collective-permute-done | bytes 1048608 | tf_op jit(solution)/shard_map/ppermute | solution.py:32
  281.0 4.5 all-to-all-start.3
  285.4 44.9 %collective-permute-done.13 = bf16[2,1,4,128,1024]{4,3,2,1,0:T(8,128)(2,1)} collective-permute-done((bf16[2,1,4,128,1024]{4,3,2,1,0:T(8,128)(2,1)}, bf16[2,1,4,128,1024]{4,3,2,1,0:T(8,128)(2,1)}, u32[]{:S(2)}, u32[]{:S(2)}) %collective-permute-start.13) | collective-permute-done | bytes 2097184 | tf_op jit(solution)/shard_map/ppermute | solution.py:32
  333.8 4.0 collective-permute-done.15
  342.0 4.3 all-to-all-done.3
  350.5 7.3 all-to-all-done.5
  357.8 4.0 all-to-all-start.4
  363.3 7.4 shard_map.138
  370.7 8.4 shard_map.139
  379.1 12.6 %fusion.1.refs_11_ = f32[2304,512]{1,0:T(8,128)} fusion(bf16[2048,512]{1,0:T(8,128)(2,1)} %bitcast.125.refs_3_, bf16[1152,2048]{1,0:T(8,128)(2,1)S(1)} %shard_map.139, bf16[1152,2048]{1,0:T(8,128)(2,1)S(1)} %shard_map.138), kind=kOutput, calls=%fused_computation.4 | convolution fusion | flops 4850712576 | bytes 16252928 | tf_op jit(solution)/shard_map/dot_general | solution.py:19
  394.3 43.4 %all-to-all-done.4 = bf16[4,512,512]{2,1,0:T(8,128)(2,1)S(1)} async-done(((bf16[4,512,512]{2,1,0:T(8,128)(2,1)}), bf16[4,512,512]{2,1,0:T(8,128)(2,1)S(1)}, u32[]{:S(2)}, u32[]{:S(2)}) %all-to-all-start.4) | async-done | bytes 2097184 | tf_op jit(solution)/shard_map/all_to_all | solution.py:488
  437.7 4.2 pad_maximum_fusion.5.refs_10_
  441.9 21.5 %shard_map.140 = (bf16[2304,2048]{1,0:T(8,128)(2,1)}, bf16[2304,512]{1,0:T(8,128)(2,1)}, bf16[2304,512]{1,0:T(8,128)(2,1)}, bf16[2304,1024]{1,0:T(8,128)(2,1)}, ...) custom-call(s32[32]{0:T(128)} %stack.310.refs_0_, s32[32,1,128]{2,1,0:T(1,128)} %bitcast.384, ...), custom_call_target="tpu_custom_call" | custom-call | flops 1 | bytes 1 | tf_op jit(solution)/shard_map/pallas_call | solution.py:470
  463.5 21.5 %shard_map.141 = (bf16[2304,2048]{1,0:T(8,128)(2,1)}, bf16[2304,512]{1,0:T(8,128)(2,1)}, bf16[2304,512]{1,0:T(8,128)(2,1)}, bf16[2304,1024]{1,0:T(8,128)(2,1)}, ...) custom-call(s32[32]{0:T(128)} %stack.310.refs_0_, ...), custom_call_target="tpu_custom_call", output_to_operand_aliasing={{0}: (13, {}), {1}: (14, {}), {2}: (15, {}), {3}: (16, {}),... | custom-call | flops 1 | bytes 1 | tf_op jit(solution)/shard_map/pallas_call | solution.py:470
  491.8 9.4 fusion.5
  501.8 5.1 all-to-all-start.7
  506.9 5.8 add_convert_fusion.4
  514.2 5.8 add_convert_fusion.5
  521.5 33.9 %all-to-all-done.7.refs_2_ = bf16[4,512,512]{2,1,0:T(8,128)(2,1)S(1)} async-done(((bf16[4,512,512]{2,1,0:T(8,128)(2,1)}), bf16[4,512,512]{2,1,0:T(8,128)(2,1)S(1)}, u32[]{:S(2)}, u32[]{:S(2)}) %all-to-all-start.7) | async-done | bytes 2097184 | tf_op jit(solution)/shard_map/all_to_all | solution.py:488
  556.9 10.8 %convolution_convert_fusion.1 = bf16[2048,512]{1,0:T(8,128)(2,1)} fusion(bf16[2304,2048]{1,0:T(8,128)(2,1)} %get-tuple-element.115, bf16[2304,1024]{1,0:T(8,128)(2,1)} %get-tuple-element.105), kind=kOutput, calls=%fused_computation.27 | convolution fusion | flops 4832886784 | bytes 13893632 | tf_op jit(solution)/shard_map/dot_general | solution.py:27
  567.7 8.6 shard_map.143
  576.4 4.9 all-to-all-start.8
  588.1 8.7 shard_map.142
  596.8 6.1 add_convert_fusion.1
  604.1 4.9 fusion.10
  617.3 13.1 %all-to-all-done.8.refs_0_ = bf16[4,512,512]{2,1,0:T(8,128)(2,1)} async-done(((bf16[4,512,512]{2,1,0:T(8,128)(2,1)}), bf16[4,512,512]{2,1,0:T(8,128)(2,1)}, u32[]{:S(2)}, u32[]{:S(2)}) %all-to-all-start.8) | async-done | bytes 2097184 | tf_op jit(solution)/shard_map/all_to_all | solution.py:488
  637.2 10.7 %convolution_convert_fusion = bf16[2048,512]{1,0:T(8,128)(2,1)} fusion(bf16[2304,2048]{1,0:T(8,128)(2,1)} %get-tuple-element.115, bf16[2304,1024]{1,0:T(8,128)(2,1)} %get-tuple-element.105), kind=kOutput, calls=%fused_computation.26 | convolution fusion | flops 4832886784 | bytes 13893632 | tf_op jit(solution)/shard_map/dot_general | solution.py:27
  647.9 33.8 %collective-permute-done.24 = bf16[2,4,128,1024]{3,2,1,0:T(8,128)(2,1)} collective-permute-done((bf16[2,4,128,1024]{3,2,1,0:T(8,128)(2,1)}, bf16[2,4,128,1024]{3,2,1,0:T(8,128)(2,1)}, u32[]{:S(2)}, u32[]{:S(2)}) %collective-permute-start.24) | collective-permute-done | bytes 2097184 | tf_op jit(solution)/shard_map/ppermute | solution.py:32
  684.2 5.0 all-to-all-start.10
  693.3 11.4 %collective-permute-done.29 = bf16[128,2048]{1,0:T(8,128)(2,1)S(1)} collective-permute-done((bf16[128,2048]{1,0:T(8,128)(2,1)}, bf16[128,2048]{1,0:T(8,128)(2,1)S(1)}, u32[]{:S(2)}, u32[]{:S(2)}) %collective-permute-start.29) | collective-permute-done | bytes 524320 | tf_op jit(solution)/shard_map/ppermute | solution.py:32
  718.5 15.8 %shard_map.144 = (f32[512,512]{1,0:T(8,128)S(1)}, f32[512,512]{1,0:T(8,128)S(1)}, bf16[512,512]{1,0:T(8,128)(2,1)S(1)}, f32[2,512]{1,0:T(2,128)S(1)}, f32[512,2]{1,0:T(8,128)S(1)}) custom-call(f32[512,1536]{1,0:T(8,128)} %copy-done, f32[512,1536]{1,0:T(8,128)} %copy-done, f32[512,2]{1,0:T(8,128)S(1)} %copy-done.10, f32[2,512]{1,0:T(2,128)S(1)} %bitcast.391, ...), custom_call_target="tpu_custom_call" | custom-call | flops 1 | bytes 1 | tf_op jit(solution)/shard_map/pallas_call | solution.py:404
  743.9 4.8 all-to-all-start.11
  760.6 15.2 %psum.15 = f32[2,512]{0,1:T(8,128)} all-reduce(f32[2,512]{0,1:T(8,128)} %bitcast.389), channel_id=1, replica_groups=mesh['expert'=2,'context'=4,'dp'=4] {'context'}, use_global_device_ids=true, to_apply=%region_21.22 | all-reduce | flops 1024 | bytes 8192 | tf_op jit(solution)/shard_map/psum | solution.py:768
  780.7 5.8 fusion.49
  786.5 13.1 %collective-permute-done.31 = bf16[1,4,64,2048]{3,2,1,0:T(8,128)(2,1)} collective-permute-done((bf16[1,4,64,2048]{3,2,1,0:T(8,128)(2,1)}, bf16[1,4,64,2048]{3,2,1,0:T(8,128)(2,1)}, u32[]{:S(2)}, u32[]{:S(2)}) %collective-permute-start.31) | collective-permute-done | bytes 1048608 | tf_op jit(solution)/shard_map/ppermute | solution.py:32
  804.6 4.8 all-to-all-start.12
  809.4 5.6 fusion.100
  815.2 5.1 dynamic-slice_convert_fusion
  822.1 11.0 %all-to-all-done.12 = bf16[4,64,2048]{2,1,0:T(8,128)(2,1)S(1)} async-done(((bf16[4,64,2048]{2,1,0:T(8,128)(2,1)}), bf16[4,64,2048]{2,1,0:T(8,128)(2,1)S(1)}, u32[]{:S(2)}, u32[]{:S(2)}) %all-to-all-start.12) | async-done | bytes 1048608 | tf_op jit(solution)/shard_map/all_to_all | solution.py:488
  833.0 4.3 all-to-all-start.13
  844.8 8.8 collective-permute-done.34
  856.2 6.4 all-to-all-done.13
  867.4 4.9 fusion.12
  874.8 4.5 all-to-all-start.14
  880.9 8.3 shard_map.145
  896.6 30.8 %all-to-all-done.14 = bf16[4,4,64,1024]{3,2,1,0:T(8,128)(2,1)} async-done(((bf16[4,4,64,1024]{3,2,1,0:T(8,128)(2,1)}), bf16[4,4,64,1024]{3,2,1,0:T(8,128)(2,1)}, u32[]{:S(2)}, u32[]{:S(2)}) %all-to-all-start.14) | async-done | bytes 2097184 | tf_op jit(solution)/shard_map/all_to_all | solution.py:488
  930.4 4.6 all-to-all-start.15
  937.1 9.6 %all-to-all-done.15 = bf16[4,64,1536]{2,1,0:T(8,128)(2,1)} async-done(((bf16[4,64,1536]{2,1,0:T(8,128)(2,1)}), bf16[4,64,1536]{2,1,0:T(8,128)(2,1)}, u32[]{:S(2)}, u32[]{:S(2)}) %all-to-all-start.15) | async-done | bytes 786464 | tf_op jit(solution)/shard_map/all_to_all | solution.py:805
  (472 shorter events, 222.3 us)
Async XLA Ops:
  8.9 29.4 %copy-start.63 = (bf16[64,8192]{1,0:T(8,128)(2,1)}, bf16[64,8192]{1,0:T(8,128)(2,1)S(1)}, u32[]{:S(2)}) copy-start(bf16[64,8192]{1,0:T(8,128)(2,1)S(1)} %convert.33) | copy-start | bytes 3145732
  14.2 25.4 %copy-start.111 = (s32[1,8]{1,0:T(1,128)S(1)}, s32[1,8]{1,0:T(1,128)}, u32[]{:S(2)}) copy-start(s32[1,8]{1,0:T(1,128)} %param.16) | copy-start | bytes 100
  14.2 21.4 %all-to-all-start = ((bf16[4,64,1536]{2,1,0:T(8,128)(2,1)}), bf16[4,64,1536]{2,1,0:T(8,128)(2,1)S(1)}, u32[]{:S(2)}, u32[]{:S(2)}) async-start(bf16[4,64,1536]{2,1,0:T(8,128)(2,1)} %reshape.1706), calls=%async_computation | async-start | bytes 1572864 | tf_op jit(solution)/shard_map/all_to_all | solution.py:618
  18.5 144.1 %all-gather.3.cloned.1.call-start = ((), (), s32[]{:S(2)}) async-start(), calls=%async_computation.17 | async-start | bytes 7077888 | tf_op jit(solution)/shard_map/all_gather | solution.py:638
  18.6 17.0 %collective-permute-start.7 = (bf16[128,2048]{1,0:T(8,128)(2,1)S(1)}, bf16[128,2048]{1,0:T(8,128)(2,1)S(1)}, u32[]{:S(2)}, u32[]{:S(2)}) collective-permute-start(bf16[128,2048]{1,0:T(8,128)(2,1)S(1)} %bitcast_convert_fusion.2), channel_id=1, source_target_pairs={{0,1},{1,2},{2,3},{3,0},{4,5},{5,6},{6,7},{7,4},{8,9},{9,10},{10,1... | collective-permute-start | bytes 1572872 | tf_op jit(solution)/shard_map/ppermute | solution.py:37
  36.5 44.9 %collective-permute-start.1 = (bf16[128,2048]{1,0:T(8,128)(2,1)S(1)}, bf16[128,2048]{1,0:T(8,128)(2,1)}, u32[]{:S(2)}, u32[]{:S(2)}) collective-permute-start(bf16[128,2048]{1,0:T(8,128)(2,1)S(1)} %bitcast.419), channel_id=1, source_target_pairs={{0,8},{4,12},{8,0},{12,4},{1,9},{5,13},{9,1},{13,5},{2,10},{6,14},... | collective-permute-start | bytes 1572872 | tf_op jit(solution)/shard_map/ppermute | solution.py:32
  38.3 90.9 %collective-permute-start = (bf16[128,2048]{1,0:T(8,128)(2,1)S(1)}, bf16[128,2048]{1,0:T(8,128)(2,1)}, u32[]{:S(2)}, u32[]{:S(2)}) collective-permute-start(bf16[128,2048]{1,0:T(8,128)(2,1)S(1)} %bitcast.420), channel_id=1, source_target_pairs={{0,4},{4,0},{8,12},{12,8},{1,5},{5,1},{9,13},{13,9},{2,6},{6,2},{1... | collective-permute-start | bytes 1572872 | tf_op jit(solution)/shard_map/ppermute | solution.py:32
  39.1 25.5 %collective-permute-start.3 = (bf16[64,2048]{1,0:T(8,128)(2,1)}, bf16[64,2048]{1,0:T(8,128)(2,1)}, u32[]{:S(2)}, u32[]{:S(2)}) collective-permute-start(bf16[64,2048]{1,0:T(8,128)(2,1)} %get-tuple-element.207), channel_id=1, source_target_pairs={{0,1},{1,2},{2,3},{3,0},{4,5},{5,6},{6,7},{7,4},{8,9},{9,10},{10,1... | collective-permute-start | bytes 786440 | tf_op jit(solution)/shard_map/ppermute | solution.py:37
  63.7 133.1 %copy-start.13 = (f32[512,128]{1,0:T(8,128)}, f32[512,128]{1,0:T(8,128)S(1)}, u32[]{:S(2)}) copy-start(f32[512,128]{1,0:T(8,128)S(1)} %get-tuple-element.231.refs_5_.refs_4_) | copy-start | bytes 786436
  63.7 54.2 %copy-start.84 = (bf16[1,64,2048]{2,1,0:T(8,128)(2,1)S(1)}, bf16[1,64,2048]{2,1,0:T(8,128)(2,1)}, u32[]{:S(2)}) copy-start(bf16[1,64,2048]{2,1,0:T(8,128)(2,1)} %get-tuple-element.206) | copy-start | bytes 786436
  63.7 133.1 %copy-start.35 = (s32[2,512]{1,0:T(2,128)}, s32[2,512]{1,0:T(2,128)S(1)}, u32[]{:S(2)}) copy-start(s32[2,512]{1,0:T(2,128)S(1)} %get-tuple-element.221.refs_8_.refs_7_) | copy-start | bytes 12292
  64.6 16.8 %collective-permute-start.4 = (bf16[64,2048]{1,0:T(8,128)(2,1)}, bf16[64,2048]{1,0:T(8,128)(2,1)S(1)}, u32[]{:S(2)}, u32[]{:S(2)}) collective-permute-start(bf16[64,2048]{1,0:T(8,128)(2,1)} %collective-permute-done.3), channel_id=1, source_target_pairs={{0,1},{1,2},{2,3},{3,0},{4,5},{5,6},{6,7},{7,4},{8,9},{9,10},{10,1... | collective-permute-start | bytes 786440 | tf_op jit(solution)/shard_map/ppermute | solution.py:37
  67.0 54.4 %collective-permute-start.8 = (bf16[128,2048]{1,0:T(8,128)(2,1)}, bf16[128,2048]{1,0:T(8,128)(2,1)}, u32[]{:S(2)}, u32[]{:S(2)}) collective-permute-start(bf16[128,2048]{1,0:T(8,128)(2,1)} %copy-done.85), channel_id=1, source_target_pairs={{0,1},{1,2},{2,3},{3,0},{4,5},{5,6},{6,7},{7,4},{8,9},{9,10},{10,1... | collective-permute-start | bytes 1572872 | tf_op jit(solution)/shard_map/ppermute | solution.py:37
  81.4 36.5 %collective-permute-start.5 = (bf16[64,2048]{1,0:T(8,128)(2,1)S(1)}, bf16[64,2048]{1,0:T(8,128)(2,1)}, u32[]{:S(2)}, u32[]{:S(2)}) collective-permute-start(bf16[64,2048]{1,0:T(8,128)(2,1)S(1)} %collective-permute-done.4), channel_id=1, source_target_pairs={{0,1},{1,2},{2,3},{3,0},{4,5},{5,6},{6,7},{7,4},{8,9},{9,10},{10,1... | collective-permute-start | bytes 786440 | tf_op jit(solution)/shard_map/ppermute | solution.py:37
  81.4 47.8 %collective-permute-start.2 = (bf16[128,2048]{1,0:T(8,128)(2,1)}, bf16[128,2048]{1,0:T(8,128)(2,1)}, u32[]{:S(2)}, u32[]{:S(2)}) collective-permute-start(bf16[128,2048]{1,0:T(8,128)(2,1)} %collective-permute-done.1), channel_id=1, source_target_pairs={{0,4},{4,0},{8,12},{12,8},{1,5},{5,1},{9,13},{13,9},{2,6},{6,2},{1... | collective-permute-start | bytes 1572872 | tf_op jit(solution)/shard_map/ppermute | solution.py:32
  84.9 26.8 %all-to-all-start.1 = ((bf16[32,2,704]{2,1,0:T(2,128)(2,1)}), bf16[32,2,704]{2,1,0:T(2,128)(2,1)S(1)}, u32[]{:S(2)}, u32[]{:S(2)}) async-start(bf16[32,2,704]{2,1,0:T(2,128)(2,1)} %reshape.1782), calls=%async_computation.1 | async-start | bytes 196608 | tf_op jit(solution)/shard_map/all_to_all | solution.py:620
  117.9 78.9 %copy-start.37 = (f32[1,2,2,256]{3,1,2,0:T(2,128)}, f32[1,2,2,256]{3,1,2,0:T(2,128)S(1)}, u32[]{:S(2)}) copy-start(f32[1,2,2,256]{3,1,2,0:T(2,128)S(1)} %copy.140) | copy-start | bytes 12292
  120.0 47.4 %collective-permute-start.6 = (bf16[4,64,2048]{2,1,0:T(8,128)(2,1)}, bf16[4,64,2048]{2,1,0:T(8,128)(2,1)}, u32[]{:S(2)}, u32[]{:S(2)}) collective-permute-start(bf16[4,64,2048]{2,1,0:T(8,128)(2,1)} %pad_maximum_fusion.16), channel_id=1, source_target_pairs={{0,16},{16,0},{1,17},{17,1},{2,18},{18,2},{3,19},{19,3},{4,20},{20... | collective-permute-start | bytes 3145736 | tf_op jit(solution)/shard_map/ppermute | solution.py:32
  121.5 49.9 %collective-permute-start.9 = (bf16[128,2048]{1,0:T(8,128)(2,1)}, bf16[128,2048]{1,0:T(8,128)(2,1)}, u32[]{:S(2)}, u32[]{:S(2)}) collective-permute-start(bf16[128,2048]{1,0:T(8,128)(2,1)} %collective-permute-done.8), channel_id=1, source_target_pairs={{0,1},{1,2},{2,3},{3,0},{4,5},{5,6},{6,7},{7,4},{8,9},{9,10},{10,1... | collective-permute-start | bytes 1572872 | tf_op jit(solution)/shard_map/ppermute | solution.py:37
  162.7 53.2 %all-to-all-start.2 = ((bf16[4,512,512]{2,1,0:T(8,128)(2,1)}), bf16[4,512,512]{2,1,0:T(8,128)(2,1)}, u32[]{:S(2)}, u32[]{:S(2)}) async-start(bf16[4,512,512]{2,1,0:T(8,128)(2,1)} %get-tuple-element.81), calls=%async_computation.2 | async-start | bytes 4194304 | tf_op jit(solution)/shard_map/all_to_all | solution.py:488
  167.1 274.8 %all-gather.5.cloned.1.call-start = ((), (), s32[]{:S(2)}) async-start(), calls=%async_computation.18 | async-start | bytes 17301504 | tf_op jit(solution)/shard_map/all_gather | solution.py:684
  179.1 26.7 %copy-start = (f32[512,1536]{1,0:T(8,128)}, f32[512,1536]{1,0:T(8,128)S(1)}, u32[]{:S(2)}) copy-start(f32[512,1536]{1,0:T(8,128)S(1)} %fusion.97.refs_0_.refs_1_.refs_2_) | copy-start | bytes 9437188
  221.1 2.9 collective-permute-start.10
  227.0 14.3 %collective-permute-start.11 = (bf16[128,2048]{1,0:T(8,128)(2,1)}, bf16[128,2048]{1,0:T(8,128)(2,1)}, u32[]{:S(2)}, u32[]{:S(2)}) collective-permute-start(bf16[128,2048]{1,0:T(8,128)(2,1)} %fusion.53), channel_id=1, source_target_pairs={{0,8},{4,12},{8,0},{12,4},{1,9},{5,13},{9,1},{13,5},{2,10},{6,14},... | collective-permute-start | bytes 1572872 | tf_op jit(solution)/shard_map/ppermute | solution.py:32
  247.5 28.2 %collective-permute-start.12 = (bf16[1,1,4,128,1024]{4,3,2,1,0:T(8,128)(2,1)S(1)}, bf16[1,1,4,128,1024]{4,3,2,1,0:T(8,128)(2,1)S(1)}, u32[]{:S(2)}, u32[]{:S(2)}) collective-permute-start(bf16[1,1,4,128,1024]{4,3,2,1,0:T(8,128)(2,1)S(1)} %maximum_bitcast_fusion), channel_id=1, source_target_pairs={{0,8},{4,12},{8,0},{12,4},{1,9},{5,13},{9,1},{13,5},{2,10},{6,14},... | collective-permute-start | bytes 3145736 | tf_op jit(solution)/shard_map/ppermute | solution.py:32
  248.3 30.5 %collective-permute-start.14 = (bf16[1,1,4,128,1024]{4,3,2,1,0:T(8,128)(2,1)S(1)}, bf16[1,1,4,128,1024]{4,3,2,1,0:T(8,128)(2,1)S(1)}, u32[]{:S(2)}, u32[]{:S(2)}) collective-permute-start(bf16[1,1,4,128,1024]{4,3,2,1,0:T(8,128)(2,1)S(1)} %maximum_bitcast_fusion.1), channel_id=1, source_target_pairs={{0,16},{16,0},{1,17},{17,1},{2,18},{18,2},{3,19},{19,3},{4,20},{20... | collective-permute-start | bytes 3145736 | tf_op jit(solution)/shard_map/ppermute | solution.py:32
  277.2 53.1 %collective-permute-start.13 = (bf16[2,1,4,128,1024]{4,3,2,1,0:T(8,128)(2,1)}, bf16[2,1,4,128,1024]{4,3,2,1,0:T(8,128)(2,1)}, u32[]{:S(2)}, u32[]{:S(2)}) collective-permute-start(bf16[2,1,4,128,1024]{4,3,2,1,0:T(8,128)(2,1)} %pad_maximum_fusion.9), channel_id=1, source_target_pairs={{0,16},{16,0},{1,17},{17,1},{2,18},{18,2},{3,19},{19,3},{4,20},{20... | collective-permute-start | bytes 6291464 | tf_op jit(solution)/shard_map/ppermute | solution.py:32
  280.5 57.3 %collective-permute-start.15 = (bf16[1,2,4,128,1024]{4,3,2,1,0:T(8,128)(2,1)}, bf16[1,2,4,128,1024]{4,3,2,1,0:T(8,128)(2,1)}, u32[]{:S(2)}, u32[]{:S(2)}) collective-permute-start(bf16[1,2,4,128,1024]{4,3,2,1,0:T(8,128)(2,1)} %pad_maximum_fusion.10), channel_id=1, source_target_pairs={{0,8},{4,12},{8,0},{12,4},{1,9},{5,13},{9,1},{13,5},{2,10},{6,14},... | collective-permute-start | bytes 6291464 | tf_op jit(solution)/shard_map/ppermute | solution.py:32
  281.0 65.3 %all-to-all-start.3 = ((bf16[4,512,512]{2,1,0:T(8,128)(2,1)}), bf16[4,512,512]{2,1,0:T(8,128)(2,1)}, u32[]{:S(2)}, u32[]{:S(2)}) async-start(bf16[4,512,512]{2,1,0:T(8,128)(2,1)} %get-tuple-element.84), calls=%async_computation.3 | async-start | bytes 4194304 | tf_op jit(solution)/shard_map/all_to_all | solution.py:488
  285.4 52.3 %copy-start.71 = (bf16[1,1,4,128,1024]{4,3,2,1,0:T(8,128)(2,1)S(1)}, bf16[1,1,4,128,1024]{4,3,2,1,0:T(8,128)(2,1)}, u32[]{:S(2)}) copy-start(bf16[1,1,4,128,1024]{4,3,2,1,0:T(8,128)(2,1)} %copy-done.70) | copy-start | bytes 3145732
  333.8 36.9 %collective-permute-start.16 = (bf16[2,2,4,128,1024]{4,3,2,1,0:T(8,128)(2,1)}, bf16[2,2,4,128,1024]{4,3,2,1,0:T(8,128)(2,1)}, u32[]{:S(2)}, u32[]{:S(2)}) collective-permute-start(bf16[2,2,4,128,1024]{4,3,2,1,0:T(8,128)(2,1)} %pad_maximum_fusion.3), channel_id=1, source_target_pairs={{0,4},{4,0},{8,12},{12,8},{1,5},{5,1},{9,13},{13,9},{2,6},{6,2},{1... | collective-permute-start | bytes 12582920 | tf_op jit(solution)/shard_map/ppermute | solution.py:32
  341.2 29.5 %collective-permute-start.17 = (bf16[2,2,4,128,1024]{4,3,2,1,0:T(8,128)(2,1)}, bf16[2,2,4,128,1024]{4,3,2,1,0:T(8,128)(2,1)}, u32[]{:S(2)}, u32[]{:S(2)}) collective-permute-start(bf16[2,2,4,128,1024]{4,3,2,1,0:T(8,128)(2,1)} %pad_maximum_fusion.4), channel_id=1, source_target_pairs={{0,4},{4,0},{8,12},{12,8},{1,5},{5,1},{9,13},{13,9},{2,6},{6,2},{1... | collective-permute-start | bytes 12582920 | tf_op jit(solution)/shard_map/ppermute | solution.py:32
  346.9 10.9 %all-to-all-start.5 = ((f32[32,1,128]{2,1,0:T(1,128)}), f32[32,1,128]{2,1,0:T(1,128)S(1)}, u32[]{:S(2)}, u32[]{:S(2)}) async-start(f32[32,1,128]{2,1,0:T(1,128)} %bitcast.129), calls=%async_computation.5 | async-start | bytes 32768 | tf_op jit(solution)/shard_map/all_to_all | solution.py:686
  357.8 79.9 %all-to-all-start.4 = ((bf16[4,512,512]{2,1,0:T(8,128)(2,1)}), bf16[4,512,512]{2,1,0:T(8,128)(2,1)S(1)}, u32[]{:S(2)}, u32[]{:S(2)}) async-start(bf16[4,512,512]{2,1,0:T(8,128)(2,1)} %get-tuple-element.86), calls=%async_computation.4 | async-start | bytes 4194304 | tf_op jit(solution)/shard_map/all_to_all | solution.py:488
  363.2 29.0 %copy-start.21 = (s32[32,128]{1,0:T(8,128)}, s32[32,128]{1,0:T(8,128)S(1)}, u32[]{:S(2)}) copy-start(s32[32,128]{1,0:T(8,128)S(1)} %gather_fusion) | copy-start | bytes 49156
  463.4 37.8 %collective-permute-start.18 = (bf16[16,128,2048]{2,1,0:T(8,128)(2,1)}, bf16[16,128,2048]{2,1,0:T(8,128)(2,1)}, u32[]{:S(2)}, u32[]{:S(2)}) collective-permute-start(bf16[16,128,2048]{2,1,0:T(8,128)(2,1)} %get-tuple-element.93), channel_id=1, source_target_pairs={{0,4},{4,0},{8,12},{12,8},{1,5},{5,1},{9,13},{13,9},{2,6},{6,2},{1... | collective-permute-start | bytes 25165832 | tf_op jit(solution)/shard_map/ppermute | solution.py:32
  488.0 13.1 %all-to-all-start.6 = ((f32[32,1,128]{2,1,0:T(1,128)}), f32[32,1,128]{2,1,0:T(1,128)S(1)}, u32[]{:S(2)}, u32[]{:S(2)}) async-start(f32[32,1,128]{2,1,0:T(1,128)} %bitcast.136), calls=%async_computation.6 | async-start | bytes 32768 | tf_op jit(solution)/shard_map/all_to_all | solution.py:715
  501.8 53.6 %all-to-all-start.7 = ((bf16[4,512,512]{2,1,0:T(8,128)(2,1)}), bf16[4,512,512]{2,1,0:T(8,128)(2,1)S(1)}, u32[]{:S(2)}, u32[]{:S(2)}) async-start(bf16[4,512,512]{2,1,0:T(8,128)(2,1)} %bitcast.433), calls=%async_computation.7 | async-start | bytes 4194304 | tf_op jit(solution)/shard_map/all_to_all | solution.py:488
  512.7 55.0 %collective-permute-start.20 = (bf16[2,4,128,1024]{3,2,1,0:T(8,128)(2,1)}, bf16[2,4,128,1024]{3,2,1,0:T(8,128)(2,1)}, u32[]{:S(2)}, u32[]{:S(2)}) collective-permute-start(bf16[2,4,128,1024]{3,2,1,0:T(8,128)(2,1)} %get-tuple-element.193), channel_id=1, source_target_pairs={{0,16},{16,0},{1,17},{17,1},{2,18},{18,2},{3,19},{19,3},{4,20},{20... | collective-permute-start | bytes 6291464 | tf_op jit(solution)/shard_map/ppermute | solution.py:32
  520.0 47.7 %collective-permute-start.19 = (bf16[2,4,128,1024]{3,2,1,0:T(8,128)(2,1)}, bf16[2,4,128,1024]{3,2,1,0:T(8,128)(2,1)}, u32[]{:S(2)}, u32[]{:S(2)}) collective-permute-start(bf16[2,4,128,1024]{3,2,1,0:T(8,128)(2,1)} %get-tuple-element.195), channel_id=1, source_target_pairs={{0,8},{4,12},{8,0},{12,4},{1,9},{5,13},{9,1},{13,5},{2,10},{6,14},... | collective-permute-start | bytes 6291464 | tf_op jit(solution)/shard_map/ppermute | solution.py:32
  576.4 20.4 %collective-permute-start.21 = (bf16[16,128,2048]{2,1,0:T(8,128)(2,1)}, bf16[16,128,2048]{2,1,0:T(8,128)(2,1)}, u32[]{:S(2)}, u32[]{:S(2)}) collective-permute-start(bf16[16,128,2048]{2,1,0:T(8,128)(2,1)} %shard_map.143), channel_id=1, source_target_pairs={{0,4},{4,0},{8,12},{12,8},{1,5},{5,1},{9,13},{13,9},{2,6},{6,2},{1... | collective-permute-start | bytes 25165832 | tf_op jit(solution)/shard_map/ppermute | solution.py:32
  576.4 54.1 %all-to-all-start.8 = ((bf16[4,512,512]{2,1,0:T(8,128)(2,1)}), bf16[4,512,512]{2,1,0:T(8,128)(2,1)}, u32[]{:S(2)}, u32[]{:S(2)}) async-start(bf16[4,512,512]{2,1,0:T(8,128)(2,1)} %bitcast.432), calls=%async_computation.8 | async-start | bytes 4194304 | tf_op jit(solution)/shard_map/all_to_all | solution.py:488
  583.4 25.6 %collective-permute-start.23 = (bf16[4,128,1024]{2,1,0:T(8,128)(2,1)S(1)}, bf16[4,128,1024]{2,1,0:T(8,128)(2,1)S(1)}, u32[]{:S(2)}, u32[]{:S(2)}) collective-permute-start(bf16[4,128,1024]{2,1,0:T(8,128)(2,1)S(1)} %fusion.40), channel_id=1, source_target_pairs={{0,8},{4,12},{8,0},{12,4},{1,9},{5,13},{9,1},{13,5},{2,10},{6,14},... | collective-permute-start | bytes 3145736 | tf_op jit(solution)/shard_map/ppermute | solution.py:32
  586.6 25.3 %collective-permute-start.22 = (bf16[4,128,1024]{2,1,0:T(8,128)(2,1)S(1)}, bf16[4,128,1024]{2,1,0:T(8,128)(2,1)S(1)}, u32[]{:S(2)}, u32[]{:S(2)}) collective-permute-start(bf16[4,128,1024]{2,1,0:T(8,128)(2,1)S(1)} %fusion.39), channel_id=1, source_target_pairs={{0,16},{16,0},{1,17},{17,1},{2,18},{18,2},{3,19},{19,3},{4,20},{20... | collective-permute-start | bytes 3145736 | tf_op jit(solution)/shard_map/ppermute | solution.py:32
  630.5 52.4 %all-to-all-start.9 = ((bf16[4,128,2048]{2,1,0:T(8,128)(2,1)}), bf16[4,128,2048]{2,1,0:T(8,128)(2,1)S(1)}, u32[]{:S(2)}, u32[]{:S(2)}) async-start(bf16[4,128,2048]{2,1,0:T(8,128)(2,1)} %pad_maximum_fusion.11), calls=%async_computation.9 | async-start | bytes 4194304 | tf_op jit(solution)/shard_map/all_to_all | solution.py:488
  634.1 47.6 %collective-permute-start.24 = (bf16[2,4,128,1024]{3,2,1,0:T(8,128)(2,1)}, bf16[2,4,128,1024]{3,2,1,0:T(8,128)(2,1)}, u32[]{:S(2)}, u32[]{:S(2)}) collective-permute-start(bf16[2,4,128,1024]{3,2,1,0:T(8,128)(2,1)} %get-tuple-element.110), channel_id=1, source_target_pairs={{0,8},{4,12},{8,0},{12,4},{1,9},{5,13},{9,1},{13,5},{2,10},{6,14},... | collective-permute-start | bytes 6291464 | tf_op jit(solution)/shard_map/ppermute | solution.py:32
  635.6 47.2 %collective-permute-start.25 = (bf16[2,4,128,1024]{3,2,1,0:T(8,128)(2,1)}, bf16[2,4,128,1024]{3,2,1,0:T(8,128)(2,1)}, u32[]{:S(2)}, u32[]{:S(2)}) collective-permute-start(bf16[2,4,128,1024]{3,2,1,0:T(8,128)(2,1)} %get-tuple-element.111), channel_id=1, source_target_pairs={{0,16},{16,0},{1,17},{17,1},{2,18},{18,2},{3,19},{19,3},{4,20},{20... | collective-permute-start | bytes 6291464 | tf_op jit(solution)/shard_map/ppermute | solution.py:32
  684.2 58.4 %all-to-all-start.10 = ((bf16[4,512,512]{2,1,0:T(8,128)(2,1)}), bf16[4,512,512]{2,1,0:T(8,128)(2,1)S(1)}, u32[]{:S(2)}, u32[]{:S(2)}) async-start(bf16[4,512,512]{2,1,0:T(8,128)(2,1)} %bitcast.431), calls=%async_computation.10 | async-start | bytes 4194304 | tf_op jit(solution)/shard_map/all_to_all | solution.py:488
  692.7 11.9 %collective-permute-start.29 = (bf16[128,2048]{1,0:T(8,128)(2,1)}, bf16[128,2048]{1,0:T(8,128)(2,1)S(1)}, u32[]{:S(2)}, u32[]{:S(2)}) collective-permute-start(bf16[128,2048]{1,0:T(8,128)(2,1)} %get-tuple-element.184), channel_id=1, source_target_pairs={{0,8},{4,12},{8,0},{12,4},{1,9},{5,13},{9,1},{13,5},{2,10},{6,14},... | collective-permute-start | bytes 1572872 | tf_op jit(solution)/shard_map/ppermute | solution.py:32
  693.3 19.4 %collective-permute-start.28 = (bf16[128,2048]{1,0:T(8,128)(2,1)}, bf16[128,2048]{1,0:T(8,128)(2,1)S(1)}, u32[]{:S(2)}, u32[]{:S(2)}) collective-permute-start(bf16[128,2048]{1,0:T(8,128)(2,1)} %get-tuple-element.184), channel_id=1, source_target_pairs={{0,4},{4,0},{8,12},{12,8},{1,5},{5,1},{9,13},{13,9},{2,6},{6,2},{1... | collective-permute-start | bytes 1572872 | tf_op jit(solution)/shard_map/ppermute | solution.py:32
  704.7 8.8 collective-permute-start.30
  707.5 26.9 %collective-permute-start.27 = (bf16[4,128,1024]{2,1,0:T(8,128)(2,1)}, bf16[4,128,1024]{2,1,0:T(8,128)(2,1)}, u32[]{:S(2)}, u32[]{:S(2)}) collective-permute-start(bf16[4,128,1024]{2,1,0:T(8,128)(2,1)} %fusion.44), channel_id=1, source_target_pairs={{0,8},{4,12},{8,0},{12,4},{1,9},{5,13},{9,1},{13,5},{2,10},{6,14},... | collective-permute-start | bytes 3145736 | tf_op jit(solution)/shard_map/ppermute | solution.py:32
  711.1 25.4 %collective-permute-start.26 = (bf16[4,128,1024]{2,1,0:T(8,128)(2,1)}, bf16[4,128,1024]{2,1,0:T(8,128)(2,1)}, u32[]{:S(2)}, u32[]{:S(2)}) collective-permute-start(bf16[4,128,1024]{2,1,0:T(8,128)(2,1)} %fusion.43), channel_id=1, source_target_pairs={{0,16},{16,0},{1,17},{17,1},{2,18},{18,2},{3,19},{19,3},{4,20},{20... | collective-permute-start | bytes 3145736 | tf_op jit(solution)/shard_map/ppermute | solution.py:32
  743.9 60.7 %all-to-all-start.11 = ((bf16[4,128,2048]{2,1,0:T(8,128)(2,1)}), bf16[4,128,2048]{2,1,0:T(8,128)(2,1)}, u32[]{:S(2)}, u32[]{:S(2)}) async-start(bf16[4,128,2048]{2,1,0:T(8,128)(2,1)} %pad_maximum_fusion.13), calls=%async_computation.11 | async-start | bytes 4194304 | tf_op jit(solution)/shard_map/all_to_all | solution.py:488
  752.8 49.3 %collective-permute-start.32 = (bf16[1,4,4,64,512]{4,3,1,2,0:T(8,128)(2,1)}, bf16[1,4,4,64,512]{4,3,1,2,0:T(8,128)(2,1)}, u32[]{:S(2)}, u32[]{:S(2)}) collective-permute-start(bf16[1,4,4,64,512]{4,3,1,2,0:T(8,128)(2,1)} %fusion.46), channel_id=1, source_target_pairs={{0,16},{16,0},{1,17},{17,1},{2,18},{18,2},{3,19},{19,3},{4,20},{20... | collective-permute-start | bytes 3145736 | tf_op jit(solution)/shard_map/ppermute | solution.py:32
  759.0 40.5 %collective-permute-start.31 = (bf16[1,4,64,2048]{3,2,1,0:T(8,128)(2,1)}, bf16[1,4,64,2048]{3,2,1,0:T(8,128)(2,1)}, u32[]{:S(2)}, u32[]{:S(2)}) collective-permute-start(bf16[1,4,64,2048]{3,2,1,0:T(8,128)(2,1)} %fusion.35), channel_id=1, source_target_pairs={{0,16},{16,0},{1,17},{17,1},{2,18},{18,2},{3,19},{19,3},{4,20},{20... | collective-permute-start | bytes 3145736 | tf_op jit(solution)/shard_map/ppermute | solution.py:32
  804.6 28.4 %all-to-all-start.12 = ((bf16[4,64,2048]{2,1,0:T(8,128)(2,1)}), bf16[4,64,2048]{2,1,0:T(8,128)(2,1)S(1)}, u32[]{:S(2)}, u32[]{:S(2)}) async-start(bf16[4,64,2048]{2,1,0:T(8,128)(2,1)} %fusion.36), calls=%async_computation.12 | async-start | bytes 2097152 | tf_op jit(solution)/shard_map/all_to_all | solution.py:488
  815.2 22.2 %collective-permute-start.33 = (bf16[2,128,2048]{2,1,0:T(8,128)(2,1)S(1)}, bf16[2,128,2048]{2,1,0:T(8,128)(2,1)}, u32[]{:S(2)}, u32[]{:S(2)}) collective-permute-start(bf16[2,128,2048]{2,1,0:T(8,128)(2,1)S(1)} %fusion.48), channel_id=1, source_target_pairs={{0,4},{4,0},{8,12},{12,8},{1,5},{5,1},{9,13},{13,9},{2,6},{6,2},{1... | collective-permute-start | bytes 3145736 | tf_op jit(solution)/shard_map/ppermute | solution.py:32
  820.3 47.1 %collective-permute-start.35 = (bf16[1,4,4,64,1024]{4,3,1,2,0:T(8,128)(2,1)}, bf16[1,4,4,64,1024]{4,3,1,2,0:T(8,128)(2,1)}, u32[]{:S(2)}, u32[]{:S(2)}) collective-permute-start(bf16[1,4,4,64,1024]{4,3,1,2,0:T(8,128)(2,1)} %dynamic-slice_convert_fusion), channel_id=1, source_target_pairs={{0,16},{16,0},{1,17},{17,1},{2,18},{18,2},{3,19},{19,3},{4,20},{20... | collective-permute-start | bytes 6291464 | tf_op jit(solution)/shard_map/ppermute | solution.py:32
  833.0 29.5 %all-to-all-start.13 = ((bf16[4,4,64,512]{3,2,1,0:T(8,128)(2,1)}), bf16[4,4,64,512]{3,2,1,0:T(8,128)(2,1)}, u32[]{:S(2)}, u32[]{:S(2)}) async-start(bf16[4,4,64,512]{3,2,1,0:T(8,128)(2,1)} %fusion.37), calls=%async_computation.13 | async-start | bytes 2097152 | tf_op jit(solution)/shard_map/all_to_all | solution.py:488
  840.5 13.2 %collective-permute-start.34 = (bf16[128,2048]{1,0:T(8,128)(2,1)}, bf16[128,2048]{1,0:T(8,128)(2,1)}, u32[]{:S(2)}, u32[]{:S(2)}) collective-permute-start(bf16[128,2048]{1,0:T(8,128)(2,1)} %fusion.54), channel_id=1, source_target_pairs={{0,8},{4,12},{8,0},{12,4},{1,9},{5,13},{9,1},{13,5},{2,10},{6,14},... | collective-permute-start | bytes 1572872 | tf_op jit(solution)/shard_map/ppermute | solution.py:32
  862.6 12.2 %all-to-all-start.16 = ((f32[32,1,1280]{2,1,0:T(1,128)}), f32[32,1,1280]{2,1,0:T(1,128)S(1)}, u32[]{:S(2)}, u32[]{:S(2)}) async-start(f32[32,1,1280]{2,1,0:T(1,128)} %copy.131), calls=%async_computation.16 | async-start | bytes 327680 | tf_op jit(solution)/shard_map/all_to_all | solution.py:818
  874.8 52.6 %all-to-all-start.14 = ((bf16[4,4,64,1024]{3,2,1,0:T(8,128)(2,1)}), bf16[4,4,64,1024]{3,2,1,0:T(8,128)(2,1)}, u32[]{:S(2)}, u32[]{:S(2)}) async-start(bf16[4,4,64,1024]{3,2,1,0:T(8,128)(2,1)} %fusion.12), calls=%async_computation.14 | async-start | bytes 4194304 | tf_op jit(solution)/shard_map/all_to_all | solution.py:488
  930.4 16.3 %all-to-all-start.15 = ((bf16[4,64,1536]{2,1,0:T(8,128)(2,1)}), bf16[4,64,1536]{2,1,0:T(8,128)(2,1)}, u32[]{:S(2)}, u32[]{:S(2)}) async-start(bf16[4,64,1536]{2,1,0:T(8,128)(2,1)} %pad_maximum_fusion.17), calls=%async_computation.15 | async-start | bytes 1572864 | tf_op jit(solution)/shard_map/all_to_all | solution.py:805
  (104 other events, 813.9 us)
Sparse Core Ops, SparseCore 0:
  36.6 125.9 all-gather.2
  245.3 186.5 all-gather.4

commit v5 on v4

--- a/solution.py
+++ b/solution.py
@@ -145,16 +145,16 @@
         far = far_steps()
         half = value.shape[1] // 2
         shape = (-1, value.shape[0], half)
-        self.near, self.other, self.first = [], [], []
+        self.near = []
         for i in range(2):
             held = jnp.stack([part[:, i * half : (i + 1) * half] for part in around])
             held = held.reshape((1,) * len(far) + held.shape)
-            for level, step in enumerate(far[::-1] if i else far):
-                got = swap(held, *step)
-                self.first += [got] if level == 0 else []
-                held = jnp.concatenate([held, got], axis=far.index(step))
+            for step in far[::-1] if i else far:
+                held = jnp.concatenate([held, swap(held, *step)], axis=far.index(step))
             self.near.append(held.reshape(shape))
-            self.other.append(swap(held, *near_step()).reshape(shape))
+
+    def others(self, *done):
+        return [swap(after(held, *done), *near_step()) for held in self.near]
 
     def order(self):
         z_count = lax.axis_size("dp")
@@ -417,15 +417,14 @@
 
 
 def expert_kernel(per, slot_cap, order_ref, slot_ref, *refs):
-    xs, (w_ref, back_ref, gate_ref) = refs[:per], refs[per : per + 3]
+    xs, (wg_ref, wu_ref, back_ref, gate_ref) = refs[:per], refs[per : per + 4]
     n_ref, act_ref, scaled_ref, gu_ref, dgate_ref, out_ref = refs[-6:]
     ffh = act_ref.shape[1]
     places = lax.broadcasted_iota(jnp.int32, (slot_cap, slot_ref.shape[2]), 0)
     picks = [(slot_ref[j] == places).astype(f32).astype(bf16) for j in range(per)]
     rows = jnp.concatenate([mm(picks[j], xs[j][0]) for j in range(per)]).astype(bf16)
     n_ref[...] = rows
-    gate_up = mm(rows, w_ref[...])
-    gate_part, up_part = gate_up[:, :ffh], gate_up[:, ffh:]
+    gate_part, up_part = mm(rows, wg_ref[...]), mm(rows, wu_ref[...])
     sig = jax.nn.sigmoid(gate_part)
     silu = gate_part * sig
     act = (silu * up_part).astype(bf16)
@@ -435,15 +434,17 @@
     scaled_ref[...] = (act_f * gate).astype(bf16)
     dgate_ref[...] = jnp.sum(act_f * back, axis=1, keepdims=True)
     grad_act = back * gate
-    gu_ref[:, :ffh] = (grad_act * up_part * sig * (1.0 + gate_part * (1.0 - sig))).astype(bf16)
-    gu_ref[:, ffh:] = (grad_act * silu).astype(bf16)
-    grad_rows = mm_nt(gu_ref[...], w_ref[...])
+    grad_gate = (grad_act * up_part * sig * (1.0 + gate_part * (1.0 - sig))).astype(bf16)
+    grad_up = (grad_act * silu).astype(bf16)
+    gu_ref[:, :ffh] = grad_gate
+    gu_ref[:, ffh:] = grad_up
+    grad_rows = mm_nt(grad_gate, wg_ref[...]) + mm_nt(grad_up, wu_ref[...])
     for j in range(per):
         part = grad_rows[j * slot_cap : (j + 1) * slot_cap].astype(bf16)
         out_ref[j] = mm_tn(picks[j], part).astype(bf16)
 
 
-def run_expert(rows, order, slots, slot_cap, w_gu, back, gate, side, held=()):
+def run_expert(rows, order, slots, slot_cap, w_gate, w_up, back, gate, side, held=()):
     total, tokens, width = rows.shape
     ffh = back.shape[1]
     per = max(sources_per_block(slot_cap), 8)
@@ -464,7 +465,8 @@
 
     in_specs = [pl.BlockSpec((per, 1, tokens), lambda i, order_ref: (i + first, 0, 0))]
     in_specs += [block_of(j) for j in range(per)]
-    in_specs += [pl.BlockSpec(w_gu.shape, lambda i, order_ref: (0, 0)), rows_of(ffh), rows_of(1)]
+    in_specs += [pl.BlockSpec(w_gate.shape, lambda i, order_ref: (0, 0))] * 2
+    in_specs += [rows_of(ffh), rows_of(1)]
     aliases = {len(in_specs) + 1 + i: i for i in range(len(held))}
     in_specs += [pl.BlockSpec(memory_space=pl.ANY) for _ in held]
     return pl.pallas_call(
@@ -481,7 +483,7 @@
         input_output_aliases=aliases,
         cost_estimate=QUICK,
         compiler_params=pltpu.CompilerParams(vmem_limit_bytes=58 * 2**20),
-    )(order, slots.reshape(total, 1, tokens), *([rows] * per), w_gu, back, gate, *held)
+    )(order, slots.reshape(total, 1, tokens), *([rows] * per), w_gate, w_up, back, gate, *held)
 
 
 def exchange(blocks, *done):
@@ -650,7 +652,7 @@
     w_down = exchange(down_blocks, packed)
     w_gate = exchange(gate_blocks, w_down)
     w_up = exchange(up_blocks, w_gate)
-    w_gu = jnp.concatenate([w_gate.reshape(width, ffh), w_up.reshape(width, ffh)], axis=1)
+    w_gate_all, w_up_all = w_gate.reshape(width, ffh), w_up.reshape(width, ffh)
 
     inputs = tokens[0].astype(f32)
     pack_x = context_gather(tokens[0]).astype(f32)
@@ -694,15 +696,15 @@
     g_rows = jnp.concatenate(
         [
             take_rows(g_gather.near, g_gather.order(), slot_of[:side], slot_cap),
-            take_rows(g_gather.other, g_gather.order(), slot_of[side:], slot_cap),
+            take_rows(g_gather.others(w_gate), g_gather.order(), slot_of[side:], slot_cap),
         ]
     )
     w_down = w_down.reshape(width, ffh)
     back = mm(g_rows, w_down)
     all_normed = after(all_normed, back)
-    *held, n2_send = run_expert(all_normed, order, slot_of, slot_cap, w_gu, back, gate, 1)
+    *held, n2_send = run_expert(all_normed, order, slot_of, slot_cap, w_gate_all, w_up_all, back, gate, 1)
     n2_sum = Scatter(n2_send, tok_rows)
-    *held, n2_keep = run_expert(all_normed, order, slot_of, slot_cap, w_gu, back, gate, 0, held)
+    *held, n2_keep = run_expert(all_normed, order, slot_of, slot_cap, w_gate_all, w_up_all, back, gate, 0, held)
     n_rows, act, act_scaled, grad_gu, grad_gate_slot = held
     grad_wd = mm_tn(g_rows, act_scaled).astype(bf16)
     grad_wd, n2_sum.got, n2_keep = tie(grad_wd, n2_sum.got, n2_keep)
@@ -765,7 +767,10 @@
         wo_send = halved(grad_wo.reshape(e_count, z_count, w_rows, width))
     v_send = halved(weight_blocks(normed_one, grad_v)).transpose(1, 0, 2, 3)
     (inner,) = y_sum.require(inner)
-    inner = lax.psum(inner.T, "context").T / width
+    inner = lax.psum(inner.T, "context")
+    if aligned:
+        inner, v_send, wo_send = tie(inner, v_send, wo_send)
+    inner = inner.T / width
     grad_qkv = jnp.concatenate(
         [
             scale_qk[:, 0:1] * pull_q - raw_q * (scale_qk[:, 0:1] ** 3 * inner[:, 0:1]),
@@ -777,9 +782,6 @@
     grad_experts = join_experts(gate_got, up_got, down_got, halves)
     qk_blocks = weight_blocks(normed_one, grad_qkv[:, : 2 * cols])
     grad_qkv, qk_blocks = tie(grad_qkv, qk_blocks)
-    if aligned:
-        grad_qkv, wo_send = tie(grad_qkv, wo_send)
-    grad_qkv, v_send = tie(grad_qkv, v_send)
     y_last = y_sum.cross(up_got)
     output = hidden + jnp.sum(y_last.astype(f32), axis=0)
     grad_n1 = context_scatter(mm_nt(grad_qkv, wqkv_all))

time: 972 us -> 954 us (0.981)
    all_to_all x11, waiting for transfers between devices: 149 us -> 132 us  [exchange(): return lax.all_to_all(after(blocks, *done), 'dp', 0, 0, tiled=True)]
    all_gather x1, waiting for transfers between devices: 0.01 us -> 12.8 us  [on_device(): all_normed = lax.all_gather(normed_two, EVERY, axis=0, tiled=True)]
    unnamed x231 -> x227, local copies, waits for them, and re-layouts: 31.6 us -> 37.8 us
  transfers between devices with their start and end apart: 55 -> 55, of which waited for: 28 -> 29; matrix products, arithmetic and copies ran while one was open for 22% -> 22% of each run, Pallas kernels for 9% -> 9%
where the time goes in v5:
time: 954 us; the launch traced here: 942 us
  waiting for transfers between devices  401 us (42%)
  Pallas kernels  116 us (12%)
  other arithmetic  115 us (12%)
  starting transfers between devices  111 us (12%)
  local copies, waits for them, and re-layouts  87.4 us (9%)
  matrix products  66.2 us (7%)
  blocking collectives  29.5 us (3%)
  between operations  16.1 us (2%)
    ppermute x30, waiting for transfers between devices, swap(): return lax.ppermute(value, axis, [(i, i ^ bit) for i in range(count)])  160 us
    all_to_all x11, waiting for transfers between devices, exchange(): return lax.all_to_all(after(blocks, *done), 'dp', 0, 0, tiled=True)  132 us
    all_to_all x11, starting transfers between devices, exchange(): return lax.all_to_all(after(blocks, *done), 'dp', 0, 0, tiled=True)  47.7 us
    pallas_call x2, Pallas kernels, run_expert(): pl.pallas_call(lambda *refs: expert_kernel(per, slot_cap, *refs), grid_sp...  43.3 us
    dot_general x7, matrix products, mm_tn(): lax.dot_general(a, b, (((0,), (0,)), ((), ())), preferred_element_type=f32)  42.6 us
    unnamed x227, local copies, waits for them, and re-layouts  37.8 us
    ppermute x6, waiting for transfers between devices, shift(): lax.ppermute(value, axis, [(i, (i + step) % count) for i in range(count)])  27.3 us
    all_gather x1, waiting for transfers between devices, on_device(): wqkv_all = packed = lax.all_gather(wqkv, around, axis=0, tiled=True)  26.9 us
  transfers between devices with their start and end apart: 55, of which 29 were waited for; matrix products, arithmetic and copies ran while one was open for 22% of the time, Pallas kernels for 9%

profile of v5, /device:TPU:0, one launch (start us, length us, event | category | flops | bytes accessed | tf_op | source)
XLA Modules:
  0.0 942.2 jit_solution(6131591235735066995)
XLA Ops:
  14.2 4.4 all-to-all-start
  21.0 14.5 %collective-permute-done.7 = bf16[128,2048]{1,0:T(8,128)(2,1)S(1)} collective-permute-done((bf16[128,2048]{1,0:T(8,128)(2,1)S(1)}, bf16[128,2048]{1,0:T(8,128)(2,1)S(1)}, u32[]{:S(2)}, u32[]{:S(2)}) %collective-permute-start.7) | collective-permute-done | bytes 524320 | tf_op jit(solution)/shard_map/ppermute | solution.py:37
  43.1 5.2 copy-done.6
  48.3 13.5 %shard_map.136 = (bf16[4,512,512]{2,1,0:T(8,128)(2,1)}, bf16[4,512,512]{2,1,0:T(8,128)(2,1)}, bf16[4,512,512]{2,1,0:T(8,128)(2,1)}) custom-call(f32[512,2,3072]{2,1,0:T(2,128)S(1)} %copy-done.6), custom_call_target="tpu_custom_call" | custom-call | flops 1 | bytes 1 | tf_op jit(solution)/shard_map/pallas_call | solution.py:506
  68.6 12.8 %collective-permute-done.4 = bf16[64,2048]{1,0:T(8,128)(2,1)S(1)} collective-permute-done((bf16[64,2048]{1,0:T(8,128)(2,1)}, bf16[64,2048]{1,0:T(8,128)(2,1)S(1)}, u32[]{:S(2)}, u32[]{:S(2)}) %collective-permute-start.4) | collective-permute-done | bytes 262176 | tf_op jit(solution)/shard_map/ppermute | solution.py:37
  84.9 5.3 all-to-all-start.1
  90.3 21.5 %all-to-all-done.1 = bf16[32,2,704]{2,1,0:T(2,128)(2,1)S(1)} async-done(((bf16[32,2,704]{2,1,0:T(2,128)(2,1)}), bf16[32,2,704]{2,1,0:T(2,128)(2,1)S(1)}, u32[]{:S(2)}, u32[]{:S(2)}) %all-to-all-start.1) | async-done | bytes 90144 | tf_op jit(solution)/shard_map/all_to_all | solution.py:622
  121.5 7.7 collective-permute-start.9
  131.5 4.3 fusion.4
  135.8 26.9 %all-gather.3.cloned.1.call-done = bf16[2048,1536]{1,0:T(8,128)(2,1)} async-done(((bf16[256,1536]{1,0:T(8,128)(2,1)}), bf16[2048,1536]{1,0:T(8,128)(2,1)}) %all-gather.3.cloned.1.call-update) | async-done | bytes 6291472 | tf_op jit(solution)/shard_map/all_gather | solution.py:640
  162.7 4.5 all-to-all-start.2
  171.4 4.2 copy.113
  180.5 15.2 %psum.14 = f32[2,512]{0,1:T(8,128)} all-reduce(f32[2,512]{0,1:T(8,128)} %copy.114), channel_id=1, replica_groups=mesh['expert'=2,'context'=4,'dp'=4] {'context'}, use_global_device_ids=true, to_apply=%region_4.5 | all-reduce | flops 1024 | bytes 8192 | tf_op jit(solution)/shard_map/psum | solution.py:677
  198.6 7.1 shard_map.137
  209.7 6.3 all-to-all-done.2
  227.6 13.7 %collective-permute-done.11 = bf16[128,2048]{1,0:T(8,128)(2,1)} collective-permute-done((bf16[128,2048]{1,0:T(8,128)(2,1)}, bf16[128,2048]{1,0:T(8,128)(2,1)}, u32[]{:S(2)}, u32[]{:S(2)}) %collective-permute-start.11) | collective-permute-done | bytes 524320 | tf_op jit(solution)/shard_map/ppermute | solution.py:32
  255.3 21.7 %collective-permute-done.12 = bf16[1,1,4,128,1024]{4,3,2,1,0:T(8,128)(2,1)} collective-permute-done((bf16[1,1,4,128,1024]{4,3,2,1,0:T(8,128)(2,1)}, bf16[1,1,4,128,1024]{4,3,2,1,0:T(8,128)(2,1)}, u32[]{:S(2)}, u32[]{:S(2)}) %collective-permute-start.12) | collective-permute-done | bytes 1048608 | tf_op jit(solution)/shard_map/ppermute | solution.py:32
  282.6 49.6 %collective-permute-done.13 = bf16[2,1,4,128,1024]{4,3,2,1,0:T(8,128)(2,1)S(1)} collective-permute-done((bf16[2,1,4,128,1024]{4,3,2,1,0:T(8,128)(2,1)S(1)}, bf16[2,1,4,128,1024]{4,3,2,1,0:T(8,128)(2,1)S(1)}, u32[]{:S(2)}, u32[]{:S(2)}) %collective-permute-start.13) | collective-permute-done | bytes 2097184 | tf_op jit(solution)/shard_map/ppermute | solution.py:32
  335.7 9.2 collective-permute-done.15
  352.9 7.4 all-to-all-done.5
  360.2 4.7 all-to-all-start.4
  378.9 7.6 shard_map.139
  388.7 10.6 %fusion.1.refs_12_ = f32[2304,512]{1,0:T(8,128)} fusion(bf16[2048,512]{1,0:T(8,128)(2,1)} %bitcast.123.refs_3_, bf16[1152,2048]{1,0:T(8,128)(2,1)S(1)} %shard_map.139, bf16[1152,2048]{1,0:T(8,128)(2,1)S(1)} %bitcast.389), kind=kOutput, calls=%fused_computation.4 | convolution fusion | flops 4850712576 | bytes 16252928 | tf_op jit(solution)/shard_map/dot_general | solution.py:19
  399.4 12.8 %all-gather.5.cloned.1.call-done = bf16[4096,2048]{1,0:T(8,128)(2,1)} async-done(((bf16[128,2048]{1,0:T(8,128)(2,1)}), bf16[4096,2048]{1,0:T(8,128)(2,1)}) %all-gather.5.cloned.1.call-update) | async-done | bytes 16777232 | tf_op jit(solution)/shard_map/all_gather | solution.py:686
  412.1 21.0 %all-to-all-done.4 = bf16[4,512,512]{2,1,0:T(8,128)(2,1)} async-done(((bf16[4,512,512]{2,1,0:T(8,128)(2,1)}), bf16[4,512,512]{2,1,0:T(8,128)(2,1)}, u32[]{:S(2)}, u32[]{:S(2)}) %all-to-all-start.4) | async-done | bytes 2097184 | tf_op jit(solution)/shard_map/all_to_all | solution.py:490
  433.1 21.5 %shard_map.140 = (bf16[2304,2048]{1,0:T(8,128)(2,1)}, bf16[2304,512]{1,0:T(8,128)(2,1)}, bf16[2304,512]{1,0:T(8,128)(2,1)}, bf16[2304,1024]{1,0:T(8,128)(2,1)}, ...) custom-call(s32[32]{0:T(128)} %stack.310.refs_0_, s32[32,1,128]{2,1,0:T(1,128)} %bitcast.390, ...), custom_call_target="tpu_custom_call" | custom-call | flops 1 | bytes 1 | tf_op jit(solution)/shard_map/pallas_call | solution.py:472
  454.8 21.8 %shard_map.141 = (bf16[2304,2048]{1,0:T(8,128)(2,1)}, bf16[2304,512]{1,0:T(8,128)(2,1)}, bf16[2304,512]{1,0:T(8,128)(2,1)}, bf16[2304,1024]{1,0:T(8,128)(2,1)}, ...) custom-call(s32[32]{0:T(128)} %stack.310.refs_0_, ...), custom_call_target="tpu_custom_call", output_to_operand_aliasing={{0}: (14, {}), {1}: (15, {}), {2}: (16, {}), {3}: (17, {}),... | custom-call | flops 1 | bytes 1 | tf_op jit(solution)/shard_map/pallas_call | solution.py:472
  479.5 3.7 all-to-all-start.6
  483.2 9.4 fusion.5
  493.2 5.0 all-to-all-start.7
  498.2 5.8 add_convert_fusion.4
  505.6 5.8 add_convert_fusion.5
  512.9 33.9 %all-to-all-done.7.refs_2_ = bf16[4,512,512]{2,1,0:T(8,128)(2,1)S(1)} async-done(((bf16[4,512,512]{2,1,0:T(8,128)(2,1)}), bf16[4,512,512]{2,1,0:T(8,128)(2,1)S(1)}, u32[]{:S(2)}, u32[]{:S(2)}) %all-to-all-start.7) | async-done | bytes 2097184 | tf_op jit(solution)/shard_map/all_to_all | solution.py:490
  548.1 10.8 %convolution_convert_fusion.1 = bf16[2048,512]{1,0:T(8,128)(2,1)} fusion(bf16[2304,2048]{1,0:T(8,128)(2,1)} %get-tuple-element.118, bf16[2304,1024]{1,0:T(8,128)(2,1)} %get-tuple-element.108), kind=kOutput, calls=%fused_computation.26 | convolution fusion | flops 4832886784 | bytes 13893632 | tf_op jit(solution)/shard_map/dot_general | solution.py:27
  558.9 8.6 shard_map.143
  567.6 4.9 all-to-all-start.8
  579.1 8.7 shard_map.142
  587.8 6.1 add_convert_fusion.1
  595.1 4.8 fusion.10
  608.3 13.1 %all-to-all-done.8.refs_0_ = bf16[4,512,512]{2,1,0:T(8,128)(2,1)} async-done(((bf16[4,512,512]{2,1,0:T(8,128)(2,1)}), bf16[4,512,512]{2,1,0:T(8,128)(2,1)}, u32[]{:S(2)}, u32[]{:S(2)}) %all-to-all-start.8) | async-done | bytes 2097184 | tf_op jit(solution)/shard_map/all_to_all | solution.py:490
  628.2 10.7 %convolution_convert_fusion = bf16[2048,512]{1,0:T(8,128)(2,1)} fusion(bf16[2304,2048]{1,0:T(8,128)(2,1)} %get-tuple-element.118, bf16[2304,1024]{1,0:T(8,128)(2,1)} %get-tuple-element.108), kind=kOutput, calls=%fused_computation.25 | convolution fusion | flops 4832886784 | bytes 13893632 | tf_op jit(solution)/shard_map/dot_general | solution.py:27
  639.0 33.5 %collective-permute-done.24 = bf16[2,4,128,1024]{3,2,1,0:T(8,128)(2,1)} collective-permute-done((bf16[2,4,128,1024]{3,2,1,0:T(8,128)(2,1)}, bf16[2,4,128,1024]{3,2,1,0:T(8,128)(2,1)}, u32[]{:S(2)}, u32[]{:S(2)}) %collective-permute-start.24) | collective-permute-done | bytes 2097184 | tf_op jit(solution)/shard_map/ppermute | solution.py:32
  678.1 4.8 all-to-all-start.10
  682.9 6.7 collective-permute-done.29
  702.1 15.8 %shard_map.144 = (f32[512,512]{1,0:T(8,128)S(1)}, f32[512,512]{1,0:T(8,128)S(1)}, bf16[512,512]{1,0:T(8,128)(2,1)S(1)}, f32[2,512]{1,0:T(2,128)S(1)}, f32[512,2]{1,0:T(8,128)S(1)}) custom-call(f32[512,1536]{1,0:T(8,128)} %copy-done, f32[512,1536]{1,0:T(8,128)} %copy-done, f32[512,2]{1,0:T(8,128)S(1)} %copy-done.12, f32[2,512]{1,0:T(2,128)S(1)} %bitcast.397, ...), custom_call_target="tpu_custom_call" | custom-call | flops 1 | bytes 1 | tf_op jit(solution)/shard_map/pallas_call | solution.py:404
  733.1 4.4 all-to-all-start.11
  741.1 14.3 %psum.15 = f32[2,512]{0,1:T(8,128)S(1)} all-reduce(f32[2,512]{0,1:T(8,128)S(1)} %bitcast.395), channel_id=1, replica_groups=mesh['expert'=2,'context'=4,'dp'=4] {'context'}, use_global_device_ids=true, to_apply=%region_21.22 | all-reduce | flops 1024 | bytes 8192 | tf_op jit(solution)/shard_map/psum | solution.py:770
  758.9 9.3 collective-permute-done.32
  772.6 5.8 fusion.49
  778.4 7.2 all-to-all-done.11
  789.2 5.6 fusion.100
  795.0 5.1 dynamic-slice_convert_fusion
  802.0 12.4 %all-to-all-done.12 = bf16[4,64,2048]{2,1,0:T(8,128)(2,1)S(1)} async-done(((bf16[4,64,2048]{2,1,0:T(8,128)(2,1)}), bf16[4,64,2048]{2,1,0:T(8,128)(2,1)S(1)}, u32[]{:S(2)}, u32[]{:S(2)}) %all-to-all-start.12) | async-done | bytes 1048608 | tf_op jit(solution)/shard_map/all_to_all | solution.py:490
  814.4 4.3 all-to-all-start.13
  826.7 8.4 collective-permute-done.34
  837.5 6.4 all-to-all-done.13
  843.9 3.9 all-to-all-start.16
  847.9 4.9 fusion.12
  852.8 3.9 all-to-all-done.16
  856.7 4.5 all-to-all-start.14
  862.8 8.3 shard_map.145
  878.5 30.8 %all-to-all-done.14 = bf16[4,4,64,1024]{3,2,1,0:T(8,128)(2,1)} async-done(((bf16[4,4,64,1024]{3,2,1,0:T(8,128)(2,1)}), bf16[4,4,64,1024]{3,2,1,0:T(8,128)(2,1)}, u32[]{:S(2)}, u32[]{:S(2)}) %all-to-all-start.14) | async-done | bytes 2097184 | tf_op jit(solution)/shard_map/all_to_all | solution.py:490
  912.3 4.5 all-to-all-start.15
  918.9 9.6 %all-to-all-done.15 = bf16[4,64,1536]{2,1,0:T(8,128)(2,1)} async-done(((bf16[4,64,1536]{2,1,0:T(8,128)(2,1)}), bf16[4,64,1536]{2,1,0:T(8,128)(2,1)}, u32[]{:S(2)}, u32[]{:S(2)}) %all-to-all-start.15) | async-done | bytes 786464 | tf_op jit(solution)/shard_map/all_to_all | solution.py:807
  (468 shorter events, 225.6 us)
Async XLA Ops:
  8.9 29.4 %copy-start.62 = (bf16[64,8192]{1,0:T(8,128)(2,1)}, bf16[64,8192]{1,0:T(8,128)(2,1)S(1)}, u32[]{:S(2)}) copy-start(bf16[64,8192]{1,0:T(8,128)(2,1)S(1)} %convert.33) | copy-start | bytes 3145732
  14.2 21.4 %all-to-all-start = ((bf16[4,64,1536]{2,1,0:T(8,128)(2,1)}), bf16[4,64,1536]{2,1,0:T(8,128)(2,1)S(1)}, u32[]{:S(2)}, u32[]{:S(2)}) async-start(bf16[4,64,1536]{2,1,0:T(8,128)(2,1)} %reshape.1700), calls=%async_computation | async-start | bytes 1572864 | tf_op jit(solution)/shard_map/all_to_all | solution.py:620
  18.5 144.2 %all-gather.3.cloned.1.call-start = ((), (), s32[]{:S(2)}) async-start(), calls=%async_computation.17 | async-start | bytes 7077888 | tf_op jit(solution)/shard_map/all_gather | solution.py:640
  18.6 17.0 %collective-permute-start.7 = (bf16[128,2048]{1,0:T(8,128)(2,1)S(1)}, bf16[128,2048]{1,0:T(8,128)(2,1)S(1)}, u32[]{:S(2)}, u32[]{:S(2)}) collective-permute-start(bf16[128,2048]{1,0:T(8,128)(2,1)S(1)} %bitcast_convert_fusion.2), channel_id=1, source_target_pairs={{0,1},{1,2},{2,3},{3,0},{4,5},{5,6},{6,7},{7,4},{8,9},{9,10},{10,1... | collective-permute-start | bytes 1572872 | tf_op jit(solution)/shard_map/ppermute | solution.py:37
  36.5 44.9 %collective-permute-start.1 = (bf16[128,2048]{1,0:T(8,128)(2,1)S(1)}, bf16[128,2048]{1,0:T(8,128)(2,1)}, u32[]{:S(2)}, u32[]{:S(2)}) collective-permute-start(bf16[128,2048]{1,0:T(8,128)(2,1)S(1)} %bitcast.426), channel_id=1, source_target_pairs={{0,8},{4,12},{8,0},{12,4},{1,9},{5,13},{9,1},{13,5},{2,10},{6,14},... | collective-permute-start | bytes 1572872 | tf_op jit(solution)/shard_map/ppermute | solution.py:32
  38.3 90.9 %collective-permute-start = (bf16[128,2048]{1,0:T(8,128)(2,1)S(1)}, bf16[128,2048]{1,0:T(8,128)(2,1)}, u32[]{:S(2)}, u32[]{:S(2)}) collective-permute-start(bf16[128,2048]{1,0:T(8,128)(2,1)S(1)} %bitcast.427), channel_id=1, source_target_pairs={{0,4},{4,0},{8,12},{12,8},{1,5},{5,1},{9,13},{13,9},{2,6},{6,2},{1... | collective-permute-start | bytes 1572872 | tf_op jit(solution)/shard_map/ppermute | solution.py:32
  39.2 25.4 %collective-permute-start.3 = (bf16[64,2048]{1,0:T(8,128)(2,1)}, bf16[64,2048]{1,0:T(8,128)(2,1)}, u32[]{:S(2)}, u32[]{:S(2)}) collective-permute-start(bf16[64,2048]{1,0:T(8,128)(2,1)} %get-tuple-element.209), channel_id=1, source_target_pairs={{0,1},{1,2},{2,3},{3,0},{4,5},{5,6},{6,7},{7,4},{8,9},{9,10},{10,1... | collective-permute-start | bytes 786440 | tf_op jit(solution)/shard_map/ppermute | solution.py:37
  63.7 133.0 %copy-start.15 = (f32[512,128]{1,0:T(8,128)}, f32[512,128]{1,0:T(8,128)S(1)}, u32[]{:S(2)}) copy-start(f32[512,128]{1,0:T(8,128)S(1)} %get-tuple-element.233.refs_5_.refs_4_) | copy-start | bytes 786436
  63.7 54.2 %copy-start.82 = (bf16[1,64,2048]{2,1,0:T(8,128)(2,1)S(1)}, bf16[1,64,2048]{2,1,0:T(8,128)(2,1)}, u32[]{:S(2)}) copy-start(bf16[1,64,2048]{2,1,0:T(8,128)(2,1)} %get-tuple-element.208) | copy-start | bytes 786436
  63.7 133.0 %copy-start.35 = (s32[2,512]{1,0:T(2,128)}, s32[2,512]{1,0:T(2,128)S(1)}, u32[]{:S(2)}) copy-start(s32[2,512]{1,0:T(2,128)S(1)} %get-tuple-element.223.refs_8_.refs_7_) | copy-start | bytes 12292
  64.6 16.8 %collective-permute-start.4 = (bf16[64,2048]{1,0:T(8,128)(2,1)}, bf16[64,2048]{1,0:T(8,128)(2,1)S(1)}, u32[]{:S(2)}, u32[]{:S(2)}) collective-permute-start(bf16[64,2048]{1,0:T(8,128)(2,1)} %collective-permute-done.3), channel_id=1, source_target_pairs={{0,1},{1,2},{2,3},{3,0},{4,5},{5,6},{6,7},{7,4},{8,9},{9,10},{10,1... | collective-permute-start | bytes 786440 | tf_op jit(solution)/shard_map/ppermute | solution.py:37
  67.0 54.5 %collective-permute-start.8 = (bf16[128,2048]{1,0:T(8,128)(2,1)}, bf16[128,2048]{1,0:T(8,128)(2,1)}, u32[]{:S(2)}, u32[]{:S(2)}) collective-permute-start(bf16[128,2048]{1,0:T(8,128)(2,1)} %copy-done.83), channel_id=1, source_target_pairs={{0,1},{1,2},{2,3},{3,0},{4,5},{5,6},{6,7},{7,4},{8,9},{9,10},{10,1... | collective-permute-start | bytes 1572872 | tf_op jit(solution)/shard_map/ppermute | solution.py:37
  81.4 36.5 %collective-permute-start.5 = (bf16[64,2048]{1,0:T(8,128)(2,1)S(1)}, bf16[64,2048]{1,0:T(8,128)(2,1)}, u32[]{:S(2)}, u32[]{:S(2)}) collective-permute-start(bf16[64,2048]{1,0:T(8,128)(2,1)S(1)} %collective-permute-done.4), channel_id=1, source_target_pairs={{0,1},{1,2},{2,3},{3,0},{4,5},{5,6},{6,7},{7,4},{8,9},{9,10},{10,1... | collective-permute-start | bytes 786440 | tf_op jit(solution)/shard_map/ppermute | solution.py:37
  81.4 47.8 %collective-permute-start.2 = (bf16[128,2048]{1,0:T(8,128)(2,1)}, bf16[128,2048]{1,0:T(8,128)(2,1)}, u32[]{:S(2)}, u32[]{:S(2)}) collective-permute-start(bf16[128,2048]{1,0:T(8,128)(2,1)} %collective-permute-done.1), channel_id=1, source_target_pairs={{0,4},{4,0},{8,12},{12,8},{1,5},{5,1},{9,13},{13,9},{2,6},{6,2},{1... | collective-permute-start | bytes 1572872 | tf_op jit(solution)/shard_map/ppermute | solution.py:32
  84.9 26.8 %all-to-all-start.1 = ((bf16[32,2,704]{2,1,0:T(2,128)(2,1)}), bf16[32,2,704]{2,1,0:T(2,128)(2,1)S(1)}, u32[]{:S(2)}, u32[]{:S(2)}) async-start(bf16[32,2,704]{2,1,0:T(2,128)(2,1)} %reshape.1774), calls=%async_computation.1 | async-start | bytes 196608 | tf_op jit(solution)/shard_map/all_to_all | solution.py:622
  117.9 78.8 %copy-start.37 = (f32[1,2,2,256]{3,1,2,0:T(2,128)}, f32[1,2,2,256]{3,1,2,0:T(2,128)S(1)}, u32[]{:S(2)}) copy-start(f32[1,2,2,256]{3,1,2,0:T(2,128)S(1)} %copy.140) | copy-start | bytes 12292
  120.1 47.3 %collective-permute-start.6 = (bf16[4,64,2048]{2,1,0:T(8,128)(2,1)}, bf16[4,64,2048]{2,1,0:T(8,128)(2,1)}, u32[]{:S(2)}, u32[]{:S(2)}) collective-permute-start(bf16[4,64,2048]{2,1,0:T(8,128)(2,1)} %pad_maximum_fusion.15), channel_id=1, source_target_pairs={{0,16},{16,0},{1,17},{17,1},{2,18},{18,2},{3,19},{19,3},{4,20},{20... | collective-permute-start | bytes 3145736 | tf_op jit(solution)/shard_map/ppermute | solution.py:32
  121.5 49.8 %collective-permute-start.9 = (bf16[128,2048]{1,0:T(8,128)(2,1)}, bf16[128,2048]{1,0:T(8,128)(2,1)}, u32[]{:S(2)}, u32[]{:S(2)}) collective-permute-start(bf16[128,2048]{1,0:T(8,128)(2,1)} %collective-permute-done.8), channel_id=1, source_target_pairs={{0,1},{1,2},{2,3},{3,0},{4,5},{5,6},{6,7},{7,4},{8,9},{9,10},{10,1... | collective-permute-start | bytes 1572872 | tf_op jit(solution)/shard_map/ppermute | solution.py:37
  162.7 53.2 %all-to-all-start.2 = ((bf16[4,512,512]{2,1,0:T(8,128)(2,1)}), bf16[4,512,512]{2,1,0:T(8,128)(2,1)}, u32[]{:S(2)}, u32[]{:S(2)}) async-start(bf16[4,512,512]{2,1,0:T(8,128)(2,1)} %get-tuple-element.82), calls=%async_computation.2 | async-start | bytes 4194304 | tf_op jit(solution)/shard_map/all_to_all | solution.py:490
  167.2 244.9 %all-gather.5.cloned.1.call-start = ((), (), s32[]{:S(2)}) async-start(), calls=%async_computation.18 | async-start | bytes 17301504 | tf_op jit(solution)/shard_map/all_gather | solution.py:686
  179.1 26.6 %copy-start = (f32[512,1536]{1,0:T(8,128)}, f32[512,1536]{1,0:T(8,128)S(1)}, u32[]{:S(2)}) copy-start(f32[512,1536]{1,0:T(8,128)S(1)} %fusion.97.refs_0_.refs_1_.refs_2_) | copy-start | bytes 9437188
  221.1 2.9 collective-permute-start.10
  227.0 14.3 %collective-permute-start.11 = (bf16[128,2048]{1,0:T(8,128)(2,1)}, bf16[128,2048]{1,0:T(8,128)(2,1)}, u32[]{:S(2)}, u32[]{:S(2)}) collective-permute-start(bf16[128,2048]{1,0:T(8,128)(2,1)} %fusion.53), channel_id=1, source_target_pairs={{0,8},{4,12},{8,0},{12,4},{1,9},{5,13},{9,1},{13,5},{2,10},{6,14},... | collective-permute-start | bytes 1572872 | tf_op jit(solution)/shard_map/ppermute | solution.py:32
  248.6 28.4 %collective-permute-start.12 = (bf16[1,1,4,128,1024]{4,3,2,1,0:T(8,128)(2,1)}, bf16[1,1,4,128,1024]{4,3,2,1,0:T(8,128)(2,1)}, u32[]{:S(2)}, u32[]{:S(2)}) collective-permute-start(bf16[1,1,4,128,1024]{4,3,2,1,0:T(8,128)(2,1)} %maximum_bitcast_fusion), channel_id=1, source_target_pairs={{0,8},{4,12},{8,0},{12,4},{1,9},{5,13},{9,1},{13,5},{2,10},{6,14},... | collective-permute-start | bytes 3145736 | tf_op jit(solution)/shard_map/ppermute | solution.py:32
  250.2 30.1 %collective-permute-start.14 = (bf16[1,1,4,128,1024]{4,3,2,1,0:T(8,128)(2,1)}, bf16[1,1,4,128,1024]{4,3,2,1,0:T(8,128)(2,1)}, u32[]{:S(2)}, u32[]{:S(2)}) collective-permute-start(bf16[1,1,4,128,1024]{4,3,2,1,0:T(8,128)(2,1)} %maximum_bitcast_fusion.1), channel_id=1, source_target_pairs={{0,16},{16,0},{1,17},{17,1},{2,18},{18,2},{3,19},{19,3},{4,20},{20... | collective-permute-start | bytes 3145736 | tf_op jit(solution)/shard_map/ppermute | solution.py:32
  251.7 96.7 %all-to-all-start.3 = ((bf16[4,512,512]{2,1,0:T(8,128)(2,1)}), bf16[4,512,512]{2,1,0:T(8,128)(2,1)S(1)}, u32[]{:S(2)}, u32[]{:S(2)}) async-start(bf16[4,512,512]{2,1,0:T(8,128)(2,1)} %get-tuple-element.84), calls=%async_computation.3 | async-start | bytes 4194304 | tf_op jit(solution)/shard_map/all_to_all | solution.py:490
  278.7 53.5 %collective-permute-start.13 = (bf16[2,1,4,128,1024]{4,3,2,1,0:T(8,128)(2,1)S(1)}, bf16[2,1,4,128,1024]{4,3,2,1,0:T(8,128)(2,1)S(1)}, u32[]{:S(2)}, u32[]{:S(2)}) collective-permute-start(bf16[2,1,4,128,1024]{4,3,2,1,0:T(8,128)(2,1)S(1)} %pad_maximum_fusion.8), channel_id=1, source_target_pairs={{0,16},{16,0},{1,17},{17,1},{2,18},{18,2},{3,19},{19,3},{4,20},{20... | collective-permute-start | bytes 6291464 | tf_op jit(solution)/shard_map/ppermute | solution.py:32
  282.1 62.8 %collective-permute-start.15 = (bf16[1,2,4,128,1024]{4,3,2,1,0:T(8,128)(2,1)S(1)}, bf16[1,2,4,128,1024]{4,3,2,1,0:T(8,128)(2,1)S(1)}, u32[]{:S(2)}, u32[]{:S(2)}) collective-permute-start(bf16[1,2,4,128,1024]{4,3,2,1,0:T(8,128)(2,1)S(1)} %pad_maximum_fusion.9), channel_id=1, source_target_pairs={{0,8},{4,12},{8,0},{12,4},{1,9},{5,13},{9,1},{13,5},{2,10},{6,14},... | collective-permute-start | bytes 6291464 | tf_op jit(solution)/shard_map/ppermute | solution.py:32
  348.4 30.5 %collective-permute-start.16 = (bf16[16,128,1024]{2,1,0:T(8,128)(2,1)}, bf16[16,128,1024]{2,1,0:T(8,128)(2,1)}, u32[]{:S(2)}, u32[]{:S(2)}) collective-permute-start(bf16[16,128,1024]{2,1,0:T(8,128)(2,1)} %bitcast.382), channel_id=1, source_target_pairs={{0,4},{4,0},{8,12},{12,8},{1,5},{5,1},{9,13},{13,9},{2,6},{6,2},{1... | collective-permute-start | bytes 12582920 | tf_op jit(solution)/shard_map/ppermute | solution.py:32
  348.4 30.5 %collective-permute-start.17 = (bf16[16,128,1024]{2,1,0:T(8,128)(2,1)}, bf16[16,128,1024]{2,1,0:T(8,128)(2,1)}, u32[]{:S(2)}, u32[]{:S(2)}) collective-permute-start(bf16[16,128,1024]{2,1,0:T(8,128)(2,1)} %bitcast.385), channel_id=1, source_target_pairs={{0,4},{4,0},{8,12},{12,8},{1,5},{5,1},{9,13},{13,9},{2,6},{6,2},{1... | collective-permute-start | bytes 12582920 | tf_op jit(solution)/shard_map/ppermute | solution.py:32
  350.4 9.9 %all-to-all-start.5 = ((f32[32,1,128]{2,1,0:T(1,128)}), f32[32,1,128]{2,1,0:T(1,128)S(1)}, u32[]{:S(2)}, u32[]{:S(2)}) async-start(f32[32,1,128]{2,1,0:T(1,128)} %bitcast.127), calls=%async_computation.5 | async-start | bytes 32768 | tf_op jit(solution)/shard_map/all_to_all | solution.py:688
  360.2 72.9 %all-to-all-start.4 = ((bf16[4,512,512]{2,1,0:T(8,128)(2,1)}), bf16[4,512,512]{2,1,0:T(8,128)(2,1)}, u32[]{:S(2)}, u32[]{:S(2)}) async-start(bf16[4,512,512]{2,1,0:T(8,128)(2,1)} %get-tuple-element.89), calls=%async_computation.4 | async-start | bytes 4194304 | tf_op jit(solution)/shard_map/all_to_all | solution.py:490
  454.7 37.9 %collective-permute-start.18 = (bf16[16,128,2048]{2,1,0:T(8,128)(2,1)}, bf16[16,128,2048]{2,1,0:T(8,128)(2,1)}, u32[]{:S(2)}, u32[]{:S(2)}) collective-permute-start(bf16[16,128,2048]{2,1,0:T(8,128)(2,1)} %get-tuple-element.96), channel_id=1, source_target_pairs={{0,4},{4,0},{8,12},{12,8},{1,5},{5,1},{9,13},{13,9},{2,6},{6,2},{1... | collective-permute-start | bytes 25165832 | tf_op jit(solution)/shard_map/ppermute | solution.py:32
  479.5 13.1 %all-to-all-start.6 = ((f32[32,1,128]{2,1,0:T(1,128)}), f32[32,1,128]{2,1,0:T(1,128)S(1)}, u32[]{:S(2)}, u32[]{:S(2)}) async-start(f32[32,1,128]{2,1,0:T(1,128)} %bitcast.134), calls=%async_computation.6 | async-start | bytes 32768 | tf_op jit(solution)/shard_map/all_to_all | solution.py:717
  493.2 53.6 %all-to-all-start.7 = ((bf16[4,512,512]{2,1,0:T(8,128)(2,1)}), bf16[4,512,512]{2,1,0:T(8,128)(2,1)S(1)}, u32[]{:S(2)}, u32[]{:S(2)}) async-start(bf16[4,512,512]{2,1,0:T(8,128)(2,1)} %bitcast.440), calls=%async_computation.7 | async-start | bytes 4194304 | tf_op jit(solution)/shard_map/all_to_all | solution.py:490
  504.1 54.8 %collective-permute-start.20 = (bf16[2,4,128,1024]{3,2,1,0:T(8,128)(2,1)}, bf16[2,4,128,1024]{3,2,1,0:T(8,128)(2,1)}, u32[]{:S(2)}, u32[]{:S(2)}) collective-permute-start(bf16[2,4,128,1024]{3,2,1,0:T(8,128)(2,1)} %get-tuple-element.195), channel_id=1, source_target_pairs={{0,16},{16,0},{1,17},{17,1},{2,18},{18,2},{3,19},{19,3},{4,20},{20... | collective-permute-start | bytes 6291464 | tf_op jit(solution)/shard_map/ppermute | solution.py:32
  511.4 47.5 %collective-permute-start.19 = (bf16[2,4,128,1024]{3,2,1,0:T(8,128)(2,1)}, bf16[2,4,128,1024]{3,2,1,0:T(8,128)(2,1)}, u32[]{:S(2)}, u32[]{:S(2)}) collective-permute-start(bf16[2,4,128,1024]{3,2,1,0:T(8,128)(2,1)} %get-tuple-element.197), channel_id=1, source_target_pairs={{0,8},{4,12},{8,0},{12,4},{1,9},{5,13},{9,1},{13,5},{2,10},{6,14},... | collective-permute-start | bytes 6291464 | tf_op jit(solution)/shard_map/ppermute | solution.py:32
  567.6 20.2 %collective-permute-start.21 = (bf16[16,128,2048]{2,1,0:T(8,128)(2,1)}, bf16[16,128,2048]{2,1,0:T(8,128)(2,1)}, u32[]{:S(2)}, u32[]{:S(2)}) collective-permute-start(bf16[16,128,2048]{2,1,0:T(8,128)(2,1)} %shard_map.143), channel_id=1, source_target_pairs={{0,4},{4,0},{8,12},{12,8},{1,5},{5,1},{9,13},{13,9},{2,6},{6,2},{1... | collective-permute-start | bytes 25165832 | tf_op jit(solution)/shard_map/ppermute | solution.py:32
  567.6 53.9 %all-to-all-start.8 = ((bf16[4,512,512]{2,1,0:T(8,128)(2,1)}), bf16[4,512,512]{2,1,0:T(8,128)(2,1)}, u32[]{:S(2)}, u32[]{:S(2)}) async-start(bf16[4,512,512]{2,1,0:T(8,128)(2,1)} %bitcast.439), calls=%async_computation.8 | async-start | bytes 4194304 | tf_op jit(solution)/shard_map/all_to_all | solution.py:490
  574.6 25.4 %collective-permute-start.23 = (bf16[4,128,1024]{2,1,0:T(8,128)(2,1)S(1)}, bf16[4,128,1024]{2,1,0:T(8,128)(2,1)S(1)}, u32[]{:S(2)}, u32[]{:S(2)}) collective-permute-start(bf16[4,128,1024]{2,1,0:T(8,128)(2,1)S(1)} %fusion.40), channel_id=1, source_target_pairs={{0,8},{4,12},{8,0},{12,4},{1,9},{5,13},{9,1},{13,5},{2,10},{6,14},... | collective-permute-start | bytes 3145736 | tf_op jit(solution)/shard_map/ppermute | solution.py:32
  577.8 25.1 %collective-permute-start.22 = (bf16[4,128,1024]{2,1,0:T(8,128)(2,1)S(1)}, bf16[4,128,1024]{2,1,0:T(8,128)(2,1)S(1)}, u32[]{:S(2)}, u32[]{:S(2)}) collective-permute-start(bf16[4,128,1024]{2,1,0:T(8,128)(2,1)S(1)} %fusion.39), channel_id=1, source_target_pairs={{0,16},{16,0},{1,17},{17,1},{2,18},{18,2},{3,19},{19,3},{4,20},{20... | collective-permute-start | bytes 3145736 | tf_op jit(solution)/shard_map/ppermute | solution.py:32
  621.5 52.2 %all-to-all-start.9 = ((bf16[4,128,2048]{2,1,0:T(8,128)(2,1)}), bf16[4,128,2048]{2,1,0:T(8,128)(2,1)S(1)}, u32[]{:S(2)}, u32[]{:S(2)}) async-start(bf16[4,128,2048]{2,1,0:T(8,128)(2,1)} %pad_maximum_fusion.10), calls=%async_computation.9 | async-start | bytes 4194304 | tf_op jit(solution)/shard_map/all_to_all | solution.py:490
  625.1 47.4 %collective-permute-start.24 = (bf16[2,4,128,1024]{3,2,1,0:T(8,128)(2,1)}, bf16[2,4,128,1024]{3,2,1,0:T(8,128)(2,1)}, u32[]{:S(2)}, u32[]{:S(2)}) collective-permute-start(bf16[2,4,128,1024]{3,2,1,0:T(8,128)(2,1)} %get-tuple-element.113), channel_id=1, source_target_pairs={{0,8},{4,12},{8,0},{12,4},{1,9},{5,13},{9,1},{13,5},{2,10},{6,14},... | collective-permute-start | bytes 6291464 | tf_op jit(solution)/shard_map/ppermute | solution.py:32
  626.6 47.1 %collective-permute-start.25 = (bf16[2,4,128,1024]{3,2,1,0:T(8,128)(2,1)}, bf16[2,4,128,1024]{3,2,1,0:T(8,128)(2,1)}, u32[]{:S(2)}, u32[]{:S(2)}) collective-permute-start(bf16[2,4,128,1024]{3,2,1,0:T(8,128)(2,1)} %get-tuple-element.114), channel_id=1, source_target_pairs={{0,16},{16,0},{1,17},{17,1},{2,18},{18,2},{3,19},{19,3},{4,20},{20... | collective-permute-start | bytes 6291464 | tf_op jit(solution)/shard_map/ppermute | solution.py:32
  639.0 35.1 %copy-start.41 = (f32[128,2048]{1,0:T(8,128)S(1)}, f32[128,2048]{1,0:T(8,128)}, u32[]{:S(2)}) copy-start(f32[128,2048]{1,0:T(8,128)} %copy-done.40) | copy-start | bytes 3145732
  639.0 35.1 %copy-start.90 = (f32[2048]{0:T(1024)S(1)}, f32[2048]{0:T(1024)}, u32[]{:S(2)}) copy-start(f32[2048]{0:T(1024)} %copy-done.89) | copy-start | bytes 24580
  639.0 35.1 %copy-start.101 = (f32[128]{0:T(128)S(1)}, f32[128]{0:T(128)}, u32[]{:S(2)}) copy-start(f32[128]{0:T(128)} %copy-done.100) | copy-start | bytes 1540
  677.2 12.3 %collective-permute-start.29 = (bf16[128,2048]{1,0:T(8,128)(2,1)S(1)}, bf16[128,2048]{1,0:T(8,128)(2,1)S(1)}, u32[]{:S(2)}, u32[]{:S(2)}) collective-permute-start(bf16[128,2048]{1,0:T(8,128)(2,1)S(1)} %get-tuple-element.186), channel_id=1, source_target_pairs={{0,8},{4,12},{8,0},{12,4},{1,9},{5,13},{9,1},{13,5},{2,10},{6,14},... | collective-permute-start | bytes 1572872 | tf_op jit(solution)/shard_map/ppermute | solution.py:32
  678.1 19.4 %collective-permute-start.28 = (bf16[128,2048]{1,0:T(8,128)(2,1)S(1)}, bf16[128,2048]{1,0:T(8,128)(2,1)}, u32[]{:S(2)}, u32[]{:S(2)}) collective-permute-start(bf16[128,2048]{1,0:T(8,128)(2,1)S(1)} %get-tuple-element.186), channel_id=1, source_target_pairs={{0,4},{4,0},{8,12},{12,8},{1,5},{5,1},{9,13},{13,9},{2,6},{6,2},{1... | collective-permute-start | bytes 1572872 | tf_op jit(solution)/shard_map/ppermute | solution.py:32
  678.1 53.6 %all-to-all-start.10 = ((bf16[4,512,512]{2,1,0:T(8,128)(2,1)}), bf16[4,512,512]{2,1,0:T(8,128)(2,1)S(1)}, u32[]{:S(2)}, u32[]{:S(2)}) async-start(bf16[4,512,512]{2,1,0:T(8,128)(2,1)} %bitcast.438), calls=%async_computation.10 | async-start | bytes 4194304 | tf_op jit(solution)/shard_map/all_to_all | solution.py:490
  689.6 7.9 collective-permute-start.30
  691.5 29.2 %collective-permute-start.27 = (bf16[4,128,1024]{2,1,0:T(8,128)(2,1)S(1)}, bf16[4,128,1024]{2,1,0:T(8,128)(2,1)}, u32[]{:S(2)}, u32[]{:S(2)}) collective-permute-start(bf16[4,128,1024]{2,1,0:T(8,128)(2,1)S(1)} %fusion.44), channel_id=1, source_target_pairs={{0,8},{4,12},{8,0},{12,4},{1,9},{5,13},{9,1},{13,5},{2,10},{6,14},... | collective-permute-start | bytes 3145736 | tf_op jit(solution)/shard_map/ppermute | solution.py:32
  695.7 25.7 %collective-permute-start.26 = (bf16[4,128,1024]{2,1,0:T(8,128)(2,1)}, bf16[4,128,1024]{2,1,0:T(8,128)(2,1)}, u32[]{:S(2)}, u32[]{:S(2)}) collective-permute-start(bf16[4,128,1024]{2,1,0:T(8,128)(2,1)} %fusion.43), channel_id=1, source_target_pairs={{0,16},{16,0},{1,17},{17,1},{2,18},{18,2},{3,19},{19,3},{4,20},{20... | collective-permute-start | bytes 3145736 | tf_op jit(solution)/shard_map/ppermute | solution.py:32
  720.5 34.9 %collective-permute-start.31 = (bf16[1,4,4,64,512]{4,3,1,2,0:T(8,128)(2,1)}, bf16[1,4,4,64,512]{4,3,1,2,0:T(8,128)(2,1)}, u32[]{:S(2)}, u32[]{:S(2)}) collective-permute-start(bf16[1,4,4,64,512]{4,3,1,2,0:T(8,128)(2,1)} %fusion.46), channel_id=1, source_target_pairs={{0,16},{16,0},{1,17},{17,1},{2,18},{18,2},{3,19},{19,3},{4,20},{20... | collective-permute-start | bytes 3145736 | tf_op jit(solution)/shard_map/ppermute | solution.py:32
  733.1 52.5 %all-to-all-start.11 = ((bf16[4,128,2048]{2,1,0:T(8,128)(2,1)}), bf16[4,128,2048]{2,1,0:T(8,128)(2,1)}, u32[]{:S(2)}, u32[]{:S(2)}) async-start(bf16[4,128,2048]{2,1,0:T(8,128)(2,1)} %pad_maximum_fusion.12), calls=%async_computation.11 | async-start | bytes 4194304 | tf_op jit(solution)/shard_map/all_to_all | solution.py:490
  739.3 28.9 %collective-permute-start.32 = (bf16[1,4,64,2048]{3,2,1,0:T(8,128)(2,1)S(1)}, bf16[1,4,64,2048]{3,2,1,0:T(8,128)(2,1)S(1)}, u32[]{:S(2)}, u32[]{:S(2)}) collective-permute-start(bf16[1,4,64,2048]{3,2,1,0:T(8,128)(2,1)S(1)} %fusion.35), channel_id=1, source_target_pairs={{0,16},{16,0},{1,17},{17,1},{2,18},{18,2},{3,19},{19,3},{4,20},{20... | collective-permute-start | bytes 3145736 | tf_op jit(solution)/shard_map/ppermute | solution.py:32
  785.7 28.7 %all-to-all-start.12 = ((bf16[4,64,2048]{2,1,0:T(8,128)(2,1)}), bf16[4,64,2048]{2,1,0:T(8,128)(2,1)S(1)}, u32[]{:S(2)}, u32[]{:S(2)}) async-start(bf16[4,64,2048]{2,1,0:T(8,128)(2,1)} %fusion.37), calls=%async_computation.12 | async-start | bytes 2097152 | tf_op jit(solution)/shard_map/all_to_all | solution.py:490
  794.9 23.7 %collective-permute-start.33 = (bf16[2,128,2048]{2,1,0:T(8,128)(2,1)S(1)}, bf16[2,128,2048]{2,1,0:T(8,128)(2,1)}, u32[]{:S(2)}, u32[]{:S(2)}) collective-permute-start(bf16[2,128,2048]{2,1,0:T(8,128)(2,1)S(1)} %fusion.48), channel_id=1, source_target_pairs={{0,4},{4,0},{8,12},{12,8},{1,5},{5,1},{9,13},{13,9},{2,6},{6,2},{1... | collective-permute-start | bytes 3145736 | tf_op jit(solution)/shard_map/ppermute | solution.py:32
  800.1 47.8 %collective-permute-start.35 = (bf16[1,4,4,64,1024]{4,3,1,2,0:T(8,128)(2,1)}, bf16[1,4,4,64,1024]{4,3,1,2,0:T(8,128)(2,1)}, u32[]{:S(2)}, u32[]{:S(2)}) collective-permute-start(bf16[1,4,4,64,1024]{4,3,1,2,0:T(8,128)(2,1)} %dynamic-slice_convert_fusion), channel_id=1, source_target_pairs={{0,16},{16,0},{1,17},{17,1},{2,18},{18,2},{3,19},{19,3},{4,20},{20... | collective-permute-start | bytes 6291464 | tf_op jit(solution)/shard_map/ppermute | solution.py:32
  814.4 29.5 %all-to-all-start.13 = ((bf16[4,4,64,512]{3,2,1,0:T(8,128)(2,1)}), bf16[4,4,64,512]{3,2,1,0:T(8,128)(2,1)}, u32[]{:S(2)}, u32[]{:S(2)}) async-start(bf16[4,4,64,512]{3,2,1,0:T(8,128)(2,1)} %fusion.36), calls=%async_computation.13 | async-start | bytes 2097152 | tf_op jit(solution)/shard_map/all_to_all | solution.py:490
  821.8 13.2 %collective-permute-start.34 = (bf16[128,2048]{1,0:T(8,128)(2,1)}, bf16[128,2048]{1,0:T(8,128)(2,1)}, u32[]{:S(2)}, u32[]{:S(2)}) collective-permute-start(bf16[128,2048]{1,0:T(8,128)(2,1)} %fusion.54), channel_id=1, source_target_pairs={{0,8},{4,12},{8,0},{12,4},{1,9},{5,13},{9,1},{13,5},{2,10},{6,14},... | collective-permute-start | bytes 1572872 | tf_op jit(solution)/shard_map/ppermute | solution.py:32
  843.9 12.8 %all-to-all-start.16 = ((f32[32,1,1280]{2,1,0:T(1,128)}), f32[32,1,1280]{2,1,0:T(1,128)S(1)}, u32[]{:S(2)}, u32[]{:S(2)}) async-start(f32[32,1,1280]{2,1,0:T(1,128)} %copy.131), calls=%async_computation.16 | async-start | bytes 327680 | tf_op jit(solution)/shard_map/all_to_all | solution.py:820
  856.7 52.6 %all-to-all-start.14 = ((bf16[4,4,64,1024]{3,2,1,0:T(8,128)(2,1)}), bf16[4,4,64,1024]{3,2,1,0:T(8,128)(2,1)}, u32[]{:S(2)}, u32[]{:S(2)}) async-start(bf16[4,4,64,1024]{3,2,1,0:T(8,128)(2,1)} %fusion.12), calls=%async_computation.14 | async-start | bytes 4194304 | tf_op jit(solution)/shard_map/all_to_all | solution.py:490
  912.3 16.2 %all-to-all-start.15 = ((bf16[4,64,1536]{2,1,0:T(8,128)(2,1)}), bf16[4,64,1536]{2,1,0:T(8,128)(2,1)}, u32[]{:S(2)}, u32[]{:S(2)}) async-start(bf16[4,64,1536]{2,1,0:T(8,128)(2,1)} %pad_maximum_fusion.16), calls=%async_computation.15 | async-start | bytes 1572864 | tf_op jit(solution)/shard_map/all_to_all | solution.py:807
  (102 other events, 771.7 us)
Sparse Core Ops, SparseCore 0:
  36.6 126.0 all-gather.2
  245.3 166.7 all-gather.4

commit v6 on v5

--- a/solution.py
+++ b/solution.py
@@ -83,6 +83,10 @@
             )
         )
     return jnp.concatenate(rows, axis=0)
+
+
+def context_sum(value):
+    return jnp.sum(lax.all_gather(value, "context"), axis=0)
 
 
 def half_step(value, axis, bit, dim):
@@ -674,9 +678,9 @@
     ).reshape(2, cols)
     raw_q, raw_k = qkv[:, :cols], qkv[:, cols : 2 * cols]
     squares = jnp.stack([jnp.sum(raw_q * raw_q, axis=1), jnp.sum(raw_k * raw_k, axis=1)])
-    scale_qk = lax.rsqrt(lax.psum(squares, "context") / width + epsilon).T
+    scale_qk = lax.rsqrt(context_sum(squares) / width + epsilon).T
     query, key, value, mixed = mix(qkv, scale_qk, my_gains, cos_all, sin_all, spots, local_heads)
-    hidden = inputs + context_scatter(mm(after(mixed, w_down), wo_all))
+    hidden = after(inputs + context_scatter(mm(mixed, wo_all)), w_down)
     scale_two = lax.rsqrt(jnp.mean(hidden * hidden, axis=-1, keepdims=True) + epsilon)
     normed_two = (hidden * scale_two * gains[1]).astype(bf16)
     logits = mm(normed_two, router_w)
@@ -715,7 +719,7 @@
     )
     sent_gates = jnp.sum(jnp.where(hits[:, :, None], sent_gates[None], 0.0), axis=1)
     got_gates = lax.all_to_all(sent_gates, EVERY, 0, 0, tiled=True)
-    grad_wd, got_gates = tie(grad_wd, got_gates)
+    grad_wd, got_gates, act = tie(grad_wd, got_gates, act)
     grad_probs = jnp.sum(got_gates.reshape(expert_count, halves, tok_rows), axis=1).T
     down_got = exchange(grad_wd.reshape(z_count, -1, ffh))
     n2_sum.begin(n2_keep)
@@ -723,8 +727,7 @@
     n_late, down_got = tie(n_rows, down_got)
     grad_wg = mm_tn(n_late, grad_gu[:, :ffh]).astype(bf16)
     gate_got = exchange(grad_wg.reshape(z_count, -1, ffh))
-    act, n_late = n2_sum.require(act, n_late)
-    act, grad_wg = tie(act, grad_wg)
+    (n_late,) = n2_sum.require(n_late)
     y_sum = Scatter(expert_output(act, gate, w_down, slot_of, slot_cap, 1), tok_rows)
     y_keep = expert_output(act, gate, w_down, slot_of, slot_cap, 0)
     n_late, y_keep = tie(n_late, y_keep)
@@ -767,7 +770,7 @@
         wo_send = halved(grad_wo.reshape(e_count, z_count, w_rows, width))
     v_send = halved(weight_blocks(normed_one, grad_v)).transpose(1, 0, 2, 3)
     (inner,) = y_sum.require(inner)
-    inner = lax.psum(inner.T, "context")
+    inner = context_sum(inner.T)
     if aligned:
         inner, v_send, wo_send = tie(inner, v_send, wo_send)
     inner = inner.T / width

time: 954 us -> 934 us (0.979)
  blocking collectives: 29.5 us -> 10.6 us
  waiting for transfers between devices: 401 us -> 411 us
    psum x2 -> x0, blocking collectives: 29.5 us -> none  [the longest x1 15.2 us: on_device(): scale_qk = lax.rsqrt(lax.psum(squares, 'context') / width + epsilon).T]
    ppermute x30, waiting for transfers between devices: 160 us -> 177 us  [swap(): return lax.ppermute(value, axis, [(i, i ^ bit) for i in range(count)])]
    all_gather x1, waiting for transfers between devices: 26.9 us -> 9.24 us  [on_device(): wqkv_all = packed = lax.all_gather(wqkv, around, axis=0, tiled=True)]
    all_gather x0 -> x2, blocking collectives: none -> 10.6 us  [context_sum(): return jnp.sum(lax.all_gather(value, 'context'), axis=0)]
    unnamed x227 -> x222, local copies, waits for them, and re-layouts: 37.8 us -> 33.8 us
  transfers between devices with their start and end apart: 55 -> 55, of which waited for: 29 -> 31; matrix products, arithmetic and copies ran while one was open for 22% -> 22% of each run, Pallas kernels for 9% -> 9%
where the time goes in v6:
time: 934 us; the launch traced here: 924 us
  waiting for transfers between devices  411 us (44%)
  Pallas kernels  117 us (13%)
  other arithmetic  115 us (12%)
  starting transfers between devices  111 us (12%)
  local copies, waits for them, and re-layouts  78 us (8%)
  matrix products  64.5 us (7%)
  between operations  16.3 us (2%)
  blocking collectives  10.6 us (1%)
    ppermute x30, waiting for transfers between devices, swap(): return lax.ppermute(value, axis, [(i, i ^ bit) for i in range(count)])  177 us
    all_to_all x11, waiting for transfers between devices, exchange(): return lax.all_to_all(after(blocks, *done), 'dp', 0, 0, tiled=True)  135 us
    all_to_all x11, starting transfers between devices, exchange(): return lax.all_to_all(after(blocks, *done), 'dp', 0, 0, tiled=True)  47.2 us
    pallas_call x2, Pallas kernels, run_expert(): pl.pallas_call(lambda *refs: expert_kernel(per, slot_cap, *refs), grid_sp...  43.1 us
    dot_general x7, matrix products, mm_tn(): lax.dot_general(a, b, (((0,), (0,)), ((), ())), preferred_element_type=f32)  42.6 us
    ppermute x6, waiting for transfers between devices, shift(): lax.ppermute(value, axis, [(i, (i + step) % count) for i in range(count)])  36.5 us
    unnamed x222, local copies, waits for them, and re-layouts  33.8 us
    ppermute x30, starting transfers between devices, swap(): return lax.ppermute(value, axis, [(i, i ^ bit) for i in range(count)])  26.5 us
  transfers between devices with their start and end apart: 55, of which 31 were waited for; matrix products, arithmetic and copies ran while one was open for 22% of the time, Pallas kernels for 9%

profile of v6, /device:TPU:0, one launch (start us, length us, event | category | flops | bytes accessed | tf_op | source)
XLA Modules:
  0.0 923.8 jit_solution(263515777261887725)
XLA Ops:
  14.2 4.4 all-to-all-start
  21.0 14.5 %collective-permute-done.7 = bf16[128,2048]{1,0:T(8,128)(2,1)S(1)} collective-permute-done((bf16[128,2048]{1,0:T(8,128)(2,1)S(1)}, bf16[128,2048]{1,0:T(8,128)(2,1)S(1)}, u32[]{:S(2)}, u32[]{:S(2)}) %collective-permute-start.7) | collective-permute-done | bytes 524320 | tf_op jit(solution)/shard_map/ppermute | solution.py:37
  42.3 5.3 copy-done.6
  47.7 13.5 %shard_map.136 = (bf16[4,512,512]{2,1,0:T(8,128)(2,1)}, bf16[4,512,512]{2,1,0:T(8,128)(2,1)}, bf16[4,512,512]{2,1,0:T(8,128)(2,1)S(1)}) custom-call(f32[512,2,3072]{2,1,0:T(2,128)S(1)} %copy-done.6), custom_call_target="tpu_custom_call" | custom-call | flops 1 | bytes 1 | tf_op jit(solution)/shard_map/pallas_call | solution.py:510
  68.3 12.9 %collective-permute-done.4 = bf16[64,2048]{1,0:T(8,128)(2,1)S(1)} collective-permute-done((bf16[64,2048]{1,0:T(8,128)(2,1)}, bf16[64,2048]{1,0:T(8,128)(2,1)S(1)}, u32[]{:S(2)}, u32[]{:S(2)}) %collective-permute-start.4) | collective-permute-done | bytes 262176 | tf_op jit(solution)/shard_map/ppermute | solution.py:37
  84.7 5.3 all-to-all-start.1
  90.0 21.2 %all-to-all-done.1 = bf16[32,2,704]{2,1,0:T(2,128)(2,1)S(1)} async-done(((bf16[32,2,704]{2,1,0:T(2,128)(2,1)}), bf16[32,2,704]{2,1,0:T(2,128)(2,1)S(1)}, u32[]{:S(2)}, u32[]{:S(2)}) %all-to-all-start.1) | async-done | bytes 90144 | tf_op jit(solution)/shard_map/all_to_all | solution.py:626
  119.1 7.9 collective-permute-start.9
  129.3 4.3 fusion.4
  133.6 10.6 %collective-permute-done.6 = bf16[4,64,2048]{2,1,0:T(8,128)(2,1)S(1)} collective-permute-done((bf16[4,64,2048]{2,1,0:T(8,128)(2,1)S(1)}, bf16[4,64,2048]{2,1,0:T(8,128)(2,1)S(1)}, u32[]{:S(2)}, u32[]{:S(2)}) %collective-permute-start.6) | collective-permute-done | bytes 1048608 | tf_op jit(solution)/shard_map/ppermute | solution.py:32
  144.3 9.1 collective-permute-done.9
  153.4 9.2 all-gather.7.cloned.1.call-done
  170.0 5.2 all-gather.2
  175.4 4.5 all-to-all-start.2
  182.8 7.1 shard_map.137
  199.9 13.5 %collective-permute-done.11 = bf16[128,2048]{1,0:T(8,128)(2,1)S(1)} collective-permute-done((bf16[128,2048]{1,0:T(8,128)(2,1)S(1)}, bf16[128,2048]{1,0:T(8,128)(2,1)S(1)}, u32[]{:S(2)}, u32[]{:S(2)}) %collective-permute-start.11) | collective-permute-done | bytes 524320 | tf_op jit(solution)/shard_map/ppermute | solution.py:32
  215.4 13.4 %all-to-all-done.2 = bf16[4,512,512]{2,1,0:T(8,128)(2,1)} async-done(((bf16[4,512,512]{2,1,0:T(8,128)(2,1)}), bf16[4,512,512]{2,1,0:T(8,128)(2,1)}, u32[]{:S(2)}, u32[]{:S(2)}) %all-to-all-start.2) | async-done | bytes 2097184 | tf_op jit(solution)/shard_map/all_to_all | solution.py:494
  240.2 21.8 %collective-permute-done.12 = bf16[1,1,4,128,1024]{4,3,2,1,0:T(8,128)(2,1)} collective-permute-done((bf16[1,1,4,128,1024]{4,3,2,1,0:T(8,128)(2,1)}, bf16[1,1,4,128,1024]{4,3,2,1,0:T(8,128)(2,1)}, u32[]{:S(2)}, u32[]{:S(2)}) %collective-permute-start.12) | collective-permute-done | bytes 1048608 | tf_op jit(solution)/shard_map/ppermute | solution.py:32
  267.7 49.7 %collective-permute-done.13 = bf16[2,1,4,128,1024]{4,3,2,1,0:T(8,128)(2,1)S(1)} collective-permute-done((bf16[2,1,4,128,1024]{4,3,2,1,0:T(8,128)(2,1)S(1)}, bf16[2,1,4,128,1024]{4,3,2,1,0:T(8,128)(2,1)S(1)}, u32[]{:S(2)}, u32[]{:S(2)}) %collective-permute-start.13) | collective-permute-done | bytes 2097184 | tf_op jit(solution)/shard_map/ppermute | solution.py:32
  320.9 9.9 %collective-permute-done.15 = bf16[1,2,4,128,1024]{4,3,2,1,0:T(8,128)(2,1)S(1)} collective-permute-done((bf16[1,2,4,128,1024]{4,3,2,1,0:T(8,128)(2,1)S(1)}, bf16[1,2,4,128,1024]{4,3,2,1,0:T(8,128)(2,1)S(1)}, u32[]{:S(2)}, u32[]{:S(2)}) %collective-permute-start.15) | collective-permute-done | bytes 2097184 | tf_op jit(solution)/shard_map/ppermute | solution.py:32
  338.8 7.3 all-to-all-done.5
  346.1 4.9 all-to-all-start.4
  365.0 7.6 shard_map.139
  374.8 10.6 %fusion.1.refs_12_ = f32[2304,512]{1,0:T(8,128)} fusion(bf16[2048,512]{1,0:T(8,128)(2,1)} %bitcast.124.refs_3_, bf16[1152,2048]{1,0:T(8,128)(2,1)S(1)} %shard_map.139, bf16[1152,2048]{1,0:T(8,128)(2,1)S(1)} %bitcast.392), kind=kOutput, calls=%fused_computation.4 | convolution fusion | flops 4850712576 | bytes 16252928 | tf_op jit(solution)/shard_map/dot_general | solution.py:19
  385.4 10.7 %all-gather.9.cloned.1.call-done = bf16[4096,2048]{1,0:T(8,128)(2,1)} async-done(((bf16[128,2048]{1,0:T(8,128)(2,1)}), bf16[4096,2048]{1,0:T(8,128)(2,1)}) %all-gather.9.cloned.1.call-update) | async-done | bytes 16777232 | tf_op jit(solution)/shard_map/all_gather | solution.py:690
  396.1 21.9 %all-to-all-done.4 = bf16[4,512,512]{2,1,0:T(8,128)(2,1)} async-done(((bf16[4,512,512]{2,1,0:T(8,128)(2,1)}), bf16[4,512,512]{2,1,0:T(8,128)(2,1)}, u32[]{:S(2)}, u32[]{:S(2)}) %all-to-all-start.4) | async-done | bytes 2097184 | tf_op jit(solution)/shard_map/all_to_all | solution.py:494
  418.0 21.5 %shard_map.140 = (bf16[2304,2048]{1,0:T(8,128)(2,1)}, bf16[2304,512]{1,0:T(8,128)(2,1)}, bf16[2304,512]{1,0:T(8,128)(2,1)}, bf16[2304,1024]{1,0:T(8,128)(2,1)}, ...) custom-call(s32[32]{0:T(128)} %stack.310.refs_0_, s32[32,1,128]{2,1,0:T(1,128)} %bitcast.393, ...), custom_call_target="tpu_custom_call" | custom-call | flops 1 | bytes 1 | tf_op jit(solution)/shard_map/pallas_call | solution.py:476
  439.6 21.5 %shard_map.141 = (bf16[2304,2048]{1,0:T(8,128)(2,1)}, bf16[2304,512]{1,0:T(8,128)(2,1)}, bf16[2304,512]{1,0:T(8,128)(2,1)}, bf16[2304,1024]{1,0:T(8,128)(2,1)}, ...) custom-call(s32[32]{0:T(128)} %stack.310.refs_0_, ...), custom_call_target="tpu_custom_call", output_to_operand_aliasing={{0}: (14, {}), {1}: (15, {}), {2}: (16, {}), {3}: (17, {}),... | custom-call | flops 1 | bytes 1 | tf_op jit(solution)/shard_map/pallas_call | solution.py:476
  464.2 3.9 all-to-all-start.6
  468.1 9.5 %fusion.5 = bf16[2048,512]{1,0:T(8,128)(2,1)} fusion(bf16[2304,512]{1,0:T(8,128)(2,1)} %get-tuple-element.94, bf16[1152,2048]{1,0:T(8,128)(2,1)} %copy-done.12, bf16[1152,2048]{1,0:T(8,128)(2,1)} %copy-done.11), kind=kOutput, calls=%fused_computation.24 | convolution fusion | flops 4851761152 | bytes 13893632 | tf_op jit(solution)/shard_map/dot_general | solution.py:27
  477.6 8.6 shard_map.143
  486.4 5.2 all-to-all-start.7
  491.7 5.8 add_convert_fusion.4
  498.9 5.8 add_convert_fusion.5
  506.2 34.3 %all-to-all-done.7.refs_2_ = bf16[4,512,512]{2,1,0:T(8,128)(2,1)} async-done(((bf16[4,512,512]{2,1,0:T(8,128)(2,1)}), bf16[4,512,512]{2,1,0:T(8,128)(2,1)}, u32[]{:S(2)}, u32[]{:S(2)}) %all-to-all-start.7) | async-done | bytes 2097184 | tf_op jit(solution)/shard_map/all_to_all | solution.py:494
  540.5 10.7 %convolution_convert_fusion.1 = bf16[2048,512]{1,0:T(8,128)(2,1)} fusion(bf16[2304,2048]{1,0:T(8,128)(2,1)} %get-tuple-element.116, bf16[2304,1024]{1,0:T(8,128)(2,1)} %get-tuple-element.114), kind=kOutput, calls=%fused_computation.26 | convolution fusion | flops 4832886784 | bytes 13893632 | tf_op jit(solution)/shard_map/dot_general | solution.py:27
  551.2 4.5 all-to-all-start.8
  562.6 8.6 shard_map.142
  571.2 5.9 add_convert_fusion.1
  578.6 4.9 fusion.10
  590.6 13.0 %all-to-all-done.8.refs_0_ = bf16[4,512,512]{2,1,0:T(8,128)(2,1)} async-done(((bf16[4,512,512]{2,1,0:T(8,128)(2,1)}), bf16[4,512,512]{2,1,0:T(8,128)(2,1)}, u32[]{:S(2)}, u32[]{:S(2)}) %all-to-all-start.8) | async-done | bytes 2097184 | tf_op jit(solution)/shard_map/all_to_all | solution.py:494
  603.6 3.8 all-to-all-start.9
  611.3 10.7 %convolution_convert_fusion = bf16[2048,512]{1,0:T(8,128)(2,1)} fusion(bf16[2304,2048]{1,0:T(8,128)(2,1)} %get-tuple-element.116, bf16[2304,1024]{1,0:T(8,128)(2,1)} %get-tuple-element.114), kind=kOutput, calls=%fused_computation.25 | convolution fusion | flops 4832886784 | bytes 13893632 | tf_op jit(solution)/shard_map/dot_general | solution.py:27
  622.1 32.2 %collective-permute-done.24 = bf16[2,4,128,1024]{3,2,1,0:T(8,128)(2,1)} collective-permute-done((bf16[2,4,128,1024]{3,2,1,0:T(8,128)(2,1)}, bf16[2,4,128,1024]{3,2,1,0:T(8,128)(2,1)}, u32[]{:S(2)}, u32[]{:S(2)}) %collective-permute-start.24) | collective-permute-done | bytes 2097184 | tf_op jit(solution)/shard_map/ppermute | solution.py:32
  660.2 4.1 all-to-all-start.10
  664.4 7.1 collective-permute-done.29
  684.8 15.8 %shard_map.144 = (f32[512,512]{1,0:T(8,128)S(1)}, f32[512,512]{1,0:T(8,128)S(1)}, bf16[512,512]{1,0:T(8,128)(2,1)S(1)}, f32[2,512]{1,0:T(2,128)S(1)}, f32[512,2]{1,0:T(8,128)S(1)}) custom-call(f32[512,1536]{1,0:T(8,128)} %copy-done, f32[512,1536]{1,0:T(8,128)} %copy-done, f32[512,2]{1,0:T(8,128)S(1)} %bitcast.389, f32[2,512]{1,0:T(2,128)S(1)} %bitcast.400, ...), custom_call_target="tpu_custom_call" | custom-call | flops 1 | bytes 1 | tf_op jit(solution)/shard_map/pallas_call | solution.py:408
  715.1 4.4 all-to-all-start.11
  723.8 5.4 all-gather.3
  733.3 17.7 %collective-permute-done.32 = bf16[1,4,64,2048]{3,2,1,0:T(8,128)(2,1)} collective-permute-done((bf16[1,4,64,2048]{3,2,1,0:T(8,128)(2,1)}, bf16[1,4,64,2048]{3,2,1,0:T(8,128)(2,1)}, u32[]{:S(2)}, u32[]{:S(2)}) %collective-permute-start.32) | collective-permute-done | bytes 1048608 | tf_op jit(solution)/shard_map/ppermute | solution.py:32
  759.5 5.8 fusion.49
  771.0 5.6 fusion.100
  776.8 5.1 dynamic-slice_convert_fusion
  783.5 12.7 %all-to-all-done.12 = bf16[4,64,2048]{2,1,0:T(8,128)(2,1)S(1)} async-done(((bf16[4,64,2048]{2,1,0:T(8,128)(2,1)}), bf16[4,64,2048]{2,1,0:T(8,128)(2,1)S(1)}, u32[]{:S(2)}, u32[]{:S(2)}) %all-to-all-start.12) | async-done | bytes 1048608 | tf_op jit(solution)/shard_map/all_to_all | solution.py:494
  796.2 4.2 all-to-all-start.13
  808.3 8.5 collective-permute-done.34
  819.3 6.4 all-to-all-done.13
  829.2 4.9 fusion.12
  834.1 3.9 all-to-all-done.16
  838.0 4.4 all-to-all-start.14
  842.5 9.1 shard_map.145
  859.0 31.6 %all-to-all-done.14 = bf16[4,4,64,1024]{3,2,1,0:T(8,128)(2,1)} async-done(((bf16[4,4,64,1024]{3,2,1,0:T(8,128)(2,1)}), bf16[4,4,64,1024]{3,2,1,0:T(8,128)(2,1)}, u32[]{:S(2)}, u32[]{:S(2)}) %all-to-all-start.14) | async-done | bytes 2097184 | tf_op jit(solution)/shard_map/all_to_all | solution.py:494
  893.6 4.6 all-to-all-start.15
  900.3 9.6 %all-to-all-done.15 = bf16[4,64,1536]{2,1,0:T(8,128)(2,1)} async-done(((bf16[4,64,1536]{2,1,0:T(8,128)(2,1)}), bf16[4,64,1536]{2,1,0:T(8,128)(2,1)}, u32[]{:S(2)}, u32[]{:S(2)}) %all-to-all-start.15) | async-done | bytes 786464 | tf_op jit(solution)/shard_map/all_to_all | solution.py:810
  (467 shorter events, 219.7 us)
Async XLA Ops:
  8.9 29.4 %copy-start.63 = (bf16[64,8192]{1,0:T(8,128)(2,1)}, bf16[64,8192]{1,0:T(8,128)(2,1)S(1)}, u32[]{:S(2)}) copy-start(bf16[64,8192]{1,0:T(8,128)(2,1)S(1)} %convert.33) | copy-start | bytes 3145732
  14.2 25.4 %copy-start.104 = (s32[1,8]{1,0:T(1,128)S(1)}, s32[1,8]{1,0:T(1,128)}, u32[]{:S(2)}) copy-start(s32[1,8]{1,0:T(1,128)} %param.16) | copy-start | bytes 100
  14.2 21.4 %all-to-all-start = ((bf16[4,64,1536]{2,1,0:T(8,128)(2,1)}), bf16[4,64,1536]{2,1,0:T(8,128)(2,1)S(1)}, u32[]{:S(2)}, u32[]{:S(2)}) async-start(bf16[4,64,1536]{2,1,0:T(8,128)(2,1)} %reshape.1700), calls=%async_computation | async-start | bytes 1572864 | tf_op jit(solution)/shard_map/all_to_all | solution.py:624
  18.5 144.1 %all-gather.7.cloned.1.call-start = ((), (), s32[]{:S(2)}) async-start(), calls=%async_computation.17 | async-start | bytes 7077888 | tf_op jit(solution)/shard_map/all_gather | solution.py:644
  18.6 17.0 %collective-permute-start.7 = (bf16[128,2048]{1,0:T(8,128)(2,1)S(1)}, bf16[128,2048]{1,0:T(8,128)(2,1)S(1)}, u32[]{:S(2)}, u32[]{:S(2)}) collective-permute-start(bf16[128,2048]{1,0:T(8,128)(2,1)S(1)} %bitcast_convert_fusion.2), channel_id=1, source_target_pairs={{0,1},{1,2},{2,3},{3,0},{4,5},{5,6},{6,7},{7,4},{8,9},{9,10},{10,1... | collective-permute-start | bytes 1572872 | tf_op jit(solution)/shard_map/ppermute | solution.py:37
  36.5 44.7 %collective-permute-start.1 = (bf16[128,2048]{1,0:T(8,128)(2,1)S(1)}, bf16[128,2048]{1,0:T(8,128)(2,1)}, u32[]{:S(2)}, u32[]{:S(2)}) collective-permute-start(bf16[128,2048]{1,0:T(8,128)(2,1)S(1)} %bitcast.429), channel_id=1, source_target_pairs={{0,8},{4,12},{8,0},{12,4},{1,9},{5,13},{9,1},{13,5},{2,10},{6,14},... | collective-permute-start | bytes 1572872 | tf_op jit(solution)/shard_map/ppermute | solution.py:32
  38.3 88.7 %collective-permute-start = (bf16[128,2048]{1,0:T(8,128)(2,1)S(1)}, bf16[128,2048]{1,0:T(8,128)(2,1)}, u32[]{:S(2)}, u32[]{:S(2)}) collective-permute-start(bf16[128,2048]{1,0:T(8,128)(2,1)S(1)} %bitcast.430), channel_id=1, source_target_pairs={{0,4},{4,0},{8,12},{12,8},{1,5},{5,1},{9,13},{13,9},{2,6},{6,2},{1... | collective-permute-start | bytes 1572872 | tf_op jit(solution)/shard_map/ppermute | solution.py:32
  39.1 25.3 %collective-permute-start.3 = (bf16[64,2048]{1,0:T(8,128)(2,1)}, bf16[64,2048]{1,0:T(8,128)(2,1)}, u32[]{:S(2)}, u32[]{:S(2)}) collective-permute-start(bf16[64,2048]{1,0:T(8,128)(2,1)} %get-tuple-element.217), channel_id=1, source_target_pairs={{0,1},{1,2},{2,3},{3,0},{4,5},{5,6},{6,7},{7,4},{8,9},{9,10},{10,1... | collective-permute-start | bytes 786440 | tf_op jit(solution)/shard_map/ppermute | solution.py:37
  63.5 54.0 %copy-start.80 = (bf16[1,64,2048]{2,1,0:T(8,128)(2,1)S(1)}, bf16[1,64,2048]{2,1,0:T(8,128)(2,1)}, u32[]{:S(2)}) copy-start(bf16[1,64,2048]{2,1,0:T(8,128)(2,1)} %get-tuple-element.216) | copy-start | bytes 786436
  63.5 116.4 %copy-start.34 = (s32[2,512]{1,0:T(2,128)}, s32[2,512]{1,0:T(2,128)S(1)}, u32[]{:S(2)}) copy-start(s32[2,512]{1,0:T(2,128)S(1)} %get-tuple-element.232.refs_8_.refs_7_) | copy-start | bytes 12292
  64.4 16.8 %collective-permute-start.4 = (bf16[64,2048]{1,0:T(8,128)(2,1)}, bf16[64,2048]{1,0:T(8,128)(2,1)S(1)}, u32[]{:S(2)}, u32[]{:S(2)}) collective-permute-start(bf16[64,2048]{1,0:T(8,128)(2,1)} %collective-permute-done.3), channel_id=1, source_target_pairs={{0,1},{1,2},{2,3},{3,0},{4,5},{5,6},{6,7},{7,4},{8,9},{9,10},{10,1... | collective-permute-start | bytes 786440 | tf_op jit(solution)/shard_map/ppermute | solution.py:37
  66.7 52.4 %collective-permute-start.8 = (bf16[128,2048]{1,0:T(8,128)(2,1)}, bf16[128,2048]{1,0:T(8,128)(2,1)}, u32[]{:S(2)}, u32[]{:S(2)}) collective-permute-start(bf16[128,2048]{1,0:T(8,128)(2,1)} %copy-done.81), channel_id=1, source_target_pairs={{0,1},{1,2},{2,3},{3,0},{4,5},{5,6},{6,7},{7,4},{8,9},{9,10},{10,1... | collective-permute-start | bytes 1572872 | tf_op jit(solution)/shard_map/ppermute | solution.py:37
  81.2 36.3 %collective-permute-start.5 = (bf16[64,2048]{1,0:T(8,128)(2,1)S(1)}, bf16[64,2048]{1,0:T(8,128)(2,1)S(1)}, u32[]{:S(2)}, u32[]{:S(2)}) collective-permute-start(bf16[64,2048]{1,0:T(8,128)(2,1)S(1)} %collective-permute-done.4), channel_id=1, source_target_pairs={{0,1},{1,2},{2,3},{3,0},{4,5},{5,6},{6,7},{7,4},{8,9},{9,10},{10,1... | collective-permute-start | bytes 786440 | tf_op jit(solution)/shard_map/ppermute | solution.py:37
  81.2 45.8 %collective-permute-start.2 = (bf16[128,2048]{1,0:T(8,128)(2,1)}, bf16[128,2048]{1,0:T(8,128)(2,1)}, u32[]{:S(2)}, u32[]{:S(2)}) collective-permute-start(bf16[128,2048]{1,0:T(8,128)(2,1)} %collective-permute-done.1), channel_id=1, source_target_pairs={{0,4},{4,0},{8,12},{12,8},{1,5},{5,1},{9,13},{13,9},{2,6},{6,2},{1... | collective-permute-start | bytes 1572872 | tf_op jit(solution)/shard_map/ppermute | solution.py:32
  84.7 26.5 %all-to-all-start.1 = ((bf16[32,2,704]{2,1,0:T(2,128)(2,1)}), bf16[32,2,704]{2,1,0:T(2,128)(2,1)S(1)}, u32[]{:S(2)}, u32[]{:S(2)}) async-start(bf16[32,2,704]{2,1,0:T(2,128)(2,1)} %reshape.1782), calls=%async_computation.1 | async-start | bytes 196608 | tf_op jit(solution)/shard_map/all_to_all | solution.py:626
  117.4 62.5 %copy-start.36 = (f32[1,2,2,256]{3,1,2,0:T(2,128)}, f32[1,2,2,256]{3,1,2,0:T(2,128)S(1)}, u32[]{:S(2)}) copy-start(f32[1,2,2,256]{3,1,2,0:T(2,128)S(1)} %copy.196) | copy-start | bytes 12292
  118.6 25.6 %collective-permute-start.6 = (bf16[4,64,2048]{2,1,0:T(8,128)(2,1)S(1)}, bf16[4,64,2048]{2,1,0:T(8,128)(2,1)S(1)}, u32[]{:S(2)}, u32[]{:S(2)}) collective-permute-start(bf16[4,64,2048]{2,1,0:T(8,128)(2,1)S(1)} %pad_maximum_fusion.15), channel_id=1, source_target_pairs={{0,16},{16,0},{1,17},{17,1},{2,18},{18,2},{3,19},{19,3},{4,20},{20... | collective-permute-start | bytes 3145736 | tf_op jit(solution)/shard_map/ppermute | solution.py:32
  119.1 34.3 %collective-permute-start.9 = (bf16[128,2048]{1,0:T(8,128)(2,1)}, bf16[128,2048]{1,0:T(8,128)(2,1)}, u32[]{:S(2)}, u32[]{:S(2)}) collective-permute-start(bf16[128,2048]{1,0:T(8,128)(2,1)} %collective-permute-done.8), channel_id=1, source_target_pairs={{0,1},{1,2},{2,3},{3,0},{4,5},{5,6},{6,7},{7,4},{8,9},{9,10},{10,1... | collective-permute-start | bytes 1572872 | tf_op jit(solution)/shard_map/ppermute | solution.py:37
  175.4 53.5 %all-to-all-start.2 = ((bf16[4,512,512]{2,1,0:T(8,128)(2,1)}), bf16[4,512,512]{2,1,0:T(8,128)(2,1)}, u32[]{:S(2)}, u32[]{:S(2)}) async-start(bf16[4,512,512]{2,1,0:T(8,128)(2,1)} %copy-done.19), calls=%async_computation.2 | async-start | bytes 4194304 | tf_op jit(solution)/shard_map/all_to_all | solution.py:494
  179.9 216.3 %all-gather.9.cloned.1.call-start = ((), (), s32[]{:S(2)}) async-start(), calls=%async_computation.18 | async-start | bytes 17301504 | tf_op jit(solution)/shard_map/all_gather | solution.py:690
  193.3 2.7 collective-permute-start.10
  199.2 14.2 %collective-permute-start.11 = (bf16[128,2048]{1,0:T(8,128)(2,1)S(1)}, bf16[128,2048]{1,0:T(8,128)(2,1)S(1)}, u32[]{:S(2)}, u32[]{:S(2)}) collective-permute-start(bf16[128,2048]{1,0:T(8,128)(2,1)S(1)} %fusion.53), channel_id=1, source_target_pairs={{0,8},{4,12},{8,0},{12,4},{1,9},{5,13},{9,1},{13,5},{2,10},{6,14},... | collective-permute-start | bytes 1572872 | tf_op jit(solution)/shard_map/ppermute | solution.py:32
  199.9 29.1 %copy-start.88 = (f32[2048]{0:T(1024)}, f32[2048]{0:T(1024)S(1)}, u32[]{:S(2)}) copy-start(f32[2048]{0:T(1024)S(1)} %mul.344) | copy-start | bytes 24580
  233.4 28.6 %collective-permute-start.12 = (bf16[1,1,4,128,1024]{4,3,2,1,0:T(8,128)(2,1)}, bf16[1,1,4,128,1024]{4,3,2,1,0:T(8,128)(2,1)}, u32[]{:S(2)}, u32[]{:S(2)}) collective-permute-start(bf16[1,1,4,128,1024]{4,3,2,1,0:T(8,128)(2,1)} %maximum_bitcast_fusion), channel_id=1, source_target_pairs={{0,8},{4,12},{8,0},{12,4},{1,9},{5,13},{9,1},{13,5},{2,10},{6,14},... | collective-permute-start | bytes 3145736 | tf_op jit(solution)/shard_map/ppermute | solution.py:32
  235.1 30.2 %collective-permute-start.14 = (bf16[1,1,4,128,1024]{4,3,2,1,0:T(8,128)(2,1)}, bf16[1,1,4,128,1024]{4,3,2,1,0:T(8,128)(2,1)}, u32[]{:S(2)}, u32[]{:S(2)}) collective-permute-start(bf16[1,1,4,128,1024]{4,3,2,1,0:T(8,128)(2,1)} %maximum_bitcast_fusion.1), channel_id=1, source_target_pairs={{0,16},{16,0},{1,17},{17,1},{2,18},{18,2},{3,19},{19,3},{4,20},{20... | collective-permute-start | bytes 3145736 | tf_op jit(solution)/shard_map/ppermute | solution.py:32
  236.6 97.6 %all-to-all-start.3 = ((bf16[4,512,512]{2,1,0:T(8,128)(2,1)}), bf16[4,512,512]{2,1,0:T(8,128)(2,1)S(1)}, u32[]{:S(2)}, u32[]{:S(2)}) async-start(bf16[4,512,512]{2,1,0:T(8,128)(2,1)} %get-tuple-element.83), calls=%async_computation.3 | async-start | bytes 4194304 | tf_op jit(solution)/shard_map/all_to_all | solution.py:494
  263.8 53.7 %collective-permute-start.13 = (bf16[2,1,4,128,1024]{4,3,2,1,0:T(8,128)(2,1)S(1)}, bf16[2,1,4,128,1024]{4,3,2,1,0:T(8,128)(2,1)S(1)}, u32[]{:S(2)}, u32[]{:S(2)}) collective-permute-start(bf16[2,1,4,128,1024]{4,3,2,1,0:T(8,128)(2,1)S(1)} %pad_maximum_fusion.8), channel_id=1, source_target_pairs={{0,16},{16,0},{1,17},{17,1},{2,18},{18,2},{3,19},{19,3},{4,20},{20... | collective-permute-start | bytes 6291464 | tf_op jit(solution)/shard_map/ppermute | solution.py:32
  267.1 63.6 %collective-permute-start.15 = (bf16[1,2,4,128,1024]{4,3,2,1,0:T(8,128)(2,1)S(1)}, bf16[1,2,4,128,1024]{4,3,2,1,0:T(8,128)(2,1)S(1)}, u32[]{:S(2)}, u32[]{:S(2)}) collective-permute-start(bf16[1,2,4,128,1024]{4,3,2,1,0:T(8,128)(2,1)S(1)} %pad_maximum_fusion.9), channel_id=1, source_target_pairs={{0,8},{4,12},{8,0},{12,4},{1,9},{5,13},{9,1},{13,5},{2,10},{6,14},... | collective-permute-start | bytes 6291464 | tf_op jit(solution)/shard_map/ppermute | solution.py:32
  334.2 30.8 %collective-permute-start.16 = (bf16[16,128,1024]{2,1,0:T(8,128)(2,1)}, bf16[16,128,1024]{2,1,0:T(8,128)(2,1)}, u32[]{:S(2)}, u32[]{:S(2)}) collective-permute-start(bf16[16,128,1024]{2,1,0:T(8,128)(2,1)} %bitcast.382), channel_id=1, source_target_pairs={{0,4},{4,0},{8,12},{12,8},{1,5},{5,1},{9,13},{13,9},{2,6},{6,2},{1... | collective-permute-start | bytes 12582920 | tf_op jit(solution)/shard_map/ppermute | solution.py:32
  334.3 30.7 %collective-permute-start.17 = (bf16[16,128,1024]{2,1,0:T(8,128)(2,1)}, bf16[16,128,1024]{2,1,0:T(8,128)(2,1)}, u32[]{:S(2)}, u32[]{:S(2)}) collective-permute-start(bf16[16,128,1024]{2,1,0:T(8,128)(2,1)} %bitcast.385), channel_id=1, source_target_pairs={{0,4},{4,0},{8,12},{12,8},{1,5},{5,1},{9,13},{13,9},{2,6},{6,2},{1... | collective-permute-start | bytes 12582920 | tf_op jit(solution)/shard_map/ppermute | solution.py:32
  336.2 9.9 %all-to-all-start.5 = ((f32[32,1,128]{2,1,0:T(1,128)}), f32[32,1,128]{2,1,0:T(1,128)S(1)}, u32[]{:S(2)}, u32[]{:S(2)}) async-start(f32[32,1,128]{2,1,0:T(1,128)} %bitcast.128), calls=%async_computation.5 | async-start | bytes 32768 | tf_op jit(solution)/shard_map/all_to_all | solution.py:692
  346.1 71.9 %all-to-all-start.4 = ((bf16[4,512,512]{2,1,0:T(8,128)(2,1)}), bf16[4,512,512]{2,1,0:T(8,128)(2,1)}, u32[]{:S(2)}, u32[]{:S(2)}) async-start(bf16[4,512,512]{2,1,0:T(8,128)(2,1)} %get-tuple-element.88), calls=%async_computation.4 | async-start | bytes 4194304 | tf_op jit(solution)/shard_map/all_to_all | solution.py:494
  439.5 38.1 %collective-permute-start.18 = (bf16[16,128,2048]{2,1,0:T(8,128)(2,1)}, bf16[16,128,2048]{2,1,0:T(8,128)(2,1)}, u32[]{:S(2)}, u32[]{:S(2)}) collective-permute-start(bf16[16,128,2048]{2,1,0:T(8,128)(2,1)} %get-tuple-element.95), channel_id=1, source_target_pairs={{0,4},{4,0},{8,12},{12,8},{1,5},{5,1},{9,13},{13,9},{2,6},{6,2},{1... | collective-permute-start | bytes 25165832 | tf_op jit(solution)/shard_map/ppermute | solution.py:32
  464.2 13.4 %all-to-all-start.6 = ((f32[32,1,128]{2,1,0:T(1,128)}), f32[32,1,128]{2,1,0:T(1,128)}, u32[]{:S(2)}, u32[]{:S(2)}) async-start(f32[32,1,128]{2,1,0:T(1,128)} %bitcast.135), calls=%async_computation.6 | async-start | bytes 32768 | tf_op jit(solution)/shard_map/all_to_all | solution.py:721
  486.3 84.9 %collective-permute-start.21 = (bf16[16,128,2048]{2,1,0:T(8,128)(2,1)}, bf16[16,128,2048]{2,1,0:T(8,128)(2,1)}, u32[]{:S(2)}, u32[]{:S(2)}) collective-permute-start(bf16[16,128,2048]{2,1,0:T(8,128)(2,1)} %shard_map.143), channel_id=1, source_target_pairs={{0,4},{4,0},{8,12},{12,8},{1,5},{5,1},{9,13},{13,9},{2,6},{6,2},{1... | collective-permute-start | bytes 25165832 | tf_op jit(solution)/shard_map/ppermute | solution.py:32
  486.4 54.0 %all-to-all-start.7 = ((bf16[4,512,512]{2,1,0:T(8,128)(2,1)}), bf16[4,512,512]{2,1,0:T(8,128)(2,1)}, u32[]{:S(2)}, u32[]{:S(2)}) async-start(bf16[4,512,512]{2,1,0:T(8,128)(2,1)} %bitcast.444), calls=%async_computation.7 | async-start | bytes 4194304 | tf_op jit(solution)/shard_map/all_to_all | solution.py:494
  497.5 58.2 %collective-permute-start.20 = (bf16[2,4,128,1024]{3,2,1,0:T(8,128)(2,1)}, bf16[2,4,128,1024]{3,2,1,0:T(8,128)(2,1)}, u32[]{:S(2)}, u32[]{:S(2)}) collective-permute-start(bf16[2,4,128,1024]{3,2,1,0:T(8,128)(2,1)} %get-tuple-element.203), channel_id=1, source_target_pairs={{0,16},{16,0},{1,17},{17,1},{2,18},{18,2},{3,19},{19,3},{4,20},{20... | collective-permute-start | bytes 6291464 | tf_op jit(solution)/shard_map/ppermute | solution.py:32
  504.7 50.9 %collective-permute-start.19 = (bf16[2,4,128,1024]{3,2,1,0:T(8,128)(2,1)}, bf16[2,4,128,1024]{3,2,1,0:T(8,128)(2,1)}, u32[]{:S(2)}, u32[]{:S(2)}) collective-permute-start(bf16[2,4,128,1024]{3,2,1,0:T(8,128)(2,1)} %get-tuple-element.205), channel_id=1, source_target_pairs={{0,8},{4,12},{8,0},{12,4},{1,9},{5,13},{9,1},{13,5},{2,10},{6,14},... | collective-permute-start | bytes 6291464 | tf_op jit(solution)/shard_map/ppermute | solution.py:32
  551.2 52.4 %all-to-all-start.8 = ((bf16[4,512,512]{2,1,0:T(8,128)(2,1)}), bf16[4,512,512]{2,1,0:T(8,128)(2,1)}, u32[]{:S(2)}, u32[]{:S(2)}) async-start(bf16[4,512,512]{2,1,0:T(8,128)(2,1)} %bitcast.443), calls=%async_computation.8 | async-start | bytes 4194304 | tf_op jit(solution)/shard_map/all_to_all | solution.py:494
  557.8 25.7 %collective-permute-start.23 = (bf16[4,128,1024]{2,1,0:T(8,128)(2,1)S(1)}, bf16[4,128,1024]{2,1,0:T(8,128)(2,1)S(1)}, u32[]{:S(2)}, u32[]{:S(2)}) collective-permute-start(bf16[4,128,1024]{2,1,0:T(8,128)(2,1)S(1)} %fusion.40), channel_id=1, source_target_pairs={{0,8},{4,12},{8,0},{12,4},{1,9},{5,13},{9,1},{13,5},{2,10},{6,14},... | collective-permute-start | bytes 3145736 | tf_op jit(solution)/shard_map/ppermute | solution.py:32
  561.0 24.2 %collective-permute-start.22 = (bf16[4,128,1024]{2,1,0:T(8,128)(2,1)S(1)}, bf16[4,128,1024]{2,1,0:T(8,128)(2,1)S(1)}, u32[]{:S(2)}, u32[]{:S(2)}) collective-permute-start(bf16[4,128,1024]{2,1,0:T(8,128)(2,1)S(1)} %fusion.39), channel_id=1, source_target_pairs={{0,16},{16,0},{1,17},{17,1},{2,18},{18,2},{3,19},{19,3},{4,20},{20... | collective-permute-start | bytes 3145736 | tf_op jit(solution)/shard_map/ppermute | solution.py:32
  603.6 52.1 %all-to-all-start.9 = ((bf16[4,128,2048]{2,1,0:T(8,128)(2,1)}), bf16[4,128,2048]{2,1,0:T(8,128)(2,1)S(1)}, u32[]{:S(2)}, u32[]{:S(2)}) async-start(bf16[4,128,2048]{2,1,0:T(8,128)(2,1)} %pad_maximum_fusion.10), calls=%async_computation.9 | async-start | bytes 4194304 | tf_op jit(solution)/shard_map/all_to_all | solution.py:494
  607.3 47.0 %collective-permute-start.24 = (bf16[2,4,128,1024]{3,2,1,0:T(8,128)(2,1)}, bf16[2,4,128,1024]{3,2,1,0:T(8,128)(2,1)}, u32[]{:S(2)}, u32[]{:S(2)}) collective-permute-start(bf16[2,4,128,1024]{3,2,1,0:T(8,128)(2,1)} %get-tuple-element.110), channel_id=1, source_target_pairs={{0,8},{4,12},{8,0},{12,4},{1,9},{5,13},{9,1},{13,5},{2,10},{6,14},... | collective-permute-start | bytes 6291464 | tf_op jit(solution)/shard_map/ppermute | solution.py:32
  609.1 46.6 %collective-permute-start.25 = (bf16[2,4,128,1024]{3,2,1,0:T(8,128)(2,1)}, bf16[2,4,128,1024]{3,2,1,0:T(8,128)(2,1)}, u32[]{:S(2)}, u32[]{:S(2)}) collective-permute-start(bf16[2,4,128,1024]{3,2,1,0:T(8,128)(2,1)} %get-tuple-element.111), channel_id=1, source_target_pairs={{0,16},{16,0},{1,17},{17,1},{2,18},{18,2},{3,19},{19,3},{4,20},{20... | collective-permute-start | bytes 6291464 | tf_op jit(solution)/shard_map/ppermute | solution.py:32
  622.1 34.0 %copy-start.39 = (f32[128,2048]{1,0:T(8,128)S(1)}, f32[128,2048]{1,0:T(8,128)}, u32[]{:S(2)}) copy-start(f32[128,2048]{1,0:T(8,128)} %copy-done.38) | copy-start | bytes 3145732
  622.1 34.0 %copy-start.89 = (f32[2048]{0:T(1024)S(1)}, f32[2048]{0:T(1024)}, u32[]{:S(2)}) copy-start(f32[2048]{0:T(1024)} %copy-done.88) | copy-start | bytes 24580
  622.1 34.0 %copy-start.98 = (f32[128]{0:T(128)S(1)}, f32[128]{0:T(128)}, u32[]{:S(2)}) copy-start(f32[128]{0:T(128)} %copy-done.97) | copy-start | bytes 1540
  659.2 12.2 %collective-permute-start.29 = (bf16[128,2048]{1,0:T(8,128)(2,1)S(1)}, bf16[128,2048]{1,0:T(8,128)(2,1)S(1)}, u32[]{:S(2)}, u32[]{:S(2)}) collective-permute-start(bf16[128,2048]{1,0:T(8,128)(2,1)S(1)} %get-tuple-element.196), channel_id=1, source_target_pairs={{0,8},{4,12},{8,0},{12,4},{1,9},{5,13},{9,1},{13,5},{2,10},{6,14},... | collective-permute-start | bytes 1572872 | tf_op jit(solution)/shard_map/ppermute | solution.py:32
  660.2 20.1 %collective-permute-start.28 = (bf16[128,2048]{1,0:T(8,128)(2,1)S(1)}, bf16[128,2048]{1,0:T(8,128)(2,1)}, u32[]{:S(2)}, u32[]{:S(2)}) collective-permute-start(bf16[128,2048]{1,0:T(8,128)(2,1)S(1)} %get-tuple-element.196), channel_id=1, source_target_pairs={{0,4},{4,0},{8,12},{12,8},{1,5},{5,1},{9,13},{13,9},{2,6},{6,2},{1... | collective-permute-start | bytes 1572872 | tf_op jit(solution)/shard_map/ppermute | solution.py:32
  660.2 53.5 %all-to-all-start.10 = ((bf16[4,512,512]{2,1,0:T(8,128)(2,1)}), bf16[4,512,512]{2,1,0:T(8,128)(2,1)S(1)}, u32[]{:S(2)}, u32[]{:S(2)}) async-start(bf16[4,512,512]{2,1,0:T(8,128)(2,1)} %bitcast.442), calls=%async_computation.10 | async-start | bytes 4194304 | tf_op jit(solution)/shard_map/all_to_all | solution.py:494
  671.4 8.9 collective-permute-start.30
  674.6 29.4 %collective-permute-start.27 = (bf16[4,128,1024]{2,1,0:T(8,128)(2,1)}, bf16[4,128,1024]{2,1,0:T(8,128)(2,1)}, u32[]{:S(2)}, u32[]{:S(2)}) collective-permute-start(bf16[4,128,1024]{2,1,0:T(8,128)(2,1)} %fusion.44), channel_id=1, source_target_pairs={{0,8},{4,12},{8,0},{12,4},{1,9},{5,13},{9,1},{13,5},{2,10},{6,14},... | collective-permute-start | bytes 3145736 | tf_op jit(solution)/shard_map/ppermute | solution.py:32
  678.8 25.4 %collective-permute-start.26 = (bf16[4,128,1024]{2,1,0:T(8,128)(2,1)}, bf16[4,128,1024]{2,1,0:T(8,128)(2,1)}, u32[]{:S(2)}, u32[]{:S(2)}) collective-permute-start(bf16[4,128,1024]{2,1,0:T(8,128)(2,1)} %fusion.43), channel_id=1, source_target_pairs={{0,16},{16,0},{1,17},{17,1},{2,18},{18,2},{3,19},{19,3},{4,20},{20... | collective-permute-start | bytes 3145736 | tf_op jit(solution)/shard_map/ppermute | solution.py:32
  703.4 26.4 %collective-permute-start.31 = (bf16[1,4,4,64,512]{4,3,1,2,0:T(8,128)(2,1)}, bf16[1,4,4,64,512]{4,3,1,2,0:T(8,128)(2,1)}, u32[]{:S(2)}, u32[]{:S(2)}) collective-permute-start(bf16[1,4,4,64,512]{4,3,1,2,0:T(8,128)(2,1)} %fusion.46), channel_id=1, source_target_pairs={{0,16},{16,0},{1,17},{17,1},{2,18},{18,2},{3,19},{19,3},{4,20},{20... | collective-permute-start | bytes 3145736 | tf_op jit(solution)/shard_map/ppermute | solution.py:32
  715.1 52.3 %all-to-all-start.11 = ((bf16[4,128,2048]{2,1,0:T(8,128)(2,1)}), bf16[4,128,2048]{2,1,0:T(8,128)(2,1)}, u32[]{:S(2)}, u32[]{:S(2)}) async-start(bf16[4,128,2048]{2,1,0:T(8,128)(2,1)} %pad_maximum_fusion.12), calls=%async_computation.11 | async-start | bytes 4194304 | tf_op jit(solution)/shard_map/all_to_all | solution.py:494
  722.3 28.7 %collective-permute-start.32 = (bf16[1,4,64,2048]{3,2,1,0:T(8,128)(2,1)}, bf16[1,4,64,2048]{3,2,1,0:T(8,128)(2,1)}, u32[]{:S(2)}, u32[]{:S(2)}) collective-permute-start(bf16[1,4,64,2048]{3,2,1,0:T(8,128)(2,1)} %fusion.35), channel_id=1, source_target_pairs={{0,16},{16,0},{1,17},{17,1},{2,18},{18,2},{3,19},{19,3},{4,20},{20... | collective-permute-start | bytes 3145736 | tf_op jit(solution)/shard_map/ppermute | solution.py:32
  767.4 28.7 %all-to-all-start.12 = ((bf16[4,64,2048]{2,1,0:T(8,128)(2,1)}), bf16[4,64,2048]{2,1,0:T(8,128)(2,1)S(1)}, u32[]{:S(2)}, u32[]{:S(2)}) async-start(bf16[4,64,2048]{2,1,0:T(8,128)(2,1)} %fusion.37), calls=%async_computation.12 | async-start | bytes 2097152 | tf_op jit(solution)/shard_map/all_to_all | solution.py:494
  776.7 23.7 %collective-permute-start.33 = (bf16[2,128,2048]{2,1,0:T(8,128)(2,1)S(1)}, bf16[2,128,2048]{2,1,0:T(8,128)(2,1)}, u32[]{:S(2)}, u32[]{:S(2)}) collective-permute-start(bf16[2,128,2048]{2,1,0:T(8,128)(2,1)S(1)} %fusion.48), channel_id=1, source_target_pairs={{0,4},{4,0},{8,12},{12,8},{1,5},{5,1},{9,13},{13,9},{2,6},{6,2},{1... | collective-permute-start | bytes 3145736 | tf_op jit(solution)/shard_map/ppermute | solution.py:32
  781.9 47.3 %collective-permute-start.35 = (bf16[1,4,4,64,1024]{4,3,1,2,0:T(8,128)(2,1)}, bf16[1,4,4,64,1024]{4,3,1,2,0:T(8,128)(2,1)}, u32[]{:S(2)}, u32[]{:S(2)}) collective-permute-start(bf16[1,4,4,64,1024]{4,3,1,2,0:T(8,128)(2,1)} %dynamic-slice_convert_fusion), channel_id=1, source_target_pairs={{0,16},{16,0},{1,17},{17,1},{2,18},{18,2},{3,19},{19,3},{4,20},{20... | collective-permute-start | bytes 6291464 | tf_op jit(solution)/shard_map/ppermute | solution.py:32
  796.2 29.5 %all-to-all-start.13 = ((bf16[4,4,64,512]{3,2,1,0:T(8,128)(2,1)}), bf16[4,4,64,512]{3,2,1,0:T(8,128)(2,1)}, u32[]{:S(2)}, u32[]{:S(2)}) async-start(bf16[4,4,64,512]{3,2,1,0:T(8,128)(2,1)} %fusion.36), calls=%async_computation.13 | async-start | bytes 2097152 | tf_op jit(solution)/shard_map/all_to_all | solution.py:494
  803.6 13.2 %collective-permute-start.34 = (bf16[128,2048]{1,0:T(8,128)(2,1)}, bf16[128,2048]{1,0:T(8,128)(2,1)}, u32[]{:S(2)}, u32[]{:S(2)}) collective-permute-start(bf16[128,2048]{1,0:T(8,128)(2,1)} %fusion.54), channel_id=1, source_target_pairs={{0,8},{4,12},{8,0},{12,4},{1,9},{5,13},{9,1},{13,5},{2,10},{6,14},... | collective-permute-start | bytes 1572872 | tf_op jit(solution)/shard_map/ppermute | solution.py:32
  825.7 12.4 %all-to-all-start.16 = ((f32[32,1,1280]{2,1,0:T(1,128)}), f32[32,1,1280]{2,1,0:T(1,128)S(1)}, u32[]{:S(2)}, u32[]{:S(2)}) async-start(f32[32,1,1280]{2,1,0:T(1,128)} %copy.187), calls=%async_computation.16 | async-start | bytes 327680 | tf_op jit(solution)/shard_map/all_to_all | solution.py:823
  838.0 52.6 %all-to-all-start.14 = ((bf16[4,4,64,1024]{3,2,1,0:T(8,128)(2,1)}), bf16[4,4,64,1024]{3,2,1,0:T(8,128)(2,1)}, u32[]{:S(2)}, u32[]{:S(2)}) async-start(bf16[4,4,64,1024]{3,2,1,0:T(8,128)(2,1)} %fusion.12), calls=%async_computation.14 | async-start | bytes 4194304 | tf_op jit(solution)/shard_map/all_to_all | solution.py:494
  893.6 16.3 %all-to-all-start.15 = ((bf16[4,64,1536]{2,1,0:T(8,128)(2,1)}), bf16[4,64,1536]{2,1,0:T(8,128)(2,1)}, u32[]{:S(2)}, u32[]{:S(2)}) async-start(bf16[4,64,1536]{2,1,0:T(8,128)(2,1)} %pad_maximum_fusion.16), calls=%async_computation.15 | async-start | bytes 1572864 | tf_op jit(solution)/shard_map/all_to_all | solution.py:810
  (99 other events, 749.6 us)
Sparse Core Ops, SparseCore 0:
  36.6 125.9 all-gather.6
  230.2 165.9 all-gather.8

commit v7 on v6

--- a/solution.py
+++ b/solution.py
@@ -146,15 +146,20 @@
         for _ in range(lax.axis_size("dp") - 1):
             around.append(shift(around[-1], "dp", 1))
         self.ring, self.around = around[-1], around
-        far = far_steps()
-        half = value.shape[1] // 2
-        shape = (-1, value.shape[0], half)
+        self.half = value.shape[1] // 2
+
+    def spread(self, done):
+        far, half = far_steps(), self.half
+        shape = (-1, self.ring.shape[0], half)
         self.near = []
         for i in range(2):
-            held = jnp.stack([part[:, i * half : (i + 1) * half] for part in around])
+            held = jnp.stack([part[:, i * half : (i + 1) * half] for part in self.around])
             held = held.reshape((1,) * len(far) + held.shape)
-            for step in far[::-1] if i else far:
-                held = jnp.concatenate([held, swap(held, *step)], axis=far.index(step))
+            for level, step in enumerate(far[::-1] if i else far):
+                got = swap(held, *step)
+                if i and level == len(far) - 1:
+                    got = after(got, done)
+                held = jnp.concatenate([held, got], axis=far.index(step))
             self.near.append(held.reshape(shape))
 
     def others(self, *done):
@@ -656,6 +661,7 @@
     w_down = exchange(down_blocks, packed)
     w_gate = exchange(gate_blocks, w_down)
     w_up = exchange(up_blocks, w_gate)
+    g_gather.spread(w_gate)
     w_gate_all, w_up_all = w_gate.reshape(width, ffh), w_up.reshape(width, ffh)
 
     inputs = tokens[0].astype(f32)

time: 934 us -> 935 us (level)
    unnamed x222 -> x220, local copies, waits for them, and re-layouts: 33.8 us -> 28.5 us
  transfers between devices with their start and end apart: 55 -> 55, of which waited for: 31 -> 31; matrix products, arithmetic and copies ran while one was open for 22% -> 22% of each run, Pallas kernels for 9% -> 10%
where the time goes in v7:
time: 935 us; the launch traced here: 925 us
  waiting for transfers between devices  413 us (44%)
  Pallas kernels  122 us (13%)
  other arithmetic  115 us (12%)
  starting transfers between devices  110 us (12%)
  local copies, waits for them, and re-layouts  72.7 us (8%)
  matrix products  64.5 us (7%)
  between operations  16.3 us (2%)
  blocking collectives  10.6 us (1%)
    ppermute x30, waiting for transfers between devices, swap(): return lax.ppermute(value, axis, [(i, i ^ bit) for i in range(count)])  175 us
    all_to_all x11, waiting for transfers between devices, exchange(): return lax.all_to_all(after(blocks, *done), 'dp', 0, 0, tiled=True)  134 us
    all_to_all x11, starting transfers between devices, exchange(): return lax.all_to_all(after(blocks, *done), 'dp', 0, 0, tiled=True)  46.4 us
    pallas_call x2, Pallas kernels, run_expert(): pl.pallas_call(lambda *refs: expert_kernel(per, slot_cap, *refs), grid_sp...  43.1 us
    dot_general x7, matrix products, mm_tn(): lax.dot_general(a, b, (((0,), (0,)), ((), ())), preferred_element_type=f32)  42.6 us
    ppermute x6, waiting for transfers between devices, shift(): lax.ppermute(value, axis, [(i, (i + step) % count) for i in range(count)])  36.5 us
    unnamed x220, local copies, waits for them, and re-layouts  28.5 us
    ppermute x30, starting transfers between devices, swap(): return lax.ppermute(value, axis, [(i, i ^ bit) for i in range(count)])  26.3 us
  transfers between devices with their start and end apart: 55, of which 31 were waited for; matrix products, arithmetic and copies ran while one was open for 22% of the time, Pallas kernels for 10%

profile of v7, /device:TPU:0, one launch (start us, length us, event | category | flops | bytes accessed | tf_op | source)
XLA Modules:
  0.0 924.7 jit_solution(17246069040706963573)
XLA Ops:
  14.2 4.4 all-to-all-start
  21.0 14.5 %collective-permute-done.7 = bf16[128,2048]{1,0:T(8,128)(2,1)S(1)} collective-permute-done((bf16[128,2048]{1,0:T(8,128)(2,1)S(1)}, bf16[128,2048]{1,0:T(8,128)(2,1)S(1)}, u32[]{:S(2)}, u32[]{:S(2)}) %collective-permute-start.7) | collective-permute-done | bytes 524320 | tf_op jit(solution)/shard_map/ppermute | solution.py:37
  42.3 5.3 copy-done.4
  47.7 13.5 %shard_map.136 = (bf16[4,512,512]{2,1,0:T(8,128)(2,1)}, bf16[4,512,512]{2,1,0:T(8,128)(2,1)}, bf16[4,512,512]{2,1,0:T(8,128)(2,1)S(1)}) custom-call(f32[512,2,3072]{2,1,0:T(2,128)S(1)} %copy-done.4), custom_call_target="tpu_custom_call" | custom-call | flops 1 | bytes 1 | tf_op jit(solution)/shard_map/pallas_call | solution.py:515
  68.3 12.8 %collective-permute-done.4 = bf16[64,2048]{1,0:T(8,128)(2,1)S(1)} collective-permute-done((bf16[64,2048]{1,0:T(8,128)(2,1)}, bf16[64,2048]{1,0:T(8,128)(2,1)S(1)}, u32[]{:S(2)}, u32[]{:S(2)}) %collective-permute-start.4) | collective-permute-done | bytes 262176 | tf_op jit(solution)/shard_map/ppermute | solution.py:37
  84.7 5.3 all-to-all-start.1
  90.0 21.2 %all-to-all-done.1 = bf16[32,2,704]{2,1,0:T(2,128)(2,1)S(1)} async-done(((bf16[32,2,704]{2,1,0:T(2,128)(2,1)}), bf16[32,2,704]{2,1,0:T(2,128)(2,1)S(1)}, u32[]{:S(2)}, u32[]{:S(2)}) %all-to-all-start.1) | async-done | bytes 90144 | tf_op jit(solution)/shard_map/all_to_all | solution.py:631
  119.1 7.9 collective-permute-start.9
  129.3 4.3 fusion.4
  133.6 10.6 %collective-permute-done.6 = bf16[4,64,2048]{2,1,0:T(8,128)(2,1)S(1)} collective-permute-done((bf16[4,64,2048]{2,1,0:T(8,128)(2,1)S(1)}, bf16[4,64,2048]{2,1,0:T(8,128)(2,1)S(1)}, u32[]{:S(2)}, u32[]{:S(2)}) %collective-permute-start.6) | collective-permute-done | bytes 1048608 | tf_op jit(solution)/shard_map/ppermute | solution.py:32
  144.3 9.1 collective-permute-done.9
  153.4 9.2 all-gather.7.cloned.1.call-done
  170.0 5.2 all-gather.2
  175.3 4.5 all-to-all-start.2
  182.8 7.1 shard_map.137
  199.9 13.5 %collective-permute-done.11 = bf16[128,2048]{1,0:T(8,128)(2,1)S(1)} collective-permute-done((bf16[128,2048]{1,0:T(8,128)(2,1)S(1)}, bf16[128,2048]{1,0:T(8,128)(2,1)S(1)}, u32[]{:S(2)}, u32[]{:S(2)}) %collective-permute-start.11) | collective-permute-done | bytes 524320 | tf_op jit(solution)/shard_map/ppermute | solution.py:32
  215.4 13.4 %all-to-all-done.2 = bf16[4,512,512]{2,1,0:T(8,128)(2,1)} async-done(((bf16[4,512,512]{2,1,0:T(8,128)(2,1)}), bf16[4,512,512]{2,1,0:T(8,128)(2,1)}, u32[]{:S(2)}, u32[]{:S(2)}) %all-to-all-start.2) | async-done | bytes 2097184 | tf_op jit(solution)/shard_map/all_to_all | solution.py:499
  239.3 21.6 %collective-permute-done.12 = bf16[1,1,4,128,1024]{4,3,2,1,0:T(8,128)(2,1)} collective-permute-done((bf16[1,1,4,128,1024]{4,3,2,1,0:T(8,128)(2,1)S(1)}, bf16[1,1,4,128,1024]{4,3,2,1,0:T(8,128)(2,1)}, u32[]{:S(2)}, u32[]{:S(2)}) %collective-permute-start.12) | collective-permute-done | bytes 1048608 | tf_op jit(solution)/shard_map/ppermute | solution.py:32
  266.2 49.7 %collective-permute-done.13 = bf16[2,1,4,128,1024]{4,3,2,1,0:T(8,128)(2,1)S(1)} collective-permute-done((bf16[2,1,4,128,1024]{4,3,2,1,0:T(8,128)(2,1)S(1)}, bf16[2,1,4,128,1024]{4,3,2,1,0:T(8,128)(2,1)S(1)}, u32[]{:S(2)}, u32[]{:S(2)}) %collective-permute-start.13) | collective-permute-done | bytes 2097184 | tf_op jit(solution)/shard_map/ppermute | solution.py:32
  319.2 7.4 collective-permute-done.15
  326.6 4.5 pad_maximum_fusion.4
  336.3 7.4 all-to-all-done.5
  343.7 4.0 all-to-all-start.4
  351.9 7.4 shard_map.138
  359.4 8.4 shard_map.139
  370.0 10.6 %fusion.1.refs_12_ = f32[2304,512]{1,0:T(8,128)} fusion(bf16[2048,512]{1,0:T(8,128)(2,1)} %bitcast.124.refs_3_, bf16[1152,2048]{1,0:T(8,128)(2,1)S(1)} %shard_map.139, bf16[1152,2048]{1,0:T(8,128)(2,1)S(1)} %shard_map.138), kind=kOutput, calls=%fused_computation.4 | convolution fusion | flops 4850712576 | bytes 16252928 | tf_op jit(solution)/shard_map/dot_general | solution.py:19
  380.6 16.8 %all-gather.9.cloned.1.call-done = bf16[4096,2048]{1,0:T(8,128)(2,1)} async-done(((bf16[128,2048]{1,0:T(8,128)(2,1)}), bf16[4096,2048]{1,0:T(8,128)(2,1)}) %all-gather.9.cloned.1.call-update) | async-done | bytes 16777232 | tf_op jit(solution)/shard_map/all_gather | solution.py:696
  397.3 20.4 %all-to-all-done.4 = bf16[4,512,512]{2,1,0:T(8,128)(2,1)S(1)} async-done(((bf16[4,512,512]{2,1,0:T(8,128)(2,1)}), bf16[4,512,512]{2,1,0:T(8,128)(2,1)S(1)}, u32[]{:S(2)}, u32[]{:S(2)}) %all-to-all-start.4) | async-done | bytes 2097184 | tf_op jit(solution)/shard_map/all_to_all | solution.py:499
  419.1 21.5 %shard_map.140 = (bf16[2304,2048]{1,0:T(8,128)(2,1)}, bf16[2304,512]{1,0:T(8,128)(2,1)}, bf16[2304,512]{1,0:T(8,128)(2,1)}, bf16[2304,1024]{1,0:T(8,128)(2,1)}, ...) custom-call(s32[32]{0:T(128)} %stack.310.refs_0_, s32[32,1,128]{2,1,0:T(1,128)} %bitcast.385, ...), custom_call_target="tpu_custom_call" | custom-call | flops 1 | bytes 1 | tf_op jit(solution)/shard_map/pallas_call | solution.py:481
  440.7 21.5 %shard_map.141 = (bf16[2304,2048]{1,0:T(8,128)(2,1)}, bf16[2304,512]{1,0:T(8,128)(2,1)}, bf16[2304,512]{1,0:T(8,128)(2,1)}, bf16[2304,1024]{1,0:T(8,128)(2,1)}, ...) custom-call(s32[32]{0:T(128)} %stack.310.refs_0_, ...), custom_call_target="tpu_custom_call", output_to_operand_aliasing={{0}: (14, {}), {1}: (15, {}), {2}: (16, {}), {3}: (17, {}),... | custom-call | flops 1 | bytes 1 | tf_op jit(solution)/shard_map/pallas_call | solution.py:481
  469.1 9.5 %fusion.5 = bf16[2048,512]{1,0:T(8,128)(2,1)} fusion(bf16[2304,512]{1,0:T(8,128)(2,1)} %get-tuple-element.96, bf16[1152,2048]{1,0:T(8,128)(2,1)} %copy-done.10, bf16[1152,2048]{1,0:T(8,128)(2,1)} %copy-done.9), kind=kOutput, calls=%fused_computation.24 | convolution fusion | flops 4851761152 | bytes 13893632 | tf_op jit(solution)/shard_map/dot_general | solution.py:27
  478.6 8.6 shard_map.143
  487.4 5.2 all-to-all-start.7
  492.6 5.8 add_convert_fusion.4
  499.9 5.8 add_convert_fusion.5
  507.2 34.2 %all-to-all-done.7.refs_2_ = bf16[4,512,512]{2,1,0:T(8,128)(2,1)} async-done(((bf16[4,512,512]{2,1,0:T(8,128)(2,1)}), bf16[4,512,512]{2,1,0:T(8,128)(2,1)}, u32[]{:S(2)}, u32[]{:S(2)}) %all-to-all-start.7) | async-done | bytes 2097184 | tf_op jit(solution)/shard_map/all_to_all | solution.py:499
  541.4 10.7 %convolution_convert_fusion.1 = bf16[2048,512]{1,0:T(8,128)(2,1)} fusion(bf16[2304,2048]{1,0:T(8,128)(2,1)} %get-tuple-element.118, bf16[2304,1024]{1,0:T(8,128)(2,1)} %get-tuple-element.116), kind=kOutput, calls=%fused_computation.26 | convolution fusion | flops 4832886784 | bytes 13893632 | tf_op jit(solution)/shard_map/dot_general | solution.py:27
  552.1 4.5 all-to-all-start.8
  563.5 8.7 shard_map.142
  572.1 6.1 add_convert_fusion.1
  579.5 4.8 fusion.10
  591.5 13.0 %all-to-all-done.8.refs_0_ = bf16[4,512,512]{2,1,0:T(8,128)(2,1)} async-done(((bf16[4,512,512]{2,1,0:T(8,128)(2,1)}), bf16[4,512,512]{2,1,0:T(8,128)(2,1)}, u32[]{:S(2)}, u32[]{:S(2)}) %all-to-all-start.8) | async-done | bytes 2097184 | tf_op jit(solution)/shard_map/all_to_all | solution.py:499
  612.2 10.8 %convolution_convert_fusion = bf16[2048,512]{1,0:T(8,128)(2,1)} fusion(bf16[2304,2048]{1,0:T(8,128)(2,1)} %get-tuple-element.118, bf16[2304,1024]{1,0:T(8,128)(2,1)} %get-tuple-element.116), kind=kOutput, calls=%fused_computation.25 | convolution fusion | flops 4832886784 | bytes 13893632 | tf_op jit(solution)/shard_map/dot_general | solution.py:27
  623.0 32.2 %collective-permute-done.24 = bf16[2,4,128,1024]{3,2,1,0:T(8,128)(2,1)} collective-permute-done((bf16[2,4,128,1024]{3,2,1,0:T(8,128)(2,1)}, bf16[2,4,128,1024]{3,2,1,0:T(8,128)(2,1)}, u32[]{:S(2)}, u32[]{:S(2)}) %collective-permute-start.24) | collective-permute-done | bytes 2097184 | tf_op jit(solution)/shard_map/ppermute | solution.py:32
  661.2 4.1 all-to-all-start.10
  665.3 7.1 collective-permute-done.29
  685.9 15.8 %shard_map.144 = (f32[512,512]{1,0:T(8,128)S(1)}, f32[512,512]{1,0:T(8,128)S(1)}, bf16[512,512]{1,0:T(8,128)(2,1)S(1)}, f32[2,512]{1,0:T(2,128)S(1)}, f32[512,2]{1,0:T(8,128)S(1)}) custom-call(f32[512,1536]{1,0:T(8,128)} %copy-done, f32[512,1536]{1,0:T(8,128)} %copy-done, f32[512,2]{1,0:T(8,128)S(1)} %bitcast.383, f32[2,512]{1,0:T(2,128)S(1)} %bitcast.392, ...), custom_call_target="tpu_custom_call" | custom-call | flops 1 | bytes 1 | tf_op jit(solution)/shard_map/pallas_call | solution.py:413
  716.0 4.4 all-to-all-start.11
  724.8 5.4 all-gather.3
  734.4 17.7 %collective-permute-done.32 = bf16[1,4,64,2048]{3,2,1,0:T(8,128)(2,1)} collective-permute-done((bf16[1,4,64,2048]{3,2,1,0:T(8,128)(2,1)}, bf16[1,4,64,2048]{3,2,1,0:T(8,128)(2,1)}, u32[]{:S(2)}, u32[]{:S(2)}) %collective-permute-start.32) | collective-permute-done | bytes 1048608 | tf_op jit(solution)/shard_map/ppermute | solution.py:32
  760.6 5.8 fusion.49
  772.1 5.6 fusion.100
  777.9 5.1 dynamic-slice_convert_fusion
  784.5 12.7 %all-to-all-done.12 = bf16[4,64,2048]{2,1,0:T(8,128)(2,1)S(1)} async-done(((bf16[4,64,2048]{2,1,0:T(8,128)(2,1)}), bf16[4,64,2048]{2,1,0:T(8,128)(2,1)S(1)}, u32[]{:S(2)}, u32[]{:S(2)}) %all-to-all-start.12) | async-done | bytes 1048608 | tf_op jit(solution)/shard_map/all_to_all | solution.py:499
  797.3 4.2 all-to-all-start.13
  809.2 8.7 collective-permute-done.34
  820.4 6.4 all-to-all-done.13
  830.1 4.9 fusion.12
  835.0 3.9 all-to-all-done.16
  838.9 4.5 all-to-all-start.14
  843.4 9.1 shard_map.145
  860.0 31.6 %all-to-all-done.14 = bf16[4,4,64,1024]{3,2,1,0:T(8,128)(2,1)} async-done(((bf16[4,4,64,1024]{3,2,1,0:T(8,128)(2,1)}), bf16[4,4,64,1024]{3,2,1,0:T(8,128)(2,1)}, u32[]{:S(2)}, u32[]{:S(2)}) %all-to-all-start.14) | async-done | bytes 2097184 | tf_op jit(solution)/shard_map/all_to_all | solution.py:499
  894.5 4.6 all-to-all-start.15
  901.2 9.7 %all-to-all-done.15 = bf16[4,64,1536]{2,1,0:T(8,128)(2,1)} async-done(((bf16[4,64,1536]{2,1,0:T(8,128)(2,1)}), bf16[4,64,1536]{2,1,0:T(8,128)(2,1)}, u32[]{:S(2)}, u32[]{:S(2)}) %all-to-all-start.15) | async-done | bytes 786464 | tf_op jit(solution)/shard_map/all_to_all | solution.py:816
  (464 shorter events, 214.2 us)
Async XLA Ops:
  8.9 29.4 %copy-start.62 = (bf16[64,8192]{1,0:T(8,128)(2,1)}, bf16[64,8192]{1,0:T(8,128)(2,1)S(1)}, u32[]{:S(2)}) copy-start(bf16[64,8192]{1,0:T(8,128)(2,1)S(1)} %convert.33) | copy-start | bytes 3145732
  14.2 25.4 %copy-start.105 = (s32[1,8]{1,0:T(1,128)S(1)}, s32[1,8]{1,0:T(1,128)}, u32[]{:S(2)}) copy-start(s32[1,8]{1,0:T(1,128)} %param.16) | copy-start | bytes 100
  14.2 21.4 %all-to-all-start = ((bf16[4,64,1536]{2,1,0:T(8,128)(2,1)}), bf16[4,64,1536]{2,1,0:T(8,128)(2,1)S(1)}, u32[]{:S(2)}, u32[]{:S(2)}) async-start(bf16[4,64,1536]{2,1,0:T(8,128)(2,1)} %reshape.1700), calls=%async_computation | async-start | bytes 1572864 | tf_op jit(solution)/shard_map/all_to_all | solution.py:629
  18.5 144.1 %all-gather.7.cloned.1.call-start = ((), (), s32[]{:S(2)}) async-start(), calls=%async_computation.17 | async-start | bytes 7077888 | tf_op jit(solution)/shard_map/all_gather | solution.py:649
  18.6 17.0 %collective-permute-start.7 = (bf16[128,2048]{1,0:T(8,128)(2,1)S(1)}, bf16[128,2048]{1,0:T(8,128)(2,1)S(1)}, u32[]{:S(2)}, u32[]{:S(2)}) collective-permute-start(bf16[128,2048]{1,0:T(8,128)(2,1)S(1)} %bitcast_convert_fusion.2), channel_id=1, source_target_pairs={{0,1},{1,2},{2,3},{3,0},{4,5},{5,6},{6,7},{7,4},{8,9},{9,10},{10,1... | collective-permute-start | bytes 1572872 | tf_op jit(solution)/shard_map/ppermute | solution.py:37
  36.5 44.7 %collective-permute-start.1 = (bf16[128,2048]{1,0:T(8,128)(2,1)S(1)}, bf16[128,2048]{1,0:T(8,128)(2,1)}, u32[]{:S(2)}, u32[]{:S(2)}) collective-permute-start(bf16[128,2048]{1,0:T(8,128)(2,1)S(1)} %bitcast.423), channel_id=1, source_target_pairs={{0,8},{4,12},{8,0},{12,4},{1,9},{5,13},{9,1},{13,5},{2,10},{6,14},... | collective-permute-start | bytes 1572872 | tf_op jit(solution)/shard_map/ppermute | solution.py:32
  38.3 88.7 %collective-permute-start = (bf16[128,2048]{1,0:T(8,128)(2,1)S(1)}, bf16[128,2048]{1,0:T(8,128)(2,1)}, u32[]{:S(2)}, u32[]{:S(2)}) collective-permute-start(bf16[128,2048]{1,0:T(8,128)(2,1)S(1)} %bitcast.424), channel_id=1, source_target_pairs={{0,4},{4,0},{8,12},{12,8},{1,5},{5,1},{9,13},{13,9},{2,6},{6,2},{1... | collective-permute-start | bytes 1572872 | tf_op jit(solution)/shard_map/ppermute | solution.py:32
  39.1 25.3 %collective-permute-start.3 = (bf16[64,2048]{1,0:T(8,128)(2,1)}, bf16[64,2048]{1,0:T(8,128)(2,1)}, u32[]{:S(2)}, u32[]{:S(2)}) collective-permute-start(bf16[64,2048]{1,0:T(8,128)(2,1)} %get-tuple-element.219), channel_id=1, source_target_pairs={{0,1},{1,2},{2,3},{3,0},{4,5},{5,6},{6,7},{7,4},{8,9},{9,10},{10,1... | collective-permute-start | bytes 786440 | tf_op jit(solution)/shard_map/ppermute | solution.py:37
  63.5 53.9 %copy-start.81 = (bf16[1,64,2048]{2,1,0:T(8,128)(2,1)S(1)}, bf16[1,64,2048]{2,1,0:T(8,128)(2,1)}, u32[]{:S(2)}) copy-start(bf16[1,64,2048]{2,1,0:T(8,128)(2,1)} %get-tuple-element.218) | copy-start | bytes 786436
  63.5 116.4 %copy-start.32 = (s32[2,512]{1,0:T(2,128)}, s32[2,512]{1,0:T(2,128)S(1)}, u32[]{:S(2)}) copy-start(s32[2,512]{1,0:T(2,128)S(1)} %get-tuple-element.234.refs_8_.refs_7_) | copy-start | bytes 12292
  64.4 16.8 %collective-permute-start.4 = (bf16[64,2048]{1,0:T(8,128)(2,1)}, bf16[64,2048]{1,0:T(8,128)(2,1)S(1)}, u32[]{:S(2)}, u32[]{:S(2)}) collective-permute-start(bf16[64,2048]{1,0:T(8,128)(2,1)} %collective-permute-done.3), channel_id=1, source_target_pairs={{0,1},{1,2},{2,3},{3,0},{4,5},{5,6},{6,7},{7,4},{8,9},{9,10},{10,1... | collective-permute-start | bytes 786440 | tf_op jit(solution)/shard_map/ppermute | solution.py:37
  66.7 52.4 %collective-permute-start.8 = (bf16[128,2048]{1,0:T(8,128)(2,1)}, bf16[128,2048]{1,0:T(8,128)(2,1)}, u32[]{:S(2)}, u32[]{:S(2)}) collective-permute-start(bf16[128,2048]{1,0:T(8,128)(2,1)} %copy-done.82), channel_id=1, source_target_pairs={{0,1},{1,2},{2,3},{3,0},{4,5},{5,6},{6,7},{7,4},{8,9},{9,10},{10,1... | collective-permute-start | bytes 1572872 | tf_op jit(solution)/shard_map/ppermute | solution.py:37
  81.2 36.3 %collective-permute-start.5 = (bf16[64,2048]{1,0:T(8,128)(2,1)S(1)}, bf16[64,2048]{1,0:T(8,128)(2,1)S(1)}, u32[]{:S(2)}, u32[]{:S(2)}) collective-permute-start(bf16[64,2048]{1,0:T(8,128)(2,1)S(1)} %collective-permute-done.4), channel_id=1, source_target_pairs={{0,1},{1,2},{2,3},{3,0},{4,5},{5,6},{6,7},{7,4},{8,9},{9,10},{10,1... | collective-permute-start | bytes 786440 | tf_op jit(solution)/shard_map/ppermute | solution.py:37
  81.2 45.8 %collective-permute-start.2 = (bf16[128,2048]{1,0:T(8,128)(2,1)}, bf16[128,2048]{1,0:T(8,128)(2,1)}, u32[]{:S(2)}, u32[]{:S(2)}) collective-permute-start(bf16[128,2048]{1,0:T(8,128)(2,1)} %collective-permute-done.1), channel_id=1, source_target_pairs={{0,4},{4,0},{8,12},{12,8},{1,5},{5,1},{9,13},{13,9},{2,6},{6,2},{1... | collective-permute-start | bytes 1572872 | tf_op jit(solution)/shard_map/ppermute | solution.py:32
  84.7 26.5 %all-to-all-start.1 = ((bf16[32,2,704]{2,1,0:T(2,128)(2,1)}), bf16[32,2,704]{2,1,0:T(2,128)(2,1)S(1)}, u32[]{:S(2)}, u32[]{:S(2)}) async-start(bf16[32,2,704]{2,1,0:T(2,128)(2,1)} %reshape.1782), calls=%async_computation.1 | async-start | bytes 196608 | tf_op jit(solution)/shard_map/all_to_all | solution.py:631
  117.4 62.5 %copy-start.34 = (f32[1,2,2,256]{3,1,2,0:T(2,128)}, f32[1,2,2,256]{3,1,2,0:T(2,128)S(1)}, u32[]{:S(2)}) copy-start(f32[1,2,2,256]{3,1,2,0:T(2,128)S(1)} %copy.196) | copy-start | bytes 12292
  118.5 25.6 %collective-permute-start.6 = (bf16[4,64,2048]{2,1,0:T(8,128)(2,1)S(1)}, bf16[4,64,2048]{2,1,0:T(8,128)(2,1)S(1)}, u32[]{:S(2)}, u32[]{:S(2)}) collective-permute-start(bf16[4,64,2048]{2,1,0:T(8,128)(2,1)S(1)} %pad_maximum_fusion.15), channel_id=1, source_target_pairs={{0,16},{16,0},{1,17},{17,1},{2,18},{18,2},{3,19},{19,3},{4,20},{20... | collective-permute-start | bytes 3145736 | tf_op jit(solution)/shard_map/ppermute | solution.py:32
  119.1 34.3 %collective-permute-start.9 = (bf16[128,2048]{1,0:T(8,128)(2,1)}, bf16[128,2048]{1,0:T(8,128)(2,1)}, u32[]{:S(2)}, u32[]{:S(2)}) collective-permute-start(bf16[128,2048]{1,0:T(8,128)(2,1)} %collective-permute-done.8), channel_id=1, source_target_pairs={{0,1},{1,2},{2,3},{3,0},{4,5},{5,6},{6,7},{7,4},{8,9},{9,10},{10,1... | collective-permute-start | bytes 1572872 | tf_op jit(solution)/shard_map/ppermute | solution.py:37
  175.3 53.5 %all-to-all-start.2 = ((bf16[4,512,512]{2,1,0:T(8,128)(2,1)}), bf16[4,512,512]{2,1,0:T(8,128)(2,1)}, u32[]{:S(2)}, u32[]{:S(2)}) async-start(bf16[4,512,512]{2,1,0:T(8,128)(2,1)} %copy-done.17), calls=%async_computation.2 | async-start | bytes 4194304 | tf_op jit(solution)/shard_map/all_to_all | solution.py:499
  179.8 217.5 %all-gather.9.cloned.1.call-start = ((), (), s32[]{:S(2)}) async-start(), calls=%async_computation.18 | async-start | bytes 17301504 | tf_op jit(solution)/shard_map/all_gather | solution.py:696
  193.2 2.7 collective-permute-start.10
  199.1 14.2 %collective-permute-start.11 = (bf16[128,2048]{1,0:T(8,128)(2,1)S(1)}, bf16[128,2048]{1,0:T(8,128)(2,1)S(1)}, u32[]{:S(2)}, u32[]{:S(2)}) collective-permute-start(bf16[128,2048]{1,0:T(8,128)(2,1)S(1)} %fusion.53), channel_id=1, source_target_pairs={{0,8},{4,12},{8,0},{12,4},{1,9},{5,13},{9,1},{13,5},{2,10},{6,14},... | collective-permute-start | bytes 1572872 | tf_op jit(solution)/shard_map/ppermute | solution.py:32
  199.9 29.1 %copy-start.89 = (f32[2048]{0:T(1024)}, f32[2048]{0:T(1024)S(1)}, u32[]{:S(2)}) copy-start(f32[2048]{0:T(1024)S(1)} %mul.344) | copy-start | bytes 24580
  232.4 28.5 %collective-permute-start.12 = (bf16[1,1,4,128,1024]{4,3,2,1,0:T(8,128)(2,1)S(1)}, bf16[1,1,4,128,1024]{4,3,2,1,0:T(8,128)(2,1)}, u32[]{:S(2)}, u32[]{:S(2)}) collective-permute-start(bf16[1,1,4,128,1024]{4,3,2,1,0:T(8,128)(2,1)S(1)} %maximum_bitcast_fusion), channel_id=1, source_target_pairs={{0,8},{4,12},{8,0},{12,4},{1,9},{5,13},{9,1},{13,5},{2,10},{6,14},... | collective-permute-start | bytes 3145736 | tf_op jit(solution)/shard_map/ppermute | solution.py:32
  234.2 29.7 %collective-permute-start.14 = (bf16[1,1,4,128,1024]{4,3,2,1,0:T(8,128)(2,1)}, bf16[1,1,4,128,1024]{4,3,2,1,0:T(8,128)(2,1)}, u32[]{:S(2)}, u32[]{:S(2)}) collective-permute-start(bf16[1,1,4,128,1024]{4,3,2,1,0:T(8,128)(2,1)} %maximum_bitcast_fusion.1), channel_id=1, source_target_pairs={{0,16},{16,0},{1,17},{17,1},{2,18},{18,2},{3,19},{19,3},{4,20},{20... | collective-permute-start | bytes 3145736 | tf_op jit(solution)/shard_map/ppermute | solution.py:32
  235.6 91.0 %all-to-all-start.3 = ((bf16[4,512,512]{2,1,0:T(8,128)(2,1)}), bf16[4,512,512]{2,1,0:T(8,128)(2,1)S(1)}, u32[]{:S(2)}, u32[]{:S(2)}) async-start(bf16[4,512,512]{2,1,0:T(8,128)(2,1)} %get-tuple-element.84), calls=%async_computation.3 | async-start | bytes 4194304 | tf_op jit(solution)/shard_map/all_to_all | solution.py:499
  262.3 53.7 %collective-permute-start.13 = (bf16[2,1,4,128,1024]{4,3,2,1,0:T(8,128)(2,1)S(1)}, bf16[2,1,4,128,1024]{4,3,2,1,0:T(8,128)(2,1)S(1)}, u32[]{:S(2)}, u32[]{:S(2)}) collective-permute-start(bf16[2,1,4,128,1024]{4,3,2,1,0:T(8,128)(2,1)S(1)} %pad_maximum_fusion.8), channel_id=1, source_target_pairs={{0,16},{16,0},{1,17},{17,1},{2,18},{18,2},{3,19},{19,3},{4,20},{20... | collective-permute-start | bytes 6291464 | tf_op jit(solution)/shard_map/ppermute | solution.py:32
  265.6 61.0 %collective-permute-start.15 = (bf16[1,2,4,128,1024]{4,3,2,1,0:T(8,128)(2,1)S(1)}, bf16[1,2,4,128,1024]{4,3,2,1,0:T(8,128)(2,1)}, u32[]{:S(2)}, u32[]{:S(2)}) collective-permute-start(bf16[1,2,4,128,1024]{4,3,2,1,0:T(8,128)(2,1)S(1)} %pad_maximum_fusion.9), channel_id=1, source_target_pairs={{0,8},{4,12},{8,0},{12,4},{1,9},{5,13},{9,1},{13,5},{2,10},{6,14},... | collective-permute-start | bytes 6291464 | tf_op jit(solution)/shard_map/ppermute | solution.py:32
  331.1 28.2 %collective-permute-start.17 = (bf16[16,128,1024]{2,1,0:T(8,128)(2,1)}, bf16[16,128,1024]{2,1,0:T(8,128)(2,1)}, u32[]{:S(2)}, u32[]{:S(2)}) collective-permute-start(bf16[16,128,1024]{2,1,0:T(8,128)(2,1)} %bitcast.88.refs_4_.refs_5_), channel_id=1, source_target_pairs={{0,4},{4,0},{8,12},{12,8},{1,5},{5,1},{9,13},{13,9},{2,6},{6,2},{1... | collective-permute-start | bytes 12582920 | tf_op jit(solution)/shard_map/ppermute | solution.py:32
  331.1 28.2 %collective-permute-start.16 = (bf16[16,128,1024]{2,1,0:T(8,128)(2,1)}, bf16[16,128,1024]{2,1,0:T(8,128)(2,1)}, u32[]{:S(2)}, u32[]{:S(2)}) collective-permute-start(bf16[16,128,1024]{2,1,0:T(8,128)(2,1)} %bitcast.82.refs_2_.refs_3_), channel_id=1, source_target_pairs={{0,4},{4,0},{8,12},{12,8},{1,5},{5,1},{9,13},{13,9},{2,6},{6,2},{1... | collective-permute-start | bytes 12582920 | tf_op jit(solution)/shard_map/ppermute | solution.py:32
  333.0 10.6 %all-to-all-start.5 = ((f32[32,1,128]{2,1,0:T(1,128)}), f32[32,1,128]{2,1,0:T(1,128)S(1)}, u32[]{:S(2)}, u32[]{:S(2)}) async-start(f32[32,1,128]{2,1,0:T(1,128)} %bitcast.128), calls=%async_computation.5 | async-start | bytes 32768 | tf_op jit(solution)/shard_map/all_to_all | solution.py:698
  343.7 74.1 %all-to-all-start.4 = ((bf16[4,512,512]{2,1,0:T(8,128)(2,1)}), bf16[4,512,512]{2,1,0:T(8,128)(2,1)S(1)}, u32[]{:S(2)}, u32[]{:S(2)}) async-start(bf16[4,512,512]{2,1,0:T(8,128)(2,1)} %get-tuple-element.90), calls=%async_computation.4 | async-start | bytes 4194304 | tf_op jit(solution)/shard_map/all_to_all | solution.py:499
  440.6 38.0 %collective-permute-start.18 = (bf16[16,128,2048]{2,1,0:T(8,128)(2,1)}, bf16[16,128,2048]{2,1,0:T(8,128)(2,1)}, u32[]{:S(2)}, u32[]{:S(2)}) collective-permute-start(bf16[16,128,2048]{2,1,0:T(8,128)(2,1)} %get-tuple-element.97), channel_id=1, source_target_pairs={{0,4},{4,0},{8,12},{12,8},{1,5},{5,1},{9,13},{13,9},{2,6},{6,2},{1... | collective-permute-start | bytes 25165832 | tf_op jit(solution)/shard_map/ppermute | solution.py:32
  465.3 13.3 %all-to-all-start.6 = ((f32[32,1,128]{2,1,0:T(1,128)}), f32[32,1,128]{2,1,0:T(1,128)}, u32[]{:S(2)}, u32[]{:S(2)}) async-start(f32[32,1,128]{2,1,0:T(1,128)} %bitcast.135), calls=%async_computation.6 | async-start | bytes 32768 | tf_op jit(solution)/shard_map/all_to_all | solution.py:727
  487.2 84.9 %collective-permute-start.21 = (bf16[16,128,2048]{2,1,0:T(8,128)(2,1)}, bf16[16,128,2048]{2,1,0:T(8,128)(2,1)}, u32[]{:S(2)}, u32[]{:S(2)}) collective-permute-start(bf16[16,128,2048]{2,1,0:T(8,128)(2,1)} %shard_map.143), channel_id=1, source_target_pairs={{0,4},{4,0},{8,12},{12,8},{1,5},{5,1},{9,13},{13,9},{2,6},{6,2},{1... | collective-permute-start | bytes 25165832 | tf_op jit(solution)/shard_map/ppermute | solution.py:32
  487.4 54.0 %all-to-all-start.7 = ((bf16[4,512,512]{2,1,0:T(8,128)(2,1)}), bf16[4,512,512]{2,1,0:T(8,128)(2,1)}, u32[]{:S(2)}, u32[]{:S(2)}) async-start(bf16[4,512,512]{2,1,0:T(8,128)(2,1)} %bitcast.438), calls=%async_computation.7 | async-start | bytes 4194304 | tf_op jit(solution)/shard_map/all_to_all | solution.py:499
  498.4 58.1 %collective-permute-start.20 = (bf16[2,4,128,1024]{3,2,1,0:T(8,128)(2,1)}, bf16[2,4,128,1024]{3,2,1,0:T(8,128)(2,1)}, u32[]{:S(2)}, u32[]{:S(2)}) collective-permute-start(bf16[2,4,128,1024]{3,2,1,0:T(8,128)(2,1)} %get-tuple-element.205), channel_id=1, source_target_pairs={{0,16},{16,0},{1,17},{17,1},{2,18},{18,2},{3,19},{19,3},{4,20},{20... | collective-permute-start | bytes 6291464 | tf_op jit(solution)/shard_map/ppermute | solution.py:32
  505.7 50.9 %collective-permute-start.19 = (bf16[2,4,128,1024]{3,2,1,0:T(8,128)(2,1)}, bf16[2,4,128,1024]{3,2,1,0:T(8,128)(2,1)}, u32[]{:S(2)}, u32[]{:S(2)}) collective-permute-start(bf16[2,4,128,1024]{3,2,1,0:T(8,128)(2,1)} %get-tuple-element.207), channel_id=1, source_target_pairs={{0,8},{4,12},{8,0},{12,4},{1,9},{5,13},{9,1},{13,5},{2,10},{6,14},... | collective-permute-start | bytes 6291464 | tf_op jit(solution)/shard_map/ppermute | solution.py:32
  552.1 52.4 %all-to-all-start.8 = ((bf16[4,512,512]{2,1,0:T(8,128)(2,1)}), bf16[4,512,512]{2,1,0:T(8,128)(2,1)}, u32[]{:S(2)}, u32[]{:S(2)}) async-start(bf16[4,512,512]{2,1,0:T(8,128)(2,1)} %bitcast.437), calls=%async_computation.8 | async-start | bytes 4194304 | tf_op jit(solution)/shard_map/all_to_all | solution.py:499
  558.7 25.6 %collective-permute-start.23 = (bf16[4,128,1024]{2,1,0:T(8,128)(2,1)S(1)}, bf16[4,128,1024]{2,1,0:T(8,128)(2,1)S(1)}, u32[]{:S(2)}, u32[]{:S(2)}) collective-permute-start(bf16[4,128,1024]{2,1,0:T(8,128)(2,1)S(1)} %fusion.40), channel_id=1, source_target_pairs={{0,8},{4,12},{8,0},{12,4},{1,9},{5,13},{9,1},{13,5},{2,10},{6,14},... | collective-permute-start | bytes 3145736 | tf_op jit(solution)/shard_map/ppermute | solution.py:32
  561.9 24.2 %collective-permute-start.22 = (bf16[4,128,1024]{2,1,0:T(8,128)(2,1)S(1)}, bf16[4,128,1024]{2,1,0:T(8,128)(2,1)S(1)}, u32[]{:S(2)}, u32[]{:S(2)}) collective-permute-start(bf16[4,128,1024]{2,1,0:T(8,128)(2,1)S(1)} %fusion.39), channel_id=1, source_target_pairs={{0,16},{16,0},{1,17},{17,1},{2,18},{18,2},{3,19},{19,3},{4,20},{20... | collective-permute-start | bytes 3145736 | tf_op jit(solution)/shard_map/ppermute | solution.py:32
  604.5 52.1 %all-to-all-start.9 = ((bf16[4,128,2048]{2,1,0:T(8,128)(2,1)}), bf16[4,128,2048]{2,1,0:T(8,128)(2,1)S(1)}, u32[]{:S(2)}, u32[]{:S(2)}) async-start(bf16[4,128,2048]{2,1,0:T(8,128)(2,1)} %pad_maximum_fusion.10), calls=%async_computation.9 | async-start | bytes 4194304 | tf_op jit(solution)/shard_map/all_to_all | solution.py:499
  608.3 47.0 %collective-permute-start.24 = (bf16[2,4,128,1024]{3,2,1,0:T(8,128)(2,1)}, bf16[2,4,128,1024]{3,2,1,0:T(8,128)(2,1)}, u32[]{:S(2)}, u32[]{:S(2)}) collective-permute-start(bf16[2,4,128,1024]{3,2,1,0:T(8,128)(2,1)} %get-tuple-element.112), channel_id=1, source_target_pairs={{0,8},{4,12},{8,0},{12,4},{1,9},{5,13},{9,1},{13,5},{2,10},{6,14},... | collective-permute-start | bytes 6291464 | tf_op jit(solution)/shard_map/ppermute | solution.py:32
  610.0 46.6 %collective-permute-start.25 = (bf16[2,4,128,1024]{3,2,1,0:T(8,128)(2,1)}, bf16[2,4,128,1024]{3,2,1,0:T(8,128)(2,1)}, u32[]{:S(2)}, u32[]{:S(2)}) collective-permute-start(bf16[2,4,128,1024]{3,2,1,0:T(8,128)(2,1)} %get-tuple-element.113), channel_id=1, source_target_pairs={{0,16},{16,0},{1,17},{17,1},{2,18},{18,2},{3,19},{19,3},{4,20},{20... | collective-permute-start | bytes 6291464 | tf_op jit(solution)/shard_map/ppermute | solution.py:32
  623.0 34.0 %copy-start.37 = (f32[128,2048]{1,0:T(8,128)S(1)}, f32[128,2048]{1,0:T(8,128)}, u32[]{:S(2)}) copy-start(f32[128,2048]{1,0:T(8,128)} %copy-done.36) | copy-start | bytes 3145732
  623.0 34.0 %copy-start.90 = (f32[2048]{0:T(1024)S(1)}, f32[2048]{0:T(1024)}, u32[]{:S(2)}) copy-start(f32[2048]{0:T(1024)} %copy-done.89) | copy-start | bytes 24580
  623.0 34.0 %copy-start.99 = (f32[128]{0:T(128)S(1)}, f32[128]{0:T(128)}, u32[]{:S(2)}) copy-start(f32[128]{0:T(128)} %copy-done.98) | copy-start | bytes 1540
  660.2 12.2 %collective-permute-start.29 = (bf16[128,2048]{1,0:T(8,128)(2,1)S(1)}, bf16[128,2048]{1,0:T(8,128)(2,1)S(1)}, u32[]{:S(2)}, u32[]{:S(2)}) collective-permute-start(bf16[128,2048]{1,0:T(8,128)(2,1)S(1)} %get-tuple-element.198), channel_id=1, source_target_pairs={{0,8},{4,12},{8,0},{12,4},{1,9},{5,13},{9,1},{13,5},{2,10},{6,14},... | collective-permute-start | bytes 1572872 | tf_op jit(solution)/shard_map/ppermute | solution.py:32
  661.2 20.1 %collective-permute-start.28 = (bf16[128,2048]{1,0:T(8,128)(2,1)S(1)}, bf16[128,2048]{1,0:T(8,128)(2,1)}, u32[]{:S(2)}, u32[]{:S(2)}) collective-permute-start(bf16[128,2048]{1,0:T(8,128)(2,1)S(1)} %get-tuple-element.198), channel_id=1, source_target_pairs={{0,4},{4,0},{8,12},{12,8},{1,5},{5,1},{9,13},{13,9},{2,6},{6,2},{1... | collective-permute-start | bytes 1572872 | tf_op jit(solution)/shard_map/ppermute | solution.py:32
  661.2 53.6 %all-to-all-start.10 = ((bf16[4,512,512]{2,1,0:T(8,128)(2,1)}), bf16[4,512,512]{2,1,0:T(8,128)(2,1)S(1)}, u32[]{:S(2)}, u32[]{:S(2)}) async-start(bf16[4,512,512]{2,1,0:T(8,128)(2,1)} %bitcast.436), calls=%async_computation.10 | async-start | bytes 4194304 | tf_op jit(solution)/shard_map/all_to_all | solution.py:499
  672.4 8.8 collective-permute-start.30
  675.5 29.5 %collective-permute-start.27 = (bf16[4,128,1024]{2,1,0:T(8,128)(2,1)}, bf16[4,128,1024]{2,1,0:T(8,128)(2,1)}, u32[]{:S(2)}, u32[]{:S(2)}) collective-permute-start(bf16[4,128,1024]{2,1,0:T(8,128)(2,1)} %fusion.44), channel_id=1, source_target_pairs={{0,8},{4,12},{8,0},{12,4},{1,9},{5,13},{9,1},{13,5},{2,10},{6,14},... | collective-permute-start | bytes 3145736 | tf_op jit(solution)/shard_map/ppermute | solution.py:32
  679.8 25.4 %collective-permute-start.26 = (bf16[4,128,1024]{2,1,0:T(8,128)(2,1)}, bf16[4,128,1024]{2,1,0:T(8,128)(2,1)}, u32[]{:S(2)}, u32[]{:S(2)}) collective-permute-start(bf16[4,128,1024]{2,1,0:T(8,128)(2,1)} %fusion.43), channel_id=1, source_target_pairs={{0,16},{16,0},{1,17},{17,1},{2,18},{18,2},{3,19},{19,3},{4,20},{20... | collective-permute-start | bytes 3145736 | tf_op jit(solution)/shard_map/ppermute | solution.py:32
  704.5 26.4 %collective-permute-start.31 = (bf16[1,4,4,64,512]{4,3,1,2,0:T(8,128)(2,1)}, bf16[1,4,4,64,512]{4,3,1,2,0:T(8,128)(2,1)}, u32[]{:S(2)}, u32[]{:S(2)}) collective-permute-start(bf16[1,4,4,64,512]{4,3,1,2,0:T(8,128)(2,1)} %fusion.46), channel_id=1, source_target_pairs={{0,16},{16,0},{1,17},{17,1},{2,18},{18,2},{3,19},{19,3},{4,20},{20... | collective-permute-start | bytes 3145736 | tf_op jit(solution)/shard_map/ppermute | solution.py:32
  716.0 52.5 %all-to-all-start.11 = ((bf16[4,128,2048]{2,1,0:T(8,128)(2,1)}), bf16[4,128,2048]{2,1,0:T(8,128)(2,1)}, u32[]{:S(2)}, u32[]{:S(2)}) async-start(bf16[4,128,2048]{2,1,0:T(8,128)(2,1)} %pad_maximum_fusion.12), calls=%async_computation.11 | async-start | bytes 4194304 | tf_op jit(solution)/shard_map/all_to_all | solution.py:499
  723.2 28.9 %collective-permute-start.32 = (bf16[1,4,64,2048]{3,2,1,0:T(8,128)(2,1)}, bf16[1,4,64,2048]{3,2,1,0:T(8,128)(2,1)}, u32[]{:S(2)}, u32[]{:S(2)}) collective-permute-start(bf16[1,4,64,2048]{3,2,1,0:T(8,128)(2,1)} %fusion.35), channel_id=1, source_target_pairs={{0,16},{16,0},{1,17},{17,1},{2,18},{18,2},{3,19},{19,3},{4,20},{20... | collective-permute-start | bytes 3145736 | tf_op jit(solution)/shard_map/ppermute | solution.py:32
  768.5 28.7 %all-to-all-start.12 = ((bf16[4,64,2048]{2,1,0:T(8,128)(2,1)}), bf16[4,64,2048]{2,1,0:T(8,128)(2,1)S(1)}, u32[]{:S(2)}, u32[]{:S(2)}) async-start(bf16[4,64,2048]{2,1,0:T(8,128)(2,1)} %fusion.37), calls=%async_computation.12 | async-start | bytes 2097152 | tf_op jit(solution)/shard_map/all_to_all | solution.py:499
  777.8 23.7 %collective-permute-start.33 = (bf16[2,128,2048]{2,1,0:T(8,128)(2,1)S(1)}, bf16[2,128,2048]{2,1,0:T(8,128)(2,1)}, u32[]{:S(2)}, u32[]{:S(2)}) collective-permute-start(bf16[2,128,2048]{2,1,0:T(8,128)(2,1)S(1)} %fusion.48), channel_id=1, source_target_pairs={{0,4},{4,0},{8,12},{12,8},{1,5},{5,1},{9,13},{13,9},{2,6},{6,2},{1... | collective-permute-start | bytes 3145736 | tf_op jit(solution)/shard_map/ppermute | solution.py:32
  783.0 47.1 %collective-permute-start.35 = (bf16[1,4,4,64,1024]{4,3,1,2,0:T(8,128)(2,1)}, bf16[1,4,4,64,1024]{4,3,1,2,0:T(8,128)(2,1)}, u32[]{:S(2)}, u32[]{:S(2)}) collective-permute-start(bf16[1,4,4,64,1024]{4,3,1,2,0:T(8,128)(2,1)} %dynamic-slice_convert_fusion), channel_id=1, source_target_pairs={{0,16},{16,0},{1,17},{17,1},{2,18},{18,2},{3,19},{19,3},{4,20},{20... | collective-permute-start | bytes 6291464 | tf_op jit(solution)/shard_map/ppermute | solution.py:32
  797.3 29.5 %all-to-all-start.13 = ((bf16[4,4,64,512]{3,2,1,0:T(8,128)(2,1)}), bf16[4,4,64,512]{3,2,1,0:T(8,128)(2,1)}, u32[]{:S(2)}, u32[]{:S(2)}) async-start(bf16[4,4,64,512]{3,2,1,0:T(8,128)(2,1)} %fusion.36), calls=%async_computation.13 | async-start | bytes 2097152 | tf_op jit(solution)/shard_map/all_to_all | solution.py:499
  804.7 13.2 %collective-permute-start.34 = (bf16[128,2048]{1,0:T(8,128)(2,1)}, bf16[128,2048]{1,0:T(8,128)(2,1)}, u32[]{:S(2)}, u32[]{:S(2)}) collective-permute-start(bf16[128,2048]{1,0:T(8,128)(2,1)} %fusion.54), channel_id=1, source_target_pairs={{0,8},{4,12},{8,0},{12,4},{1,9},{5,13},{9,1},{13,5},{2,10},{6,14},... | collective-permute-start | bytes 1572872 | tf_op jit(solution)/shard_map/ppermute | solution.py:32
  826.8 12.1 %all-to-all-start.16 = ((f32[32,1,1280]{2,1,0:T(1,128)}), f32[32,1,1280]{2,1,0:T(1,128)S(1)}, u32[]{:S(2)}, u32[]{:S(2)}) async-start(f32[32,1,1280]{2,1,0:T(1,128)} %copy.187), calls=%async_computation.16 | async-start | bytes 327680 | tf_op jit(solution)/shard_map/all_to_all | solution.py:829
  838.9 52.6 %all-to-all-start.14 = ((bf16[4,4,64,1024]{3,2,1,0:T(8,128)(2,1)}), bf16[4,4,64,1024]{3,2,1,0:T(8,128)(2,1)}, u32[]{:S(2)}, u32[]{:S(2)}) async-start(bf16[4,4,64,1024]{3,2,1,0:T(8,128)(2,1)} %fusion.12), calls=%async_computation.14 | async-start | bytes 4194304 | tf_op jit(solution)/shard_map/all_to_all | solution.py:499
  894.5 16.3 %all-to-all-start.15 = ((bf16[4,64,1536]{2,1,0:T(8,128)(2,1)}), bf16[4,64,1536]{2,1,0:T(8,128)(2,1)}, u32[]{:S(2)}, u32[]{:S(2)}) async-start(bf16[4,64,1536]{2,1,0:T(8,128)(2,1)} %pad_maximum_fusion.16), calls=%async_computation.15 | async-start | bytes 1572864 | tf_op jit(solution)/shard_map/all_to_all | solution.py:816
  (98 other events, 740.2 us)
Sparse Core Ops, SparseCore 0:
  36.6 125.9 all-gather.6
  230.1 167.1 all-gather.8
